TPU v7x, 128 devices: a whole 4x4x4 slice. The times are simulated.
128 devices in a mesh: dp: 4 (over z), expert: 8 (over y, core), tensor: 4 (over x).
Axes of the slice: x: 4, y: 4, z: 4, core: 2. Of those that a mesh axis runs over, the one named last changes fastest.
Arguments:
- tokens: bfloat16 [5120, 2048], P(('dp', 'expert')), may hold values from -6 to 6
- cotangent: bfloat16 [5120, 2048], P(('dp', 'expert')), may hold values from -6 to 6
- attn_gain: bfloat16 [2048], replicated, may hold values from 0.5 to 1.5
- mlp_gain: bfloat16 [2048], replicated, may hold values from 0.5 to 1.5
- attn_router: bfloat16 [2048, 8], P(('dp', 'expert')), may hold values from -0.09375 to 0.09375
- key_value_weight: bfloat16 [2048, 2, 2048], P(('dp', 'expert'), None, 'tensor'), may hold values from -0.125 to 0.125
- query_matrix: bfloat16 [2048, 8, 2048], P(('dp', 'expert'), None, 'tensor'), may hold values from -0.125 to 0.125
- output_matrix: bfloat16 [2048, 8, 2048], P(('dp', 'expert'), None, 'tensor'), may hold values from -0.75 to 0.75
- mlp_router: bfloat16 [2048, 8], P(('dp', 'expert')), may hold values from -0.09375 to 0.09375
- gate_up_weight: bfloat16 [8, 2048, 2, 5632], P('expert', 'dp', None, 'tensor'), may hold values from -0.125 to 0.125
- down_weight: bfloat16 [8, 5632, 2048], P('expert', 'tensor', 'dp'), may hold values from -0.15625 to 0.15625
- attn_routes: int32 [5120, 2], P(('dp', 'expert')), may hold values from 0 to 7, all different within a row
- mlp_routes: int32 [5120, 2], P(('dp', 'expert')), may hold values from 0 to 7, all different within a row
- priority: int32 [32, 160], P(('dp', 'expert')), may hold values from 0 to 159, each once within a row
- segments: int32 [5120], replicated, may hold values from 0 to 2, as said below
Outputs:
- output: bfloat16 [5120, 2048], P(('dp', 'expert'))
- input_grad: bfloat16 [5120, 2048], P(('dp', 'expert'))
- attn_gain_grad: float32 [2048], P(('dp', 'expert'))
- mlp_gain_grad: float32 [2048], P(('dp', 'expert'))
- attn_router_grad: float32 [2048, 8], P(('dp', 'expert'))
- kv_grad: float32 [2048, 2, 2048], P(('dp', 'expert'), None, 'tensor')
- query_grad: float32 [2048, 8, 2048], P(('dp', 'expert'), None, 'tensor')
- out_grad: float32 [2048, 8, 2048], P(('dp', 'expert'), None, 'tensor')
- mlp_router_grad: float32 [2048, 8], P(('dp', 'expert'))
- gate_up_grad: float32 [8, 2048, 2, 5632], P('expert', 'dp', None, 'tensor')
- down_grad: float32 [8, 5632, 2048], P('expert', 'tensor', 'dp')
Inputs may be any that keep to these rules, and one draw needn't show every extreme that they name: `attn_routes`: each token names two different attention experts. `mlp_routes`: each token names two different feed-forward experts. `priority`: each row is an order of the 160 tokens of one group. `segments`: each sequence of 1280 tokens holds three documents numbered 0, 1, 2 in order; the first ends within the sequence's first 40 tokens and the last begins within its last 40 tokens.
All inputs are finite; a program needn't handle non-finite values.
Results may differ from a plain program's by a relative error of at most 0.025.
Values may be sent and summed in bfloat16 or wider, within the bound.
No kernel may reach another device: no remote copies, remote signals or barrier semaphores. Data moves between devices by JAX's collectives and lax.ppermute only.
A program may use at most 320 MiB of HBM per device.

v0:
```python
import jax
import jax.numpy as jnp
from jax import lax
from jax.sharding import PartitionSpec as P

MODEL_WIDTH = 2048
HEAD_SIZE = 128
ATTENTION_EXPERTS = 8
WINDOW = 1024


NORM_EPS = 1e-06


def side_by_side(arrays, axis, dim, along):
    columns = [a.reshape(*a.shape[:along], -1) for a in arrays]
    both = jnp.concatenate(columns, axis=along)
    result, at, gathered = (lax.all_gather(both, axis, axis=dim, tiled=True), 0, [])
    for a, column in zip(arrays, columns):
        piece = result[..., at : at + column.shape[along]]
        gathered.append(piece.reshape(*piece.shape[:along], *a.shape[along:]))
        at += column.shape[along]
    return tuple(gathered)


def in_one_piece(arrays, axis, dim, along):
    ends, at = ([], 0)
    for a in arrays[:-1]:
        at += a.shape[along]
        ends.append(at)
    both = jnp.concatenate(arrays, axis=along)
    return tuple(jnp.split(lax.all_gather(both, axis, axis=dim, tiled=True), ends, axis=along))


def copy_for_each(shard, axis):
    copies = jnp.broadcast_to(shard, (lax.axis_size(axis), *shard.shape))
    return lax.all_to_all(copies, axis, split_axis=0, concat_axis=0, tiled=True)


def taken_together(shard, axis):
    return copy_for_each(shard, axis).sum(axis=0)


def split_up(shard, dim, length):
    before, after = (shard.shape[:dim], shard.shape[dim + 1 :])
    return jnp.moveaxis(shard.reshape(*before, length, -1, *after), dim, 0)


def sum_together(arrays, axis, dims):
    length = lax.axis_size(axis)
    blocks = [split_up(a, dim, length) for a, dim in zip(arrays, dims)]
    lines = jnp.concatenate([b.reshape(length, -1) for b in blocks], axis=1)
    span = max(16, -(-lines.shape[1] // 1024) * 8)
    lines = jnp.pad(lines, ((0, 0), (0, span * 128 - lines.shape[1]))).reshape(-1, 128)
    line, at, gathered = (lax.psum_scatter(lines, axis, tiled=True).reshape(-1), 0, [])
    for b in blocks:
        part = b[0]
        gathered.append(line[at : at + part.size].reshape(part.shape))
        at += part.size
    return tuple(gathered)


def over_copies(shard, axis):
    return copy_for_each(shard, axis).astype(jnp.float32).sum(axis=0)


def rms_scale(values):
    return lax.rsqrt(jnp.mean(values * values, axis=-1, keepdims=True) + NORM_EPS)


def apply_rotary(heads, cosine_table, sine_table):
    half_width = heads.shape[-1] // 2
    first_half = heads[..., :half_width]
    second_half = heads[..., half_width:]
    return jnp.concatenate(
        [
            first_half * cosine_table - second_half * sine_table,
            second_half * cosine_table + first_half * sine_table,
        ],
        axis=-1,
    )


def rotary_back(heads, cosine_table, sine_table):
    half_width = heads.shape[-1] // 2
    first_half = heads[..., :half_width]
    second_half = heads[..., half_width:]
    return jnp.concatenate(
        [
            first_half * cosine_table + second_half * sine_table,
            second_half * cosine_table - first_half * sine_table,
        ],
        axis=-1,
    )


def pair_gates(logits, routes):
    chosen = jnp.take_along_axis(logits, routes, axis=1)
    row_max = jnp.max(chosen, axis=1, keepdims=True)
    weights = jnp.exp(chosen - row_max)
    return weights / jnp.sum(weights, axis=1, keepdims=True)


def gate_back(gates, grad_gates, routes, count):
    inner = gates * (grad_gates - jnp.sum(gates * grad_gates, axis=1, keepdims=True))
    choose = (routes[:, :, None] == jnp.arange(count, dtype=jnp.int32)[None, None, :]).astype(
        jnp.float32
    )
    return jnp.sum(inner[:, :, None] * choose, axis=1)


def norm_back(grad_normed, values, factor, gain):
    gain_part = jnp.sum(grad_normed * values * factor, axis=0)
    inner = grad_normed * gain
    grad_values = factor * inner - values * factor * factor * factor * jnp.mean(
        inner * values, axis=-1, keepdims=True
    )
    return (grad_values, gain_part)


def gather_attention(attn_router, key_value_weight, query_matrix, output_matrix, mlp_router):
    return side_by_side(
        (attn_router, key_value_weight, query_matrix, output_matrix, mlp_router),
        ("dp", "expert"),
        0,
        1,
    )


def gather_experts(gate_up_weight, down_weight):
    return (
        lax.all_gather(gate_up_weight, "dp", axis=1, tiled=True),
        lax.all_gather(down_weight, "dp", axis=2, tiled=True),
    )


def body(
    tokens,
    cotangent,
    attn_gain,
    mlp_gain,
    attn_router,
    key_value_weight,
    query_matrix,
    output_matrix,
    mlp_router,
    gate_up_weight,
    down_weight,
    attn_routes,
    mlp_routes,
    priority,
    segments,
):
    row_count = tokens.shape[0]
    experts = lax.axis_size("expert")
    seq_len = row_count * experts
    capacity = (10 * row_count + 4 * experts - 1) // (4 * experts)
    width = key_value_weight.shape[2]
    local_heads = width // HEAD_SIZE
    contract_rows = (((0,), (0,)), ((), ()))
    contract_last = (((1,), (1,)), ((), ()))
    router_a, kv_full, query_full, out_full, router_m = gather_attention(
        attn_router, key_value_weight, query_matrix, output_matrix, mlp_router
    )
    gate_up_full, down_full = gather_experts(gate_up_weight, down_weight)
    gain_a = attn_gain.astype(jnp.float32)
    gain_m = mlp_gain.astype(jnp.float32)
    x_float = tokens.astype(jnp.float32)
    factor_a = rms_scale(x_float)
    xn1 = (x_float * factor_a * gain_a).astype(jnp.bfloat16)
    first_row = lax.axis_index("expert") * row_count
    place = first_row + jnp.arange(row_count, dtype=jnp.int32)
    inverse = 10000.0 ** (-(jnp.arange(HEAD_SIZE // 2).astype(jnp.float32) * 2.0 / HEAD_SIZE))
    angle = place.astype(jnp.float32)[:, None] * inverse[None, :]
    cosine_table = jnp.cos(angle)[:, None, :]
    sine_table = jnp.sin(angle)[:, None, :]
    key_value_projected = jnp.dot(
        xn1, kv_full.reshape(MODEL_WIDTH, 2 * width), preferred_element_type=jnp.float32
    ).reshape(row_count, 2, width)
    key_head_rows = apply_rotary(
        key_value_projected[:, 0].reshape(row_count, local_heads, HEAD_SIZE),
        cosine_table,
        sine_table,
    ).astype(jnp.bfloat16)
    value_head_rows = (
        key_value_projected[:, 1].reshape(row_count, local_heads, HEAD_SIZE).astype(jnp.bfloat16)
    )
    all_keys, all_values = in_one_piece((key_head_rows, value_head_rows), "expert", 0, 1)
    q_all = jnp.dot(
        xn1,
        query_full.reshape(MODEL_WIDTH, ATTENTION_EXPERTS * width),
        preferred_element_type=jnp.float32,
    ).reshape(row_count, ATTENTION_EXPERTS, width)
    query_selected = jnp.take_along_axis(q_all, attn_routes[:, :, None], axis=1)
    query_rows = (
        apply_rotary(
            query_selected.reshape(row_count, 2 * local_heads, HEAD_SIZE), cosine_table, sine_table
        )
        .reshape(row_count, 2, local_heads, HEAD_SIZE)
        .astype(jnp.bfloat16)
    )
    sequence = lax.dynamic_slice_in_dim(segments, lax.axis_index("dp") * seq_len, seq_len)
    own_segments = lax.dynamic_slice_in_dim(sequence, first_row, row_count)
    spots = jnp.arange(seq_len, dtype=jnp.int32)
    allowed = (
        (spots[None, :] <= place[:, None])
        & (place[:, None] - spots[None, :] < WINDOW)
        & (own_segments[:, None] == sequence[None, :])
    )
    scale = HEAD_SIZE ** (-0.5)

    def scores_of(query_heads):
        raw_scores = (
            jnp.einsum("sjhd,khd->jhsk", query_heads, all_keys, preferred_element_type=jnp.float32)
            * scale
        )
        return jnp.where(allowed[None, None], raw_scores, -1e30)

    score = scores_of(query_rows)
    row_max = jnp.max(score, axis=-1, keepdims=True)
    weights = jnp.exp(score - row_max)
    totals = jnp.sum(weights, axis=-1, keepdims=True)
    prob = weights / totals
    log_total = row_max + jnp.log(totals)
    attended_rows = jnp.einsum(
        "jhsk,khd->sjhd", prob.astype(jnp.bfloat16), all_values, preferred_element_type=jnp.float32
    ).reshape(row_count, 2, width)
    gate_a = pair_gates(jnp.dot(xn1, router_a, preferred_element_type=jnp.float32), attn_routes)
    pick_a = (
        attn_routes[:, :, None] == jnp.arange(ATTENTION_EXPERTS, dtype=jnp.int32)[None, None, :]
    ).astype(jnp.float32)
    mixed = jnp.einsum("sje,sjh->seh", pick_a * gate_a[:, :, None], attended_rows).astype(
        jnp.bfloat16
    )
    partial_branch = lax.dot_general(
        mixed.reshape(row_count, ATTENTION_EXPERTS * width),
        out_full.reshape(MODEL_WIDTH, ATTENTION_EXPERTS * width),
        contract_last,
        preferred_element_type=jnp.float32,
    )
    branch = taken_together(partial_branch, "tensor")
    hidden = x_float + branch
    factor_m = rms_scale(hidden)
    xn2 = (hidden * factor_m * gain_m).astype(jnp.bfloat16)
    gate_m = pair_gates(jnp.dot(xn2, router_m, preferred_element_type=jnp.float32), mlp_routes)
    ranking = priority[0]
    at_rank = (
        jnp.zeros((row_count,), jnp.int32).at[ranking].set(jnp.arange(row_count, dtype=jnp.int32))
    )
    ordered = mlp_routes[at_rank].reshape(2 * row_count)
    onehot = (ordered[:, None] == jnp.arange(experts, dtype=jnp.int32)[None, :]).astype(jnp.int32)
    earlier = jnp.cumsum(onehot, axis=0) - onehot
    slots = jnp.sum(earlier * onehot, axis=1).reshape(row_count, 2)[ranking]
    kept = slots < capacity
    slot_total = experts * capacity
    dest = jnp.where(kept, mlp_routes * capacity + slots, slot_total).reshape(-1)
    fetch = jnp.minimum(dest, slot_total - 1)
    keep_float = kept.astype(jnp.float32)
    pair_rows = jnp.broadcast_to(xn2[:, None, :], (row_count, 2, MODEL_WIDTH)).reshape(
        2 * row_count, MODEL_WIDTH
    )
    send_rows = (
        jnp.zeros((slot_total + 1, MODEL_WIDTH), jnp.bfloat16).at[dest].set(pair_rows)[:slot_total]
    )
    received = lax.all_to_all(
        send_rows.reshape(experts, capacity, MODEL_WIDTH),
        "expert",
        split_axis=0,
        concat_axis=0,
        tiled=True,
    ).reshape(slot_total, MODEL_WIDTH)
    w_pair = gate_up_full[0].reshape(MODEL_WIDTH, -1)
    w_back = down_full[0]
    half_width = w_pair.shape[1] // 2
    gate_up = jnp.dot(received, w_pair, preferred_element_type=jnp.float32)
    gate_part = gate_up[:, :half_width]
    activated = (gate_part * jax.nn.sigmoid(gate_part) * gate_up[:, half_width:]).astype(
        jnp.bfloat16
    )
    expert_part = jnp.dot(activated, w_back, preferred_element_type=jnp.float32)
    expert_out = lax.psum(expert_part.astype(jnp.bfloat16), "tensor")
    returned = lax.all_to_all(
        expert_out.reshape(experts, capacity, MODEL_WIDTH),
        "expert",
        split_axis=0,
        concat_axis=0,
        tiled=True,
    ).reshape(slot_total, MODEL_WIDTH)
    fetched = returned[fetch].reshape(row_count, 2, MODEL_WIDTH).astype(jnp.float32)
    weight_m = gate_m * keep_float
    output = hidden + weight_m[:, 0:1] * fetched[:, 0] + weight_m[:, 1:2] * fetched[:, 1]
    router_a, kv_full, query_full, out_full, router_m = gather_attention(
        attn_router, key_value_weight, query_matrix, output_matrix, mlp_router
    )
    gate_up_full, down_full = gather_experts(gate_up_weight, down_weight)
    w_pair = gate_up_full[0].reshape(MODEL_WIDTH, -1)
    w_back = down_full[0]
    grad_out = cotangent.astype(jnp.float32)
    grad_gate_m = jnp.sum(grad_out[:, None, :] * fetched, axis=-1) * keep_float
    grad_pairs = (
        (weight_m[:, :, None] * grad_out[:, None, :])
        .astype(jnp.bfloat16)
        .reshape(2 * row_count, MODEL_WIDTH)
    )
    grad_send = (
        jnp.zeros((slot_total + 1, MODEL_WIDTH), jnp.bfloat16).at[dest].set(grad_pairs)[:slot_total]
    )
    grad_received = lax.all_to_all(
        grad_send.reshape(experts, capacity, MODEL_WIDTH),
        "expert",
        split_axis=0,
        concat_axis=0,
        tiled=True,
    ).reshape(slot_total, MODEL_WIDTH)
    grad_act = lax.dot_general(
        grad_received, w_back, contract_last, preferred_element_type=jnp.float32
    )
    up_back_part = gate_up[:, half_width:]
    sigmoid_gate = jax.nn.sigmoid(gate_part)
    silu_gate = gate_part * sigmoid_gate
    grad_gate_up = jnp.concatenate(
        [
            grad_act * up_back_part * sigmoid_gate * (1.0 + gate_part * (1.0 - sigmoid_gate)),
            grad_act * silu_gate,
        ],
        axis=1,
    ).astype(jnp.bfloat16)
    grad_rows_part = lax.dot_general(
        grad_gate_up, w_pair, contract_last, preferred_element_type=jnp.float32
    )
    grad_w_pair = lax.dot_general(
        received, grad_gate_up, contract_rows, preferred_element_type=jnp.float32
    )
    grad_w_back = lax.dot_general(
        activated, grad_received, contract_rows, preferred_element_type=jnp.float32
    )
    grad_rows = lax.psum(grad_rows_part.astype(jnp.bfloat16), "tensor")
    grad_returned = lax.all_to_all(
        grad_rows.reshape(experts, capacity, MODEL_WIDTH),
        "expert",
        split_axis=0,
        concat_axis=0,
        tiled=True,
    ).reshape(slot_total, MODEL_WIDTH)
    grad_fetched = (
        grad_returned[fetch].reshape(row_count, 2, MODEL_WIDTH).astype(jnp.float32)
        * keep_float[:, :, None]
    )
    gate_up_grad, down_grad = (
        lax.psum_scatter(
            grad_w_pair.reshape(1, MODEL_WIDTH, 2, half_width).astype(jnp.bfloat16),
            "dp",
            scatter_dimension=1,
            tiled=True,
        ).astype(jnp.float32),
        lax.psum_scatter(
            grad_w_back.reshape(1, half_width, MODEL_WIDTH).astype(jnp.bfloat16),
            "dp",
            scatter_dimension=2,
            tiled=True,
        ).astype(jnp.float32),
    )
    grad_logit_m = gate_back(gate_m, grad_gate_m, mlp_routes, experts)
    grad_xn2 = (
        grad_fetched[:, 0]
        + grad_fetched[:, 1]
        + jnp.dot(grad_logit_m, router_m.astype(jnp.float32).T)
    )
    grad_hidden_norm, gain_m_part = norm_back(grad_xn2, hidden, factor_m, gain_m)
    grad_hidden = grad_out + grad_hidden_norm
    grad_branch = grad_hidden.astype(jnp.bfloat16)
    grad_mixed = jnp.dot(
        grad_branch,
        out_full.reshape(MODEL_WIDTH, ATTENTION_EXPERTS * width),
        preferred_element_type=jnp.float32,
    ).reshape(row_count, ATTENTION_EXPERTS, width)
    grad_pick = jnp.take_along_axis(grad_mixed, attn_routes[:, :, None], axis=1)
    grad_gate_part = jnp.sum(grad_pick * attended_rows, axis=-1)
    grad_attended = (
        (gate_a[:, :, None] * grad_pick)
        .astype(jnp.bfloat16)
        .reshape(row_count, 2, local_heads, HEAD_SIZE)
    )
    score_back = scores_of(query_rows)
    prob_back = jnp.exp(score_back - log_total)
    grad_prob = jnp.einsum(
        "sjhd,khd->jhsk", grad_attended, all_values, preferred_element_type=jnp.float32
    )
    row_delta = jnp.sum(prob_back * grad_prob, axis=-1, keepdims=True)
    grad_score = (prob_back * (grad_prob - row_delta)).astype(jnp.bfloat16)
    grad_query = (
        jnp.einsum("jhsk,khd->sjhd", grad_score, all_keys, preferred_element_type=jnp.float32)
        * scale
    )
    grad_keys = (
        jnp.einsum("jhsk,sjhd->khd", grad_score, query_rows, preferred_element_type=jnp.float32)
        * scale
    )
    grad_values = jnp.einsum(
        "jhsk,sjhd->khd",
        prob_back.astype(jnp.bfloat16),
        grad_attended,
        preferred_element_type=jnp.float32,
    )
    own_grad_keys, own_grad_values = tuple(
        (
            part.astype(jnp.float32)
            for part in sum_together(
                (grad_keys.astype(jnp.bfloat16), grad_values.astype(jnp.bfloat16)), "expert", (0, 0)
            )
        )
    )
    grad_key_rows = rotary_back(own_grad_keys, cosine_table, sine_table).reshape(row_count, width)
    grad_kv = jnp.stack([grad_key_rows, own_grad_values.reshape(row_count, width)], axis=1).astype(
        jnp.bfloat16
    )
    grad_qpick = rotary_back(
        grad_query.reshape(row_count, 2 * local_heads, HEAD_SIZE), cosine_table, sine_table
    ).reshape(row_count, 2, width)
    grad_q_all = jnp.einsum("sje,sjh->seh", pick_a, grad_qpick).astype(jnp.bfloat16)
    grad_xn1_part = lax.dot_general(
        grad_q_all.reshape(row_count, ATTENTION_EXPERTS * width),
        query_full.reshape(MODEL_WIDTH, ATTENTION_EXPERTS * width),
        contract_last,
        preferred_element_type=jnp.float32,
    )
    grad_xn1_part = grad_xn1_part + lax.dot_general(
        grad_kv.reshape(row_count, 2 * width),
        kv_full.reshape(MODEL_WIDTH, 2 * width),
        contract_last,
        preferred_element_type=jnp.float32,
    )
    grad_xn1, grad_gate_a = (
        over_copies(grad_xn1_part.astype(jnp.bfloat16), "tensor").astype(jnp.float32),
        over_copies(grad_gate_part.astype(jnp.bfloat16), "tensor").astype(jnp.float32),
    )
    grad_logit_a = gate_back(gate_a, grad_gate_a, attn_routes, ATTENTION_EXPERTS)
    grad_xn1 = grad_xn1 + jnp.dot(grad_logit_a, router_a.astype(jnp.float32).T)
    grad_x_norm, gain_a_part = norm_back(grad_xn1, x_float, factor_a, gain_a)
    input_grad = (grad_hidden + grad_x_norm).astype(jnp.bfloat16)
    small_count = ATTENTION_EXPERTS + experts + 2
    filler_width = -small_count % 128
    flat_q = grad_q_all.reshape(row_count, ATTENTION_EXPERTS * width)
    flat_mixed = mixed.reshape(row_count, ATTENTION_EXPERTS * width)
    flat_kv = grad_kv.reshape(row_count, 2 * width)
    term_query = lax.dot_general(xn1, flat_q, contract_rows, preferred_element_type=jnp.float32)
    term_out = lax.dot_general(
        grad_branch, flat_mixed, contract_rows, preferred_element_type=jnp.float32
    )
    term_kv = lax.dot_general(xn1, flat_kv, contract_rows, preferred_element_type=jnp.float32)
    term_router_a = lax.dot_general(xn1.astype(jnp.float32), grad_logit_a, contract_rows)
    term_router_m = lax.dot_general(xn2.astype(jnp.float32), grad_logit_m, contract_rows)
    gain_terms = jnp.stack([gain_a_part, gain_m_part], axis=1)
    filler = jnp.zeros(
        (
            MODEL_WIDTH // lax.axis_size(("dp", "expert")) * lax.axis_size(("dp", "expert")),
            filler_width,
        ),
        jnp.float32,
    )
    summed = lax.psum_scatter(
        jnp.concatenate(
            [term_query, term_out, term_kv, term_router_a, term_router_m, gain_terms, filler],
            axis=1,
        ).astype(jnp.bfloat16),
        ("dp", "expert"),
        scatter_dimension=0,
        tiled=True,
    ).astype(jnp.float32)
    local_rows = summed.shape[0]
    span = ATTENTION_EXPERTS * width
    query_grad = summed[:, :span].reshape(local_rows, ATTENTION_EXPERTS, width)
    out_grad = summed[:, span : 2 * span].reshape(local_rows, ATTENTION_EXPERTS, width)
    kv_grad = summed[:, 2 * span : 2 * span + 2 * width].reshape(local_rows, 2, width)
    base = 2 * span + 2 * width
    attn_router_grad = summed[:, base : base + ATTENTION_EXPERTS]
    mlp_router_grad = summed[:, base + ATTENTION_EXPERTS : base + ATTENTION_EXPERTS + experts]
    attn_gain_grad = summed[:, base + ATTENTION_EXPERTS + experts]
    mlp_gain_grad = summed[:, base + ATTENTION_EXPERTS + experts + 1]
    return (
        output.astype(jnp.bfloat16),
        input_grad,
        attn_gain_grad,
        mlp_gain_grad,
        attn_router_grad,
        kv_grad,
        query_grad,
        out_grad,
        mlp_router_grad,
        gate_up_grad,
        down_grad,
    )


def solution(mesh):
    placed = (
        P(("dp", "expert"), None),
        P(("dp", "expert"), None),
        P(),
        P(),
        P(("dp", "expert"), None),
        P(("dp", "expert"), None, "tensor"),
        P(("dp", "expert"), None, "tensor"),
        P(("dp", "expert"), None, "tensor"),
        P(("dp", "expert"), None),
        P("expert", "dp", None, "tensor"),
        P("expert", "tensor", "dp"),
        P(("dp", "expert"), None),
        P(("dp", "expert"), None),
        P(("dp", "expert"), None),
        P(),
    )
    return jax.shard_map(
        body,
        mesh=mesh,
        in_specs=placed,
        out_specs=(
            P(("dp", "expert"), None),
            P(("dp", "expert"), None),
            P(("dp", "expert")),
            P(("dp", "expert")),
            P(("dp", "expert"), None),
            P(("dp", "expert"), None, "tensor"),
            P(("dp", "expert"), None, "tensor"),
            P(("dp", "expert"), None, "tensor"),
            P(("dp", "expert"), None),
            P("expert", "dp", None, "tensor"),
            P("expert", "tensor", "dp"),
        ),
        check_vma=False,
    )
```

profile of v0, /device:TPU:0, one launch (start us, length us, event | category | flops | bytes accessed | tf_op | source)
XLA Modules:
  0.0 982.1 jit_solution(5742271879554593242)
XLA Ops:
  13.8 128.1 %all-gather.5.cloned.1.call-done = bf16[2048,9232]{1,0:T(8,128)(2,1)} async-done(((bf16[64,9232]{1,0:T(8,128)(2,1)}), bf16[2048,9232]{1,0:T(8,128)(2,1)}) %all-gather.5.cloned.1.call-update) | async-done | bytes 37814288 | tf_op jit(solution)/shard_map/all_gather | solution.py:18
  141.8 4.0 fusion.20
  153.1 9.5 fusion.6
  164.8 5.4 gather_fusion.5
  189.3 11.7 %fusion.2 = f32[160,2048]{1,0:T(8,128)S(1)} fusion(bf16[160,4096]{1,0:T(8,128)(2,1)S(1)} %bitcast.202, bf16[2048,9232]{1,0:T(8,128)(2,1)} %all-gather.5.cloned.1.call-done), kind=kOutput, calls=%fused_computation.15 | convolution fusion | flops 2684354560 | bytes 19398656 | tf_op jit(solution)/shard_map/dot_general | solution.py:235
  204.0 5.2 all-to-all-start
  214.5 55.6 %all-to-all-done = f32[4,160,2048]{2,1,0:T(8,128)} async-done(((f32[4,160,2048]{2,1,0:T(8,128)}), f32[4,160,2048]{2,1,0:T(8,128)}, u32[]{:S(2)}, u32[]{:S(2)}) %all-to-all-start) | async-done | bytes 5242912 | tf_op jit(solution)/shard_map/all_to_all | solution.py:37
  270.1 3.1 reduce_sum.183
  277.0 3.8 scatter_custom_fusion.1
  284.7 4.4 all-to-all-start.1
  291.9 4.5 mul.478
  301.7 5.3 scatter_custom_fusion.2
  313.5 4.3 all-to-all-start.3
  317.9 11.3 %copy.414 = bf16[256,8,2,1408]{3,1,2,0:T(8,128)(2,1)} copy(bf16[256,8,2,1408]{3,2,1,0:T(2,128)(2,1)} %bitcast.198) | data formatting | bytes 23068672
  330.6 11.6 %all-to-all-done.3 = bf16[8,50,2048]{2,1,0:T(8,128)(2,1)} async-done(((bf16[8,50,2048]{2,1,0:T(8,128)(2,1)}), bf16[8,50,2048]{2,1,0:T(8,128)(2,1)}, u32[]{:S(2)}, u32[]{:S(2)}) %all-to-all-start.3) | async-done | bytes 1638432 | tf_op jit(solution)/shard_map/all_to_all | solution.py:308
  343.9 12.3 %fusion.139 = f32[400,2816]{1,0:T(8,128)} fusion(bf16[400,2048]{1,0:T(8,128)(2,1)} %reshape.460, bf16[2048,2816]{1,0:T(8,128)(2,1)} %bitcast.199), kind=kOutput, calls=%fused_computation.240 | convolution fusion | flops 4613734400 | bytes 17678336 | tf_op jit(solution)/shard_map/dot_general | solution.py:275
  356.2 8.9 multiply_convert_fusion.2
  370.3 9.8 convolution_convert_fusion.4
  382.0 80.2 %all-reduce.4.cloned.1.call-done = (bf16[8,50,2048]{2,1,0:T(8,128)(2,1)}, bf16[8,50,2048]{2,1,0:T(8,128)(2,1)}) async-done(((bf16[8,50,2048]{2,1,0:T(8,128)(2,1)}, bf16[8,50,2048]{2,1,0:T(8,128)(2,1)}), (bf16[8,50,2048]{2,1,0:T(8,128)(2,1)}, bf16[8,50,2048]{2,1,0:T(8,128)(2,1)})) %all-reduce.4.cloned.1.call-update) | async-done | bytes 3276816 | tf_op jit(solution)/shard_map/psum | solution.py:281
  462.2 4.3 all-to-all-start.2
  468.6 22.3 %all-to-all-done.2 = bf16[8,50,2048]{2,1,0:T(8,128)(2,1)S(1)} async-done(((bf16[8,50,2048]{2,1,0:T(8,128)(2,1)}), bf16[8,50,2048]{2,1,0:T(8,128)(2,1)S(1)}, u32[]{:S(2)}, u32[]{:S(2)}) %all-to-all-start.2) | async-done | bytes 1638432 | tf_op jit(solution)/shard_map/all_to_all | solution.py:282
  492.1 4.3 all-to-all-start.4
  498.2 3.0 gather_fusion.2
  501.3 3.1 reshape.478
  507.8 3.5 fusion.131
  511.3 9.6 all-to-all-done.4
  522.6 3.0 gather_fusion.3
  525.6 3.3 reshape.479
  535.3 9.8 fusion
  547.4 4.3 gather_fusion.7
  553.1 4.1 fusion.49
  559.4 3.5 reshape_reshape.7
  562.9 4.3 fusion.8
  582.2 6.2 fusion.11
  592.6 8.9 convert_bitcast_fusion
  611.0 3.4 all-to-all-start.6
  616.9 8.8 convolution_convert_fusion
  627.4 5.4 fusion.18
  632.8 13.0 %fusion.55 = bf16[160,2048]{1,0:T(8,128)(2,1)S(1)} fusion(f32[160,2048]{1,0:T(8,128)} %fusion.18, bf16[160,4096]{1,0:T(8,128)(2,1)S(1)} %bitcast.204, bf16[2048,9232]{1,0:T(8,128)(2,1)} %all-gather.5.cloned.1.call-done), kind=kOutput, calls=%fused_computation.71 | convolution fusion | flops 2685009920 | bytes 20054016 | tf_op jit(solution)/shard_map/dot_general | solution.py:421
  647.6 4.9 all-to-all-start.5
  652.6 8.5 convolution_convert_fusion.1
  663.1 3.4 convolution_convert_fusion.3
  666.4 18.0 %all-to-all-done.5 = bf16[4,160,2048]{2,1,0:T(8,128)(2,1)} async-done(((bf16[4,160,2048]{2,1,0:T(8,128)(2,1)}), bf16[4,160,2048]{2,1,0:T(8,128)(2,1)}, u32[]{:S(2)}, u32[]{:S(2)}) %all-to-all-start.5) | async-done | bytes 2621472 | tf_op jit(solution)/shard_map/all_to_all | solution.py:37
  690.7 58.6 %concatenate.41 = bf16[2048,9344]{1,0:T(8,128)(2,1)} concatenate(bf16[2048,4096]{1,0:T(8,128)(2,1)} %convolution_convert_fusion.1, bf16[2048,4096]{1,0:T(8,128)(2,1)} %convolution_convert_fusion, bf16[2048,1024]{1,0:T(8,128)(2,1)} %convolution_convert_fusion.3, bf16[2048,8]{1,0:T(8,128)(2,1)} %copy.375, bf16[2048,8]{1,0:T(8,128)(2,1)} %copy.376, bf16[2048,1]{1,0:T(8,128)(2,1)} %stack.15, ...), dimensions={1} | concatenate | bytes 76546048 | tf_op jit(solution)/shard_map/concatenate | solution.py:462
  749.4 3.3 convert_element_type.231
  754.0 29.6 %reduce-scatter.9.cloned.1.call-done = bf16[1,512,2,1408]{3,1,2,0:T(8,128)(2,1)} async-done(((bf16[1,2048,2,1408]{3,1,2,0:T(8,128)(2,1)}), bf16[1,512,2,1408]{3,1,2,0:T(8,128)(2,1)}) %reduce-scatter.9.cloned.1.call-update) | async-done | bytes 2883600 | tf_op jit(solution)/shard_map/reduce_scatter | solution.py:350
  783.7 7.3 copy.382
  791.0 176.4 %reduce-scatter.7.cloned.1.call-done = bf16[64,9344]{1,0:T(8,128)(2,1)} async-done(((bf16[2048,9344]{1,0:T(8,128)(2,1)}), bf16[64,9344]{1,0:T(8,128)(2,1)}) %reduce-scatter.7.cloned.1.call-update) | async-done | bytes 1196048 | tf_op jit(solution)/shard_map/reduce_scatter | solution.py:461
  (353 shorter events, 149.5 us)
Async XLA Ops:
  7.2 134.6 %all-gather.5.cloned.1.call-start = ((), (), s32[]{:S(2)}) async-start(), calls=%async_computation.11 | async-start | bytes 39469056 | tf_op jit(solution)/shard_map/all_gather | solution.py:18
  13.0 165.9 %all-gather.7.cloned.1.call-start = ((), (), s32[]{:S(2)}) async-start(), calls=%async_computation.12 | async-start | bytes 2949120 | tf_op jit(solution)/shard_map/all_gather | solution.py:32
  13.1 160.9 %copy-start.34 = (f32[2048]{0:T(1024)}, f32[2048]{0:T(1024)S(1)}, u32[]{:S(2)}) copy-start(f32[2048]{0:T(1024)S(1)} %convert_element_type.185) | copy-start | bytes 24580
  13.4 160.6 %copy-start.45 = (f32[160]{0:T(256)}, f32[160]{0:T(256)S(1)}, u32[]{:S(2)}) copy-start(f32[160]{0:T(256)S(1)} %add_rsqrt_fusion.1) | copy-start | bytes 1924
  13.8 159.6 %copy-start.26 = (f32[160,64]{1,0:T(8,128)}, f32[160,64]{1,0:T(8,128)S(1)}, u32[]{:S(2)}) copy-start(f32[160,64]{1,0:T(8,128)S(1)} %get-tuple-element.143) | copy-start | bytes 122884
  13.8 159.6 %copy-start.28 = (f32[160,64]{1,0:T(8,128)}, f32[160,64]{1,0:T(8,128)S(1)}, u32[]{:S(2)}) copy-start(f32[160,64]{1,0:T(8,128)S(1)} %get-tuple-element.144) | copy-start | bytes 122884
  148.3 169.6 %all-gather.9.cloned.1.call-start = ((), (), s32[]{:S(2)}) async-start(), calls=%async_computation.13 | async-start | bytes 14417920 | tf_op jit(solution)/shard_map/all_gather | solution.py:132
  149.2 38.4 %copy-start.37 = (s32[160,2]{1,0:T(8,128)}, s32[160,2]{1,0:T(8,128)S(1)}, u32[]{:S(2)}) copy-start(s32[160,2]{1,0:T(8,128)S(1)} %copy.328) | copy-start | bytes 3844
  149.5 15.3 %copy-start.1 = (s32[320]{0:T(512)}, s32[320]{0:T(512)S(1)}, u32[]{:S(2)}) copy-start(s32[320]{0:T(512)S(1)} %reshape.577) | copy-start | bytes 3844
  149.5 13.1 %copy-start.63 = (pred[160,2]{0,1:T(4,128)(4,1)}, pred[160,2]{0,1:T(4,128)(4,1)S(1)}, u32[]{:S(2)}) copy-start(pred[160,2]{0,1:T(4,128)(4,1)S(1)} %and_bitcast_fusion) | copy-start | bytes 964
  174.0 4.9 copy-start.40
  189.2 11.8 %copy-start.18 = (bf16[20,8,8,512]{3,1,2,0:T(8,128)(2,1)}, bf16[20,8,8,512]{3,1,2,0:T(8,128)(2,1)S(1)}, u32[]{:S(2)}) copy-start(bf16[20,8,8,512]{3,1,2,0:T(8,128)(2,1)S(1)} %copy.413) | copy-start | bytes 3932164
  204.0 5.8 copy-start.67
  204.0 5.8 copy-start.56
  204.0 5.9 copy-start.69
  204.0 66.1 %all-to-all-start = ((f32[4,160,2048]{2,1,0:T(8,128)}), f32[4,160,2048]{2,1,0:T(8,128)}, u32[]{:S(2)}, u32[]{:S(2)}) async-start(f32[4,160,2048]{2,1,0:T(8,128)} %broadcast_in_dim.45), calls=%async_computation | async-start | bytes 10485760 | tf_op jit(solution)/shard_map/all_to_all | solution.py:37
  209.2 147.0 %all-gather.11.cloned.1.call-start = ((), (), s32[]{:S(2)}) async-start(), calls=%async_computation.14 | async-start | bytes 7208960 | tf_op jit(solution)/shard_map/all_gather | solution.py:133
  274.8 22.1 %copy-start.14 = (bf16[160,2048]{1,0:T(8,128)(2,1)}, bf16[160,2048]{1,0:T(8,128)(2,1)S(1)}, u32[]{:S(2)}) copy-start(bf16[160,2048]{1,0:T(8,128)(2,1)S(1)} %multiply_convert_fusion.5) | copy-start | bytes 1966084
  284.7 28.7 %all-to-all-start.1 = ((bf16[8,50,2048]{2,1,0:T(8,128)(2,1)}), bf16[8,50,2048]{2,1,0:T(8,128)(2,1)S(1)}, u32[]{:S(2)}, u32[]{:S(2)}) async-start(bf16[8,50,2048]{2,1,0:T(8,128)(2,1)} %reshape.459), calls=%async_computation.1 | async-start | bytes 3670016 | tf_op jit(solution)/shard_map/all_to_all | solution.py:265
  301.5 5.6 copy-start.59
  313.5 15.7 %copy-start.7 = (bf16[8,50,2048]{2,1,0:T(8,128)(2,1)}, bf16[8,50,2048]{2,1,0:T(8,128)(2,1)S(1)}, u32[]{:S(2)}) copy-start(bf16[8,50,2048]{2,1,0:T(8,128)(2,1)S(1)} %all-to-all-done.1) | copy-start | bytes 4915204
  313.5 28.7 %all-to-all-start.3 = ((bf16[8,50,2048]{2,1,0:T(8,128)(2,1)}), bf16[8,50,2048]{2,1,0:T(8,128)(2,1)}, u32[]{:S(2)}, u32[]{:S(2)}) async-start(bf16[8,50,2048]{2,1,0:T(8,128)(2,1)} %reshape.463), calls=%async_computation.3 | async-start | bytes 3670016 | tf_op jit(solution)/shard_map/all_to_all | solution.py:308
  317.8 144.4 %all-reduce.4.cloned.1.call-start = ((), (), s32[]{:S(2)}) async-start(), calls=%async_computation.19 | async-start | bytes 7340032 | tf_op jit(solution)/shard_map/psum | solution.py:281
  343.9 12.3 %copy-start.30 = (bf16[400,2048]{1,0:T(8,128)(2,1)}, bf16[400,2048]{1,0:T(8,128)(2,1)S(1)}, u32[]{:S(2)}) copy-start(bf16[400,2048]{1,0:T(8,128)(2,1)S(1)} %reshape.464) | copy-start | bytes 4915204
  356.2 9.9 %copy-start.70 = (bf16[1,1408,2048]{2,1,0:T(8,128)(2,1)S(1)}, bf16[1,1408,2048]{2,1,0:T(8,128)(2,1)}, u32[]{:S(2)}) copy-start(bf16[1,1408,2048]{2,1,0:T(8,128)(2,1)} %all-gather.11.cloned.1.call-done) | copy-start | bytes 17301508
  462.2 28.7 %all-to-all-start.2 = ((bf16[8,50,2048]{2,1,0:T(8,128)(2,1)}), bf16[8,50,2048]{2,1,0:T(8,128)(2,1)S(1)}, u32[]{:S(2)}, u32[]{:S(2)}) async-start(bf16[8,50,2048]{2,1,0:T(8,128)(2,1)} %get-tuple-element.100), calls=%async_computation.2 | async-start | bytes 3670016 | tf_op jit(solution)/shard_map/all_to_all | solution.py:282
  492.1 28.7 %all-to-all-start.4 = ((bf16[8,50,2048]{2,1,0:T(8,128)(2,1)}), bf16[8,50,2048]{2,1,0:T(8,128)(2,1)}, u32[]{:S(2)}, u32[]{:S(2)}) async-start(bf16[8,50,2048]{2,1,0:T(8,128)(2,1)} %get-tuple-element.101), calls=%async_computation.4 | async-start | bytes 3670016 | tf_op jit(solution)/shard_map/all_to_all | solution.py:338
  496.5 129.2 %reduce-scatter.5.cloned.1.call-start = ((), (), s32[]{:S(2)}) async-start(), calls=%async_computation.15 | async-start | bytes 2949120 | tf_op jit(solution)/shard_map/reduce_scatter | solution.py:55
  535.3 9.8 copy-start.9
  547.3 4.7 copy-start.55
  559.4 7.8 slice-start
  580.8 168.6 %reduce-scatter.11.cloned.1.call-start = ((), (), s32[]{:S(2)}) async-start(), calls=%async_computation.18 | async-start | bytes 7208960 | tf_op jit(solution)/shard_map/reduce_scatter | solution.py:356
  588.5 195.2 %reduce-scatter.9.cloned.1.call-start = ((), (), s32[]{:S(2)}) async-start(), calls=%async_computation.17 | async-start | bytes 14417920 | tf_op jit(solution)/shard_map/reduce_scatter | solution.py:350
  608.7 5.7 copy-start.15
  608.7 8.1 copy-start.10
  608.7 8.1 copy-start.19
  611.0 34.8 %all-to-all-start.6 = ((bf16[4,160,2]{1,2,0:T(2,128)(2,1)}), bf16[4,160,2]{1,2,0:T(2,128)(2,1)S(1)}, u32[]{:S(2)}, u32[]{:S(2)}) async-start(bf16[4,160,2]{1,2,0:T(2,128)(2,1)} %broadcast_in_dim.51), calls=%async_computation.7 | async-start | bytes 8192 | tf_op jit(solution)/shard_map/all_to_all | solution.py:37
  627.4 5.4 copy-start.32
  627.4 5.4 copy-start.20
  647.6 4.9 copy-start.4
  647.6 4.9 copy-start.35
  647.6 5.0 copy-start.46
  647.6 36.8 %all-to-all-start.5 = ((bf16[4,160,2048]{2,1,0:T(8,128)(2,1)}), bf16[4,160,2048]{2,1,0:T(8,128)(2,1)}, u32[]{:S(2)}, u32[]{:S(2)}) async-start(bf16[4,160,2048]{2,1,0:T(8,128)(2,1)} %broadcast_in_dim.50), calls=%async_computation.6 | async-start | bytes 5242880 | tf_op jit(solution)/shard_map/all_to_all | solution.py:37
  652.5 8.6 copy-start.44
  652.5 8.6 copy-start.53
  652.5 8.6 copy-start.62
  652.5 8.8 copy-start.39
  652.5 314.8 %reduce-scatter.7.cloned.1.call-start = ((), (), s32[]{:S(2)}) async-start(), calls=%async_computation.16 | async-start | bytes 39469056 | tf_op jit(solution)/shard_map/reduce_scatter | solution.py:461
  (42 other events, 96.4 us)
Sparse Core Ops, SparseCore 0:
  13.2 128.6 all-gather.4
  148.4 25.3 all-gather.6
  175.5 110.3 all-gather.8
  287.4 62.4 all-gather.10
  382.1 80.0 all-reduce.3
  580.9 32.7 reduce-scatter.4
  616.7 58.6 reduce-scatter.10
  677.8 105.7 reduce-scatter.8
  787.6 179.7 reduce-scatter.6
where the time goes:
time: 990 us; the launch traced here: 982 us
  waiting for transfers between devices  533 us (54%)
  local copies, waits for them, and re-layouts  211 us (21%)
  matrix products  148 us (15%)
  other arithmetic  42 us (4%)
  starting transfers between devices  31.4 us (3%)
  between operations  15.7 us (2%)
    reduce_scatter x1, waiting for transfers between devices, body(): lax.psum_scatter(jnp.concatenate([term_query, term_out, term_kv, term_rou...  176 us
    all_gather x1, waiting for transfers between devices, side_by_side(): lax.all_gather(both, axis, axis=dim, tiled=True)  128 us
    psum x1, waiting for transfers between devices, body(): expert_out = lax.psum(expert_part.astype(jnp.bfloat16), 'tensor')  80.2 us
    all_to_all x3, waiting for transfers between devices, copy_for_each(): return lax.all_to_all(copies, axis, split_axis=0, concat_axis=0, tiled=True)  73.5 us
    concatenate x1, local copies, waits for them, and re-layouts, body(): jnp.concatenate([term_query, term_out, term_kv, term_router_a, term_route...  58.6 us
    unnamed x166, local copies, waits for them, and re-layouts  47.4 us
    reduce_scatter x1, waiting for transfers between devices, body(): lax.psum_scatter(grad_w_pair.reshape(1, MODEL_WIDTH, 2, half_width).astyp...  29.6 us
    all_to_all x1, waiting for transfers between devices, body(): lax.all_to_all(expert_out.reshape(experts, capacity, MODEL_WIDTH), 'exper...  22.3 us
  transfers between devices with their start and end apart: 16, of which 10 were waited for; matrix products, arithmetic and copies ran while one was open for 29% of the time, Pallas kernels for 0%

commit v1 on v0

v1 whole, which is shorter than its diff:
```python
import jax
import jax.numpy as jnp
from jax import lax
from jax.experimental import pallas as pl
from jax.experimental.pallas import tpu as pltpu
from jax.sharding import Mesh
from jax.sharding import PartitionSpec as P

MODEL_WIDTH = 2048
HEAD_SIZE = 128
EXPERTS = 8
WINDOW = 1024
NORM_EPS = 1e-06
BF = jnp.bfloat16
F32 = jnp.float32
ROWS = (((0,), (0,)), ((), ()))
LAST = (((1,), (1,)), ((), ()))
UP = [(0, 1), (1, 2), (2, 3), (3, 0)]
DOWN = [(0, 3), (1, 0), (2, 1), (3, 2)]
SWAP = [(0, 1), (1, 0)]


def exchange(blocks, axis):
    return lax.all_to_all(blocks, axis, split_axis=0, concat_axis=0, tiled=True)


def spread(block, axis, count):
    return exchange(jnp.broadcast_to(block, (count, *block.shape)), axis)


def from_ahead(block, axis, steps):
    return lax.ppermute(block, axis, [(i, (i - steps) % 4) for i in range(4)])


def in_order(pieces, first):
    both = jnp.stack(pieces + pieces[:3])
    return lax.dynamic_slice_in_dim(both, lax.rem(4 - first, 4), 4)


def gather_direct(block, axis):
    pieces = [block] + [from_ahead(block, axis, k) for k in (1, 2, 3)]
    return in_order(pieces, lax.axis_index(axis))


def pick_block(blocks, index):
    return lax.dynamic_index_in_dim(blocks, lax.rem(index, 4), 0, keepdims=False)


def send_direct(blocks, axis):
    me = lax.axis_index(axis)
    return [pick_block(blocks, me)] + [
        from_ahead(pick_block(blocks, me + 4 - k), axis, k) for k in (1, 2, 3)
    ]


def sum_direct(blocks, axis):
    return sum(p.astype(F32) for p in send_direct(blocks, axis))


def ring_pieces(block, axis):
    half = block.shape[0] // 2
    before = lax.ppermute(block, axis, UP)
    after = lax.ppermute(block, axis, DOWN)
    far_low = lax.ppermute(before[:half], axis, UP)
    far_high = lax.ppermute(after[half:], axis, DOWN)
    return [block, after, far_low, far_high, before]


def ring_sum(blocks, axis):
    me = lax.axis_index(axis)
    half = blocks.shape[1] // 2
    far = pick_block(blocks, me + 2)
    low = lax.ppermute(far[:half], axis, UP)
    high = lax.ppermute(far[half:], axis, DOWN)
    right, left = pick_block(blocks, me + 1), pick_block(blocks, me + 3)
    right = jnp.concatenate([(right[:half].astype(F32) + low.astype(F32)).astype(BF), right[half:]])
    left = jnp.concatenate([left[:half], (left[half:].astype(F32) + high.astype(F32)).astype(BF)])
    return (
        pick_block(blocks, me).astype(F32)
        + lax.ppermute(right, axis, UP).astype(F32)
        + lax.ppermute(left, axis, DOWN).astype(F32)
    )


def assemble(own, other, place, core, columns):
    def kernel(at_ref, *refs):
        out, sem = refs[10], refs[11]
        z, c = at_ref[0], at_ref[1]
        copies = []
        for half, pieces in ((c, refs[:5]), (1 - c, refs[5:10])):
            for piece, shift, low, count in zip(
                pieces, (0, 1, 2, 2, 3), (0, 0, 0, 2, 0), (4, 4, 2, 2, 4)
            ):
                copies.append(
                    pltpu.make_async_copy(
                        piece, out.at[lax.rem(z + shift, 4), pl.ds(low, count), half], sem.at[len(copies)]
                    )
                )
        for copy in copies:
            copy.start()
        for copy in copies:
            copy.wait()

    shaped = [p.reshape(-1, 64, columns) for p in (*own, *other)]
    return pl.pallas_call(
        kernel,
        out_shape=jax.ShapeDtypeStruct((4, 4, 2, 64, columns), BF),
        in_specs=[pl.BlockSpec(memory_space=pltpu.SMEM)] + [pl.BlockSpec(memory_space=pl.ANY)] * 10,
        out_specs=pl.BlockSpec(memory_space=pltpu.VMEM),
        scratch_shapes=[pltpu.SemaphoreType.DMA((10,))],
        compiler_params=pltpu.CompilerParams(vmem_limit_bytes=16 * 1024 * 1024),
        cost_estimate=pl.CostEstimate(
            flops=0, bytes_accessed=8 * MODEL_WIDTH * columns, transcendentals=0
        ),
    )(jnp.stack([place, core]), *shaped).reshape(MODEL_WIDTH, columns)


def heads_first(shard):
    columns = shard.shape[1] * HEAD_SIZE
    return shard.reshape(64, -1, 4, HEAD_SIZE).transpose(2, 0, 1, 3).reshape(4, 64, columns)


def gather_rows(by_head, place, core):
    columns = by_head.shape[2]
    own = ring_pieces(exchange(by_head, "y").reshape(256, columns), "dp")
    other = [lax.ppermute(p, "core", SWAP) for p in own]
    return assemble(own, other, place, core, columns), own


def scatter_rows(grad, core):
    columns = grad.shape[1]
    parts = grad.reshape(16, 2, 64, columns)
    keep = lax.dynamic_index_in_dim(parts, core, 1, keepdims=False)
    give = lax.dynamic_index_in_dim(parts, 1 - core, 1, keepdims=False)
    both = keep.astype(F32) + lax.ppermute(give, "core", SWAP).astype(F32)
    summed = ring_sum(both.astype(BF).reshape(4, 256, columns), "dp")
    return in_order(
        send_direct(summed.astype(BF).reshape(4, 64, columns), "y"), lax.axis_index("y")
    )


def heads_last(blocks):
    heads = blocks.shape[2] // HEAD_SIZE
    return (
        blocks.reshape(4, 64, heads, HEAD_SIZE)
        .transpose(1, 2, 0, 3)
        .reshape(64, heads, 4 * HEAD_SIZE)
        .astype(F32)
    )


def rms_scale(values):
    return lax.rsqrt(jnp.mean(values * values, axis=-1, keepdims=True) + NORM_EPS)


def turn(heads, cosine, sine):
    first, second = heads[..., :64], heads[..., 64:]
    return jnp.concatenate([first * cosine - second * sine, second * cosine + first * sine], axis=-1)


def pick_of(routes):
    return (routes[:, :, None] == jnp.arange(EXPERTS, dtype=jnp.int32)[None, None, :]).astype(F32)


def pair_gates(logits, pick):
    chosen = jnp.sum(logits[:, None, :] * pick, axis=-1)
    weights = jnp.exp(chosen - jnp.max(chosen, axis=1, keepdims=True))
    return weights / jnp.sum(weights, axis=1, keepdims=True)


def gate_back(gates, grad_gates, pick):
    inner = gates * (grad_gates - jnp.sum(gates * grad_gates, axis=1, keepdims=True))
    return jnp.sum(inner[:, :, None] * pick, axis=1)


def norm_back(grad_normed, values, factor, gain):
    gain_part = jnp.sum(grad_normed * values * factor, axis=0)
    inner = grad_normed * gain
    grad_values = factor * inner - values * factor * factor * factor * jnp.mean(
        inner * values, axis=-1, keepdims=True
    )
    return grad_values, gain_part


def in_two(values):
    high = values.astype(BF)
    low = (values - high.astype(F32)).astype(BF)
    return jnp.concatenate([high, low], axis=1)


def widen(columns):
    return jnp.pad(columns, ((0, 0), (0, HEAD_SIZE - columns.shape[1])))


def body(
    tokens,
    cotangent,
    attn_gain,
    mlp_gain,
    attn_router,
    key_value_weight,
    query_matrix,
    output_matrix,
    mlp_router,
    gate_up_weight,
    down_weight,
    attn_routes,
    mlp_routes,
    priority,
    segments,
):
    z, y = lax.axis_index("dp"), lax.axis_index("y")
    core, x = lax.axis_index("core"), lax.axis_index("tensor")
    count = tokens.shape[0]
    quarter = count // 4
    capacity = 50
    room = 56
    sequence = 8 * count
    plane = ("y", "tensor")

    gate_up_w = lax.all_gather(gate_up_weight[0].reshape(512, 2816), "dp", axis=0, tiled=True)

    routers_own = jnp.concatenate([attn_router, mlp_router], axis=1)
    in_own = jnp.concatenate([query_matrix, key_value_weight], axis=1)
    in_w, _ = gather_rows(
        jnp.concatenate(
            [heads_first(in_own), jnp.broadcast_to(widen(routers_own), (4, 64, HEAD_SIZE))], axis=2
        ),
        z,
        core,
    )
    out_w, out_pieces = gather_rows(heads_first(output_matrix), z, core)
    router_m = in_w[:, 1288:1296]

    down_own, _ = lax.optimization_barrier((down_weight[0], out_pieces[2]))
    down_pieces = ring_pieces(down_own, "dp")
    down_w = lax.dynamic_slice_in_dim(
        jnp.concatenate(
            [
                down_pieces[0],
                down_pieces[1],
                jnp.concatenate([down_pieces[2], down_pieces[3]], axis=0),
                down_pieces[4],
                down_pieces[0],
                down_pieces[1],
                jnp.concatenate([down_pieces[2], down_pieces[3]], axis=0),
            ],
            axis=1,
        ),
        lax.rem(4 - z, 4) * 512,
        MODEL_WIDTH,
        axis=1,
    )

    sent = jnp.concatenate([tokens, widen(attn_routes.astype(BF))], axis=1)
    arrived = gather_direct(sent, "y").reshape(4 * count, MODEL_WIDTH + HEAD_SIZE)
    values = arrived[:, :MODEL_WIDTH].astype(F32)
    routes = arrived[:, MODEL_WIDTH : MODEL_WIDTH + 2].astype(jnp.int32)
    gain_a, gain_m = attn_gain.astype(F32), mlp_gain.astype(F32)
    xn1 = (values * rms_scale(values) * gain_a).astype(BF)
    pick_a = pick_of(routes)

    ranking = priority[0]
    pick_m = pick_of(mlp_routes)
    before = (ranking[None, :] < ranking[:, None]).astype(BF)
    earlier = jnp.dot(before, jnp.sum(pick_m, axis=1).astype(BF), preferred_element_type=F32)
    slots = jnp.sum(pick_m * earlier[:, None, :], axis=-1).astype(jnp.int32)
    kept = slots < capacity
    dest = jnp.where(kept, mlp_routes * room + slots, -1)
    lanes = jnp.arange(EXPERTS * room, dtype=jnp.int32)
    to_row = (dest.T[:, :, None] == lanes[None, None, :]).astype(BF)
    any_row = to_row[0] + to_row[1]
    both_rows = to_row.reshape(2 * count, EXPERTS * room)

    def to_experts(rows):
        columns = rows.shape[1]
        return exchange(rows.reshape(EXPERTS, room, columns), ("y", "core")).reshape(
            EXPERTS * room, columns
        )

    def with_other(j):
        others = jnp.concatenate([pick_m[:, 1 - j], jnp.ones((count, 1), F32)], axis=1)
        return jnp.concatenate([cotangent, widen(others.astype(BF))], axis=1)

    grad_sent = lax.dot_general(
        both_rows,
        jnp.concatenate([with_other(0), with_other(1)], axis=0),
        ROWS,
        preferred_element_type=F32,
    ).astype(BF)
    grad_sent, _ = lax.optimization_barrier((grad_sent, out_pieces[0]))
    grad_landed = to_experts(grad_sent)

    def places(half):
        blocks = 2 * jnp.arange(4, dtype=jnp.int32)[:, None] + half
        return (blocks * count + jnp.arange(count, dtype=jnp.int32)[None, :]).reshape(-1)

    place = places(core)
    key_place = jnp.concatenate([place, places(1 - core)])
    of_sequence = lax.dynamic_slice_in_dim(segments, z * sequence, sequence)
    own_segment = jnp.take(of_sequence, place)
    key_segment = jnp.concatenate([own_segment, jnp.take(of_sequence, places(1 - core))])
    allowed = (
        (key_place[None, :] <= place[:, None])
        & (place[:, None] - key_place[None, :] < WINDOW)
        & (own_segment[:, None] == key_segment[None, :])
    )
    inverse = 10000.0 ** (-(jnp.arange(HEAD_SIZE // 2).astype(F32) * 2.0 / HEAD_SIZE))
    angle = place.astype(F32)[:, None] * inverse[None, :]
    cosine, sine = jnp.cos(angle), jnp.sin(angle)

    projected = jnp.dot(xn1, in_w, preferred_element_type=F32)
    gate_a = pair_gates(projected[:, 1280:1288], pick_a)
    key_own = turn(projected[:, 1024:1152], cosine, sine).astype(BF)
    value_own = projected[:, 1152:1280].astype(BF)
    kv_own = jnp.concatenate([key_own, value_own], axis=1)
    kv_other = lax.ppermute(kv_own, "core", SWAP)
    keys = jnp.concatenate([key_own, kv_other[:, :HEAD_SIZE]], axis=0)
    vals = jnp.concatenate([value_own, kv_other[:, HEAD_SIZE:]], axis=0)
    q_all = projected[:, :1024].reshape(-1, EXPERTS, HEAD_SIZE)
    q_pick = jnp.sum(pick_a[:, :, :, None] * q_all[:, None], axis=2)
    query = turn(q_pick, cosine[:, None], sine[:, None]).astype(BF)
    scale = HEAD_SIZE ** (-0.5)
    score = jnp.where(
        allowed[None], jnp.einsum("sjd,kd->jsk", query, keys, preferred_element_type=F32) * scale, -1e30
    )
    row_max = jnp.max(score, axis=-1, keepdims=True)
    weights = jnp.exp(score - row_max)
    totals = jnp.sum(weights, axis=-1, keepdims=True)
    prob = weights / totals
    attended = jnp.einsum("jsk,kd->sjd", prob.astype(BF), vals, preferred_element_type=F32)
    mixed = jnp.sum(
        (pick_a * gate_a[:, :, None])[:, :, :, None] * attended[:, :, None, :], axis=1
    ).astype(BF).reshape(-1, EXPERTS * HEAD_SIZE)
    branch_part = lax.dot_general(mixed, out_w, LAST, preferred_element_type=F32).astype(BF)
    branch = exchange(branch_part.reshape(16, quarter, MODEL_WIDTH), plane).astype(F32).sum(axis=0)

    first = x * quarter
    own_values = lax.dynamic_slice_in_dim(tokens, first, quarter).astype(F32)
    own_factor = rms_scale(own_values)
    hidden = own_values + branch
    factor_m = rms_scale(hidden)
    xn2_own = (hidden * factor_m * gain_m).astype(BF)
    xn2 = spread(xn2_own, "tensor", 4).reshape(count, MODEL_WIDTH)
    gate_m = pair_gates(jnp.dot(xn2, router_m, preferred_element_type=F32), pick_m)
    weight_m = gate_m * kept.astype(F32)

    received = to_experts(
        lax.dot_general(any_row, xn2, ROWS, preferred_element_type=F32).astype(BF)
    )
    grad_received = grad_landed[:, :MODEL_WIDTH]
    other_pick = grad_landed[:, MODEL_WIDTH : MODEL_WIDTH + EXPERTS].astype(F32)
    valid = grad_landed[:, MODEL_WIDTH + EXPERTS : MODEL_WIDTH + EXPERTS + 1].astype(F32)
    row_logits = jnp.dot(received, router_m, preferred_element_type=F32)
    here = (jnp.arange(EXPERTS, dtype=jnp.int32) == 2 * y + core).astype(F32)
    own_logit = jnp.sum(row_logits * here[None], axis=1, keepdims=True)
    other_logit = jnp.sum(row_logits * other_pick, axis=1, keepdims=True)
    top = jnp.maximum(own_logit, other_logit)
    own_weight = jnp.exp(own_logit - top)
    row_gate = valid * own_weight / (own_weight + jnp.exp(other_logit - top))

    width = down_weight.shape[1]
    grad_act_raw = lax.dot_general(grad_received, down_w, LAST, preferred_element_type=F32)
    grad_expert = (row_gate * grad_received.astype(F32)).astype(BF)
    gate_up = jnp.dot(received, gate_up_w, preferred_element_type=F32)
    gate_part, up_part = gate_up[:, :width], gate_up[:, width:]
    sigmoid_gate = jax.nn.sigmoid(gate_part)
    silu_gate = gate_part * sigmoid_gate
    activated = (silu_gate * up_part).astype(BF)
    grad_act = row_gate * grad_act_raw
    grad_gate_up = jnp.concatenate(
        [
            grad_act * up_part * sigmoid_gate * (1.0 + gate_part * (1.0 - sigmoid_gate)),
            grad_act * silu_gate,
        ],
        axis=1,
    ).astype(BF)
    row_gate_grad = jnp.sum(activated.astype(F32) * grad_act_raw, axis=1, keepdims=True)
    grad_rows = lax.dot_general(grad_gate_up, gate_up_w, LAST, preferred_element_type=F32).astype(BF)
    grad_returned = to_experts(jnp.concatenate([grad_rows, widen(in_two(row_gate_grad))], axis=1))
    grad_gate_up_w = lax.dot_general(
        received, grad_gate_up, ROWS, preferred_element_type=F32
    ).astype(BF)
    grad_down_w = lax.dot_general(activated, grad_expert, ROWS, preferred_element_type=F32).astype(BF)
    gate_up_grad = (
        lax.psum_scatter(grad_gate_up_w, "dp", scatter_dimension=0, tiled=True)
        .reshape(1, 512, 2, width)
        .astype(F32)
    )
    down_grad = ring_sum(grad_down_w.reshape(width, 4, 512).transpose(1, 0, 2), "dp")[None]

    grad_xn2_part = jnp.dot(
        any_row, grad_returned[:, :MODEL_WIDTH], preferred_element_type=F32
    ).astype(BF)
    row_gate_parts = grad_returned[:, MODEL_WIDTH : MODEL_WIDTH + 2]
    gate_m_part = jnp.sum(
        jnp.einsum("jtr,rd->tjd", to_row, row_gate_parts, preferred_element_type=F32), axis=2
    )
    shares = jnp.concatenate([grad_xn2_part, widen(in_two(gate_m_part))], axis=1)
    landed = (
        exchange(shares.reshape(4, quarter, MODEL_WIDTH + HEAD_SIZE), "tensor")
        .astype(F32)
        .sum(axis=0)
    )
    grad_gate_m = (
        landed[:, MODEL_WIDTH : MODEL_WIDTH + 2] + landed[:, MODEL_WIDTH + 2 : MODEL_WIDTH + 4]
    )

    def quarter_of(array, offset=0):
        return lax.dynamic_slice_in_dim(array, first + offset, quarter)

    grad_logit_m = gate_back(quarter_of(gate_m), grad_gate_m, quarter_of(pick_m))
    grad_xn2 = landed[:, :MODEL_WIDTH] + lax.dot_general(
        grad_logit_m, router_m.astype(F32), LAST, preferred_element_type=F32
    )
    grad_norm, gain_m_part = norm_back(grad_xn2, hidden, factor_m, gain_m)
    grad_hidden = quarter_of(cotangent).astype(F32) + grad_norm
    grad_branch = spread(grad_hidden.astype(BF), plane, 16).reshape(4 * count, MODEL_WIDTH)

    expert_part = jnp.dot(activated, down_w, preferred_element_type=F32).astype(BF)
    expert_part, _ = lax.optimization_barrier((expert_part, grad_branch))
    returned = to_experts(expert_part)
    fetched = jnp.einsum("jtr,rd->jtd", to_row, returned, preferred_element_type=F32)
    moe_part = jnp.sum(weight_m.T[:, :, None] * fetched, axis=0).astype(BF)
    moe = sum_direct(moe_part.reshape(4, quarter, MODEL_WIDTH), "tensor")
    output = gather_direct((hidden + moe).astype(BF), "tensor").reshape(count, MODEL_WIDTH)

    grad_mixed = jnp.dot(grad_branch, out_w, preferred_element_type=F32).reshape(
        -1, EXPERTS, HEAD_SIZE
    )
    grad_pick = jnp.sum(pick_a[:, :, :, None] * grad_mixed[:, None], axis=2)
    grad_gate_part = jnp.sum(grad_pick * attended, axis=-1)
    grad_attended = (gate_a[:, :, None] * grad_pick).astype(BF)
    grad_prob = jnp.einsum("sjd,kd->jsk", grad_attended, vals, preferred_element_type=F32)
    row_delta = jnp.sum(prob * grad_prob, axis=-1, keepdims=True)
    grad_score = (prob * (grad_prob - row_delta)).astype(BF)
    grad_query = jnp.einsum("jsk,kd->sjd", grad_score, keys, preferred_element_type=F32) * scale
    grad_keys = jnp.einsum("jsk,sjd->kd", grad_score, query, preferred_element_type=F32) * scale
    grad_vals = jnp.einsum("jsk,sjd->kd", prob.astype(BF), grad_attended, preferred_element_type=F32)
    half = 4 * count
    grad_kv_raw = jnp.concatenate([grad_keys, grad_vals], axis=1)
    from_other = lax.ppermute(grad_kv_raw[half:].astype(BF), "core", SWAP).astype(F32)
    own_grad_kv = grad_kv_raw[:half] + from_other
    grad_kv = jnp.concatenate(
        [turn(own_grad_kv[:, :HEAD_SIZE], cosine, -sine), own_grad_kv[:, HEAD_SIZE:]], axis=1
    ).astype(BF)
    grad_q_pick = turn(grad_query, cosine[:, None], -sine[:, None])
    grad_q_all = (
        jnp.sum(pick_a[:, :, :, None] * grad_q_pick[:, :, None, :], axis=1)
        .astype(BF)
        .reshape(-1, EXPERTS * HEAD_SIZE)
    )
    out_grad = heads_last(
        scatter_rows(
            lax.dot_general(grad_branch, mixed, ROWS, preferred_element_type=F32).astype(BF), core
        )
    )
    grad_logit_a = gate_back(gate_a, grad_gate_part, pick_a)
    grad_in = jnp.concatenate([grad_q_all, grad_kv, widen(grad_logit_a.astype(BF))], axis=1)
    grad_xn1_part = lax.dot_general(grad_in, in_w, LAST, preferred_element_type=F32).astype(BF)
    landed_a = (
        exchange(grad_xn1_part.reshape(16, quarter, MODEL_WIDTH), plane).astype(F32).sum(axis=0)
    )
    grad_x_norm, _ = norm_back(landed_a, own_values, own_factor, gain_a)
    input_grad = gather_direct((grad_hidden + grad_x_norm).astype(BF), "tensor").reshape(
        count, MODEL_WIDTH
    )

    small = jnp.concatenate(
        [
            jnp.zeros((MODEL_WIDTH, 1288), BF),
            lax.dot_general(
                xn2_own, grad_logit_m.astype(BF), ROWS, preferred_element_type=F32
            ).astype(BF),
            gain_m_part[:, None].astype(BF),
            jnp.zeros((MODEL_WIDTH, 111), BF),
        ],
        axis=1,
    )
    in_parts = scatter_rows(
        lax.dot_general(xn1, grad_in, ROWS, preferred_element_type=F32).astype(BF) + small, core
    )
    in_grad = heads_last(in_parts[:, :, :1280])
    query_grad, kv_grad = in_grad[:, :8], in_grad[:, 8:]
    small_part = jnp.sum(in_parts[:, :, 1280:].astype(F32), axis=0)
    gain_rows = lax.dynamic_slice_in_dim(gain_a, z * 512 + y * 128 + core * 64, 64)
    gain_a_part = (
        jnp.sum(in_grad * in_own.astype(F32), axis=(1, 2))
        + jnp.sum(small_part[:, :8] * attn_router.astype(F32), axis=1)
    ) / gain_rows
    small_sent = jnp.concatenate([small_part[:, :17], gain_a_part[:, None]], axis=1)
    small_bf = widen(small_sent.astype(BF))
    small_sum = sum(
        p.astype(F32) for p in [small_bf] + [from_ahead(small_bf, "tensor", k) for k in (1, 2, 3)]
    )
    return (
        output,
        input_grad,
        small_sum[:, 17],
        small_sum[:, 16],
        small_sum[:, :8],
        kv_grad,
        query_grad,
        out_grad,
        small_sum[:, 8:16],
        gate_up_grad,
        down_grad,
    )


def solution(mesh):
    split = Mesh(mesh.devices.reshape(4, 4, 2, 4), ("dp", "y", "core", "tensor"))
    rows = ("dp", "y", "core")
    expert = ("y", "core")
    placed = (
        P(rows, None),
        P(rows, None),
        P(),
        P(),
        P(rows, None),
        P(rows, None, "tensor"),
        P(rows, None, "tensor"),
        P(rows, None, "tensor"),
        P(rows, None),
        P(expert, "dp", None, "tensor"),
        P(expert, "tensor", "dp"),
        P(rows, None),
        P(rows, None),
        P(rows, None),
        P(),
    )
    return jax.shard_map(
        body,
        mesh=split,
        in_specs=placed,
        out_specs=(
            P(rows, None),
            P(rows, None),
            P(rows),
            P(rows),
            P(rows, None),
            P(rows, None, "tensor"),
            P(rows, None, "tensor"),
            P(rows, None, "tensor"),
            P(rows, None),
            P(expert, "dp", None, "tensor"),
            P(expert, "tensor", "dp"),
        ),
        check_vma=False,
    )
```

time: 990 us -> 759 us (0.77)
  waiting for transfers between devices: 533 us -> 241 us
  starting transfers between devices: 31.4 us -> 123 us
  local copies, waits for them, and re-layouts: 211 us -> 152 us
  other arithmetic: 42 us -> 73.1 us
  matrix products: 148 us -> 137 us
    reduce_scatter x4 -> x1, waiting for transfers between devices: 206 us -> 0.01 us  [body(): lax.psum_scatter(grad_gate_up_w, 'dp', scatter_dimension=0, tiled=True)]
    ppermute x0 -> x59, waiting for transfers between devices: none -> 157 us  [the longest x21 48.1 us: from_ahead(): return lax.ppermute(block, axis, [(i, (i - steps) % 4) for i in range(4)])]
    all_gather x4 -> x1, waiting for transfers between devices: 128 us -> 0.02 us  [body(): lax.all_gather(gate_up_weight[0].reshape(512, 2816), 'dp', axis=0, tiled=...]
    psum x1 -> x0, waiting for transfers between devices: 80.2 us -> none  [body(): expert_out = lax.psum(expert_part.astype(jnp.bfloat16), 'tensor')]
    ppermute x0 -> x59, starting transfers between devices: none -> 70.4 us  [the longest x21 25.5 us: from_ahead(): return lax.ppermute(block, axis, [(i, (i - steps) % 4) for i in range(4)])]
    concatenate x4 -> x6, local copies, waits for them, and re-layouts: 61.2 us -> 13.7 us  [the longest x1 10.1 us: body(): jnp.concatenate([jnp.zeros((MODEL_WIDTH, 1288), BF), lax.dot_general(xn2_...]
    all_to_all x7 -> x11, waiting for transfers between devices: 118 us -> 83.9 us  [exchange(): return lax.all_to_all(blocks, axis, split_axis=0, concat_axis=0, tiled=True)]
    all_to_all x7 -> x11, starting transfers between devices: 30.8 us -> 52.3 us  [exchange(): return lax.all_to_all(blocks, axis, split_axis=0, concat_axis=0, tiled=True)]
  transfers between devices with their start and end apart: 16 -> 72, of which waited for: 10 -> 28; matrix products, arithmetic and copies ran while one was open for 29% -> 42% of each run, Pallas kernels for 0% -> 1%
where the time goes in v1:
time: 759 us; the launch traced here: 748 us
  waiting for transfers between devices  241 us (32%)
  local copies, waits for them, and re-layouts  152 us (20%)
  matrix products  137 us (18%)
  starting transfers between devices  123 us (16%)
  other arithmetic  73.1 us (10%)
  between operations  16.6 us (2%)
    all_to_all x11, waiting for transfers between devices, exchange(): return lax.all_to_all(blocks, axis, split_axis=0, concat_axis=0, tiled=True)  83.9 us
    all_to_all x11, starting transfers between devices, exchange(): return lax.all_to_all(blocks, axis, split_axis=0, concat_axis=0, tiled=True)  52.3 us
    ppermute x21, waiting for transfers between devices, from_ahead(): return lax.ppermute(block, axis, [(i, (i - steps) % 4) for i in range(4)])  48.1 us
    ppermute x3, waiting for transfers between devices, ring_pieces(): far_low = lax.ppermute(before[:half], axis, UP)  47.5 us
    unnamed x199, local copies, waits for them, and re-layouts  38.9 us
    ppermute x21, starting transfers between devices, from_ahead(): return lax.ppermute(block, axis, [(i, (i - steps) % 4) for i in range(4)])  25.5 us
    another operation x1, local copies, waits for them, and re-layouts  18.4 us
    ppermute x3, waiting for transfers between devices, ring_sum(): lax.ppermute(left, axis, DOWN).astype(F32)  16.8 us
  transfers between devices with their start and end apart: 72, of which 28 were waited for; matrix products, arithmetic and copies ran while one was open for 42% of the time, Pallas kernels for 1%

profile of v1, /device:TPU:0, one launch (start us, length us, event | category | flops | bytes accessed | tf_op | source)
XLA Modules:
  0.0 747.9 jit_solution(8015355800401259426)
XLA Ops:
  38.1 14.6 %all-to-all-done.1.refs_0_ = bf16[4,64,1024]{2,1,0:T(8,128)(2,1)S(1)} async-done(((bf16[4,64,1024]{2,1,0:T(8,128)(2,1)}), bf16[4,64,1024]{2,1,0:T(8,128)(2,1)S(1)}, u32[]{:S(2)}, u32[]{:S(2)}) %all-to-all-start.1) | async-done | bytes 524320 | tf_op jit(solution)/shard_map/all_to_all | solution.py:24
  62.3 4.5 all-to-all-done.refs_0_
  76.8 10.8 %collective-permute-done.14 = bf16[256,1024]{1,0:T(8,128)(2,1)} collective-permute-done((bf16[256,1024]{1,0:T(8,128)(2,1)S(1)}, bf16[256,1024]{1,0:T(8,128)(2,1)}, u32[]{:S(2)}, u32[]{:S(2)}) %collective-permute-start.14) | collective-permute-done | bytes 524320 | tf_op jit(solution)/shard_map/ppermute | solution.py:62
  94.0 34.8 %collective-permute-done.15 = bf16[128,1024]{1,0:T(8,128)(2,1)S(1)} collective-permute-done((bf16[128,1024]{1,0:T(8,128)(2,1)S(1)}, bf16[128,1024]{1,0:T(8,128)(2,1)S(1)}, u32[]{:S(2)}, u32[]{:S(2)}) %collective-permute-start.15) | collective-permute-done | bytes 262176 | tf_op jit(solution)/shard_map/ppermute | solution.py:64
  145.8 7.7 %collective-permute-done.5 = bf16[128,1408]{1,0:T(8,128)(2,1)} collective-permute-done((bf16[128,1408]{1,0:T(8,128)(2,1)}, bf16[128,1408]{1,0:T(8,128)(2,1)}, u32[]{:S(2)}, u32[]{:S(2)}) %collective-permute-start.5) | collective-permute-done | bytes 360480 | tf_op jit(solution)/shard_map/ppermute | solution.py:64
  163.4 4.3 fusion.80
  181.1 6.7 fusion.161
  194.9 6.9 convolution_convert_fusion.6
  201.8 7.5 %all-to-all-start.2 = ((bf16[16,40,2048]{2,1,0:T(8,128)(2,1)}), bf16[16,40,2048]{2,1,0:T(8,128)(2,1)S(1)}, u32[]{:S(2)}, u32[]{:S(2)}) async-start(bf16[16,40,2048]{2,1,0:T(8,128)(2,1)} %bitcast.439), calls=%async_computation.2 | async-start | bytes 5242880 | tf_op jit(solution)/shard_map/all_to_all | solution.py:24
  210.1 40.1 %all-to-all-done.2 = bf16[16,40,2048]{2,1,0:T(8,128)(2,1)S(1)} async-done(((bf16[16,40,2048]{2,1,0:T(8,128)(2,1)}), bf16[16,40,2048]{2,1,0:T(8,128)(2,1)S(1)}, u32[]{:S(2)}, u32[]{:S(2)}) %all-to-all-start.2) | async-done | bytes 2621472 | tf_op jit(solution)/shard_map/all_to_all | solution.py:24
  260.5 7.0 all-to-all-done.3
  273.3 4.5 all-to-all-start.5
  281.9 6.6 copy.595
  303.4 4.7 all-to-all-start.4
  309.5 5.0 collective-permute-done.24
  326.5 6.0 all-to-all-done.4
  335.0 9.3 %fusion.162 = f32[448,2816]{1,0:T(8,128)S(1)} fusion(bf16[448,2048]{1,0:T(8,128)(2,1)} %bitcast.44, bf16[2048,2816]{1,0:T(8,128)(2,1)} %all-gather.2.cloned.1.call-done), kind=kOutput, calls=%fused_computation.393 | convolution fusion | flops 5167382528 | bytes 18415616 | tf_op jit(solution)/shard_map/dot_general | solution.py:365
  344.3 8.2 %multiply_convert_fusion.2 = (bf16[448,1408]{1,0:T(8,128)(2,1)S(1)}, bf16[448,1408]{1,0:T(8,128)(2,1)}, f32[448]{0:T(512)S(1)}, bf16[448,1408]{1,0:T(8,128)(2,1)S(1)}) fusion(f32[448,2816]{1,0:T(8,128)S(1)} %fusion.162, f32[448]{0:T(512)S(1)} %bitcast.454, bf16[1408,3584]{1,0:T(8,128)(2,1)} %fusion.62, s32[]{:T(128)S(6)} %select_n.108, ...), kind=kOutput, calls=%fused_computation.60 | convolution fusion | flops 2595675648 | bytes 16436740 | tf_op jit(solution)/shard_map/dot_general | solution.py:363
  352.8 9.3 %convolution_convert_fusion.8 = bf16[448,2048]{1,0:T(8,128)(2,1)S(1)} fusion(bf16[2048,2816]{1,0:T(8,128)(2,1)} %all-gather.2.cloned.1.call-done, bf16[448,1408]{1,0:T(8,128)(2,1)} %get-tuple-element.153, bf16[448,1408]{1,0:T(8,128)(2,1)S(1)} %get-tuple-element.152), kind=kOutput, calls=%fused_computation.50 | convolution fusion | flops 5173346304 | bytes 15892480 | tf_op jit(solution)/shard_map/dot_general | solution.py:379
  363.5 4.5 all-to-all-start.6
  368.1 7.3 convolution_convert_fusion.1
  375.4 10.5 %reshape.754 = bf16[1408,4,512]{2,1,0:T(4,128)(2,1)} reshape(bf16[1408,2048]{1,0:T(8,128)(2,1)} %convolution_convert_fusion.1) | data formatting | bytes 11534336 | tf_op jit(solution)/shard_map/reshape | solution.py:390
  385.9 18.4 %constant_dynamic-slice_fusion.3 = (bf16[1408,1,512]{2,1,0:T(2,128)(2,1)S(1)}, bf16[1408,1,512]{2,1,0:T(2,128)(2,1)S(1)}, bf16[1408,1,512]{2,1,0:T(2,128)(2,1)S(1)}, bf16[1408,1,512]{2,1,0:T(2,128)(2,1)S(1)}) fusion(bf16[1408,4,512]{2,1,0:T(4,128)(2,1)} %reshape.754, s32[]{:T(128)S(6)} %select_n.116, s32[]{:T(128)S(6)} %select_n.118, s32[]{:T(128)S(6)} %select_n.117, ...), kind=kLoop, calls=%fused_computation.324 | loop fusion | bytes 11534352 | tf_op jit(solution)/shard_map/dynamic-slice
  410.4 13.9 %collective-permute-done.57 = bf16[704,512]{1,0:T(8,128)(2,1)S(1)} collective-permute-done((bf16[704,512]{1,0:T(8,128)(2,1)S(1)}, bf16[704,512]{1,0:T(8,128)(2,1)S(1)}, u32[]{:S(2)}, u32[]{:S(2)}) %collective-permute-start.57) | collective-permute-done | bytes 720928 | tf_op jit(solution)/shard_map/ppermute | solution.py:74
  441.0 8.4 %all-to-all-done.7 = bf16[4,40,2176]{2,1,0:T(8,128)(2,1)} async-done(((bf16[4,40,2176]{2,1,0:T(8,128)(2,1)}), bf16[4,40,2176]{2,1,0:T(8,128)(2,1)}, u32[]{:S(2)}, u32[]{:S(2)}) %all-to-all-start.7) | async-done | bytes 696352 | tf_op jit(solution)/shard_map/all_to_all | solution.py:24
  457.8 4.9 all-to-all-start.8
  463.0 10.8 %convolution_convert_fusion = bf16[2048,2816]{1,0:T(8,128)(2,1)} fusion(bf16[448,2048]{1,0:T(8,128)(2,1)} %bitcast.44, bf16[448,1408]{1,0:T(8,128)(2,1)} %get-tuple-element.153, bf16[448,1408]{1,0:T(8,128)(2,1)} %copy-done.73), kind=kOutput, calls=%fused_computation.3 | convolution fusion | flops 5178195968 | bytes 15892480 | tf_op jit(solution)/shard_map/dot_general | solution.py:381
  473.8 7.3 fusion.21
  481.1 4.9 fusion.25
  489.8 10.1 %concatenate.144 = bf16[2048,1408]{1,0:T(8,128)(2,1)} concatenate(bf16[2048,1288]{1,0:T(8,128)(2,1)} %broadcast_in_dim.39, bf16[2048,8]{1,0:T(8,128)(2,1)S(1)} %copy.610, bf16[2048,1]{1,0:T(8,128)(2,1)S(1)} %convert_element_type.647, bf16[2048,111]{1,0:T(8,128)(2,1)S(1)} %broadcast_in_dim.40), dimensions={1} | concatenate | bytes 11534336 | tf_op jit(solution)/shard_map/concatenate | solution.py:469
  499.9 5.5 fusion.163
  509.6 4.4 convolution_bitcast_fusion
  514.9 7.5 %convolution_convert_fusion.4 = bf16[2048,1024]{1,0:T(8,128)(2,1)} fusion(bf16[640,2048]{1,0:T(8,128)(2,1)} %bitcast.59, bf16[80,8,8,128]{3,2,1,0:T(8,128)(2,1)} %bitcast.444), kind=kOutput, calls=%fused_computation.37 | convolution fusion | flops 2686451712 | bytes 8126464 | tf_op jit(solution)/shard_map/dot_general | solution.py:455
  522.4 4.5 all-to-all-start.9
  527.0 6.7 fusion.1
  556.9 9.0 %convolution_convert_fusion.5 = bf16[640,2048]{1,0:T(8,128)(2,1)} fusion(bf16[640,1408]{1,0:T(8,128)(2,1)} %concatenate.143, bf16[2048,1408]{1,0:T(8,128)(2,1)} %bitcast.384), kind=kOutput, calls=%fused_computation.46 | convolution fusion | flops 3692298240 | bytes 10190848 | tf_op jit(solution)/shard_map/dot_general | solution.py:460
  565.8 7.0 all-to-all-start.10
  581.6 7.5 fusion.4
  589.1 22.5 %collective-permute-done.28 = bf16[40,2048]{1,0:T(8,128)(2,1)S(1)} collective-permute-done((bf16[40,2048]{1,0:T(8,128)(2,1)S(1)}, bf16[40,2048]{1,0:T(8,128)(2,1)S(1)}, u32[]{:S(2)}, u32[]{:S(2)}) %collective-permute-start.28) | collective-permute-done | bytes 163872 | tf_op jit(solution)/shard_map/ppermute | solution.py:32
  611.7 8.5 %collective-permute-done.27 = bf16[40,2048]{1,0:T(8,128)(2,1)S(1)} collective-permute-done((bf16[40,2048]{1,0:T(8,128)(2,1)S(1)}, bf16[40,2048]{1,0:T(8,128)(2,1)S(1)}, u32[]{:S(2)}, u32[]{:S(2)}) %collective-permute-start.27) | collective-permute-done | bytes 163872 | tf_op jit(solution)/shard_map/ppermute | solution.py:32
  626.2 4.8 collective-permute-done.30
  641.1 5.3 collective-permute-done.48
  655.0 6.0 collective-permute-done.51
  661.0 4.2 collective-permute-done.49
  679.3 4.5 collective-permute-done.37
  688.0 10.8 %collective-permute-done.40 = bf16[256,1408]{1,0:T(8,128)(2,1)S(1)} collective-permute-done((bf16[256,1408]{1,0:T(8,128)(2,1)S(1)}, bf16[256,1408]{1,0:T(8,128)(2,1)S(1)}, u32[]{:S(2)}, u32[]{:S(2)}) %collective-permute-start.40) | collective-permute-done | bytes 720928 | tf_op jit(solution)/shard_map/ppermute | solution.py:81
  707.9 5.1 collective-permute-done.42
  733.5 7.2 reshape.766
  (517 shorter events, 300.7 us)
Async XLA Ops:
  10.2 50.1 %collective-permute-start = (bf16[160,2176]{1,0:T(8,128)(2,1)}, bf16[160,2176]{1,0:T(8,128)(2,1)}, u32[]{:S(2)}, u32[]{:S(2)}) collective-permute-start(bf16[160,2176]{1,0:T(8,128)(2,1)} %fusion.66), channel_id=1, source_target_pairs={{0,24},{8,0},{16,8},{24,16},{1,25},{9,1},{17,9},{25,17},{2,26},{10... | collective-permute-start | bytes 2088968 | tf_op jit(solution)/shard_map/ppermute | solution.py:32
  13.3 53.5 %collective-permute-start.1 = (bf16[160,2176]{1,0:T(8,128)(2,1)}, bf16[160,2176]{1,0:T(8,128)(2,1)}, u32[]{:S(2)}, u32[]{:S(2)}) collective-permute-start(bf16[160,2176]{1,0:T(8,128)(2,1)} %fusion.66), channel_id=1, source_target_pairs={{0,16},{8,24},{16,0},{24,8},{1,17},{9,25},{17,1},{25,9},{2,18},{10... | collective-permute-start | bytes 2088968 | tf_op jit(solution)/shard_map/ppermute | solution.py:32
  14.0 58.9 %collective-permute-start.2 = (bf16[160,2176]{1,0:T(8,128)(2,1)}, bf16[160,2176]{1,0:T(8,128)(2,1)}, u32[]{:S(2)}, u32[]{:S(2)}) collective-permute-start(bf16[160,2176]{1,0:T(8,128)(2,1)} %fusion.66), channel_id=1, source_target_pairs={{0,8},{8,16},{16,24},{24,0},{1,9},{9,17},{17,25},{25,1},{2,10},{10... | collective-permute-start | bytes 2088968 | tf_op jit(solution)/shard_map/ppermute | solution.py:32
  17.9 34.8 %all-to-all-start.1 = ((bf16[4,64,1024]{2,1,0:T(8,128)(2,1)}), bf16[4,64,1024]{2,1,0:T(8,128)(2,1)S(1)}, u32[]{:S(2)}, u32[]{:S(2)}) async-start(bf16[4,64,1024]{2,1,0:T(8,128)(2,1)} %reshape.720), calls=%async_computation.1 | async-start | bytes 1048576 | tf_op jit(solution)/shard_map/all_to_all | solution.py:24
  21.4 313.6 %all-gather.2.cloned.1.call-start = ((), (), s32[]{:S(2)}) async-start(), calls=%async_computation.12 | async-start | bytes 14417920 | tf_op jit(solution)/shard_map/all_gather | solution.py:221
  52.7 14.1 %all-to-all-start = ((bf16[4,64,1408]{2,1,0:T(8,128)(2,1)}), bf16[4,64,1408]{2,1,0:T(8,128)(2,1)S(1)}, u32[]{:S(2)}, u32[]{:S(2)}) async-start(bf16[4,64,1408]{2,1,0:T(8,128)(2,1)} %pad_maximum_fusion.7), calls=%async_computation | async-start | bytes 1441792 | tf_op jit(solution)/shard_map/all_to_all | solution.py:24
  56.2 34.5 %collective-permute-start.13 = (bf16[256,1024]{1,0:T(8,128)(2,1)S(1)}, bf16[256,1024]{1,0:T(8,128)(2,1)S(1)}, u32[]{:S(2)}, u32[]{:S(2)}) collective-permute-start(bf16[256,1024]{1,0:T(8,128)(2,1)S(1)} %bitcast.388), channel_id=1, source_target_pairs={{0,96},{32,0},{64,32},{96,64},{1,97},{33,1},{65,33},{97,65},{2,98}... | collective-permute-start | bytes 1572872 | tf_op jit(solution)/shard_map/ppermute | solution.py:63
  60.3 27.3 %collective-permute-start.14 = (bf16[256,1024]{1,0:T(8,128)(2,1)S(1)}, bf16[256,1024]{1,0:T(8,128)(2,1)}, u32[]{:S(2)}, u32[]{:S(2)}) collective-permute-start(bf16[256,1024]{1,0:T(8,128)(2,1)S(1)} %bitcast.389), channel_id=1, source_target_pairs={{0,32},{32,64},{64,96},{96,0},{1,33},{33,65},{65,97},{97,1},{2,34}... | collective-permute-start | bytes 1572872 | tf_op jit(solution)/shard_map/ppermute | solution.py:62
  60.3 73.0 %collective-permute-start.17 = (bf16[256,1024]{1,0:T(8,128)(2,1)S(1)}, bf16[256,1024]{1,0:T(8,128)(2,1)}, u32[]{:S(2)}, u32[]{:S(2)}) collective-permute-start(bf16[256,1024]{1,0:T(8,128)(2,1)S(1)} %bitcast.390), channel_id=1, source_target_pairs={{0,4},{4,0},{1,5},{5,1},{2,6},{6,2},{3,7},{7,3},{8,12},{12,8},{9,1... | collective-permute-start | bytes 1572872 | tf_op jit(solution)/shard_map/ppermute | solution.py:126
  66.8 65.3 %collective-permute-start.3 = (bf16[256,1408]{1,0:T(8,128)(2,1)S(1)}, bf16[256,1408]{1,0:T(8,128)(2,1)S(1)}, u32[]{:S(2)}, u32[]{:S(2)}) collective-permute-start(bf16[256,1408]{1,0:T(8,128)(2,1)S(1)} %bitcast.385), channel_id=1, source_target_pairs={{0,96},{32,0},{64,32},{96,64},{1,97},{33,1},{65,33},{97,65},{2,98}... | collective-permute-start | bytes 2162696 | tf_op jit(solution)/shard_map/ppermute | solution.py:63
  72.8 55.9 %collective-permute-start.4 = (bf16[256,1408]{1,0:T(8,128)(2,1)S(1)}, bf16[256,1408]{1,0:T(8,128)(2,1)S(1)}, u32[]{:S(2)}, u32[]{:S(2)}) collective-permute-start(bf16[256,1408]{1,0:T(8,128)(2,1)S(1)} %bitcast.386), channel_id=1, source_target_pairs={{0,32},{32,64},{64,96},{96,0},{1,33},{33,65},{65,97},{97,1},{2,34}... | collective-permute-start | bytes 2162696 | tf_op jit(solution)/shard_map/ppermute | solution.py:62
  88.6 40.2 %collective-permute-start.15 = (bf16[128,1024]{1,0:T(8,128)(2,1)S(1)}, bf16[128,1024]{1,0:T(8,128)(2,1)S(1)}, u32[]{:S(2)}, u32[]{:S(2)}) collective-permute-start(bf16[128,1024]{1,0:T(8,128)(2,1)S(1)} %slice.351), channel_id=1, source_target_pairs={{0,32},{32,64},{64,96},{96,0},{1,33},{33,65},{65,97},{97,1},{2,34}... | collective-permute-start | bytes 786440 | tf_op jit(solution)/shard_map/ppermute | solution.py:64
  90.7 41.3 %collective-permute-start.16 = (bf16[128,1024]{1,0:T(8,128)(2,1)S(1)}, bf16[128,1024]{1,0:T(8,128)(2,1)}, u32[]{:S(2)}, u32[]{:S(2)}) collective-permute-start(bf16[128,1024]{1,0:T(8,128)(2,1)S(1)} %slice.352), channel_id=1, source_target_pairs={{0,96},{32,0},{64,32},{96,64},{1,97},{33,1},{65,33},{97,65},{2,98}... | collective-permute-start | bytes 786440 | tf_op jit(solution)/shard_map/ppermute | solution.py:65
  128.8 14.5 %collective-permute-start.21 = (bf16[256,1024]{1,0:T(8,128)(2,1)}, bf16[256,1024]{1,0:T(8,128)(2,1)}, u32[]{:S(2)}, u32[]{:S(2)}) collective-permute-start(bf16[256,1024]{1,0:T(8,128)(2,1)} %collective-permute-done.14), channel_id=1, source_target_pairs={{0,4},{4,0},{1,5},{5,1},{2,6},{6,2},{3,7},{7,3},{8,12},{12,8},{9,1... | collective-permute-start | bytes 1572872 | tf_op jit(solution)/shard_map/ppermute | solution.py:126
  133.3 20.2 %collective-permute-start.5 = (bf16[128,1408]{1,0:T(8,128)(2,1)}, bf16[128,1408]{1,0:T(8,128)(2,1)}, u32[]{:S(2)}, u32[]{:S(2)}) collective-permute-start(bf16[128,1408]{1,0:T(8,128)(2,1)} %slice.340), channel_id=1, source_target_pairs={{0,32},{32,64},{64,96},{96,0},{1,33},{33,65},{65,97},{97,1},{2,34}... | collective-permute-start | bytes 1081352 | tf_op jit(solution)/shard_map/ppermute | solution.py:64
  134.1 19.6 %collective-permute-start.6 = (bf16[128,1408]{1,0:T(8,128)(2,1)}, bf16[128,1408]{1,0:T(8,128)(2,1)}, u32[]{:S(2)}, u32[]{:S(2)}) collective-permute-start(bf16[128,1408]{1,0:T(8,128)(2,1)} %slice.341), channel_id=1, source_target_pairs={{0,96},{32,0},{64,32},{96,64},{1,97},{33,1},{65,33},{97,65},{2,98}... | collective-permute-start | bytes 1081352 | tf_op jit(solution)/shard_map/ppermute | solution.py:65
  142.6 17.8 %collective-permute-start.7 = (bf16[256,1408]{1,0:T(8,128)(2,1)S(1)}, bf16[256,1408]{1,0:T(8,128)(2,1)}, u32[]{:S(2)}, u32[]{:S(2)}) collective-permute-start(bf16[256,1408]{1,0:T(8,128)(2,1)S(1)} %bitcast.387), channel_id=1, source_target_pairs={{0,4},{4,0},{1,5},{5,1},{2,6},{6,2},{3,7},{7,3},{8,12},{12,8},{9,1... | collective-permute-start | bytes 2162696 | tf_op jit(solution)/shard_map/ppermute | solution.py:126
  142.7 17.7 %collective-permute-start.8 = (bf16[256,1408]{1,0:T(8,128)(2,1)S(1)}, bf16[256,1408]{1,0:T(8,128)(2,1)}, u32[]{:S(2)}, u32[]{:S(2)}) collective-permute-start(bf16[256,1408]{1,0:T(8,128)(2,1)S(1)} %collective-permute-done.3), channel_id=1, source_target_pairs={{0,4},{4,0},{1,5},{5,1},{2,6},{6,2},{3,7},{7,3},{8,12},{12,8},{9,1... | collective-permute-start | bytes 2162696 | tf_op jit(solution)/shard_map/ppermute | solution.py:126
  143.2 17.3 %collective-permute-start.11 = (bf16[256,1408]{1,0:T(8,128)(2,1)S(1)}, bf16[256,1408]{1,0:T(8,128)(2,1)}, u32[]{:S(2)}, u32[]{:S(2)}) collective-permute-start(bf16[256,1408]{1,0:T(8,128)(2,1)S(1)} %collective-permute-done.4), channel_id=1, source_target_pairs={{0,4},{4,0},{1,5},{5,1},{2,6},{6,2},{3,7},{7,3},{8,12},{12,8},{9,1... | collective-permute-start | bytes 2162696 | tf_op jit(solution)/shard_map/ppermute | solution.py:126
  201.8 48.5 %all-to-all-start.2 = ((bf16[16,40,2048]{2,1,0:T(8,128)(2,1)}), bf16[16,40,2048]{2,1,0:T(8,128)(2,1)S(1)}, u32[]{:S(2)}, u32[]{:S(2)}) async-start(bf16[16,40,2048]{2,1,0:T(8,128)(2,1)} %bitcast.439), calls=%async_computation.2 | async-start | bytes 5242880 | tf_op jit(solution)/shard_map/all_to_all | solution.py:24
  257.4 33.3 %collective-permute-start.22 = (bf16[1408,512]{1,0:T(8,128)(2,1)}, bf16[1408,512]{1,0:T(8,128)(2,1)S(1)}, u32[]{:S(2)}, u32[]{:S(2)}) collective-permute-start(bf16[1408,512]{1,0:T(8,128)(2,1)} %bitcast.416), channel_id=1, source_target_pairs={{0,96},{32,0},{64,32},{96,64},{1,97},{33,1},{65,33},{97,65},{2,98}... | collective-permute-start | bytes 4325384 | tf_op jit(solution)/shard_map/ppermute | solution.py:63
  260.5 34.7 %collective-permute-start.23 = (bf16[1408,512]{1,0:T(8,128)(2,1)}, bf16[1408,512]{1,0:T(8,128)(2,1)}, u32[]{:S(2)}, u32[]{:S(2)}) collective-permute-start(bf16[1408,512]{1,0:T(8,128)(2,1)} %bitcast.417), channel_id=1, source_target_pairs={{0,32},{32,64},{64,96},{96,0},{1,33},{33,65},{65,97},{97,1},{2,34}... | collective-permute-start | bytes 4325384 | tf_op jit(solution)/shard_map/ppermute | solution.py:62
  273.3 30.1 %all-to-all-start.5 = ((bf16[8,56,2176]{2,1,0:T(8,128)(2,1)}), bf16[8,56,2176]{2,1,0:T(8,128)(2,1)}, u32[]{:S(2)}, u32[]{:S(2)}) async-start(bf16[8,56,2176]{2,1,0:T(8,128)(2,1)} %bitcast.441), calls=%async_computation.5 | async-start | bytes 3899392 | tf_op jit(solution)/shard_map/all_to_all | solution.py:24
  291.6 17.8 %collective-permute-start.25 = (bf16[704,512]{1,0:T(8,128)(2,1)}, bf16[704,512]{1,0:T(8,128)(2,1)S(1)}, u32[]{:S(2)}, u32[]{:S(2)}) collective-permute-start(bf16[704,512]{1,0:T(8,128)(2,1)} %slice.359), channel_id=1, source_target_pairs={{0,96},{32,0},{64,32},{96,64},{1,97},{33,1},{65,33},{97,65},{2,98}... | collective-permute-start | bytes 2162696 | tf_op jit(solution)/shard_map/ppermute | solution.py:65
  297.3 17.2 %collective-permute-start.24 = (bf16[704,512]{1,0:T(8,128)(2,1)}, bf16[704,512]{1,0:T(8,128)(2,1)}, u32[]{:S(2)}, u32[]{:S(2)}) collective-permute-start(bf16[704,512]{1,0:T(8,128)(2,1)} %slice.358), channel_id=1, source_target_pairs={{0,32},{32,64},{64,96},{96,0},{1,33},{33,65},{65,97},{97,1},{2,34}... | collective-permute-start | bytes 2162696 | tf_op jit(solution)/shard_map/ppermute | solution.py:64
  303.4 29.1 %all-to-all-start.4 = ((bf16[8,56,2048]{2,1,0:T(8,128)(2,1)}), bf16[8,56,2048]{2,1,0:T(8,128)(2,1)}, u32[]{:S(2)}, u32[]{:S(2)}) async-start(bf16[8,56,2048]{2,1,0:T(8,128)(2,1)} %bitcast.409), calls=%async_computation.4 | async-start | bytes 3670016 | tf_op jit(solution)/shard_map/all_to_all | solution.py:24
  363.5 65.9 %all-to-all-start.6 = ((bf16[8,56,2176]{2,1,0:T(8,128)(2,1)}), bf16[8,56,2176]{2,1,0:T(8,128)(2,1)}, u32[]{:S(2)}, u32[]{:S(2)}) async-start(bf16[8,56,2176]{2,1,0:T(8,128)(2,1)} %bitcast.54), calls=%async_computation.6 | async-start | bytes 3899392 | tf_op jit(solution)/shard_map/all_to_all | solution.py:24
  405.6 18.7 %collective-permute-start.57 = (bf16[704,512]{1,0:T(8,128)(2,1)S(1)}, bf16[704,512]{1,0:T(8,128)(2,1)S(1)}, u32[]{:S(2)}, u32[]{:S(2)}) collective-permute-start(bf16[704,512]{1,0:T(8,128)(2,1)S(1)} %get-tuple-element.177), channel_id=1, source_target_pairs={{0,96},{32,0},{64,32},{96,64},{1,97},{33,1},{65,33},{97,65},{2,98}... | collective-permute-start | bytes 2162696 | tf_op jit(solution)/shard_map/ppermute | solution.py:74
  409.2 29.0 %collective-permute-start.55 = (bf16[704,512]{1,0:T(8,128)(2,1)}, bf16[704,512]{1,0:T(8,128)(2,1)}, u32[]{:S(2)}, u32[]{:S(2)}) collective-permute-start(bf16[704,512]{1,0:T(8,128)(2,1)} %get-tuple-element.176), channel_id=1, source_target_pairs={{0,32},{32,64},{64,96},{96,0},{1,33},{33,65},{65,97},{97,1},{2,34}... | collective-permute-start | bytes 2162696 | tf_op jit(solution)/shard_map/ppermute | solution.py:73
  425.8 55.4 %collective-permute-start.58 = (bf16[1408,512]{1,0:T(8,128)(2,1)}, bf16[1408,512]{1,0:T(8,128)(2,1)}, u32[]{:S(2)}, u32[]{:S(2)}) collective-permute-start(bf16[1408,512]{1,0:T(8,128)(2,1)} %pad_maximum_fusion.5), channel_id=1, source_target_pairs={{0,96},{32,0},{64,32},{96,64},{1,97},{33,1},{65,33},{97,65},{2,98}... | collective-permute-start | bytes 4325384 | tf_op jit(solution)/shard_map/ppermute | solution.py:81
  434.0 15.4 %all-to-all-start.7 = ((bf16[4,40,2176]{2,1,0:T(8,128)(2,1)}), bf16[4,40,2176]{2,1,0:T(8,128)(2,1)}, u32[]{:S(2)}, u32[]{:S(2)}) async-start(bf16[4,40,2176]{2,1,0:T(8,128)(2,1)} %bitcast.435), calls=%async_computation.7 | async-start | bytes 1392640 | tf_op jit(solution)/shard_map/all_to_all | solution.py:24
  441.0 40.2 %collective-permute-start.56 = (bf16[1408,512]{1,0:T(8,128)(2,1)}, bf16[1408,512]{1,0:T(8,128)(2,1)}, u32[]{:S(2)}, u32[]{:S(2)}) collective-permute-start(bf16[1408,512]{1,0:T(8,128)(2,1)} %pad_maximum_fusion.4), channel_id=1, source_target_pairs={{0,32},{32,64},{64,96},{96,0},{1,33},{33,65},{65,97},{97,1},{2,34}... | collective-permute-start | bytes 4325384 | tf_op jit(solution)/shard_map/ppermute | solution.py:80
  457.8 42.1 %all-to-all-start.8 = ((bf16[16,40,2048]{2,1,0:T(8,128)(2,1)}), bf16[16,40,2048]{2,1,0:T(8,128)(2,1)}, u32[]{:S(2)}, u32[]{:S(2)}) async-start(bf16[16,40,2048]{2,1,0:T(8,128)(2,1)} %broadcast_in_dim.38), calls=%async_computation.8 | async-start | bytes 5242880 | tf_op jit(solution)/shard_map/all_to_all | solution.py:24
  462.7 270.8 %reduce-scatter.2.cloned.1.call-start = ((), (), s32[]{:S(2)}) async-start(), calls=%async_computation.13 | async-start | bytes 14417920 | tf_op jit(solution)/shard_map/reduce_scatter | solution.py:386
  522.4 43.4 %all-to-all-start.9 = ((bf16[8,56,2048]{2,1,0:T(8,128)(2,1)}), bf16[8,56,2048]{2,1,0:T(8,128)(2,1)}, u32[]{:S(2)}, u32[]{:S(2)}) async-start(bf16[8,56,2048]{2,1,0:T(8,128)(2,1)} %bitcast.442), calls=%async_computation.9 | async-start | bytes 3670016 | tf_op jit(solution)/shard_map/all_to_all | solution.py:24
  544.4 89.7 %collective-permute-start.47 = (bf16[16,64,1024]{2,1,0:T(8,128)(2,1)}, bf16[16,64,1024]{2,1,0:T(8,128)(2,1)}, u32[]{:S(2)}, u32[]{:S(2)}) collective-permute-start(bf16[16,64,1024]{2,1,0:T(8,128)(2,1)} %dynamic-slice_bitcast_fusion.1), channel_id=1, source_target_pairs={{0,4},{4,0},{1,5},{5,1},{2,6},{6,2},{3,7},{7,3},{8,12},{12,8},{9,1... | collective-permute-start | bytes 6291464 | tf_op jit(solution)/shard_map/ppermute | solution.py:135
  565.8 85.4 %all-to-all-start.10 = ((bf16[16,40,2048]{2,1,0:T(8,128)(2,1)}), bf16[16,40,2048]{2,1,0:T(8,128)(2,1)S(1)}, u32[]{:S(2)}, u32[]{:S(2)}) async-start(bf16[16,40,2048]{2,1,0:T(8,128)(2,1)} %bitcast.438), calls=%async_computation.10 | async-start | bytes 5242880 | tf_op jit(solution)/shard_map/all_to_all | solution.py:24
  575.5 36.2 %collective-permute-start.28 = (bf16[40,2048]{1,0:T(8,128)(2,1)S(1)}, bf16[40,2048]{1,0:T(8,128)(2,1)S(1)}, u32[]{:S(2)}, u32[]{:S(2)}) collective-permute-start(bf16[40,2048]{1,0:T(8,128)(2,1)S(1)} %get-tuple-element.187), channel_id=1, source_target_pairs={{0,1},{1,2},{2,3},{3,0},{4,5},{5,6},{6,7},{7,4},{8,9},{9,10},{10,1... | collective-permute-start | bytes 491528 | tf_op jit(solution)/shard_map/ppermute | solution.py:32
  577.5 42.7 %collective-permute-start.27 = (bf16[40,2048]{1,0:T(8,128)(2,1)S(1)}, bf16[40,2048]{1,0:T(8,128)(2,1)S(1)}, u32[]{:S(2)}, u32[]{:S(2)}) collective-permute-start(bf16[40,2048]{1,0:T(8,128)(2,1)S(1)} %get-tuple-element.188), channel_id=1, source_target_pairs={{0,2},{1,3},{2,0},{3,1},{4,6},{5,7},{6,4},{7,5},{8,10},{9,11},{10,... | collective-permute-start | bytes 491528 | tf_op jit(solution)/shard_map/ppermute | solution.py:32
  580.2 40.0 %collective-permute-start.26 = (bf16[40,2048]{1,0:T(8,128)(2,1)S(1)}, bf16[40,2048]{1,0:T(8,128)(2,1)S(1)}, u32[]{:S(2)}, u32[]{:S(2)}) collective-permute-start(bf16[40,2048]{1,0:T(8,128)(2,1)S(1)} %get-tuple-element.186), channel_id=1, source_target_pairs={{0,3},{1,0},{2,1},{3,2},{4,7},{5,4},{6,5},{7,6},{8,11},{9,8},{10,9... | collective-permute-start | bytes 491528 | tf_op jit(solution)/shard_map/ppermute | solution.py:32
  622.4 49.0 %collective-permute-start.36 = (bf16[16,64,1408]{2,1,0:T(8,128)(2,1)}, bf16[16,64,1408]{2,1,0:T(8,128)(2,1)}, u32[]{:S(2)}, u32[]{:S(2)}) collective-permute-start(bf16[16,64,1408]{2,1,0:T(8,128)(2,1)} %dynamic-slice_bitcast_fusion), channel_id=1, source_target_pairs={{0,4},{4,0},{1,5},{5,1},{2,6},{6,2},{3,7},{7,3},{8,12},{12,8},{9,1... | collective-permute-start | bytes 8650760 | tf_op jit(solution)/shard_map/ppermute | solution.py:135
  651.2 14.0 %collective-permute-start.49 = (bf16[256,1024]{1,0:T(8,128)(2,1)}, bf16[256,1024]{1,0:T(8,128)(2,1)}, u32[]{:S(2)}, u32[]{:S(2)}) collective-permute-start(bf16[256,1024]{1,0:T(8,128)(2,1)} %pad_maximum_fusion.12), channel_id=1, source_target_pairs={{0,32},{32,64},{64,96},{96,0},{1,33},{33,65},{65,97},{97,1},{2,34}... | collective-permute-start | bytes 1572872 | tf_op jit(solution)/shard_map/ppermute | solution.py:80
  654.0 14.6 %collective-permute-start.33 = (bf16[40,2048]{1,0:T(8,128)(2,1)S(1)}, bf16[40,2048]{1,0:T(8,128)(2,1)S(1)}, u32[]{:S(2)}, u32[]{:S(2)}) collective-permute-start(bf16[40,2048]{1,0:T(8,128)(2,1)S(1)} %get-tuple-element.137), channel_id=1, source_target_pairs={{0,3},{1,0},{2,1},{3,2},{4,7},{5,4},{6,5},{7,6},{8,11},{9,8},{10,9... | collective-permute-start | bytes 491528 | tf_op jit(solution)/shard_map/ppermute | solution.py:32
  654.3 15.7 %collective-permute-start.34 = (bf16[40,2048]{1,0:T(8,128)(2,1)S(1)}, bf16[40,2048]{1,0:T(8,128)(2,1)S(1)}, u32[]{:S(2)}, u32[]{:S(2)}) collective-permute-start(bf16[40,2048]{1,0:T(8,128)(2,1)S(1)} %get-tuple-element.137), channel_id=1, source_target_pairs={{0,2},{1,3},{2,0},{3,1},{4,6},{5,7},{6,4},{7,5},{8,10},{9,11},{10,... | collective-permute-start | bytes 491528 | tf_op jit(solution)/shard_map/ppermute | solution.py:32
  668.6 19.3 %collective-permute-start.53 = (bf16[64,1024]{1,0:T(8,128)(2,1)S(1)}, bf16[64,1024]{1,0:T(8,128)(2,1)S(1)}, u32[]{:S(2)}, u32[]{:S(2)}) collective-permute-start(bf16[64,1024]{1,0:T(8,128)(2,1)S(1)} %get-tuple-element.193), channel_id=1, source_target_pairs={{0,16},{8,24},{16,0},{24,8},{1,17},{9,25},{17,1},{25,9},{2,18},{10... | collective-permute-start | bytes 393224 | tf_op jit(solution)/shard_map/ppermute | solution.py:32
  669.9 18.0 %collective-permute-start.54 = (bf16[64,1024]{1,0:T(8,128)(2,1)S(1)}, bf16[64,1024]{1,0:T(8,128)(2,1)S(1)}, u32[]{:S(2)}, u32[]{:S(2)}) collective-permute-start(bf16[64,1024]{1,0:T(8,128)(2,1)S(1)} %get-tuple-element.191), channel_id=1, source_target_pairs={{0,8},{8,16},{16,24},{24,0},{1,9},{9,17},{17,25},{25,1},{2,10},{10... | collective-permute-start | bytes 393224 | tf_op jit(solution)/shard_map/ppermute | solution.py:32
  684.1 14.7 %collective-permute-start.40 = (bf16[256,1408]{1,0:T(8,128)(2,1)S(1)}, bf16[256,1408]{1,0:T(8,128)(2,1)S(1)}, u32[]{:S(2)}, u32[]{:S(2)}) collective-permute-start(bf16[256,1408]{1,0:T(8,128)(2,1)S(1)} %pad_maximum_fusion.9), channel_id=1, source_target_pairs={{0,96},{32,0},{64,32},{96,64},{1,97},{33,1},{65,33},{97,65},{2,98}... | collective-permute-start | bytes 2162696 | tf_op jit(solution)/shard_map/ppermute | solution.py:81
  687.8 14.1 %collective-permute-start.38 = (bf16[256,1408]{1,0:T(8,128)(2,1)S(1)}, bf16[256,1408]{1,0:T(8,128)(2,1)S(1)}, u32[]{:S(2)}, u32[]{:S(2)}) collective-permute-start(bf16[256,1408]{1,0:T(8,128)(2,1)S(1)} %pad_maximum_fusion.8), channel_id=1, source_target_pairs={{0,32},{32,64},{64,96},{96,0},{1,33},{33,65},{65,97},{97,1},{2,34}... | collective-permute-start | bytes 2162696 | tf_op jit(solution)/shard_map/ppermute | solution.py:80
  (100 other events, 1101.9 us)
Sparse Core Ops, SparseCore 0:
  24.5 152.5 all-gather.1
  474.0 105.2 reduce-scatter.1

commit v2 on v1

--- a/solution.py
+++ b/solution.py
@@ -82,58 +82,30 @@
     )
 
 
-def assemble(own, other, place, core, columns):
-    def kernel(at_ref, *refs):
-        out, sem = refs[10], refs[11]
-        z, c = at_ref[0], at_ref[1]
-        copies = []
-        for half, pieces in ((c, refs[:5]), (1 - c, refs[5:10])):
-            for piece, shift, low, count in zip(
-                pieces, (0, 1, 2, 2, 3), (0, 0, 0, 2, 0), (4, 4, 2, 2, 4)
-            ):
-                copies.append(
-                    pltpu.make_async_copy(
-                        piece, out.at[lax.rem(z + shift, 4), pl.ds(low, count), half], sem.at[len(copies)]
-                    )
-                )
-        for copy in copies:
-            copy.start()
-        for copy in copies:
-            copy.wait()
-
-    shaped = [p.reshape(-1, 64, columns) for p in (*own, *other)]
-    return pl.pallas_call(
-        kernel,
-        out_shape=jax.ShapeDtypeStruct((4, 4, 2, 64, columns), BF),
-        in_specs=[pl.BlockSpec(memory_space=pltpu.SMEM)] + [pl.BlockSpec(memory_space=pl.ANY)] * 10,
-        out_specs=pl.BlockSpec(memory_space=pltpu.VMEM),
-        scratch_shapes=[pltpu.SemaphoreType.DMA((10,))],
-        compiler_params=pltpu.CompilerParams(vmem_limit_bytes=16 * 1024 * 1024),
-        cost_estimate=pl.CostEstimate(
-            flops=0, bytes_accessed=8 * MODEL_WIDTH * columns, transcendentals=0
-        ),
-    )(jnp.stack([place, core]), *shaped).reshape(MODEL_WIDTH, columns)
-
-
 def heads_first(shard):
     columns = shard.shape[1] * HEAD_SIZE
     return shard.reshape(64, -1, 4, HEAD_SIZE).transpose(2, 0, 1, 3).reshape(4, 64, columns)
 
 
-def gather_rows(by_head, place, core):
-    columns = by_head.shape[2]
-    own = ring_pieces(exchange(by_head, "y").reshape(256, columns), "dp")
-    other = [lax.ppermute(p, "core", SWAP) for p in own]
-    return assemble(own, other, place, core, columns), own
+def after(value, other):
+    return lax.optimization_barrier((value, other))[0]
+
+
+def core_first(rows):
+    return rows.reshape(-1, 4, 4, 2, 64).transpose(0, 1, 3, 2, 4).reshape(-1, MODEL_WIDTH)
+
+
+def core_last(rows):
+    return rows.reshape(-1, 4, 2, 4, 64).transpose(0, 1, 3, 2, 4).reshape(-1, MODEL_WIDTH)
 
 
 def scatter_rows(grad, core):
     columns = grad.shape[1]
-    parts = grad.reshape(16, 2, 64, columns)
+    parts = grad.reshape(4, 2, 256, columns)
     keep = lax.dynamic_index_in_dim(parts, core, 1, keepdims=False)
     give = lax.dynamic_index_in_dim(parts, 1 - core, 1, keepdims=False)
     both = keep.astype(F32) + lax.ppermute(give, "core", SWAP).astype(F32)
-    summed = ring_sum(both.astype(BF).reshape(4, 256, columns), "dp")
+    summed = ring_sum(both.astype(BF), "dp")
     return in_order(
         send_direct(summed.astype(BF).reshape(4, 64, columns), "y"), lax.axis_index("y")
     )
@@ -156,6 +128,151 @@
 def turn(heads, cosine, sine):
     first, second = heads[..., :64], heads[..., 64:]
     return jnp.concatenate([first * cosine - second * sine, second * cosine + first * sine], axis=-1)
+
+
+EXTENTS = (256, 384, 512, 640)
+SCALE = HEAD_SIZE**-0.5
+
+
+def masked_scores(query, key, row_meta, key_meta):
+    raw = lax.dot_general(query, key, LAST, preferred_element_type=F32) * SCALE
+    gap = row_meta[:, 0:1] - key_meta[0:1]
+    allowed = (gap >= 0) & (gap < WINDOW) & (row_meta[:, 1:2] == key_meta[1:2])
+    return jnp.where(jnp.concatenate([allowed, allowed], axis=0), raw, -1e30)
+
+
+def forward_kernel(proj, own, other, routes, cosine, sine, row_meta, key_meta, *outs):
+    query_out, attended_out, total_out, gates_out, mixed_out = outs
+    count = proj.shape[0] // 4
+    for i in range(4):
+        rows = pl.ds(count * i, count)
+        extent = EXTENTS[i]
+        logits = proj[rows, 1280:1288]
+        lane = lax.broadcasted_iota(jnp.int32, (count, EXPERTS), 1)
+        named = [routes[rows, 0:1], routes[rows, 1:2]]
+        chosen = [jnp.sum(jnp.where(lane == n, logits, 0.0), axis=1, keepdims=True) for n in named]
+        top = jnp.maximum(chosen[0], chosen[1])
+        power = [jnp.exp(c - top) for c in chosen]
+        gates = [p / (power[0] + power[1]) for p in power]
+        gates_out[rows, 0:1] = gates[0]
+        gates_out[rows, 1:2] = gates[1]
+        cos, sin = cosine[rows, :], sine[rows, :]
+        picked = []
+        for n in named:
+            q = jnp.zeros((count, HEAD_SIZE), F32)
+            for e in range(EXPERTS):
+                q = q + jnp.where(n == e, proj[rows, HEAD_SIZE * e : HEAD_SIZE * (e + 1)], 0.0)
+            picked.append(q * cos + pltpu.roll(q, 64, 1) * sin)
+        query = jnp.concatenate(picked, axis=0).astype(BF)
+        query_out[i] = query
+        halves = (own, other)
+        scores = [
+            masked_scores(
+                query, h[:extent, :HEAD_SIZE], row_meta[rows, :], key_meta[k, :, :extent]
+            )
+            for k, h in enumerate(halves)
+        ]
+        row_max = jnp.maximum(
+            jnp.max(scores[0], axis=1, keepdims=True), jnp.max(scores[1], axis=1, keepdims=True)
+        )
+        weights = [jnp.exp(s - row_max) for s in scores]
+        total = jnp.sum(weights[0], axis=1, keepdims=True) + jnp.sum(weights[1], axis=1, keepdims=True)
+        inverse = 1.0 / total
+        attended = sum(
+            jnp.dot((w * inverse).astype(BF), h[:extent, HEAD_SIZE:], preferred_element_type=F32)
+            for w, h in zip(weights, halves)
+        )
+        attended_out[i] = attended
+        total_out[i] = row_max + jnp.log(total)
+        for e in range(EXPERTS):
+            mixed_out[rows, HEAD_SIZE * e : HEAD_SIZE * (e + 1)] = (
+                jnp.where(named[0] == e, gates[0], 0.0) * attended[:count]
+                + jnp.where(named[1] == e, gates[1], 0.0) * attended[count:]
+            ).astype(BF)
+
+
+def backward_kernel(
+    grad_mixed, query_in, own, other, attended_in, total_in, gates_in, routes, cosine, sine, row_meta, key_meta, *outs
+):
+    grad_query_out, grad_logit_out, grad_own_out, grad_other_out, sums = outs
+    count = grad_mixed.shape[0] // 4
+    sums[...] = jnp.zeros_like(sums)
+    for i in range(4):
+        rows = pl.ds(count * i, count)
+        extent = EXTENTS[i]
+        named = [routes[rows, 0:1], routes[rows, 1:2]]
+        gates = [gates_in[rows, 0:1], gates_in[rows, 1:2]]
+        cos, sin = cosine[rows, :], sine[rows, :]
+        attended = attended_in[i]
+        picked = []
+        for n in named:
+            g = jnp.zeros((count, HEAD_SIZE), F32)
+            for e in range(EXPERTS):
+                g = g + jnp.where(n == e, grad_mixed[rows, HEAD_SIZE * e : HEAD_SIZE * (e + 1)], 0.0)
+            picked.append(g)
+        gate_grads = [
+            jnp.sum(p * attended[count * j : count * (j + 1)], axis=1, keepdims=True)
+            for j, p in enumerate(picked)
+        ]
+        level = gates[0] * gate_grads[0] + gates[1] * gate_grads[1]
+        lane = lax.broadcasted_iota(jnp.int32, (count, HEAD_SIZE), 1)
+        grad_logit_out[rows, :] = sum(
+            jnp.where(lane == n, g * (d - level), 0.0) for n, g, d in zip(named, gates, gate_grads)
+        ).astype(BF)
+        grad_attended = jnp.concatenate(
+            [gates[0] * picked[0], gates[1] * picked[1]], axis=0
+        ).astype(BF)
+        query = query_in[i]
+        total = total_in[i]
+        probs, grad_probs = [], []
+        delta = jnp.zeros((2 * count, 1), F32)
+        for k, h in enumerate((own, other)):
+            score = masked_scores(
+                query, h[:extent, :HEAD_SIZE], row_meta[rows, :], key_meta[k, :, :extent]
+            )
+            prob = jnp.exp(score - total)
+            grad_prob = lax.dot_general(
+                grad_attended, h[:extent, HEAD_SIZE:], LAST, preferred_element_type=F32
+            )
+            delta = delta + jnp.sum(prob * grad_prob, axis=1, keepdims=True)
+            probs.append(prob)
+            grad_probs.append(grad_prob)
+        grad_query = jnp.zeros((2 * count, HEAD_SIZE), F32)
+        for k, h in enumerate((own, other)):
+            grad_score = (probs[k] * (grad_probs[k] - delta)).astype(BF)
+            grad_query = grad_query + jnp.dot(
+                grad_score, h[:extent, :HEAD_SIZE], preferred_element_type=F32
+            )
+            sums[k, :extent, :HEAD_SIZE] += (
+                lax.dot_general(grad_score, query, ROWS, preferred_element_type=F32) * SCALE
+            )
+            sums[k, :extent, HEAD_SIZE:] += lax.dot_general(
+                probs[k].astype(BF), grad_attended, ROWS, preferred_element_type=F32
+            )
+        grad_query = grad_query * SCALE
+        turned = [
+            g * cos - pltpu.roll(g, 64, 1) * sin for g in (grad_query[:count], grad_query[count:])
+        ]
+        for e in range(EXPERTS):
+            grad_query_out[rows, HEAD_SIZE * e : HEAD_SIZE * (e + 1)] = (
+                jnp.where(named[0] == e, turned[0], 0.0) + jnp.where(named[1] == e, turned[1], 0.0)
+            ).astype(BF)
+    grad_own_out[...] = sums[0]
+    grad_other_out[...] = sums[1].astype(BF)
+
+
+def in_vmem(kernel, outs, scratch, flops, *args):
+    spec = pl.BlockSpec(memory_space=pltpu.VMEM)
+    moved = sum(a.size * a.dtype.itemsize for a in args)
+    return pl.pallas_call(
+        kernel,
+        out_shape=outs,
+        in_specs=[spec] * len(args),
+        out_specs=[spec] * len(outs),
+        scratch_shapes=scratch,
+        compiler_params=pltpu.CompilerParams(vmem_limit_bytes=40 * 1024 * 1024),
+        cost_estimate=pl.CostEstimate(flops=flops, bytes_accessed=moved, transcendentals=1 << 20),
+    )(*args)
 
 
 def pick_of(routes):
@@ -218,47 +335,49 @@
     sequence = 8 * count
     plane = ("y", "tensor")
 
-    gate_up_w = lax.all_gather(gate_up_weight[0].reshape(512, 2816), "dp", axis=0, tiled=True)
-
     routers_own = jnp.concatenate([attn_router, mlp_router], axis=1)
     in_own = jnp.concatenate([query_matrix, key_value_weight], axis=1)
-    in_w, _ = gather_rows(
-        jnp.concatenate(
-            [heads_first(in_own), jnp.broadcast_to(widen(routers_own), (4, 64, HEAD_SIZE))], axis=2
-        ),
-        z,
-        core,
-    )
-    out_w, out_pieces = gather_rows(heads_first(output_matrix), z, core)
-    router_m = in_w[:, 1288:1296]
-
-    down_own, _ = lax.optimization_barrier((down_weight[0], out_pieces[2]))
-    down_pieces = ring_pieces(down_own, "dp")
-    down_w = lax.dynamic_slice_in_dim(
+    mine = exchange(
         jnp.concatenate(
             [
-                down_pieces[0],
-                down_pieces[1],
-                jnp.concatenate([down_pieces[2], down_pieces[3]], axis=0),
-                down_pieces[4],
-                down_pieces[0],
-                down_pieces[1],
-                jnp.concatenate([down_pieces[2], down_pieces[3]], axis=0),
+                heads_first(in_own),
+                jnp.broadcast_to(widen(routers_own), (4, 64, HEAD_SIZE)),
+                heads_first(output_matrix),
             ],
-            axis=1,
+            axis=2,
         ),
-        lax.rem(4 - z, 4) * 512,
-        MODEL_WIDTH,
+        "y",
+    ).reshape(256, 2432)
+    lines = ("dp", "core")
+    in_w = lax.all_gather(mine[:, :1408], lines, axis=0, tiled=True)
+    out_w = lax.all_gather(after(mine[:, 1408:], in_w), lines, axis=0, tiled=True)
+    gate_up_w = lax.all_gather(
+        after(gate_up_weight[0].reshape(512, 2816), out_w), "dp", axis=0, tiled=True
+    )
+    router_m = in_w[:, 1288:1296].reshape(4, 2, 4, 64, 8).transpose(0, 2, 1, 3, 4).reshape(-1, 8)
+
+    down_pieces = ring_pieces(down_weight[0], "dp")
+    down_w = jnp.concatenate(
+        [
+            down_pieces[0],
+            down_pieces[1],
+            jnp.concatenate([down_pieces[2], down_pieces[3]], axis=0),
+            down_pieces[4],
+        ],
         axis=1,
     )
 
-    sent = jnp.concatenate([tokens, widen(attn_routes.astype(BF))], axis=1)
-    arrived = gather_direct(sent, "y").reshape(4 * count, MODEL_WIDTH + HEAD_SIZE)
+    def turned(columns, blocks):
+        twice = jnp.concatenate([columns, columns], axis=1)
+        return lax.dynamic_slice_in_dim(twice, blocks * 512, MODEL_WIDTH, axis=1)
+
+    sent = jnp.concatenate([core_first(tokens), widen(attn_routes.astype(BF))], axis=1)
+    arrived = spread(after(sent, mine), "y", 4).reshape(4 * count, MODEL_WIDTH + HEAD_SIZE)
     values = arrived[:, :MODEL_WIDTH].astype(F32)
     routes = arrived[:, MODEL_WIDTH : MODEL_WIDTH + 2].astype(jnp.int32)
-    gain_a, gain_m = attn_gain.astype(F32), mlp_gain.astype(F32)
+    gain_a = core_first(attn_gain.astype(F32))[0]
+    gain_m = core_first(mlp_gain.astype(F32))[0]
     xn1 = (values * rms_scale(values) * gain_a).astype(BF)
-    pick_a = pick_of(routes)
 
     ranking = priority[0]
     pick_m = pick_of(mlp_routes)
@@ -288,60 +407,63 @@
         ROWS,
         preferred_element_type=F32,
     ).astype(BF)
-    grad_sent, _ = lax.optimization_barrier((grad_sent, out_pieces[0]))
-    grad_landed = to_experts(grad_sent)
+    grad_landed = to_experts(after(grad_sent, arrived))
 
     def places(half):
         blocks = 2 * jnp.arange(4, dtype=jnp.int32)[:, None] + half
         return (blocks * count + jnp.arange(count, dtype=jnp.int32)[None, :]).reshape(-1)
 
-    place = places(core)
-    key_place = jnp.concatenate([place, places(1 - core)])
-    of_sequence = lax.dynamic_slice_in_dim(segments, z * sequence, sequence)
-    own_segment = jnp.take(of_sequence, place)
-    key_segment = jnp.concatenate([own_segment, jnp.take(of_sequence, places(1 - core))])
-    allowed = (
-        (key_place[None, :] <= place[:, None])
-        & (place[:, None] - key_place[None, :] < WINDOW)
-        & (own_segment[:, None] == key_segment[None, :])
-    )
+    of_sequence = lax.dynamic_slice_in_dim(segments, z * sequence, sequence).reshape(4, 2, count)
+
+    def meta(half):
+        documents = lax.dynamic_index_in_dim(of_sequence, half, 1, keepdims=False).reshape(-1)
+        return jnp.stack([places(half), documents])
+
+    key_meta = jnp.stack([meta(core), meta(1 - core)])
+    row_meta = key_meta[0].T
     inverse = 10000.0 ** (-(jnp.arange(HEAD_SIZE // 2).astype(F32) * 2.0 / HEAD_SIZE))
-    angle = place.astype(F32)[:, None] * inverse[None, :]
-    cosine, sine = jnp.cos(angle), jnp.sin(angle)
-
+    angle = places(core).astype(F32)[:, None] * inverse[None, :]
+    cosine = jnp.tile(jnp.cos(angle), (1, 2))
+    sine = jnp.concatenate([-jnp.sin(angle), jnp.sin(angle)], axis=1)
+
+    def swapped(rows):
+        return jnp.concatenate([rows[:, 64:], rows[:, :64]], axis=1)
+
+    half = 4 * count
     projected = jnp.dot(xn1, in_w, preferred_element_type=F32)
-    gate_a = pair_gates(projected[:, 1280:1288], pick_a)
-    key_own = turn(projected[:, 1024:1152], cosine, sine).astype(BF)
-    value_own = projected[:, 1152:1280].astype(BF)
-    kv_own = jnp.concatenate([key_own, value_own], axis=1)
+    key_raw = projected[:, 1024:1152]
+    kv_own = jnp.concatenate(
+        [key_raw * cosine + swapped(key_raw) * sine, projected[:, 1152:1280]], axis=1
+    ).astype(BF)
     kv_other = lax.ppermute(kv_own, "core", SWAP)
-    keys = jnp.concatenate([key_own, kv_other[:, :HEAD_SIZE]], axis=0)
-    vals = jnp.concatenate([value_own, kv_other[:, HEAD_SIZE:]], axis=0)
-    q_all = projected[:, :1024].reshape(-1, EXPERTS, HEAD_SIZE)
-    q_pick = jnp.sum(pick_a[:, :, :, None] * q_all[:, None], axis=2)
-    query = turn(q_pick, cosine[:, None], sine[:, None]).astype(BF)
-    scale = HEAD_SIZE ** (-0.5)
-    score = jnp.where(
-        allowed[None], jnp.einsum("sjd,kd->jsk", query, keys, preferred_element_type=F32) * scale, -1e30
-    )
-    row_max = jnp.max(score, axis=-1, keepdims=True)
-    weights = jnp.exp(score - row_max)
-    totals = jnp.sum(weights, axis=-1, keepdims=True)
-    prob = weights / totals
-    attended = jnp.einsum("jsk,kd->sjd", prob.astype(BF), vals, preferred_element_type=F32)
-    mixed = jnp.sum(
-        (pick_a * gate_a[:, :, None])[:, :, :, None] * attended[:, :, None, :], axis=1
-    ).astype(BF).reshape(-1, EXPERTS * HEAD_SIZE)
+    shared = (routes, cosine, sine, row_meta, key_meta)
+    query, attended, totals, gate_a, mixed = in_vmem(
+        forward_kernel,
+        [
+            jax.ShapeDtypeStruct((4, 2 * count, HEAD_SIZE), BF),
+            jax.ShapeDtypeStruct((4, 2 * count, HEAD_SIZE), F32),
+            jax.ShapeDtypeStruct((4, 2 * count, 1), F32),
+            jax.ShapeDtypeStruct((half, 2), F32),
+            jax.ShapeDtypeStruct((half, EXPERTS * HEAD_SIZE), BF),
+        ],
+        [],
+        6 << 28,
+        projected,
+        kv_own,
+        kv_other,
+        *shared,
+    )
     branch_part = lax.dot_general(mixed, out_w, LAST, preferred_element_type=F32).astype(BF)
+    branch_part = after(branch_part, grad_landed)
     branch = exchange(branch_part.reshape(16, quarter, MODEL_WIDTH), plane).astype(F32).sum(axis=0)
 
     first = x * quarter
-    own_values = lax.dynamic_slice_in_dim(tokens, first, quarter).astype(F32)
+    own_values = core_first(lax.dynamic_slice_in_dim(tokens, first, quarter)).astype(F32)
     own_factor = rms_scale(own_values)
     hidden = own_values + branch
     factor_m = rms_scale(hidden)
     xn2_own = (hidden * factor_m * gain_m).astype(BF)
-    xn2 = spread(xn2_own, "tensor", 4).reshape(count, MODEL_WIDTH)
+    xn2 = spread(core_last(xn2_own), "tensor", 4).reshape(count, MODEL_WIDTH)
     gate_m = pair_gates(jnp.dot(xn2, router_m, preferred_element_type=F32), pick_m)
     weight_m = gate_m * kept.astype(F32)
 
@@ -360,7 +482,9 @@
     row_gate = valid * own_weight / (own_weight + jnp.exp(other_logit - top))
 
     width = down_weight.shape[1]
-    grad_act_raw = lax.dot_general(grad_received, down_w, LAST, preferred_element_type=F32)
+    grad_act_raw = lax.dot_general(
+        turned(grad_received, z), down_w, LAST, preferred_element_type=F32
+    )
     grad_expert = (row_gate * grad_received.astype(F32)).astype(BF)
     gate_up = jnp.dot(received, gate_up_w, preferred_element_type=F32)
     gate_part, up_part = gate_up[:, :width], gate_up[:, width:]
@@ -382,12 +506,11 @@
         received, grad_gate_up, ROWS, preferred_element_type=F32
     ).astype(BF)
     grad_down_w = lax.dot_general(activated, grad_expert, ROWS, preferred_element_type=F32).astype(BF)
-    gate_up_grad = (
-        lax.psum_scatter(grad_gate_up_w, "dp", scatter_dimension=0, tiled=True)
-        .reshape(1, 512, 2, width)
-        .astype(F32)
-    )
-    down_grad = ring_sum(grad_down_w.reshape(width, 4, 512).transpose(1, 0, 2), "dp")[None]
+    gate_up_sum = lax.psum_scatter(grad_gate_up_w, "dp", scatter_dimension=0, tiled=True)
+    gate_up_grad = gate_up_sum.reshape(1, 512, 2, width).astype(F32)
+    down_grad = lax.psum_scatter(
+        after(grad_down_w, gate_up_sum), "dp", scatter_dimension=1, tiled=True
+    ).astype(F32)[None]
 
     grad_xn2_part = jnp.dot(
         any_row, grad_returned[:, :MODEL_WIDTH], preferred_element_type=F32
@@ -413,77 +536,75 @@
     grad_xn2 = landed[:, :MODEL_WIDTH] + lax.dot_general(
         grad_logit_m, router_m.astype(F32), LAST, preferred_element_type=F32
     )
-    grad_norm, gain_m_part = norm_back(grad_xn2, hidden, factor_m, gain_m)
-    grad_hidden = quarter_of(cotangent).astype(F32) + grad_norm
+    grad_norm, gain_m_part = norm_back(core_first(grad_xn2), hidden, factor_m, gain_m)
+    grad_hidden = core_first(quarter_of(cotangent)).astype(F32) + grad_norm
     grad_branch = spread(grad_hidden.astype(BF), plane, 16).reshape(4 * count, MODEL_WIDTH)
 
-    expert_part = jnp.dot(activated, down_w, preferred_element_type=F32).astype(BF)
-    expert_part, _ = lax.optimization_barrier((expert_part, grad_branch))
-    returned = to_experts(expert_part)
+    expert_part = turned(
+        jnp.dot(activated, down_w, preferred_element_type=F32).astype(BF), lax.rem(4 - z, 4)
+    )
+    returned = to_experts(after(expert_part, grad_branch))
     fetched = jnp.einsum("jtr,rd->jtd", to_row, returned, preferred_element_type=F32)
     moe_part = jnp.sum(weight_m.T[:, :, None] * fetched, axis=0).astype(BF)
     moe = sum_direct(moe_part.reshape(4, quarter, MODEL_WIDTH), "tensor")
-    output = gather_direct((hidden + moe).astype(BF), "tensor").reshape(count, MODEL_WIDTH)
-
-    grad_mixed = jnp.dot(grad_branch, out_w, preferred_element_type=F32).reshape(
-        -1, EXPERTS, HEAD_SIZE
-    )
-    grad_pick = jnp.sum(pick_a[:, :, :, None] * grad_mixed[:, None], axis=2)
-    grad_gate_part = jnp.sum(grad_pick * attended, axis=-1)
-    grad_attended = (gate_a[:, :, None] * grad_pick).astype(BF)
-    grad_prob = jnp.einsum("sjd,kd->jsk", grad_attended, vals, preferred_element_type=F32)
-    row_delta = jnp.sum(prob * grad_prob, axis=-1, keepdims=True)
-    grad_score = (prob * (grad_prob - row_delta)).astype(BF)
-    grad_query = jnp.einsum("jsk,kd->sjd", grad_score, keys, preferred_element_type=F32) * scale
-    grad_keys = jnp.einsum("jsk,sjd->kd", grad_score, query, preferred_element_type=F32) * scale
-    grad_vals = jnp.einsum("jsk,sjd->kd", prob.astype(BF), grad_attended, preferred_element_type=F32)
-    half = 4 * count
-    grad_kv_raw = jnp.concatenate([grad_keys, grad_vals], axis=1)
-    from_other = lax.ppermute(grad_kv_raw[half:].astype(BF), "core", SWAP).astype(F32)
-    own_grad_kv = grad_kv_raw[:half] + from_other
+    output_own = (core_last(hidden) + moe).astype(BF)
+
+    grad_mixed = jnp.dot(grad_branch, out_w, preferred_element_type=F32)
+    grad_q_all, grad_logit_a, grad_kv_own, grad_kv_give = in_vmem(
+        backward_kernel,
+        [
+            jax.ShapeDtypeStruct((half, EXPERTS * HEAD_SIZE), BF),
+            jax.ShapeDtypeStruct((half, HEAD_SIZE), BF),
+            jax.ShapeDtypeStruct((half, 2 * HEAD_SIZE), F32),
+            jax.ShapeDtypeStruct((half, 2 * HEAD_SIZE), BF),
+        ],
+        [pltpu.VMEM((2, half, 2 * HEAD_SIZE), F32)],
+        12 << 28,
+        grad_mixed,
+        query,
+        kv_own,
+        kv_other,
+        attended,
+        totals,
+        gate_a,
+        *shared,
+    )
+    own_grad_kv = grad_kv_own + lax.ppermute(grad_kv_give, "core", SWAP).astype(F32)
+    grad_key = own_grad_kv[:, :HEAD_SIZE]
     grad_kv = jnp.concatenate(
-        [turn(own_grad_kv[:, :HEAD_SIZE], cosine, -sine), own_grad_kv[:, HEAD_SIZE:]], axis=1
+        [grad_key * cosine - swapped(grad_key) * sine, own_grad_kv[:, HEAD_SIZE:]], axis=1
     ).astype(BF)
-    grad_q_pick = turn(grad_query, cosine[:, None], -sine[:, None])
-    grad_q_all = (
-        jnp.sum(pick_a[:, :, :, None] * grad_q_pick[:, :, None, :], axis=1)
-        .astype(BF)
-        .reshape(-1, EXPERTS * HEAD_SIZE)
-    )
+    grad_in = jnp.concatenate([grad_q_all, grad_kv, grad_logit_a], axis=1)
     out_grad = heads_last(
         scatter_rows(
             lax.dot_general(grad_branch, mixed, ROWS, preferred_element_type=F32).astype(BF), core
         )
     )
-    grad_logit_a = gate_back(gate_a, grad_gate_part, pick_a)
-    grad_in = jnp.concatenate([grad_q_all, grad_kv, widen(grad_logit_a.astype(BF))], axis=1)
     grad_xn1_part = lax.dot_general(grad_in, in_w, LAST, preferred_element_type=F32).astype(BF)
     landed_a = (
         exchange(grad_xn1_part.reshape(16, quarter, MODEL_WIDTH), plane).astype(F32).sum(axis=0)
     )
     grad_x_norm, _ = norm_back(landed_a, own_values, own_factor, gain_a)
-    input_grad = gather_direct((grad_hidden + grad_x_norm).astype(BF), "tensor").reshape(
-        count, MODEL_WIDTH
-    )
-
-    small = jnp.concatenate(
-        [
-            jnp.zeros((MODEL_WIDTH, 1288), BF),
-            lax.dot_general(
-                xn2_own, grad_logit_m.astype(BF), ROWS, preferred_element_type=F32
-            ).astype(BF),
-            gain_m_part[:, None].astype(BF),
-            jnp.zeros((MODEL_WIDTH, 111), BF),
-        ],
-        axis=1,
-    )
+    ends = jnp.concatenate(
+        [output_own, core_last((grad_hidden + grad_x_norm).astype(BF))], axis=1
+    )
+    both_ends = spread(ends, "tensor", 4).reshape(count, 2 * MODEL_WIDTH)
+    output, input_grad = both_ends[:, :MODEL_WIDTH], both_ends[:, MODEL_WIDTH:]
+
+    gain_row = jnp.pad(gain_m_part[None].astype(BF), ((0, 7), (0, 0)))
+    tall = jnp.concatenate([xn1, xn2_own, gain_row], axis=0)
+    router_cols = jnp.pad(grad_logit_m.astype(BF), ((0, 0), (1288, 112)))
+    gain_cols = (
+        (jnp.arange(8)[:, None] == 0) & (jnp.arange(1408)[None, :] == 1296)
+    ).astype(BF)
+    grad_tall = jnp.concatenate([grad_in, router_cols, gain_cols], axis=0)
     in_parts = scatter_rows(
-        lax.dot_general(xn1, grad_in, ROWS, preferred_element_type=F32).astype(BF) + small, core
+        lax.dot_general(tall, grad_tall, ROWS, preferred_element_type=F32).astype(BF), core
     )
     in_grad = heads_last(in_parts[:, :, :1280])
     query_grad, kv_grad = in_grad[:, :8], in_grad[:, 8:]
     small_part = jnp.sum(in_parts[:, :, 1280:].astype(F32), axis=0)
-    gain_rows = lax.dynamic_slice_in_dim(gain_a, z * 512 + y * 128 + core * 64, 64)
+    gain_rows = lax.dynamic_slice_in_dim(attn_gain.astype(F32), z * 512 + y * 128 + core * 64, 64)
     gain_a_part = (
         jnp.sum(in_grad * in_own.astype(F32), axis=(1, 2))
         + jnp.sum(small_part[:, :8] * attn_router.astype(F32), axis=1)

time: 759 us -> 727 us (0.958)
  waiting for transfers between devices: 241 us -> 306 us
  local copies, waits for them, and re-layouts: 152 us -> 91.8 us
  matrix products: 137 us -> 108 us
  starting transfers between devices: 123 us -> 101 us
  blocking collectives: 0 us -> 21.5 us
  other arithmetic: 73.1 us -> 59.4 us
  Pallas kernels: 5.25 us -> 15.3 us
    all_gather x1 -> x3, waiting for transfers between devices: 0.02 us -> 74.1 us  [the longest x1 42.5 us: body(): in_w = lax.all_gather(mine[:, :1408], lines, axis=0, tiled=True)]
    ppermute x3 -> x1, waiting for transfers between devices: 47.5 us -> 1.1 us  [ring_pieces(): far_low = lax.ppermute(before[:half], axis, UP)]
    all_to_all x11, waiting for transfers between devices: 83.9 us -> 126 us  [exchange(): return lax.all_to_all(blocks, axis, split_axis=0, concat_axis=0, tiled=True)]
    ppermute x3 -> x1, waiting for transfers between devices: 2.22 us -> 31.7 us  [ring_pieces(): after = lax.ppermute(block, axis, DOWN)]
    all_to_all x0 -> x1, blocking collectives: none -> 21.5 us  [exchange(): return lax.all_to_all(blocks, axis, split_axis=0, concat_axis=0, tiled=True)]
    ppermute x21 -> x12, waiting for transfers between devices: 48.1 us -> 27 us  [from_ahead(): return lax.ppermute(block, axis, [(i, (i - steps) % 4) for i in range(4)])]
    unnamed x199 -> x145, local copies, waits for them, and re-layouts: 38.9 us -> 19.3 us
    another operation x1 -> x4, local copies, waits for them, and re-layouts: 18.4 us -> 0.37 us  [the longest x2 0.19 us: body(): cosine = jnp.tile(jnp.cos(angle), (1, 2))]
  transfers between devices with their start and end apart: 72 -> 44, of which waited for: 28 -> 21; matrix products, arithmetic and copies ran while one was open for 42% -> 31% of each run, Pallas kernels for 1% -> 2%
where the time goes in v2:
time: 727 us; the launch traced here: 718 us
  waiting for transfers between devices  306 us (42%)
  matrix products  108 us (15%)
  starting transfers between devices  101 us (14%)
  local copies, waits for them, and re-layouts  91.8 us (13%)
  other arithmetic  59.4 us (8%)
  blocking collectives  21.5 us (3%)
  between operations  15.4 us (2%)
  Pallas kernels  15.3 us (2%)
    all_to_all x11, waiting for transfers between devices, exchange(): return lax.all_to_all(blocks, axis, split_axis=0, concat_axis=0, tiled=True)  126 us
    all_to_all x11, starting transfers between devices, exchange(): return lax.all_to_all(blocks, axis, split_axis=0, concat_axis=0, tiled=True)  57.5 us
    all_gather x1, waiting for transfers between devices, body(): in_w = lax.all_gather(mine[:, :1408], lines, axis=0, tiled=True)  42.5 us
    ppermute x1, waiting for transfers between devices, ring_pieces(): after = lax.ppermute(block, axis, DOWN)  31.7 us
    all_gather x1, waiting for transfers between devices, body(): lax.all_gather(after(mine[:, 1408:], in_w), lines, axis=0, tiled=True)  31.6 us
    ppermute x12, waiting for transfers between devices, from_ahead(): return lax.ppermute(block, axis, [(i, (i - steps) % 4) for i in range(4)])  27 us
    ppermute x12, starting transfers between devices, from_ahead(): return lax.ppermute(block, axis, [(i, (i - steps) % 4) for i in range(4)])  24.4 us
    all_to_all x1, blocking collectives, exchange(): return lax.all_to_all(blocks, axis, split_axis=0, concat_axis=0, tiled=True)  21.5 us
  transfers between devices with their start and end apart: 44, of which 21 were waited for; matrix products, arithmetic and copies ran while one was open for 31% of the time, Pallas kernels for 2%

profile of v2, /device:TPU:0, one launch (start us, length us, event | category | flops | bytes accessed | tf_op | source)
XLA Modules:
  0.0 718.2 jit_solution(6750790133528745678)
XLA Ops:
  11.7 21.5 %all_to_all.60 = bf16[4,64,2432]{2,1,0:T(8,128)(2,1)S(1)} all-to-all(bf16[4,64,2432]{2,1,0:T(8,128)(2,1)S(1)} %pad_maximum_fusion.4), channel_id=1, replica_groups=mesh['dp'=4,'y'=4,'core'=2,'tensor'=4] {'y'}, dimensions={0} | all-to-all | bytes 2490368 | tf_op jit(solution)/shard_map/all_to_all | solution.py:24
  35.4 42.5 %all-gather.4.cloned.1.call-done = bf16[2048,1408]{0,1:T(8,128)(2,1)} async-done(((bf16[256,1408]{0,1:T(8,128)(2,1)}), bf16[2048,1408]{0,1:T(8,128)(2,1)}) %all-gather.4.cloned.1.call-update) | async-done | bytes 5767184 | tf_op jit(solution)/shard_map/all_gather | solution.py:352
  78.0 3.8 copy.502
  81.8 31.6 %all-gather.6.cloned.1.call-done = bf16[2048,1024]{1,0:T(8,128)(2,1)} async-done(((bf16[256,1024]{1,0:T(8,128)(2,1)}), bf16[2048,1024]{1,0:T(8,128)(2,1)}) %all-gather.6.cloned.1.call-update) | async-done | bytes 4194320 | tf_op jit(solution)/shard_map/all_gather | solution.py:353
  120.6 4.7 all-to-all-start.1
  130.5 29.3 %all-to-all-done.1 = bf16[4,160,2176]{2,1,0:T(8,128)(2,1)} async-done(((bf16[4,160,2176]{2,1,0:T(8,128)(2,1)}), bf16[4,160,2176]{2,1,0:T(8,128)(2,1)}, u32[]{:S(2)}, u32[]{:S(2)}) %all-to-all-start.1) | async-done | bytes 2785312 | tf_op jit(solution)/shard_map/all_to_all | solution.py:24
  159.8 4.8 all-to-all-start.2
  169.6 4.3 fusion.127.proj
  176.6 6.9 shard_map.230
  187.1 4.2 convolution_convert_fusion.6
  191.3 7.4 %all-to-all-start.3 = ((bf16[16,40,2048]{2,1,0:T(8,128)(2,1)}), bf16[16,40,2048]{2,1,0:T(8,128)(2,1)}, u32[]{:S(2)}, u32[]{:S(2)}) async-start(bf16[16,40,2048]{2,1,0:T(8,128)(2,1)} %bitcast.286), calls=%async_computation.3 | async-start | bytes 5242880 | tf_op jit(solution)/shard_map/all_to_all | solution.py:24
  200.9 38.4 %all-to-all-done.3 = bf16[16,40,2048]{2,1,0:T(8,128)(2,1)} async-done(((bf16[16,40,2048]{2,1,0:T(8,128)(2,1)}), bf16[16,40,2048]{2,1,0:T(8,128)(2,1)}, u32[]{:S(2)}, u32[]{:S(2)}) %all-to-all-start.3) | async-done | bytes 2621472 | tf_op jit(solution)/shard_map/all_to_all | solution.py:24
  249.0 4.2 all-to-all-start.4
  254.1 9.6 %all-to-all-done.4 = bf16[4,40,2048]{2,1,0:T(8,128)(2,1)} async-done(((bf16[4,40,2048]{2,1,0:T(8,128)(2,1)}), bf16[4,40,2048]{2,1,0:T(8,128)(2,1)}, u32[]{:S(2)}, u32[]{:S(2)}) %all-to-all-start.4) | async-done | bytes 655392 | tf_op jit(solution)/shard_map/all_to_all | solution.py:24
  266.8 4.5 all-to-all-start.5
  274.0 31.7 %collective-permute-done.1 = bf16[1408,512]{1,0:T(8,128)(2,1)} collective-permute-done((bf16[1408,512]{1,0:T(8,128)(2,1)}, bf16[1408,512]{1,0:T(8,128)(2,1)}, u32[]{:S(2)}, u32[]{:S(2)}) %collective-permute-start.1) | collective-permute-done | bytes 1441824 | tf_op jit(solution)/shard_map/ppermute | solution.py:63
  320.1 9.4 %fusion.129 = f32[448,2816]{1,0:T(8,128)S(1)} fusion(bf16[448,2048]{1,0:T(8,128)(2,1)} %bitcast.31, bf16[2048,2816]{1,0:T(8,128)(2,1)} %all-gather.8.cloned.1.call-done), kind=kOutput, calls=%fused_computation.307 | convolution fusion | flops 5167382528 | bytes 18415616 | tf_op jit(solution)/shard_map/dot_general | solution.py:489
  330.6 10.7 %multiply_convert_fusion.2 = (bf16[448,1408]{1,0:T(8,128)(2,1)}, bf16[448,1408]{1,0:T(8,128)(2,1)}, f32[448]{0:T(512)S(1)}, bf16[448,1408]{1,0:T(8,128)(2,1)}) fusion(f32[448,2816]{1,0:T(8,128)S(1)} %fusion.129, f32[448]{0:T(512)S(1)} %bitcast.304, bf16[1408,512]{1,0:T(8,128)(2,1)} %collective-permute-done.2, bf16[704,512]{1,0:T(8,128)(2,1)} %collective-permute-done.4, ...), kind=kOutput, calls=%fused_computation.46 | convolution fusion | flops 2628181504 | bytes 16436740 | tf_op jit(solution)/shard_map/dot_general | solution.py:485
  341.3 10.9 %convolution_convert_fusion = bf16[2048,2816]{1,0:T(8,128)(2,1)} fusion(bf16[448,2048]{1,0:T(8,128)(2,1)} %bitcast.31, bf16[448,1408]{1,0:T(8,128)(2,1)} %get-tuple-element.163, bf16[448,1408]{1,0:T(8,128)(2,1)} %get-tuple-element.162), kind=kOutput, calls=%fused_computation | convolution fusion | flops 5178195968 | bytes 15892480 | tf_op jit(solution)/shard_map/dot_general | solution.py:505
  352.5 9.0 %convolution_convert_fusion.8 = bf16[448,2048]{1,0:T(8,128)(2,1)S(1)} fusion(bf16[2048,2816]{1,0:T(8,128)(2,1)} %all-gather.8.cloned.1.call-done, bf16[448,1408]{1,0:T(8,128)(2,1)} %get-tuple-element.163, bf16[448,1408]{1,0:T(8,128)(2,1)} %get-tuple-element.162), kind=kOutput, calls=%fused_computation.33 | convolution fusion | flops 5173346304 | bytes 15892480 | tf_op jit(solution)/shard_map/dot_general | solution.py:503
  362.9 4.7 all-to-all-start.6
  381.0 12.2 %all-to-all-done.6 = bf16[8,56,2176]{2,1,0:T(8,128)(2,1)} async-done(((bf16[8,56,2176]{2,1,0:T(8,128)(2,1)}), bf16[8,56,2176]{2,1,0:T(8,128)(2,1)}, u32[]{:S(2)}, u32[]{:S(2)}) %all-to-all-start.6) | async-done | bytes 1949728 | tf_op jit(solution)/shard_map/all_to_all | solution.py:24
  397.8 4.2 all-to-all-start.7
  404.2 9.2 %all-to-all-done.7 = bf16[4,40,2176]{2,1,0:T(8,128)(2,1)} async-done(((bf16[4,40,2176]{2,1,0:T(8,128)(2,1)}), bf16[4,40,2176]{2,1,0:T(8,128)(2,1)}, u32[]{:S(2)}, u32[]{:S(2)}) %all-to-all-start.7) | async-done | bytes 696352 | tf_op jit(solution)/shard_map/all_to_all | solution.py:24
  430.8 5.0 all-to-all-start.8
  439.7 7.3 %convolution_convert_fusion.9 = bf16[448,2048]{1,0:T(8,128)(2,1)S(1)} fusion(bf16[448,1408]{1,0:T(8,128)(2,1)} %get-tuple-element.165, bf16[1408,512]{1,0:T(8,128)(2,1)} %collective-permute-done.2, bf16[704,512]{1,0:T(8,128)(2,1)} %collective-permute-done.4, bf16[704,512]{1,0:T(8,128)(2,1)} %collective-permute-done.3, ...), kind=kOutput, calls=%fused_computation.34 | convolution fusion | flops 2613444608 | bytes 8863744 | tf_op jit(solution)/shard_map/dot_general | solution.py:544
  449.3 7.3 %convolution_convert_fusion.1 = bf16[1408,2048]{1,0:T(8,128)(2,1)} fusion(bf16[448,1408]{1,0:T(8,128)(2,1)S(1)} %copy-done.59, f32[448]{0:T(512)S(1)} %bitcast.305, bf16[448,2176]{1,0:T(8,128)(2,1)} %bitcast.20), kind=kOutput, calls=%fused_computation.1 | convolution fusion | flops 2589327360 | bytes 8865536 | tf_op jit(solution)/shard_map/dot_general | solution.py:508
  456.6 16.6 %all-to-all-done.8 = bf16[16,40,2048]{2,1,0:T(8,128)(2,1)} async-done(((bf16[16,40,2048]{2,1,0:T(8,128)(2,1)}), bf16[16,40,2048]{2,1,0:T(8,128)(2,1)}, u32[]{:S(2)}, u32[]{:S(2)}) %all-to-all-start.8) | async-done | bytes 2621472 | tf_op jit(solution)/shard_map/all_to_all | solution.py:24
  473.2 5.7 fusion.130.grad_mixed
  479.0 8.4 %shard_map.231 = (bf16[640,1024]{1,0:T(8,128)(2,1)S(1)}, bf16[640,128]{1,0:T(8,128)(2,1)S(1)}, f32[640,256]{1,0:T(8,128)S(1)}, bf16[640,256]{1,0:T(8,128)(2,1)S(1)}) custom-call(f32[640,1024]{1,0:T(8,128)S(1)} %fusion.130.grad_mixed, bf16[4,320,128]{2,1,0:T(8,128)(2,1)S(1)} %get-tuple-element.34.query_in, bf16[640,256]{1,0:T(8,128)(2,1)S(1)} %pad_maximum_fusion.11.own, ...), custom_call_target="tpu_custom_call" | custom-call | flops 3221225472 | bytes 4945920 | tf_op jit(solution)/shard_map/pallas_call | solution.py:267
  487.6 7.2 convolution_convert_fusion.4
  494.7 4.3 all-to-all-start.9
  503.9 8.3 %convolution_convert_fusion.5 = bf16[640,2048]{1,0:T(8,128)(2,1)} fusion(bf16[2048,1408]{0,1:T(8,128)(2,1)} %all-gather.4.cloned.1.call-done, bf16[640,128]{1,0:T(8,128)(2,1)S(1)} %get-tuple-element.41, bf16[640,128]{1,0:T(8,128)(2,1)S(1)} %slice.344, bf16[640,128]{1,0:T(8,128)(2,1)S(1)} %fusion.70, bf16[640,1024]{1,0:T(8,128)(2,1)S(1)} %copy-done.11), kind=kOutput, calls=%fused_computation.30 | convolution fusion | flops 3699507200 | bytes 10190848 | tf_op jit(solution)/shard_map/dot_general | solution.py:583
  512.3 11.2 %all-to-all-done.9 = bf16[8,56,2048]{2,1,0:T(8,128)(2,1)} async-done(((bf16[8,56,2048]{2,1,0:T(8,128)(2,1)}), bf16[8,56,2048]{2,1,0:T(8,128)(2,1)}, u32[]{:S(2)}, u32[]{:S(2)}) %all-to-all-start.9) | async-done | bytes 1835040 | tf_op jit(solution)/shard_map/all_to_all | solution.py:24
  523.5 4.6 all-to-all-start.10
  528.1 6.9 convolution_convert_fusion.2
  550.6 15.9 %collective-permute-done.7 = bf16[40,2048]{1,0:T(8,128)(2,1)S(1)} collective-permute-done((bf16[40,2048]{1,0:T(8,128)(2,1)S(1)}, bf16[40,2048]{1,0:T(8,128)(2,1)S(1)}, u32[]{:S(2)}, u32[]{:S(2)}) %collective-permute-start.7) | collective-permute-done | bytes 163872 | tf_op jit(solution)/shard_map/ppermute | solution.py:32
  568.9 4.7 collective-permute-done.6
  580.0 3.5 convert_reduce_fusion
  591.2 9.2 %all-to-all-start.11 = ((bf16[4,40,4096]{2,1,0:T(8,128)(2,1)}), bf16[4,40,4096]{2,1,0:T(8,128)(2,1)}, u32[]{:S(2)}, u32[]{:S(2)}) async-start(bf16[4,40,4096]{2,1,0:T(8,128)(2,1)} %broadcast_in_dim.27), calls=%async_computation.11 | async-start | bytes 2621440 | tf_op jit(solution)/shard_map/all_to_all | solution.py:24
  600.3 4.6 collective-permute-done.22
  617.8 14.7 %collective-permute-done.10 = bf16[128,1408]{1,0:T(8,128)(2,1)S(1)} collective-permute-done((bf16[128,1408]{1,0:T(8,128)(2,1)S(1)}, bf16[128,1408]{1,0:T(8,128)(2,1)S(1)}, u32[]{:S(2)}, u32[]{:S(2)}) %collective-permute-start.10) | collective-permute-done | bytes 360480 | tf_op jit(solution)/shard_map/ppermute | solution.py:73
  633.3 3.8 collective-permute-start.13
  637.6 20.6 %collective-permute-done.13 = bf16[256,1408]{1,0:T(8,128)(2,1)S(1)} collective-permute-done((bf16[256,1408]{1,0:T(8,128)(2,1)S(1)}, bf16[256,1408]{1,0:T(8,128)(2,1)S(1)}, u32[]{:S(2)}, u32[]{:S(2)}) %collective-permute-start.13) | collective-permute-done | bytes 720928 | tf_op jit(solution)/shard_map/ppermute | solution.py:81
  658.2 4.6 collective-permute-done.11
  668.8 4.6 collective-permute-done.15
  684.6 3.8 collective-permute-start.18
  700.9 7.2 %reshape.610 = f32[1,512,2,1408]{3,2,1,0:T(2,128)} reshape(bf16[512,2816]{1,0:T(8,128)(2,1)} %reduce-scatter.3.cloned.1.call-done) | data formatting | bytes 8650752 | tf_op jit(solution)/shard_map/convert_element_type | solution.py:510
  (397 shorter events, 193.3 us)
Async XLA Ops:
  7.2 70.7 %all-gather.4.cloned.1.call-start = ((), (), s32[]{:S(2)}) async-start(), calls=%async_computation.14 | async-start | bytes 6488064 | tf_op jit(solution)/shard_map/all_gather | solution.py:352
  34.5 78.9 %all-gather.6.cloned.1.call-start = ((), (), s32[]{:S(2)}) async-start(), calls=%async_computation.15 | async-start | bytes 4718592 | tf_op jit(solution)/shard_map/all_gather | solution.py:353
  78.0 242.1 %all-gather.8.cloned.1.call-start = ((), (), s32[]{:S(2)}) async-start(), calls=%async_computation.16 | async-start | bytes 14417920 | tf_op jit(solution)/shard_map/all_gather | solution.py:354
  81.8 31.8 %copy-start.54 = (s32[160,2]{0,1:T(2,128)S(1)}, s32[160,2]{0,1:T(2,128)}, u32[]{:S(2)}) copy-start(s32[160,2]{0,1:T(2,128)} %param.26) | copy-start | bytes 3844
  81.8 31.8 %copy-start.29 = (bf16[160,2048]{1,0:T(8,128)(2,1)S(1)}, bf16[160,2048]{1,0:T(8,128)(2,1)}, u32[]{:S(2)}) copy-start(bf16[160,2048]{1,0:T(8,128)(2,1)} %param.15) | copy-start | bytes 1966084
  120.6 39.2 %all-to-all-start.1 = ((bf16[4,160,2176]{2,1,0:T(8,128)(2,1)}), bf16[4,160,2176]{2,1,0:T(8,128)(2,1)}, u32[]{:S(2)}, u32[]{:S(2)}) async-start(bf16[4,160,2176]{2,1,0:T(8,128)(2,1)} %broadcast_in_dim.23), calls=%async_computation.1 | async-start | bytes 5570560 | tf_op jit(solution)/shard_map/all_to_all | solution.py:24
  126.9 126.3 %copy-start.41 = (s32[2,160]{1,0:T(2,128)}, s32[2,160]{1,0:T(2,128)S(1)}, u32[]{:S(2)}) copy-start(s32[2,160]{1,0:T(2,128)S(1)} %select_bitcast_fusion.1) | copy-start | bytes 3844
  159.8 31.5 %all-to-all-start.2 = ((bf16[8,56,2176]{2,1,0:T(8,128)(2,1)}), bf16[8,56,2176]{2,1,0:T(8,128)(2,1)}, u32[]{:S(2)}, u32[]{:S(2)}) async-start(bf16[8,56,2176]{2,1,0:T(8,128)(2,1)} %bitcast.19), calls=%async_computation.2 | async-start | bytes 3899392 | tf_op jit(solution)/shard_map/all_to_all | solution.py:24
  174.4 2.3 collective-permute-start
  191.3 48.1 %all-to-all-start.3 = ((bf16[16,40,2048]{2,1,0:T(8,128)(2,1)}), bf16[16,40,2048]{2,1,0:T(8,128)(2,1)}, u32[]{:S(2)}, u32[]{:S(2)}) async-start(bf16[16,40,2048]{2,1,0:T(8,128)(2,1)} %bitcast.286), calls=%async_computation.3 | async-start | bytes 5242880 | tf_op jit(solution)/shard_map/all_to_all | solution.py:24
  200.1 167.5 %copy-start.12 = (f32[40,4,4,2,64]{4,3,2,1,0:T(2,128)}, f32[40,4,4,2,64]{4,3,2,1,0:T(2,128)S(1)}, u32[]{:S(2)}) copy-start(f32[40,4,4,2,64]{4,3,2,1,0:T(2,128)S(1)} %reshape.613) | copy-start | bytes 983044
  249.0 14.6 %all-to-all-start.4 = ((bf16[4,40,2048]{2,1,0:T(8,128)(2,1)}), bf16[4,40,2048]{2,1,0:T(8,128)(2,1)}, u32[]{:S(2)}, u32[]{:S(2)}) async-start(bf16[4,40,2048]{2,1,0:T(8,128)(2,1)} %broadcast_in_dim.25), calls=%async_computation.4 | async-start | bytes 1310720 | tf_op jit(solution)/shard_map/all_to_all | solution.py:24
  266.8 51.1 %all-to-all-start.5 = ((bf16[8,56,2048]{2,1,0:T(8,128)(2,1)}), bf16[8,56,2048]{2,1,0:T(8,128)(2,1)}, u32[]{:S(2)}, u32[]{:S(2)}) async-start(bf16[8,56,2048]{2,1,0:T(8,128)(2,1)} %bitcast.268), calls=%async_computation.5 | async-start | bytes 3670016 | tf_op jit(solution)/shard_map/all_to_all | solution.py:24
  271.3 302.4 %reduce-scatter.3.cloned.1.call-start = ((), (), s32[]{:S(2)}) async-start(), calls=%async_computation.17 | async-start | bytes 14417920 | tf_op jit(solution)/shard_map/reduce_scatter | solution.py:509
  271.4 34.3 %collective-permute-start.1 = (bf16[1408,512]{1,0:T(8,128)(2,1)}, bf16[1408,512]{1,0:T(8,128)(2,1)}, u32[]{:S(2)}, u32[]{:S(2)}) collective-permute-start(bf16[1408,512]{1,0:T(8,128)(2,1)} %bitcast.308), channel_id=1, source_target_pairs={{0,96},{32,0},{64,32},{96,64},{1,97},{33,1},{65,33},{97,65},{2,98}... | collective-permute-start | bytes 4325384 | tf_op jit(solution)/shard_map/ppermute | solution.py:63
  272.2 37.5 %collective-permute-start.2 = (bf16[1408,512]{1,0:T(8,128)(2,1)}, bf16[1408,512]{1,0:T(8,128)(2,1)}, u32[]{:S(2)}, u32[]{:S(2)}) collective-permute-start(bf16[1408,512]{1,0:T(8,128)(2,1)} %bitcast.309), channel_id=1, source_target_pairs={{0,32},{32,64},{64,96},{96,0},{1,33},{33,65},{65,97},{97,1},{2,34}... | collective-permute-start | bytes 4325384 | tf_op jit(solution)/shard_map/ppermute | solution.py:62
  307.7 21.8 %collective-permute-start.4 = (bf16[704,512]{1,0:T(8,128)(2,1)}, bf16[704,512]{1,0:T(8,128)(2,1)}, u32[]{:S(2)}, u32[]{:S(2)}) collective-permute-start(bf16[704,512]{1,0:T(8,128)(2,1)} %slice.273), channel_id=1, source_target_pairs={{0,96},{32,0},{64,32},{96,64},{1,97},{33,1},{65,33},{97,65},{2,98}... | collective-permute-start | bytes 2162696 | tf_op jit(solution)/shard_map/ppermute | solution.py:65
  311.7 18.9 %collective-permute-start.3 = (bf16[704,512]{1,0:T(8,128)(2,1)}, bf16[704,512]{1,0:T(8,128)(2,1)}, u32[]{:S(2)}, u32[]{:S(2)}) collective-permute-start(bf16[704,512]{1,0:T(8,128)(2,1)} %slice.272), channel_id=1, source_target_pairs={{0,32},{32,64},{64,96},{96,0},{1,33},{33,65},{65,97},{97,1},{2,34}... | collective-permute-start | bytes 2162696 | tf_op jit(solution)/shard_map/ppermute | solution.py:64
  362.9 30.3 %all-to-all-start.6 = ((bf16[8,56,2176]{2,1,0:T(8,128)(2,1)}), bf16[8,56,2176]{2,1,0:T(8,128)(2,1)}, u32[]{:S(2)}, u32[]{:S(2)}) async-start(bf16[8,56,2176]{2,1,0:T(8,128)(2,1)} %bitcast.266), calls=%async_computation.6 | async-start | bytes 3899392 | tf_op jit(solution)/shard_map/all_to_all | solution.py:24
  397.8 15.6 %all-to-all-start.7 = ((bf16[4,40,2176]{2,1,0:T(8,128)(2,1)}), bf16[4,40,2176]{2,1,0:T(8,128)(2,1)}, u32[]{:S(2)}, u32[]{:S(2)}) async-start(bf16[4,40,2176]{2,1,0:T(8,128)(2,1)} %bitcast.282), calls=%async_computation.7 | async-start | bytes 1392640 | tf_op jit(solution)/shard_map/all_to_all | solution.py:24
  430.8 42.4 %all-to-all-start.8 = ((bf16[16,40,2048]{2,1,0:T(8,128)(2,1)}), bf16[16,40,2048]{2,1,0:T(8,128)(2,1)}, u32[]{:S(2)}, u32[]{:S(2)}) async-start(bf16[16,40,2048]{2,1,0:T(8,128)(2,1)} %broadcast_in_dim.26), calls=%async_computation.8 | async-start | bytes 5242880 | tf_op jit(solution)/shard_map/all_to_all | solution.py:24
  487.4 15.1 %collective-permute-start.8 = (bf16[640,256]{1,0:T(8,128)(2,1)S(1)}, bf16[640,256]{1,0:T(8,128)(2,1)S(1)}, u32[]{:S(2)}, u32[]{:S(2)}) collective-permute-start(bf16[640,256]{1,0:T(8,128)(2,1)S(1)} %get-tuple-element.40), channel_id=1, source_target_pairs={{0,4},{4,0},{1,5},{5,1},{2,6},{6,2},{3,7},{7,3},{8,12},{12,8},{9,1... | collective-permute-start | bytes 983048 | tf_op jit(solution)/shard_map/ppermute | solution.py:572
  494.7 28.7 %all-to-all-start.9 = ((bf16[8,56,2048]{2,1,0:T(8,128)(2,1)}), bf16[8,56,2048]{2,1,0:T(8,128)(2,1)}, u32[]{:S(2)}, u32[]{:S(2)}) async-start(bf16[8,56,2048]{2,1,0:T(8,128)(2,1)} %bitcast.267), calls=%async_computation.9 | async-start | bytes 3670016 | tf_op jit(solution)/shard_map/all_to_all | solution.py:24
  502.2 44.8 %collective-permute-start.20 = (bf16[4,256,1024]{2,1,0:T(8,128)(2,1)}, bf16[4,256,1024]{2,1,0:T(8,128)(2,1)}, u32[]{:S(2)}, u32[]{:S(2)}) collective-permute-start(bf16[4,256,1024]{2,1,0:T(8,128)(2,1)} %dynamic-slice_bitcast_fusion.1), channel_id=1, source_target_pairs={{0,4},{4,0},{1,5},{5,1},{2,6},{6,2},{3,7},{7,3},{8,12},{12,8},{9,1... | collective-permute-start | bytes 6291464 | tf_op jit(solution)/shard_map/ppermute | solution.py:107
  523.5 56.5 %all-to-all-start.10 = ((bf16[16,40,2048]{2,1,0:T(8,128)(2,1)}), bf16[16,40,2048]{2,1,0:T(8,128)(2,1)}, u32[]{:S(2)}, u32[]{:S(2)}) async-start(bf16[16,40,2048]{2,1,0:T(8,128)(2,1)} %bitcast.285), calls=%async_computation.10 | async-start | bytes 5242880 | tf_op jit(solution)/shard_map/all_to_all | solution.py:24
  528.1 180.1 %reduce-scatter.5.cloned.1.call-start = ((), (), s32[]{:S(2)}) async-start(), calls=%async_computation.18 | async-start | bytes 7208960 | tf_op jit(solution)/shard_map/reduce_scatter | solution.py:511
  538.4 72.6 %collective-permute-start.9 = (bf16[4,256,1408]{2,1,0:T(8,128)(2,1)}, bf16[4,256,1408]{2,1,0:T(8,128)(2,1)}, u32[]{:S(2)}, u32[]{:S(2)}) collective-permute-start(bf16[4,256,1408]{2,1,0:T(8,128)(2,1)} %dynamic-slice_bitcast_fusion), channel_id=1, source_target_pairs={{0,4},{4,0},{1,5},{5,1},{2,6},{6,2},{3,7},{7,3},{8,12},{12,8},{9,1... | collective-permute-start | bytes 8650760 | tf_op jit(solution)/shard_map/ppermute | solution.py:107
  541.1 25.4 %collective-permute-start.7 = (bf16[40,2048]{1,0:T(8,128)(2,1)S(1)}, bf16[40,2048]{1,0:T(8,128)(2,1)S(1)}, u32[]{:S(2)}, u32[]{:S(2)}) collective-permute-start(bf16[40,2048]{1,0:T(8,128)(2,1)S(1)} %get-tuple-element.189), channel_id=1, source_target_pairs={{0,1},{1,2},{2,3},{3,0},{4,5},{5,6},{6,7},{7,4},{8,9},{9,10},{10,1... | collective-permute-start | bytes 491528 | tf_op jit(solution)/shard_map/ppermute | solution.py:32
  542.9 30.6 %collective-permute-start.6 = (bf16[40,2048]{1,0:T(8,128)(2,1)S(1)}, bf16[40,2048]{1,0:T(8,128)(2,1)S(1)}, u32[]{:S(2)}, u32[]{:S(2)}) collective-permute-start(bf16[40,2048]{1,0:T(8,128)(2,1)S(1)} %get-tuple-element.190), channel_id=1, source_target_pairs={{0,2},{1,3},{2,0},{3,1},{4,6},{5,7},{6,4},{7,5},{8,10},{9,11},{10,... | collective-permute-start | bytes 491528 | tf_op jit(solution)/shard_map/ppermute | solution.py:32
  545.6 28.0 %collective-permute-start.5 = (bf16[40,2048]{1,0:T(8,128)(2,1)S(1)}, bf16[40,2048]{1,0:T(8,128)(2,1)S(1)}, u32[]{:S(2)}, u32[]{:S(2)}) collective-permute-start(bf16[40,2048]{1,0:T(8,128)(2,1)S(1)} %get-tuple-element.188), channel_id=1, source_target_pairs={{0,3},{1,0},{2,1},{3,2},{4,7},{5,4},{6,5},{7,6},{8,11},{9,8},{10,9... | collective-permute-start | bytes 491528 | tf_op jit(solution)/shard_map/ppermute | solution.py:32
  550.6 23.2 %collective-permute-start.21 = (bf16[128,1024]{1,0:T(8,128)(2,1)}, bf16[128,1024]{1,0:T(8,128)(2,1)}, u32[]{:S(2)}, u32[]{:S(2)}) collective-permute-start(bf16[128,1024]{1,0:T(8,128)(2,1)} %get-tuple-element.176), channel_id=1, source_target_pairs={{0,32},{32,64},{64,96},{96,0},{1,33},{33,65},{65,97},{97,1},{2,34}... | collective-permute-start | bytes 786440 | tf_op jit(solution)/shard_map/ppermute | solution.py:73
  566.5 7.3 %collective-permute-start.23 = (bf16[128,1024]{1,0:T(8,128)(2,1)S(1)}, bf16[128,1024]{1,0:T(8,128)(2,1)}, u32[]{:S(2)}, u32[]{:S(2)}) collective-permute-start(bf16[128,1024]{1,0:T(8,128)(2,1)S(1)} %get-tuple-element.178), channel_id=1, source_target_pairs={{0,96},{32,0},{64,32},{96,64},{1,97},{33,1},{65,33},{97,65},{2,98}... | collective-permute-start | bytes 786440 | tf_op jit(solution)/shard_map/ppermute | solution.py:74
  575.8 24.5 %collective-permute-start.24 = (bf16[256,1024]{1,0:T(8,128)(2,1)}, bf16[256,1024]{1,0:T(8,128)(2,1)}, u32[]{:S(2)}, u32[]{:S(2)}) collective-permute-start(bf16[256,1024]{1,0:T(8,128)(2,1)} %pad_maximum_fusion.9), channel_id=1, source_target_pairs={{0,96},{32,0},{64,32},{96,64},{1,97},{33,1},{65,33},{97,65},{2,98}... | collective-permute-start | bytes 1572872 | tf_op jit(solution)/shard_map/ppermute | solution.py:81
  579.5 25.4 %collective-permute-start.22 = (bf16[256,1024]{1,0:T(8,128)(2,1)}, bf16[256,1024]{1,0:T(8,128)(2,1)}, u32[]{:S(2)}, u32[]{:S(2)}) collective-permute-start(bf16[256,1024]{1,0:T(8,128)(2,1)} %pad_maximum_fusion.8), channel_id=1, source_target_pairs={{0,32},{32,64},{64,96},{96,0},{1,33},{33,65},{65,97},{97,1},{2,34}... | collective-permute-start | bytes 1572872 | tf_op jit(solution)/shard_map/ppermute | solution.py:80
  591.2 99.8 %all-to-all-start.11 = ((bf16[4,40,4096]{2,1,0:T(8,128)(2,1)}), bf16[4,40,4096]{2,1,0:T(8,128)(2,1)}, u32[]{:S(2)}, u32[]{:S(2)}) async-start(bf16[4,40,4096]{2,1,0:T(8,128)(2,1)} %broadcast_in_dim.27), calls=%async_computation.11 | async-start | bytes 2621440 | tf_op jit(solution)/shard_map/all_to_all | solution.py:24
  606.6 11.2 %collective-permute-start.25 = (bf16[64,1024]{1,0:T(8,128)(2,1)S(1)}, bf16[64,1024]{1,0:T(8,128)(2,1)S(1)}, u32[]{:S(2)}, u32[]{:S(2)}) collective-permute-start(bf16[64,1024]{1,0:T(8,128)(2,1)S(1)} %get-tuple-element.196), channel_id=1, source_target_pairs={{0,24},{8,0},{16,8},{24,16},{1,25},{9,1},{17,9},{25,17},{2,26},{10... | collective-permute-start | bytes 393224 | tf_op jit(solution)/shard_map/ppermute | solution.py:32
  608.3 9.5 %collective-permute-start.26 = (bf16[64,1024]{1,0:T(8,128)(2,1)S(1)}, bf16[64,1024]{1,0:T(8,128)(2,1)S(1)}, u32[]{:S(2)}, u32[]{:S(2)}) collective-permute-start(bf16[64,1024]{1,0:T(8,128)(2,1)S(1)} %get-tuple-element.195), channel_id=1, source_target_pairs={{0,16},{8,24},{16,0},{24,8},{1,17},{9,25},{17,1},{25,9},{2,18},{10... | collective-permute-start | bytes 393224 | tf_op jit(solution)/shard_map/ppermute | solution.py:32
  609.7 27.5 %collective-permute-start.27 = (bf16[64,1024]{1,0:T(8,128)(2,1)S(1)}, bf16[64,1024]{1,0:T(8,128)(2,1)S(1)}, u32[]{:S(2)}, u32[]{:S(2)}) collective-permute-start(bf16[64,1024]{1,0:T(8,128)(2,1)S(1)} %get-tuple-element.193), channel_id=1, source_target_pairs={{0,8},{8,16},{16,24},{24,0},{1,9},{9,17},{17,25},{25,1},{2,10},{10... | collective-permute-start | bytes 393224 | tf_op jit(solution)/shard_map/ppermute | solution.py:32
  614.5 18.0 %collective-permute-start.10 = (bf16[128,1408]{1,0:T(8,128)(2,1)S(1)}, bf16[128,1408]{1,0:T(8,128)(2,1)S(1)}, u32[]{:S(2)}, u32[]{:S(2)}) collective-permute-start(bf16[128,1408]{1,0:T(8,128)(2,1)S(1)} %get-tuple-element.170), channel_id=1, source_target_pairs={{0,32},{32,64},{64,96},{96,0},{1,33},{33,65},{65,97},{97,1},{2,34}... | collective-permute-start | bytes 1081352 | tf_op jit(solution)/shard_map/ppermute | solution.py:73
  614.6 18.4 %collective-permute-start.12 = (bf16[128,1408]{1,0:T(8,128)(2,1)S(1)}, bf16[128,1408]{1,0:T(8,128)(2,1)S(1)}, u32[]{:S(2)}, u32[]{:S(2)}) collective-permute-start(bf16[128,1408]{1,0:T(8,128)(2,1)S(1)} %get-tuple-element.172), channel_id=1, source_target_pairs={{0,96},{32,0},{64,32},{96,64},{1,97},{33,1},{65,33},{97,65},{2,98}... | collective-permute-start | bytes 1081352 | tf_op jit(solution)/shard_map/ppermute | solution.py:74
  633.3 24.9 %collective-permute-start.13 = (bf16[256,1408]{1,0:T(8,128)(2,1)S(1)}, bf16[256,1408]{1,0:T(8,128)(2,1)S(1)}, u32[]{:S(2)}, u32[]{:S(2)}) collective-permute-start(bf16[256,1408]{1,0:T(8,128)(2,1)S(1)} %pad_maximum_fusion.7), channel_id=1, source_target_pairs={{0,96},{32,0},{64,32},{96,64},{1,97},{33,1},{65,33},{97,65},{2,98}... | collective-permute-start | bytes 2162696 | tf_op jit(solution)/shard_map/ppermute | solution.py:81
  637.1 25.7 %collective-permute-start.11 = (bf16[256,1408]{1,0:T(8,128)(2,1)S(1)}, bf16[256,1408]{1,0:T(8,128)(2,1)S(1)}, u32[]{:S(2)}, u32[]{:S(2)}) collective-permute-start(bf16[256,1408]{1,0:T(8,128)(2,1)S(1)} %pad_maximum_fusion.6), channel_id=1, source_target_pairs={{0,32},{32,64},{64,96},{96,0},{1,33},{33,65},{65,97},{97,1},{2,34}... | collective-permute-start | bytes 2162696 | tf_op jit(solution)/shard_map/ppermute | solution.py:80
  663.1 5.6 collective-permute-start.14
  666.3 7.1 collective-permute-start.15
  667.3 7.9 %collective-permute-start.16 = (bf16[64,1408]{1,0:T(8,128)(2,1)S(1)}, bf16[64,1408]{1,0:T(8,128)(2,1)S(1)}, u32[]{:S(2)}, u32[]{:S(2)}) collective-permute-start(bf16[64,1408]{1,0:T(8,128)(2,1)S(1)} %get-tuple-element.182), channel_id=1, source_target_pairs={{0,8},{8,16},{16,24},{24,0},{1,9},{9,17},{17,25},{25,1},{2,10},{10... | collective-permute-start | bytes 540680 | tf_op jit(solution)/shard_map/ppermute | solution.py:32
  681.4 18.4 %collective-permute-start.19 = (bf16[64,128]{0,1:T(8,128)(2,1)S(1)}, bf16[64,128]{0,1:T(8,128)(2,1)S(1)}, u32[]{:S(2)}, u32[]{:S(2)}) collective-permute-start(bf16[64,128]{0,1:T(8,128)(2,1)S(1)} %fusion.95), channel_id=1, source_target_pairs={{0,1},{1,2},{2,3},{3,0},{4,5},{5,6},{6,7},{7,4},{8,9},{9,10},{10,1... | collective-permute-start | bytes 49160 | tf_op jit(solution)/shard_map/ppermute | solution.py:32
  684.6 15.2 %collective-permute-start.18 = (bf16[64,128]{0,1:T(8,128)(2,1)S(1)}, bf16[64,128]{0,1:T(8,128)(2,1)S(1)}, u32[]{:S(2)}, u32[]{:S(2)}) collective-permute-start(bf16[64,128]{0,1:T(8,128)(2,1)S(1)} %fusion.95), channel_id=1, source_target_pairs={{0,2},{1,3},{2,0},{3,1},{4,6},{5,7},{6,4},{7,5},{8,10},{9,11},{10,... | collective-permute-start | bytes 49160 | tf_op jit(solution)/shard_map/ppermute | solution.py:32
  688.4 11.4 %collective-permute-start.17 = (bf16[64,128]{0,1:T(8,128)(2,1)S(1)}, bf16[64,128]{0,1:T(8,128)(2,1)S(1)}, u32[]{:S(2)}, u32[]{:S(2)}) collective-permute-start(bf16[64,128]{0,1:T(8,128)(2,1)S(1)} %fusion.95), channel_id=1, source_target_pairs={{0,3},{1,0},{2,1},{3,2},{4,7},{5,4},{6,5},{7,6},{8,11},{9,8},{10,9... | collective-permute-start | bytes 49160 | tf_op jit(solution)/shard_map/ppermute | solution.py:32
  (58 other events, 424.4 us)
Sparse Core Ops, SparseCore 0:
  34.6 43.2 all-gather.3
  80.2 33.1 all-gather.5
  115.7 109.5 all-gather.7
  352.4 104.9 reduce-scatter.2
  573.8 87.0 reduce-scatter.4

commit v3 on v2

--- a/solution.py
+++ b/solution.py
@@ -37,11 +37,6 @@
     return lax.dynamic_slice_in_dim(both, lax.rem(4 - first, 4), 4)
 
 
-def gather_direct(block, axis):
-    pieces = [block] + [from_ahead(block, axis, k) for k in (1, 2, 3)]
-    return in_order(pieces, lax.axis_index(axis))
-
-
 def pick_block(blocks, index):
     return lax.dynamic_index_in_dim(blocks, lax.rem(index, 4), 0, keepdims=False)
 
@@ -66,7 +61,32 @@
     return [block, after, far_low, far_high, before]
 
 
-def ring_sum(blocks, axis):
+def heads_first(shard):
+    columns = shard.shape[1] * HEAD_SIZE
+    return shard.reshape(64, -1, 4, HEAD_SIZE).transpose(2, 0, 1, 3).reshape(4, 64, columns)
+
+
+def after(value, other):
+    return lax.optimization_barrier((value, other))[0]
+
+
+def core_first(rows):
+    return rows.reshape(-1, 4, 4, 2, 64).transpose(0, 1, 3, 2, 4).reshape(-1, MODEL_WIDTH)
+
+
+def core_last(rows):
+    return rows.reshape(-1, 4, 2, 4, 64).transpose(0, 1, 3, 2, 4).reshape(-1, MODEL_WIDTH)
+
+
+def core_sum(grad, core):
+    columns = grad.shape[1]
+    parts = grad.reshape(4, 2, 256, columns)
+    keep = lax.dynamic_index_in_dim(parts, core, 1, keepdims=False)
+    give = lax.dynamic_index_in_dim(parts, 1 - core, 1, keepdims=False)
+    return (keep.astype(F32) + lax.ppermute(give, "core", SWAP).astype(F32)).astype(BF)
+
+
+def ring_first(blocks, axis):
     me = lax.axis_index(axis)
     half = blocks.shape[1] // 2
     far = pick_block(blocks, me + 2)
@@ -75,39 +95,14 @@
     right, left = pick_block(blocks, me + 1), pick_block(blocks, me + 3)
     right = jnp.concatenate([(right[:half].astype(F32) + low.astype(F32)).astype(BF), right[half:]])
     left = jnp.concatenate([left[:half], (left[half:].astype(F32) + high.astype(F32)).astype(BF)])
+    return right, left
+
+
+def ring_second(blocks, right, left, axis):
     return (
-        pick_block(blocks, me).astype(F32)
+        pick_block(blocks, lax.axis_index(axis)).astype(F32)
         + lax.ppermute(right, axis, UP).astype(F32)
         + lax.ppermute(left, axis, DOWN).astype(F32)
-    )
-
-
-def heads_first(shard):
-    columns = shard.shape[1] * HEAD_SIZE
-    return shard.reshape(64, -1, 4, HEAD_SIZE).transpose(2, 0, 1, 3).reshape(4, 64, columns)
-
-
-def after(value, other):
-    return lax.optimization_barrier((value, other))[0]
-
-
-def core_first(rows):
-    return rows.reshape(-1, 4, 4, 2, 64).transpose(0, 1, 3, 2, 4).reshape(-1, MODEL_WIDTH)
-
-
-def core_last(rows):
-    return rows.reshape(-1, 4, 2, 4, 64).transpose(0, 1, 3, 2, 4).reshape(-1, MODEL_WIDTH)
-
-
-def scatter_rows(grad, core):
-    columns = grad.shape[1]
-    parts = grad.reshape(4, 2, 256, columns)
-    keep = lax.dynamic_index_in_dim(parts, core, 1, keepdims=False)
-    give = lax.dynamic_index_in_dim(parts, 1 - core, 1, keepdims=False)
-    both = keep.astype(F32) + lax.ppermute(give, "core", SWAP).astype(F32)
-    summed = ring_sum(both.astype(BF), "dp")
-    return in_order(
-        send_direct(summed.astype(BF).reshape(4, 64, columns), "y"), lax.axis_index("y")
     )
 
 
@@ -337,6 +332,7 @@
 
     routers_own = jnp.concatenate([attn_router, mlp_router], axis=1)
     in_own = jnp.concatenate([query_matrix, key_value_weight], axis=1)
+    down_pieces = ring_pieces(down_weight[0], "dp")
     mine = exchange(
         jnp.concatenate(
             [
@@ -348,20 +344,24 @@
         ),
         "y",
     ).reshape(256, 2432)
-    lines = ("dp", "core")
-    in_w = lax.all_gather(mine[:, :1408], lines, axis=0, tiled=True)
-    out_w = lax.all_gather(after(mine[:, 1408:], in_w), lines, axis=0, tiled=True)
-    gate_up_w = lax.all_gather(
-        after(gate_up_weight[0].reshape(512, 2816), out_w), "dp", axis=0, tiled=True
-    )
-    router_m = in_w[:, 1288:1296].reshape(4, 2, 4, 64, 8).transpose(0, 2, 1, 3, 4).reshape(-1, 8)
-
-    down_pieces = ring_pieces(down_weight[0], "dp")
+    sent = jnp.concatenate([core_first(tokens), widen(attn_routes.astype(BF))], axis=1)
+    arrived = spread(after(sent, mine), "y", 4).reshape(4 * count, MODEL_WIDTH + HEAD_SIZE)
+    all_w = lax.all_gather(
+        after(mine, (down_pieces[1], down_pieces[4])), ("dp", "core"), axis=0, tiled=True
+    )
+    all_w, arrived, far_low, far_high = lax.optimization_barrier(
+        (all_w, arrived, down_pieces[2], down_pieces[3])
+    )
+    in_w, out_w = all_w[:, :1408], all_w[:, 1408:]
+    gate_up_own = gate_up_weight.reshape(4, 2, 64, 2816).transpose(1, 0, 2, 3).reshape(512, 2816)
+    gate_up_w = lax.all_gather(after(gate_up_own, all_w), "dp", axis=0, tiled=True)
+    router_m = in_w[:, 1288:1296]
+
     down_w = jnp.concatenate(
         [
             down_pieces[0],
             down_pieces[1],
-            jnp.concatenate([down_pieces[2], down_pieces[3]], axis=0),
+            jnp.concatenate([far_low, far_high], axis=0),
             down_pieces[4],
         ],
         axis=1,
@@ -371,8 +371,6 @@
         twice = jnp.concatenate([columns, columns], axis=1)
         return lax.dynamic_slice_in_dim(twice, blocks * 512, MODEL_WIDTH, axis=1)
 
-    sent = jnp.concatenate([core_first(tokens), widen(attn_routes.astype(BF))], axis=1)
-    arrived = spread(after(sent, mine), "y", 4).reshape(4 * count, MODEL_WIDTH + HEAD_SIZE)
     values = arrived[:, :MODEL_WIDTH].astype(F32)
     routes = arrived[:, MODEL_WIDTH : MODEL_WIDTH + 2].astype(jnp.int32)
     gain_a = core_first(attn_gain.astype(F32))[0]
@@ -455,7 +453,15 @@
     )
     branch_part = lax.dot_general(mixed, out_w, LAST, preferred_element_type=F32).astype(BF)
     branch_part = after(branch_part, grad_landed)
-    branch = exchange(branch_part.reshape(16, quarter, MODEL_WIDTH), plane).astype(F32).sum(axis=0)
+    grad_received = grad_landed[:, :MODEL_WIDTH]
+    grad_act_raw = lax.dot_general(
+        turned(grad_received, z), down_w, LAST, preferred_element_type=F32
+    )
+    branch = (
+        after(exchange(branch_part.reshape(16, quarter, MODEL_WIDTH), plane), grad_act_raw)
+        .astype(F32)
+        .sum(axis=0)
+    )
 
     first = x * quarter
     own_values = core_first(lax.dynamic_slice_in_dim(tokens, first, quarter)).astype(F32)
@@ -463,14 +469,13 @@
     hidden = own_values + branch
     factor_m = rms_scale(hidden)
     xn2_own = (hidden * factor_m * gain_m).astype(BF)
-    xn2 = spread(core_last(xn2_own), "tensor", 4).reshape(count, MODEL_WIDTH)
+    xn2 = spread(xn2_own, "tensor", 4).reshape(count, MODEL_WIDTH)
     gate_m = pair_gates(jnp.dot(xn2, router_m, preferred_element_type=F32), pick_m)
     weight_m = gate_m * kept.astype(F32)
 
     received = to_experts(
         lax.dot_general(any_row, xn2, ROWS, preferred_element_type=F32).astype(BF)
     )
-    grad_received = grad_landed[:, :MODEL_WIDTH]
     other_pick = grad_landed[:, MODEL_WIDTH : MODEL_WIDTH + EXPERTS].astype(F32)
     valid = grad_landed[:, MODEL_WIDTH + EXPERTS : MODEL_WIDTH + EXPERTS + 1].astype(F32)
     row_logits = jnp.dot(received, router_m, preferred_element_type=F32)
@@ -482,9 +487,6 @@
     row_gate = valid * own_weight / (own_weight + jnp.exp(other_logit - top))
 
     width = down_weight.shape[1]
-    grad_act_raw = lax.dot_general(
-        turned(grad_received, z), down_w, LAST, preferred_element_type=F32
-    )
     grad_expert = (row_gate * grad_received.astype(F32)).astype(BF)
     gate_up = jnp.dot(received, gate_up_w, preferred_element_type=F32)
     gate_part, up_part = gate_up[:, :width], gate_up[:, width:]
@@ -502,15 +504,26 @@
     row_gate_grad = jnp.sum(activated.astype(F32) * grad_act_raw, axis=1, keepdims=True)
     grad_rows = lax.dot_general(grad_gate_up, gate_up_w, LAST, preferred_element_type=F32).astype(BF)
     grad_returned = to_experts(jnp.concatenate([grad_rows, widen(in_two(row_gate_grad))], axis=1))
+    late_grad, late_act, _ = lax.optimization_barrier((grad_gate_up, activated, grad_rows))
+    grad_down_w = lax.dot_general(late_act, grad_expert, ROWS, preferred_element_type=F32).astype(BF)
     grad_gate_up_w = lax.dot_general(
-        received, grad_gate_up, ROWS, preferred_element_type=F32
-    ).astype(BF)
-    grad_down_w = lax.dot_general(activated, grad_expert, ROWS, preferred_element_type=F32).astype(BF)
+        received, late_grad, ROWS, preferred_element_type=F32
+    ).astype(BF)
     gate_up_sum = lax.psum_scatter(grad_gate_up_w, "dp", scatter_dimension=0, tiled=True)
-    gate_up_grad = gate_up_sum.reshape(1, 512, 2, width).astype(F32)
-    down_grad = lax.psum_scatter(
-        after(grad_down_w, gate_up_sum), "dp", scatter_dimension=1, tiled=True
-    ).astype(F32)[None]
+    gate_up_grad = (
+        gate_up_sum.reshape(2, 4, 64, 2816)
+        .transpose(1, 0, 2, 3)
+        .reshape(1, 512, 2, width)
+        .astype(F32)
+    )
+    down_grad = lax.psum_scatter(grad_down_w, "dp", scatter_dimension=1, tiled=True).astype(F32)[None]
+    expert_part = turned(
+        jnp.dot(late_act, down_w, preferred_element_type=F32).astype(BF), lax.rem(4 - z, 4)
+    )
+    grad_returned = after(grad_returned, (grad_gate_up_w, grad_down_w, expert_part))
+    expert_out = sum_direct(
+        jnp.stack([expert_part[:, 512 * i : 512 * (i + 1)] for i in range(4)]), "tensor"
+    ).astype(BF)
 
     grad_xn2_part = jnp.dot(
         any_row, grad_returned[:, :MODEL_WIDTH], preferred_element_type=F32
@@ -525,6 +538,8 @@
         .astype(F32)
         .sum(axis=0)
     )
+    landed, expert_out = lax.optimization_barrier((landed, expert_out))
+    returned = to_experts(expert_out)
     grad_gate_m = (
         landed[:, MODEL_WIDTH : MODEL_WIDTH + 2] + landed[:, MODEL_WIDTH + 2 : MODEL_WIDTH + 4]
     )
@@ -536,18 +551,15 @@
     grad_xn2 = landed[:, :MODEL_WIDTH] + lax.dot_general(
         grad_logit_m, router_m.astype(F32), LAST, preferred_element_type=F32
     )
-    grad_norm, gain_m_part = norm_back(core_first(grad_xn2), hidden, factor_m, gain_m)
+    grad_norm, gain_m_part = norm_back(grad_xn2, hidden, factor_m, gain_m)
     grad_hidden = core_first(quarter_of(cotangent)).astype(F32) + grad_norm
-    grad_branch = spread(grad_hidden.astype(BF), plane, 16).reshape(4 * count, MODEL_WIDTH)
-
-    expert_part = turned(
-        jnp.dot(activated, down_w, preferred_element_type=F32).astype(BF), lax.rem(4 - z, 4)
-    )
-    returned = to_experts(after(expert_part, grad_branch))
+    grad_sent_back, returned = lax.optimization_barrier((grad_hidden.astype(BF), returned))
+    grad_branch = spread(grad_sent_back, plane, 16).reshape(4 * count, MODEL_WIDTH)
+
     fetched = jnp.einsum("jtr,rd->jtd", to_row, returned, preferred_element_type=F32)
     moe_part = jnp.sum(weight_m.T[:, :, None] * fetched, axis=0).astype(BF)
-    moe = sum_direct(moe_part.reshape(4, quarter, MODEL_WIDTH), "tensor")
-    output_own = (core_last(hidden) + moe).astype(BF)
+    grad_branch, moe_part = lax.optimization_barrier((grad_branch, moe_part))
+    moe_pieces = exchange(moe_part.reshape(4, quarter, MODEL_WIDTH // 4), "tensor")
 
     grad_mixed = jnp.dot(grad_branch, out_w, preferred_element_type=F32)
     grad_q_all, grad_logit_a, grad_kv_own, grad_kv_give = in_vmem(
@@ -569,38 +581,48 @@
         gate_a,
         *shared,
     )
-    own_grad_kv = grad_kv_own + lax.ppermute(grad_kv_give, "core", SWAP).astype(F32)
+    out_terms = lax.dot_general(grad_branch, mixed, ROWS, preferred_element_type=F32).astype(BF)
+    kv_back, out_terms, moe_pieces = lax.optimization_barrier(
+        (lax.ppermute(grad_kv_give, "core", SWAP), out_terms, moe_pieces)
+    )
+    out_parts = core_sum(out_terms, core)
+    moe = moe_pieces.transpose(1, 0, 2).reshape(quarter, MODEL_WIDTH).astype(F32)
+    output_own = (core_last(hidden) + moe).astype(BF)
+    own_grad_kv = grad_kv_own + kv_back.astype(F32)
     grad_key = own_grad_kv[:, :HEAD_SIZE]
     grad_kv = jnp.concatenate(
         [grad_key * cosine - swapped(grad_key) * sine, own_grad_kv[:, HEAD_SIZE:]], axis=1
     ).astype(BF)
     grad_in = jnp.concatenate([grad_q_all, grad_kv, grad_logit_a], axis=1)
-    out_grad = heads_last(
-        scatter_rows(
-            lax.dot_general(grad_branch, mixed, ROWS, preferred_element_type=F32).astype(BF), core
-        )
-    )
     grad_xn1_part = lax.dot_general(grad_in, in_w, LAST, preferred_element_type=F32).astype(BF)
-    landed_a = (
-        exchange(grad_xn1_part.reshape(16, quarter, MODEL_WIDTH), plane).astype(F32).sum(axis=0)
-    )
-    grad_x_norm, _ = norm_back(landed_a, own_values, own_factor, gain_a)
-    ends = jnp.concatenate(
-        [output_own, core_last((grad_hidden + grad_x_norm).astype(BF))], axis=1
-    )
-    both_ends = spread(ends, "tensor", 4).reshape(count, 2 * MODEL_WIDTH)
-    output, input_grad = both_ends[:, :MODEL_WIDTH], both_ends[:, MODEL_WIDTH:]
-
+    out_right, out_left = ring_first(out_parts, "dp")
     gain_row = jnp.pad(gain_m_part[None].astype(BF), ((0, 7), (0, 0)))
     tall = jnp.concatenate([xn1, xn2_own, gain_row], axis=0)
     router_cols = jnp.pad(grad_logit_m.astype(BF), ((0, 0), (1288, 112)))
     gain_cols = (
         (jnp.arange(8)[:, None] == 0) & (jnp.arange(1408)[None, :] == 1296)
     ).astype(BF)
-    grad_tall = jnp.concatenate([grad_in, router_cols, gain_cols], axis=0)
-    in_parts = scatter_rows(
+    grad_tall = jnp.concatenate([after(grad_in, grad_xn1_part), router_cols, gain_cols], axis=0)
+    in_parts = core_sum(
         lax.dot_general(tall, grad_tall, ROWS, preferred_element_type=F32).astype(BF), core
     )
+    in_right, in_left = ring_first(in_parts, "dp")
+    out_sum = ring_second(out_parts, out_right, out_left, "dp").astype(BF)
+    landed_raw = exchange(grad_xn1_part.reshape(16, quarter, MODEL_WIDTH), plane)
+    in_sum = ring_second(in_parts, in_right, in_left, "dp").astype(BF)
+    landed_raw, in_sum, out_sum = lax.optimization_barrier((landed_raw, in_sum, out_sum))
+    landed_a = landed_raw.astype(F32).sum(axis=0)
+    grad_x_norm, _ = norm_back(landed_a, own_values, own_factor, gain_a)
+    ends = jnp.concatenate(
+        [output_own, core_last((grad_hidden + grad_x_norm).astype(BF))], axis=1
+    )
+    both_ends = after(spread(ends, "tensor", 4), gate_up_grad).reshape(count, 2 * MODEL_WIDTH)
+    output, input_grad = both_ends[:, :MODEL_WIDTH], both_ends[:, MODEL_WIDTH:]
+
+    both_sums = jnp.concatenate([in_sum, out_sum], axis=1).reshape(4, 64, 2432)
+    both_parts = in_order(send_direct(both_sums, "y"), y)
+    in_parts, out_parts = both_parts[:, :, :1408], both_parts[:, :, 1408:]
+    out_grad = heads_last(out_parts)
     in_grad = heads_last(in_parts[:, :, :1280])
     query_grad, kv_grad = in_grad[:, :8], in_grad[:, 8:]
     small_part = jnp.sum(in_parts[:, :, 1280:].astype(F32), axis=0)

time: 727 us -> 621 us (0.85)
  waiting for transfers between devices: 306 us -> 213 us
    all_gather x3 -> x2, waiting for transfers between devices: 74.1 us -> 24.7 us  [the longest x1 24.7 us: body(): lax.all_gather(after(mine, (down_pieces[1], down_pieces[4])), ('dp', 'cor...]
    ppermute x1, waiting for transfers between devices: 31.7 us -> 0.01 us  [ring_pieces(): after = lax.ppermute(block, axis, DOWN)]
    ppermute x1, waiting for transfers between devices: 1.1 us -> 16.3 us  [ring_pieces(): far_low = lax.ppermute(before[:half], axis, UP)]
    all_to_all x11 -> x12, waiting for transfers between devices: 126 us -> 113 us  [exchange(): return lax.all_to_all(blocks, axis, split_axis=0, concat_axis=0, tiled=True)]
    ppermute x12 -> x9, waiting for transfers between devices: 27 us -> 13.7 us  [from_ahead(): return lax.ppermute(block, axis, [(i, (i - steps) % 4) for i in range(4)])]
    ppermute x11, waiting for transfers between devices: 44.9 us -> 33.2 us  [the longest x2 20.1 us: ring_second(): lax.ppermute(left, axis, DOWN).astype(F32)]
    ppermute x12 -> x9, starting transfers between devices: 24.4 us -> 12.7 us  [from_ahead(): return lax.ppermute(block, axis, [(i, (i - steps) % 4) for i in range(4)])]
    all_to_all x11 -> x12, starting transfers between devices: 57.5 us -> 66.3 us  [exchange(): return lax.all_to_all(blocks, axis, split_axis=0, concat_axis=0, tiled=True)]
  transfers between devices with their start and end apart: 44 -> 41, of which waited for: 21 -> 21; matrix products, arithmetic and copies ran while one was open for 31% -> 34% of each run, Pallas kernels for 2% -> 3%
where the time goes in v3:
time: 621 us; the launch traced here: 611 us
  waiting for transfers between devices  213 us (34%)
  matrix products  101 us (16%)
  starting transfers between devices  100 us (16%)
  local copies, waits for them, and re-layouts  86.6 us (14%)
  other arithmetic  57.9 us (9%)
  blocking collectives  21.4 us (3%)
  Pallas kernels  16 us (3%)
  between operations  15.8 us (3%)
    all_to_all x12, waiting for transfers between devices, exchange(): return lax.all_to_all(blocks, axis, split_axis=0, concat_axis=0, tiled=True)  113 us
    all_to_all x12, starting transfers between devices, exchange(): return lax.all_to_all(blocks, axis, split_axis=0, concat_axis=0, tiled=True)  66.3 us
    all_gather x1, waiting for transfers between devices, body(): lax.all_gather(after(mine, (down_pieces[1], down_pieces[4])), ('dp', 'cor...  24.7 us
    all_to_all x1, blocking collectives, exchange(): return lax.all_to_all(blocks, axis, split_axis=0, concat_axis=0, tiled=True)  21.4 us
    ppermute x2, waiting for transfers between devices, ring_second(): lax.ppermute(left, axis, DOWN).astype(F32)  20.1 us
    unnamed x130, local copies, waits for them, and re-layouts  19.2 us
    ppermute x1, waiting for transfers between devices, ring_pieces(): far_low = lax.ppermute(before[:half], axis, UP)  16.3 us
    pallas_call x2, Pallas kernels, in_vmem(): pl.pallas_call(kernel, out_shape=outs, in_specs=[spec] * len(args), out_s...  16 us
  transfers between devices with their start and end apart: 41, of which 21 were waited for; matrix products, arithmetic and copies ran while one was open for 34% of the time, Pallas kernels for 3%

profile of v3, /device:TPU:0, one launch (start us, length us, event | category | flops | bytes accessed | tf_op | source)
XLA Modules:
  0.0 611.2 jit_solution(13608936293353667277)
XLA Ops:
  15.0 21.4 %all_to_all.65 = bf16[4,64,2432]{2,1,0:T(8,128)(2,1)} all-to-all(bf16[4,64,2432]{2,1,0:T(8,128)(2,1)S(1)} %pad_maximum_fusion.4), channel_id=1, replica_groups=mesh['dp'=4,'y'=4,'core'=2,'tensor'=4] {'y'}, dimensions={0} | all-to-all | bytes 2490368 | tf_op jit(solution)/shard_map/all_to_all | solution.py:24
  36.4 6.9 %collective-permute-done.1 = bf16[1408,512]{1,0:T(8,128)(2,1)} collective-permute-done((bf16[1408,512]{1,0:T(8,128)(2,1)}, bf16[1408,512]{1,0:T(8,128)(2,1)}, u32[]{:S(2)}, u32[]{:S(2)}) %collective-permute-start.1) | collective-permute-done | bytes 1441824 | tf_op jit(solution)/shard_map/ppermute | solution.py:57
  46.7 4.5 all-to-all-start.1
  58.5 7.4 %reshape.482 = bf16[4,2,64,2816]{3,2,1,0:T(8,128)(2,1)} reshape(bf16[1,512,2,1408]{3,2,1,0:T(2,128)(2,1)} %param.24) | data formatting | bytes 5767168 | tf_op jit(solution)/shard_map/reshape | solution.py:356
  65.9 3.7 copy.313
  69.5 16.3 %collective-permute-done.2 = bf16[704,512]{1,0:T(8,128)(2,1)} collective-permute-done((bf16[704,512]{1,0:T(8,128)(2,1)}, bf16[704,512]{1,0:T(8,128)(2,1)}, u32[]{:S(2)}, u32[]{:S(2)}) %collective-permute-start.2) | collective-permute-done | bytes 720928 | tf_op jit(solution)/shard_map/ppermute | solution.py:59
  85.8 4.1 collective-permute-done.3
  89.8 24.7 %all-gather.3.cloned.1.call-done = bf16[2048,2432]{1,0:T(8,128)(2,1)} async-done(((bf16[256,2432]{1,0:T(8,128)(2,1)}), bf16[2048,2432]{1,0:T(8,128)(2,1)}) %all-gather.3.cloned.1.call-update) | async-done | bytes 9961488 | tf_op jit(solution)/shard_map/all_gather | solution.py:349
  123.0 4.8 all-to-all-start.2
  133.3 7.8 %fusion.7.proj = f32[640,1408]{1,0:T(8,128)S(1)} fusion(bf16[640,2048]{1,0:T(8,128)(2,1)S(1)} %fusion.4, bf16[2048,2432]{1,0:T(8,128)(2,1)} %all-gather.3.cloned.1.call-done), kind=kOutput, calls=%fused_computation.20 | convolution fusion | flops 3690987520 | bytes 11993088 | tf_op jit(solution)/shard_map/dot_general | solution.py:431
  143.3 6.9 %shard_map.230 = (bf16[4,320,128]{2,1,0:T(8,128)(2,1)S(1)}, f32[4,320,128]{2,1,0:T(8,128)S(1)}, f32[4,320,1]{2,1,0:T(8,128)S(1)}, f32[640,2]{1,0:T(8,128)S(1)}, bf16[640,1024]{1,0:T(8,128)(2,1)S(1)}) custom-call(f32[640,1408]{1,0:T(8,128)S(1)} %fusion.7.proj, bf16[640,256]{1,0:T(8,128)(2,1)S(1)} %pad_maximum_fusion.12.own, ...), custom_call_target="tpu_custom_call" | custom-call | flops 1610612736 | bytes 4935680 | tf_op jit(solution)/shard_map/pallas_call | solution.py:262
  153.8 6.5 %fusion.20 = bf16[640,2048]{1,0:T(8,128)(2,1)} fusion(bf16[640,1024]{1,0:T(8,128)(2,1)S(1)} %get-tuple-element.51, bf16[2048,2432]{1,0:T(8,128)(2,1)} %all-gather.3.cloned.1.call-done), kind=kOutput, calls=%fused_computation.40 | convolution fusion | flops 2685665280 | bytes 8126464 | tf_op jit(solution)/shard_map/dot_general | solution.py:454
  160.2 19.8 %all-to-all-start.3 = ((bf16[16,40,2048]{2,1,0:T(8,128)(2,1)}), bf16[16,40,2048]{2,1,0:T(8,128)(2,1)}, u32[]{:S(2)}, u32[]{:S(2)}) async-start(bf16[16,40,2048]{2,1,0:T(8,128)(2,1)} %bitcast.262), calls=%async_computation.3 | async-start | bytes 5242880 | tf_op jit(solution)/shard_map/all_to_all | solution.py:24
  185.2 6.8 %fusion.43 = f32[448,1408]{1,0:T(8,128)} fusion(s32[]{:T(128)S(6)} %select_n.87, bf16[448,2048]{1,0:T(8,128)(2,1)S(1)} %slice.289, bf16[1408,512]{1,0:T(8,128)(2,1)} %collective-permute-done.1, bf16[704,512]{1,0:T(8,128)(2,1)} %collective-permute-done.3, bf16[704,512]{1,0:T(8,128)(2,1)} %collective-permute-done.2, ...), kind=kOutput, calls=%fused_computation.74 | convolution fusion | flops 2616197120 | bytes 10125316 | tf_op jit(solution)/shard_map/dot_general | solution.py:457
  192.0 27.5 %all-to-all-done.3 = bf16[16,40,2048]{2,1,0:T(8,128)(2,1)} async-done(((bf16[16,40,2048]{2,1,0:T(8,128)(2,1)}), bf16[16,40,2048]{2,1,0:T(8,128)(2,1)}, u32[]{:S(2)}, u32[]{:S(2)}) %all-to-all-start.3) | async-done | bytes 2621472 | tf_op jit(solution)/shard_map/all_to_all | solution.py:24
  225.3 3.5 all-to-all-start.4
  228.9 10.8 %all-to-all-done.4 = bf16[4,40,2048]{2,1,0:T(8,128)(2,1)S(1)} async-done(((bf16[4,40,2048]{2,1,0:T(8,128)(2,1)}), bf16[4,40,2048]{2,1,0:T(8,128)(2,1)S(1)}, u32[]{:S(2)}, u32[]{:S(2)}) %all-to-all-start.4) | async-done | bytes 655392 | tf_op jit(solution)/shard_map/all_to_all | solution.py:24
  241.6 3.6 all-to-all-start.5
  248.9 20.6 %all-to-all-done.5 = bf16[8,56,2048]{2,1,0:T(8,128)(2,1)S(1)} async-done(((bf16[8,56,2048]{2,1,0:T(8,128)(2,1)}), bf16[8,56,2048]{2,1,0:T(8,128)(2,1)S(1)}, u32[]{:S(2)}, u32[]{:S(2)}) %all-to-all-start.5) | async-done | bytes 1835040 | tf_op jit(solution)/shard_map/all_to_all | solution.py:24
  271.9 8.8 %fusion.128 = f32[448,2816]{1,0:T(8,128)S(1)} fusion(bf16[448,2048]{1,0:T(8,128)(2,1)S(1)} %bitcast.244, bf16[2048,2816]{1,0:T(8,128)(2,1)} %all-gather.5.cloned.1.call-done), kind=kOutput, calls=%fused_computation.300 | convolution fusion | flops 5167382528 | bytes 18415616 | tf_op jit(solution)/shard_map/dot_general | solution.py:491
  286.4 6.6 %convolution_convert_fusion.6 = bf16[448,2048]{1,0:T(8,128)(2,1)} fusion(bf16[2048,2816]{1,0:T(8,128)(2,1)S(1)} %copy-done.57, bf16[448,1408]{1,0:T(8,128)(2,1)S(1)} %get-tuple-element.170, bf16[448,1408]{1,0:T(8,128)(2,1)S(1)} %get-tuple-element.169), kind=kOutput, calls=%fused_computation.42 | convolution fusion | flops 5173346304 | bytes 15892480 | tf_op jit(solution)/shard_map/dot_general | solution.py:505
  292.9 7.2 %convolution_convert_fusion.2 = bf16[1408,2048]{1,0:T(8,128)(2,1)} fusion(bf16[448,1408]{1,0:T(8,128)(2,1)S(1)} %get-tuple-element.59, f32[448]{0:T(512)S(1)} %bitcast.276, bf16[448,2176]{1,0:T(8,128)(2,1)} %bitcast.21), kind=kOutput, calls=%fused_computation.2 | convolution fusion | flops 2589327360 | bytes 8865536 | tf_op jit(solution)/shard_map/dot_general | solution.py:508
  308.1 4.0 all-to-all-start.6
  312.1 7.3 %convolution_convert_fusion.7 = bf16[448,2048]{1,0:T(8,128)(2,1)S(1)} fusion(bf16[448,1408]{1,0:T(8,128)(2,1)} %copy-done.38, bf16[1408,512]{1,0:T(8,128)(2,1)} %collective-permute-done.1, bf16[704,512]{1,0:T(8,128)(2,1)} %collective-permute-done.3, bf16[704,512]{1,0:T(8,128)(2,1)} %collective-permute-done.2, bf16[1408,512]{1,0:T(8,128)(2,1)} %collective-permute-done, ...), kind=kOutput, calls=%fused_computation.43 | convolution fusion | flops 2613444608 | bytes 8863744 | tf_op jit(solution)/shard_map/dot_general | solution.py:521
  325.9 8.9 %convolution_convert_fusion = bf16[2048,2816]{1,0:T(8,128)(2,1)} fusion(bf16[448,2048]{1,0:T(8,128)(2,1)S(1)} %bitcast.245, bf16[448,2816]{1,0:T(8,128)(2,1)S(1)} %copy-done.32), kind=kOutput, calls=%fused_computation | convolution fusion | flops 5173149696 | bytes 15892480 | tf_op jit(solution)/shard_map/dot_general | solution.py:509
  343.7 3.5 all-to-all-start.7
  350.8 7.7 %all-to-all-done.7 = bf16[4,40,2176]{2,1,0:T(8,128)(2,1)S(1)} async-done(((bf16[4,40,2176]{2,1,0:T(8,128)(2,1)}), bf16[4,40,2176]{2,1,0:T(8,128)(2,1)S(1)}, u32[]{:S(2)}, u32[]{:S(2)}) %all-to-all-start.7) | async-done | bytes 696352 | tf_op jit(solution)/shard_map/all_to_all | solution.py:24
  358.9 4.1 all-to-all-start.8
  366.4 6.3 %all-to-all-done.8 = bf16[8,56,512]{2,1,0:T(8,128)(2,1)} async-done(((bf16[8,56,512]{2,1,0:T(8,128)(2,1)}), bf16[8,56,512]{2,1,0:T(8,128)(2,1)}, u32[]{:S(2)}, u32[]{:S(2)}) %all-to-all-start.8) | async-done | bytes 458784 | tf_op jit(solution)/shard_map/all_to_all | solution.py:24
  374.6 4.5 all-to-all-start.9
  381.9 37.1 %all-to-all-done.9 = bf16[16,40,2048]{2,1,0:T(8,128)(2,1)} async-done(((bf16[16,40,2048]{2,1,0:T(8,128)(2,1)}), bf16[16,40,2048]{2,1,0:T(8,128)(2,1)}, u32[]{:S(2)}, u32[]{:S(2)}) %all-to-all-start.9) | async-done | bytes 2621472 | tf_op jit(solution)/shard_map/all_to_all | solution.py:24
  419.0 4.1 all-to-all-start.10
  423.2 5.7 fusion.13.grad_mixed
  429.1 9.1 %shard_map.231 = (bf16[640,1024]{1,0:T(8,128)(2,1)S(1)}, bf16[640,128]{1,0:T(8,128)(2,1)S(1)}, f32[640,256]{1,0:T(8,128)S(1)}, bf16[640,256]{1,0:T(8,128)(2,1)}) custom-call(f32[640,1024]{1,0:T(8,128)S(1)} %fusion.13.grad_mixed, bf16[4,320,128]{2,1,0:T(8,128)(2,1)S(1)} %copy-done.13, bf16[640,256]{1,0:T(8,128)(2,1)S(1)} %pad_maximum_fusion.12.own, ...), custom_call_target="tpu_custom_call" | custom-call | flops 3221225472 | bytes 4945920 | tf_op jit(solution)/shard_map/pallas_call | solution.py:262
  438.4 6.8 %convolution_convert_fusion.4 = bf16[2048,1024]{1,0:T(8,128)(2,1)} fusion(bf16[640,2048]{1,0:T(8,128)(2,1)} %bitcast.51, bf16[640,1024]{1,0:T(8,128)(2,1)S(1)} %copy-done.7), kind=kOutput, calls=%fused_computation.29 | convolution fusion | flops 2686451712 | bytes 8126464 | tf_op jit(solution)/shard_map/dot_general | solution.py:584
  445.8 8.4 %fusion.17 = bf16[640,2048]{1,0:T(8,128)(2,1)} fusion(bf16[2048,2432]{1,0:T(8,128)(2,1)} %all-gather.3.cloned.1.call-done, bf16[640,128]{1,0:T(8,128)(2,1)S(1)} %get-tuple-element.76, bf16[640,128]{1,0:T(8,128)(2,1)S(1)} %slice.395, bf16[640,128]{1,0:T(8,128)(2,1)S(1)} %fusion.81, bf16[640,1024]{1,0:T(8,128)(2,1)S(1)} %get-tuple-element.73), kind=kOutput, calls=%fused_computation.39 | convolution fusion | flops 3699507200 | bytes 10190848 | tf_op jit(solution)/shard_map/dot_general | solution.py:597
  454.2 5.3 convolution_convert_fusion.1
  470.3 5.5 all-to-all-start.11
  475.9 3.2 fusion.9
  482.5 3.4 fusion
  489.3 5.4 collective-permute-done.15
  497.4 5.0 collective-permute-done.10
  504.9 7.4 %collective-permute-done.18 = bf16[256,1024]{1,0:T(8,128)(2,1)S(1)} collective-permute-done((bf16[256,1024]{1,0:T(8,128)(2,1)S(1)}, bf16[256,1024]{1,0:T(8,128)(2,1)S(1)}, u32[]{:S(2)}, u32[]{:S(2)}) %collective-permute-start.18) | collective-permute-done | bytes 524320 | tf_op jit(solution)/shard_map/ppermute | solution.py:105
  514.7 12.7 %collective-permute-done.13 = bf16[256,1408]{1,0:T(8,128)(2,1)S(1)} collective-permute-done((bf16[256,1408]{1,0:T(8,128)(2,1)S(1)}, bf16[256,1408]{1,0:T(8,128)(2,1)S(1)}, u32[]{:S(2)}, u32[]{:S(2)}) %collective-permute-start.13) | collective-permute-done | bytes 720928 | tf_op jit(solution)/shard_map/ppermute | solution.py:105
  540.9 4.3 all-to-all-start.12
  548.4 12.7 %collective-permute-done.20 = bf16[64,2432]{1,0:T(8,128)(2,1)S(1)} collective-permute-done((bf16[64,2432]{1,0:T(8,128)(2,1)S(1)}, bf16[64,2432]{1,0:T(8,128)(2,1)S(1)}, u32[]{:S(2)}, u32[]{:S(2)}) %collective-permute-start.20) | collective-permute-done | bytes 311328 | tf_op jit(solution)/shard_map/ppermute | solution.py:32
  585.2 3.3 bitcast_convert_fusion
  593.9 7.8 %reshape.511 = f32[1,512,2,1408]{3,2,1,0:T(2,128)} reshape(f32[4,2,64,2816]{3,2,1,0:T(8,128)} %copy.327) | data formatting | bytes 11534336 | tf_op jit(solution)/shard_map/convert_element_type | solution.py:517
  (375 shorter events, 171.8 us)
Async XLA Ops:
  7.2 107.4 %all-gather.3.cloned.1.call-start = ((), (), s32[]{:S(2)}) async-start(), calls=%async_computation.15 | async-start | bytes 11206656 | tf_op jit(solution)/shard_map/all_gather | solution.py:349
  7.2 36.1 %collective-permute-start.1 = (bf16[1408,512]{1,0:T(8,128)(2,1)}, bf16[1408,512]{1,0:T(8,128)(2,1)}, u32[]{:S(2)}, u32[]{:S(2)}) collective-permute-start(bf16[1408,512]{1,0:T(8,128)(2,1)} %bitcast.278), channel_id=1, source_target_pairs={{0,32},{32,64},{64,96},{96,0},{1,33},{33,65},{65,97},{97,1},{2,34}... | collective-permute-start | bytes 4325384 | tf_op jit(solution)/shard_map/ppermute | solution.py:57
  9.3 34.0 %collective-permute-start = (bf16[1408,512]{1,0:T(8,128)(2,1)}, bf16[1408,512]{1,0:T(8,128)(2,1)}, u32[]{:S(2)}, u32[]{:S(2)}) collective-permute-start(bf16[1408,512]{1,0:T(8,128)(2,1)} %bitcast.279), channel_id=1, source_target_pairs={{0,96},{32,0},{64,32},{96,64},{1,97},{33,1},{65,33},{97,65},{2,98}... | collective-permute-start | bytes 4325384 | tf_op jit(solution)/shard_map/ppermute | solution.py:58
  14.9 28.5 %copy-start.56 = (s32[160,2]{0,1:T(2,128)S(1)}, s32[160,2]{0,1:T(2,128)}, u32[]{:S(2)}) copy-start(s32[160,2]{0,1:T(2,128)} %param.26) | copy-start | bytes 3844
  14.9 28.5 %copy-start.39 = (bf16[160,2048]{1,0:T(8,128)(2,1)S(1)}, bf16[160,2048]{1,0:T(8,128)(2,1)}, u32[]{:S(2)}) copy-start(bf16[160,2048]{1,0:T(8,128)(2,1)} %param.15) | copy-start | bytes 1966084
  46.7 43.2 %all-to-all-start.1 = ((bf16[4,160,2176]{2,1,0:T(8,128)(2,1)}), bf16[4,160,2176]{2,1,0:T(8,128)(2,1)S(1)}, u32[]{:S(2)}, u32[]{:S(2)}) async-start(bf16[4,160,2176]{2,1,0:T(8,128)(2,1)} %broadcast_in_dim.23), calls=%async_computation.1 | async-start | bytes 5570560 | tf_op jit(solution)/shard_map/all_to_all | solution.py:24
  51.1 220.7 %all-gather.5.cloned.1.call-start = ((), (), s32[]{:S(2)}) async-start(), calls=%async_computation.16 | async-start | bytes 14417920 | tf_op jit(solution)/shard_map/all_gather | solution.py:357
  53.2 32.6 %collective-permute-start.2 = (bf16[704,512]{1,0:T(8,128)(2,1)}, bf16[704,512]{1,0:T(8,128)(2,1)}, u32[]{:S(2)}, u32[]{:S(2)}) collective-permute-start(bf16[704,512]{1,0:T(8,128)(2,1)} %slice.281), channel_id=1, source_target_pairs={{0,32},{32,64},{64,96},{96,0},{1,33},{33,65},{65,97},{97,1},{2,34}... | collective-permute-start | bytes 2162696 | tf_op jit(solution)/shard_map/ppermute | solution.py:59
  56.5 33.3 %collective-permute-start.3 = (bf16[704,512]{1,0:T(8,128)(2,1)}, bf16[704,512]{1,0:T(8,128)(2,1)}, u32[]{:S(2)}, u32[]{:S(2)}) collective-permute-start(bf16[704,512]{1,0:T(8,128)(2,1)} %slice.282), channel_id=1, source_target_pairs={{0,96},{32,0},{64,32},{96,64},{1,97},{33,1},{65,33},{97,65},{2,98}... | collective-permute-start | bytes 2162696 | tf_op jit(solution)/shard_map/ppermute | solution.py:60
  69.5 46.6 %copy-start.51 = (bf16[2048]{0:T(1024)(128)(2,1)S(1)}, bf16[2048]{0:T(1024)(128)(2,1)}, u32[]{:S(2)}) copy-start(bf16[2048]{0:T(1024)(128)(2,1)} %param.17) | copy-start | bytes 12292
  69.5 46.7 %copy-start.49 = (s32[160,2]{0,1:T(2,128)S(1)}, s32[160,2]{0,1:T(2,128)}, u32[]{:S(2)}) copy-start(s32[160,2]{0,1:T(2,128)} %param.27) | copy-start | bytes 3844
  69.5 47.3 %copy-start.54 = (s32[1,160]{1,0:T(1,128)S(1)}, s32[1,160]{1,0:T(1,128)}, u32[]{:S(2)}) copy-start(s32[1,160]{1,0:T(1,128)} %param.28) | copy-start | bytes 1924
  123.0 37.3 %all-to-all-start.2 = ((bf16[8,56,2176]{2,1,0:T(8,128)(2,1)}), bf16[8,56,2176]{2,1,0:T(8,128)(2,1)}, u32[]{:S(2)}, u32[]{:S(2)}) async-start(bf16[8,56,2176]{2,1,0:T(8,128)(2,1)} %bitcast.20), calls=%async_computation.2 | async-start | bytes 3899392 | tf_op jit(solution)/shard_map/all_to_all | solution.py:24
  141.6 1.8 collective-permute-start.4
  160.2 59.3 %all-to-all-start.3 = ((bf16[16,40,2048]{2,1,0:T(8,128)(2,1)}), bf16[16,40,2048]{2,1,0:T(8,128)(2,1)}, u32[]{:S(2)}, u32[]{:S(2)}) async-start(bf16[16,40,2048]{2,1,0:T(8,128)(2,1)} %bitcast.262), calls=%async_computation.3 | async-start | bytes 5242880 | tf_op jit(solution)/shard_map/all_to_all | solution.py:24
  182.4 39.8 %copy-start.17 = (f32[40,4,4,2,64]{4,3,2,1,0:T(2,128)}, f32[40,4,4,2,64]{4,3,2,1,0:T(2,128)S(1)}, u32[]{:S(2)}) copy-start(f32[40,4,4,2,64]{4,3,2,1,0:T(2,128)S(1)} %reshape.515) | copy-start | bytes 983044
  183.1 40.5 %copy-start.26 = (f32[40,2048]{1,0:T(8,128)}, f32[40,2048]{1,0:T(8,128)S(1)}, u32[]{:S(2)}) copy-start(f32[40,2048]{1,0:T(8,128)S(1)} %reshape.499) | copy-start | bytes 983044
  225.3 14.4 %all-to-all-start.4 = ((bf16[4,40,2048]{2,1,0:T(8,128)(2,1)}), bf16[4,40,2048]{2,1,0:T(8,128)(2,1)S(1)}, u32[]{:S(2)}, u32[]{:S(2)}) async-start(bf16[4,40,2048]{2,1,0:T(8,128)(2,1)} %broadcast_in_dim.25), calls=%async_computation.4 | async-start | bytes 1310720 | tf_op jit(solution)/shard_map/all_to_all | solution.py:24
  241.6 27.9 %all-to-all-start.5 = ((bf16[8,56,2048]{2,1,0:T(8,128)(2,1)}), bf16[8,56,2048]{2,1,0:T(8,128)(2,1)S(1)}, u32[]{:S(2)}, u32[]{:S(2)}) async-start(bf16[8,56,2048]{2,1,0:T(8,128)(2,1)} %bitcast.246), calls=%async_computation.5 | async-start | bytes 3670016 | tf_op jit(solution)/shard_map/all_to_all | solution.py:24
  245.2 340.0 %reduce-scatter.5.cloned.1.call-start = ((), (), s32[]{:S(2)}) async-start(), calls=%async_computation.18 | async-start | bytes 7208960 | tf_op jit(solution)/shard_map/reduce_scatter | solution.py:519
  308.1 29.5 %all-to-all-start.6 = ((bf16[8,56,2176]{2,1,0:T(8,128)(2,1)}), bf16[8,56,2176]{2,1,0:T(8,128)(2,1)S(1)}, u32[]{:S(2)}, u32[]{:S(2)}) async-start(bf16[8,56,2176]{2,1,0:T(8,128)(2,1)} %bitcast.242), calls=%async_computation.6 | async-start | bytes 3899392 | tf_op jit(solution)/shard_map/all_to_all | solution.py:24
  323.2 24.2 %collective-permute-start.5 = (bf16[448,512]{1,0:T(8,128)(2,1)}, bf16[448,512]{1,0:T(8,128)(2,1)}, u32[]{:S(2)}, u32[]{:S(2)}) collective-permute-start(bf16[448,512]{1,0:T(8,128)(2,1)} %get-tuple-element.187), channel_id=1, source_target_pairs={{0,3},{1,0},{2,1},{3,2},{4,7},{5,4},{6,5},{7,6},{8,11},{9,8},{10,9... | collective-permute-start | bytes 1376264 | tf_op jit(solution)/shard_map/ppermute | solution.py:32
  324.4 23.9 %collective-permute-start.7 = (bf16[448,512]{1,0:T(8,128)(2,1)}, bf16[448,512]{1,0:T(8,128)(2,1)}, u32[]{:S(2)}, u32[]{:S(2)}) collective-permute-start(bf16[448,512]{1,0:T(8,128)(2,1)} %get-tuple-element.188), channel_id=1, source_target_pairs={{0,1},{1,2},{2,3},{3,0},{4,5},{5,6},{6,7},{7,4},{8,9},{9,10},{10,1... | collective-permute-start | bytes 1376264 | tf_op jit(solution)/shard_map/ppermute | solution.py:32
  325.2 23.1 %collective-permute-start.6 = (bf16[448,512]{1,0:T(8,128)(2,1)}, bf16[448,512]{1,0:T(8,128)(2,1)}, u32[]{:S(2)}, u32[]{:S(2)}) collective-permute-start(bf16[448,512]{1,0:T(8,128)(2,1)} %get-tuple-element.189), channel_id=1, source_target_pairs={{0,2},{1,3},{2,0},{3,1},{4,6},{5,7},{6,4},{7,5},{8,10},{9,11},{10,... | collective-permute-start | bytes 1376264 | tf_op jit(solution)/shard_map/ppermute | solution.py:32
  343.7 14.9 %all-to-all-start.7 = ((bf16[4,40,2176]{2,1,0:T(8,128)(2,1)}), bf16[4,40,2176]{2,1,0:T(8,128)(2,1)S(1)}, u32[]{:S(2)}, u32[]{:S(2)}) async-start(bf16[4,40,2176]{2,1,0:T(8,128)(2,1)} %bitcast.40), calls=%async_computation.7 | async-start | bytes 1392640 | tf_op jit(solution)/shard_map/all_to_all | solution.py:24
  358.9 13.8 %all-to-all-start.8 = ((bf16[8,56,512]{2,1,0:T(8,128)(2,1)}), bf16[8,56,512]{2,1,0:T(8,128)(2,1)}, u32[]{:S(2)}, u32[]{:S(2)}) async-start(bf16[8,56,512]{2,1,0:T(8,128)(2,1)} %bitcast.49), calls=%async_computation.8 | async-start | bytes 917504 | tf_op jit(solution)/shard_map/all_to_all | solution.py:24
  374.6 44.5 %all-to-all-start.9 = ((bf16[16,40,2048]{2,1,0:T(8,128)(2,1)}), bf16[16,40,2048]{2,1,0:T(8,128)(2,1)}, u32[]{:S(2)}, u32[]{:S(2)}) async-start(bf16[16,40,2048]{2,1,0:T(8,128)(2,1)} %broadcast_in_dim.26), calls=%async_computation.9 | async-start | bytes 5242880 | tf_op jit(solution)/shard_map/all_to_all | solution.py:24
  379.0 209.5 %reduce-scatter.3.cloned.1.call-start = ((), (), s32[]{:S(2)}) async-start(), calls=%async_computation.17 | async-start | bytes 14417920 | tf_op jit(solution)/shard_map/reduce_scatter | solution.py:512
  419.0 26.2 %all-to-all-start.10 = ((bf16[4,40,512]{2,1,0:T(8,128)(2,1)}), bf16[4,40,512]{2,1,0:T(8,128)(2,1)}, u32[]{:S(2)}, u32[]{:S(2)}) async-start(bf16[4,40,512]{2,1,0:T(8,128)(2,1)} %bitcast.54), calls=%async_computation.10 | async-start | bytes 327680 | tf_op jit(solution)/shard_map/all_to_all | solution.py:24
  438.1 7.0 %collective-permute-start.8 = (bf16[640,256]{1,0:T(8,128)(2,1)}, bf16[640,256]{1,0:T(8,128)(2,1)S(1)}, u32[]{:S(2)}, u32[]{:S(2)}) collective-permute-start(bf16[640,256]{1,0:T(8,128)(2,1)} %get-tuple-element.70), channel_id=1, source_target_pairs={{0,4},{4,0},{1,5},{5,1},{2,6},{6,2},{3,7},{7,3},{8,12},{12,8},{9,1... | collective-permute-start | bytes 983048 | tf_op jit(solution)/shard_map/ppermute | solution.py:586
  463.9 18.6 %collective-permute-start.9 = (bf16[4,256,1408]{2,1,0:T(8,128)(2,1)}, bf16[4,256,1408]{2,1,0:T(8,128)(2,1)}, u32[]{:S(2)}, u32[]{:S(2)}) collective-permute-start(bf16[4,256,1408]{2,1,0:T(8,128)(2,1)} %dynamic-slice_bitcast_fusion), channel_id=1, source_target_pairs={{0,4},{4,0},{1,5},{5,1},{2,6},{6,2},{3,7},{7,3},{8,12},{12,8},{9,1... | collective-permute-start | bytes 8650760 | tf_op jit(solution)/shard_map/ppermute | solution.py:86
  466.3 9.5 %collective-permute-start.14 = (bf16[4,256,1024]{2,1,0:T(8,128)(2,1)}, bf16[4,256,1024]{2,1,0:T(8,128)(2,1)}, u32[]{:S(2)}, u32[]{:S(2)}) collective-permute-start(bf16[4,256,1024]{2,1,0:T(8,128)(2,1)} %dynamic-slice_bitcast_fusion.1), channel_id=1, source_target_pairs={{0,4},{4,0},{1,5},{5,1},{2,6},{6,2},{3,7},{7,3},{8,12},{12,8},{9,1... | collective-permute-start | bytes 6291464 | tf_op jit(solution)/shard_map/ppermute | solution.py:86
  470.3 59.6 %all-to-all-start.11 = ((bf16[16,40,2048]{2,1,0:T(8,128)(2,1)}), bf16[16,40,2048]{2,1,0:T(8,128)(2,1)S(1)}, u32[]{:S(2)}, u32[]{:S(2)}) async-start(bf16[16,40,2048]{2,1,0:T(8,128)(2,1)} %bitcast.261), calls=%async_computation.11 | async-start | bytes 5242880 | tf_op jit(solution)/shard_map/all_to_all | solution.py:24
  479.1 15.5 %collective-permute-start.15 = (bf16[128,1024]{1,0:T(8,128)(2,1)S(1)}, bf16[128,1024]{1,0:T(8,128)(2,1)S(1)}, u32[]{:S(2)}, u32[]{:S(2)}) collective-permute-start(bf16[128,1024]{1,0:T(8,128)(2,1)S(1)} %get-tuple-element.183), channel_id=1, source_target_pairs={{0,32},{32,64},{64,96},{96,0},{1,33},{33,65},{65,97},{97,1},{2,34}... | collective-permute-start | bytes 786440 | tf_op jit(solution)/shard_map/ppermute | solution.py:93
  481.2 13.4 %collective-permute-start.17 = (bf16[128,1024]{1,0:T(8,128)(2,1)S(1)}, bf16[128,1024]{1,0:T(8,128)(2,1)S(1)}, u32[]{:S(2)}, u32[]{:S(2)}) collective-permute-start(bf16[128,1024]{1,0:T(8,128)(2,1)S(1)} %get-tuple-element.185), channel_id=1, source_target_pairs={{0,96},{32,0},{64,32},{96,64},{1,97},{33,1},{65,33},{97,65},{2,98}... | collective-permute-start | bytes 786440 | tf_op jit(solution)/shard_map/ppermute | solution.py:94
  486.0 16.4 %collective-permute-start.10 = (bf16[128,1408]{1,0:T(8,128)(2,1)S(1)}, bf16[128,1408]{1,0:T(8,128)(2,1)S(1)}, u32[]{:S(2)}, u32[]{:S(2)}) collective-permute-start(bf16[128,1408]{1,0:T(8,128)(2,1)S(1)} %get-tuple-element.177), channel_id=1, source_target_pairs={{0,32},{32,64},{64,96},{96,0},{1,33},{33,65},{65,97},{97,1},{2,34}... | collective-permute-start | bytes 1081352 | tf_op jit(solution)/shard_map/ppermute | solution.py:93
  486.8 15.6 %collective-permute-start.12 = (bf16[128,1408]{1,0:T(8,128)(2,1)S(1)}, bf16[128,1408]{1,0:T(8,128)(2,1)S(1)}, u32[]{:S(2)}, u32[]{:S(2)}) collective-permute-start(bf16[128,1408]{1,0:T(8,128)(2,1)S(1)} %get-tuple-element.179), channel_id=1, source_target_pairs={{0,96},{32,0},{64,32},{96,64},{1,97},{33,1},{65,33},{97,65},{2,98}... | collective-permute-start | bytes 1081352 | tf_op jit(solution)/shard_map/ppermute | solution.py:94
  494.9 17.4 %collective-permute-start.18 = (bf16[256,1024]{1,0:T(8,128)(2,1)S(1)}, bf16[256,1024]{1,0:T(8,128)(2,1)S(1)}, u32[]{:S(2)}, u32[]{:S(2)}) collective-permute-start(bf16[256,1024]{1,0:T(8,128)(2,1)S(1)} %pad_maximum_fusion.10), channel_id=1, source_target_pairs={{0,96},{32,0},{64,32},{96,64},{1,97},{33,1},{65,33},{97,65},{2,98}... | collective-permute-start | bytes 1572872 | tf_op jit(solution)/shard_map/ppermute | solution.py:105
  496.0 17.6 %collective-permute-start.16 = (bf16[256,1024]{1,0:T(8,128)(2,1)S(1)}, bf16[256,1024]{1,0:T(8,128)(2,1)S(1)}, u32[]{:S(2)}, u32[]{:S(2)}) collective-permute-start(bf16[256,1024]{1,0:T(8,128)(2,1)S(1)} %pad_maximum_fusion.9), channel_id=1, source_target_pairs={{0,32},{32,64},{64,96},{96,0},{1,33},{33,65},{65,97},{97,1},{2,34}... | collective-permute-start | bytes 1572872 | tf_op jit(solution)/shard_map/ppermute | solution.py:104
  502.6 24.7 %collective-permute-start.13 = (bf16[256,1408]{1,0:T(8,128)(2,1)S(1)}, bf16[256,1408]{1,0:T(8,128)(2,1)S(1)}, u32[]{:S(2)}, u32[]{:S(2)}) collective-permute-start(bf16[256,1408]{1,0:T(8,128)(2,1)S(1)} %pad_maximum_fusion.8), channel_id=1, source_target_pairs={{0,96},{32,0},{64,32},{96,64},{1,97},{33,1},{65,33},{97,65},{2,98}... | collective-permute-start | bytes 2162696 | tf_op jit(solution)/shard_map/ppermute | solution.py:105
  503.5 25.2 %collective-permute-start.11 = (bf16[256,1408]{1,0:T(8,128)(2,1)S(1)}, bf16[256,1408]{1,0:T(8,128)(2,1)S(1)}, u32[]{:S(2)}, u32[]{:S(2)}) collective-permute-start(bf16[256,1408]{1,0:T(8,128)(2,1)S(1)} %pad_maximum_fusion.7), channel_id=1, source_target_pairs={{0,32},{32,64},{64,96},{96,0},{1,33},{33,65},{65,97},{97,1},{2,34}... | collective-permute-start | bytes 2162696 | tf_op jit(solution)/shard_map/ppermute | solution.py:104
  537.0 10.6 %collective-permute-start.19 = (bf16[64,2432]{1,0:T(8,128)(2,1)S(1)}, bf16[64,2432]{1,0:T(8,128)(2,1)S(1)}, u32[]{:S(2)}, u32[]{:S(2)}) collective-permute-start(bf16[64,2432]{1,0:T(8,128)(2,1)S(1)} %get-tuple-element.201), channel_id=1, source_target_pairs={{0,24},{8,0},{16,8},{24,16},{1,25},{9,1},{17,9},{25,17},{2,26},{10... | collective-permute-start | bytes 933896 | tf_op jit(solution)/shard_map/ppermute | solution.py:32
  540.9 60.8 %all-to-all-start.12 = ((bf16[4,40,4096]{2,1,0:T(8,128)(2,1)}), bf16[4,40,4096]{2,1,0:T(8,128)(2,1)}, u32[]{:S(2)}, u32[]{:S(2)}) async-start(bf16[4,40,4096]{2,1,0:T(8,128)(2,1)} %broadcast_in_dim.27), calls=%async_computation.12 | async-start | bytes 2621440 | tf_op jit(solution)/shard_map/all_to_all | solution.py:24
  545.3 16.6 %collective-permute-start.21 = (bf16[64,2432]{1,0:T(8,128)(2,1)S(1)}, bf16[64,2432]{1,0:T(8,128)(2,1)S(1)}, u32[]{:S(2)}, u32[]{:S(2)}) collective-permute-start(bf16[64,2432]{1,0:T(8,128)(2,1)S(1)} %get-tuple-element.198), channel_id=1, source_target_pairs={{0,8},{8,16},{16,24},{24,0},{1,9},{9,17},{17,25},{25,1},{2,10},{10... | collective-permute-start | bytes 933896 | tf_op jit(solution)/shard_map/ppermute | solution.py:32
  545.3 15.7 %collective-permute-start.20 = (bf16[64,2432]{1,0:T(8,128)(2,1)S(1)}, bf16[64,2432]{1,0:T(8,128)(2,1)S(1)}, u32[]{:S(2)}, u32[]{:S(2)}) collective-permute-start(bf16[64,2432]{1,0:T(8,128)(2,1)S(1)} %get-tuple-element.200), channel_id=1, source_target_pairs={{0,16},{8,24},{16,0},{24,8},{1,17},{9,25},{17,1},{25,9},{2,18},{10... | collective-permute-start | bytes 933896 | tf_op jit(solution)/shard_map/ppermute | solution.py:32
  570.4 13.7 %collective-permute-start.22 = (bf16[64,128]{0,1:T(8,128)(2,1)S(1)}, bf16[64,128]{0,1:T(8,128)(2,1)S(1)}, u32[]{:S(2)}, u32[]{:S(2)}) collective-permute-start(bf16[64,128]{0,1:T(8,128)(2,1)S(1)} %fusion.101), channel_id=1, source_target_pairs={{0,3},{1,0},{2,1},{3,2},{4,7},{5,4},{6,5},{7,6},{8,11},{9,8},{10,9... | collective-permute-start | bytes 49160 | tf_op jit(solution)/shard_map/ppermute | solution.py:32
  573.3 10.8 %collective-permute-start.23 = (bf16[64,128]{0,1:T(8,128)(2,1)S(1)}, bf16[64,128]{0,1:T(8,128)(2,1)S(1)}, u32[]{:S(2)}, u32[]{:S(2)}) collective-permute-start(bf16[64,128]{0,1:T(8,128)(2,1)S(1)} %fusion.101), channel_id=1, source_target_pairs={{0,2},{1,3},{2,0},{3,1},{4,6},{5,7},{6,4},{7,5},{8,10},{9,11},{10,... | collective-permute-start | bytes 49160 | tf_op jit(solution)/shard_map/ppermute | solution.py:32
  574.1 9.9 %collective-permute-start.24 = (bf16[64,128]{0,1:T(8,128)(2,1)S(1)}, bf16[64,128]{0,1:T(8,128)(2,1)S(1)}, u32[]{:S(2)}, u32[]{:S(2)}) collective-permute-start(bf16[64,128]{0,1:T(8,128)(2,1)S(1)} %fusion.101), channel_id=1, source_target_pairs={{0,1},{1,2},{2,3},{3,0},{4,5},{5,6},{6,7},{7,4},{8,9},{9,10},{10,1... | collective-permute-start | bytes 49160 | tf_op jit(solution)/shard_map/ppermute | solution.py:32
  (52 other events, 330.7 us)
Sparse Core Ops, SparseCore 0:
  43.5 71.0 all-gather.2
  116.8 111.7 all-gather.4
  300.3 57.9 reduce-scatter.4
  382.0 113.7 reduce-scatter.2

commit v4 on v3

--- a/solution.py
+++ b/solution.py
@@ -50,15 +50,6 @@
 
 def sum_direct(blocks, axis):
     return sum(p.astype(F32) for p in send_direct(blocks, axis))
-
-
-def ring_pieces(block, axis):
-    half = block.shape[0] // 2
-    before = lax.ppermute(block, axis, UP)
-    after = lax.ppermute(block, axis, DOWN)
-    far_low = lax.ppermute(before[:half], axis, UP)
-    far_high = lax.ppermute(after[half:], axis, DOWN)
-    return [block, after, far_low, far_high, before]
 
 
 def heads_first(shard):
@@ -332,7 +323,9 @@
 
     routers_own = jnp.concatenate([attn_router, mlp_router], axis=1)
     in_own = jnp.concatenate([query_matrix, key_value_weight], axis=1)
-    down_pieces = ring_pieces(down_weight[0], "dp")
+    down_own = down_weight[0]
+    down_before = lax.ppermute(down_own, "dp", UP)
+    down_after = lax.ppermute(down_own, "dp", DOWN)
     mine = exchange(
         jnp.concatenate(
             [
@@ -347,24 +340,21 @@
     sent = jnp.concatenate([core_first(tokens), widen(attn_routes.astype(BF))], axis=1)
     arrived = spread(after(sent, mine), "y", 4).reshape(4 * count, MODEL_WIDTH + HEAD_SIZE)
     all_w = lax.all_gather(
-        after(mine, (down_pieces[1], down_pieces[4])), ("dp", "core"), axis=0, tiled=True
-    )
-    all_w, arrived, far_low, far_high = lax.optimization_barrier(
-        (all_w, arrived, down_pieces[2], down_pieces[3])
+        after(mine, (down_before, down_after)), ("dp", "core"), axis=0, tiled=True
+    )
+    all_w, down_before, down_after, _ = lax.optimization_barrier(
+        (all_w, down_before, down_after, arrived)
     )
     in_w, out_w = all_w[:, :1408], all_w[:, 1408:]
+    low_rows = down_own.shape[0] // 2
+    far_low = lax.ppermute(down_before[:low_rows], "dp", UP)
+    far_high = lax.ppermute(down_after[low_rows:], "dp", DOWN)
     gate_up_own = gate_up_weight.reshape(4, 2, 64, 2816).transpose(1, 0, 2, 3).reshape(512, 2816)
     gate_up_w = lax.all_gather(after(gate_up_own, all_w), "dp", axis=0, tiled=True)
     router_m = in_w[:, 1288:1296]
 
     down_w = jnp.concatenate(
-        [
-            down_pieces[0],
-            down_pieces[1],
-            jnp.concatenate([far_low, far_high], axis=0),
-            down_pieces[4],
-        ],
-        axis=1,
+        [down_own, down_after, jnp.concatenate([far_low, far_high], axis=0), down_before], axis=1
     )
 
     def turned(columns, blocks):
@@ -457,16 +447,12 @@
     grad_act_raw = lax.dot_general(
         turned(grad_received, z), down_w, LAST, preferred_element_type=F32
     )
-    branch = (
-        after(exchange(branch_part.reshape(16, quarter, MODEL_WIDTH), plane), grad_act_raw)
-        .astype(F32)
-        .sum(axis=0)
-    )
+    branch = exchange(branch_part.reshape(16, quarter, MODEL_WIDTH), plane).astype(F32).sum(axis=0)
 
     first = x * quarter
     own_values = core_first(lax.dynamic_slice_in_dim(tokens, first, quarter)).astype(F32)
     own_factor = rms_scale(own_values)
-    hidden = own_values + branch
+    hidden = after(own_values, grad_act_raw) + branch
     factor_m = rms_scale(hidden)
     xn2_own = (hidden * factor_m * gain_m).astype(BF)
     xn2 = spread(xn2_own, "tensor", 4).reshape(count, MODEL_WIDTH)
@@ -503,9 +489,9 @@
     ).astype(BF)
     row_gate_grad = jnp.sum(activated.astype(F32) * grad_act_raw, axis=1, keepdims=True)
     grad_rows = lax.dot_general(grad_gate_up, gate_up_w, LAST, preferred_element_type=F32).astype(BF)
-    grad_returned = to_experts(jnp.concatenate([grad_rows, widen(in_two(row_gate_grad))], axis=1))
-    late_grad, late_act, _ = lax.optimization_barrier((grad_gate_up, activated, grad_rows))
-    grad_down_w = lax.dot_general(late_act, grad_expert, ROWS, preferred_element_type=F32).astype(BF)
+    grad_back = jnp.concatenate([grad_rows, widen(in_two(row_gate_grad))], axis=1)
+    grad_back, late_grad, late_act = lax.optimization_barrier((grad_back, grad_gate_up, activated))
+    grad_returned = to_experts(grad_back)
     grad_gate_up_w = lax.dot_general(
         received, late_grad, ROWS, preferred_element_type=F32
     ).astype(BF)
@@ -516,17 +502,16 @@
         .reshape(1, 512, 2, width)
         .astype(F32)
     )
-    down_grad = lax.psum_scatter(grad_down_w, "dp", scatter_dimension=1, tiled=True).astype(F32)[None]
     expert_part = turned(
         jnp.dot(late_act, down_w, preferred_element_type=F32).astype(BF), lax.rem(4 - z, 4)
     )
-    grad_returned = after(grad_returned, (grad_gate_up_w, grad_down_w, expert_part))
+    late_any = after(any_row, (grad_gate_up_w, expert_part))
     expert_out = sum_direct(
         jnp.stack([expert_part[:, 512 * i : 512 * (i + 1)] for i in range(4)]), "tensor"
     ).astype(BF)
 
     grad_xn2_part = jnp.dot(
-        any_row, grad_returned[:, :MODEL_WIDTH], preferred_element_type=F32
+        late_any, grad_returned[:, :MODEL_WIDTH], preferred_element_type=F32
     ).astype(BF)
     row_gate_parts = grad_returned[:, MODEL_WIDTH : MODEL_WIDTH + 2]
     gate_m_part = jnp.sum(
@@ -558,7 +543,11 @@
 
     fetched = jnp.einsum("jtr,rd->jtd", to_row, returned, preferred_element_type=F32)
     moe_part = jnp.sum(weight_m.T[:, :, None] * fetched, axis=0).astype(BF)
-    grad_branch, moe_part = lax.optimization_barrier((grad_branch, moe_part))
+    grad_down_w = lax.dot_general(
+        after(late_act, returned), grad_expert, ROWS, preferred_element_type=F32
+    ).astype(BF)
+    down_sum = lax.psum_scatter(grad_down_w, "dp", scatter_dimension=1, tiled=True)
+    grad_branch, moe_part, _ = lax.optimization_barrier((grad_branch, moe_part, grad_down_w))
     moe_pieces = exchange(moe_part.reshape(4, quarter, MODEL_WIDTH // 4), "tensor")
 
     grad_mixed = jnp.dot(grad_branch, out_w, preferred_element_type=F32)
@@ -602,44 +591,47 @@
     gain_cols = (
         (jnp.arange(8)[:, None] == 0) & (jnp.arange(1408)[None, :] == 1296)
     ).astype(BF)
-    grad_tall = jnp.concatenate([after(grad_in, grad_xn1_part), router_cols, gain_cols], axis=0)
+    grad_tall = jnp.concatenate([after(grad_in, (grad_xn1_part, out_parts, gate_up_sum)), router_cols, gain_cols], axis=0)
     in_parts = core_sum(
         lax.dot_general(tall, grad_tall, ROWS, preferred_element_type=F32).astype(BF), core
     )
     in_right, in_left = ring_first(in_parts, "dp")
-    out_sum = ring_second(out_parts, out_right, out_left, "dp").astype(BF)
+    out_sum = ring_second(after(out_parts, gate_up_grad), out_right, out_left, "dp").astype(BF)
     landed_raw = exchange(grad_xn1_part.reshape(16, quarter, MODEL_WIDTH), plane)
     in_sum = ring_second(in_parts, in_right, in_left, "dp").astype(BF)
     landed_raw, in_sum, out_sum = lax.optimization_barrier((landed_raw, in_sum, out_sum))
     landed_a = landed_raw.astype(F32).sum(axis=0)
     grad_x_norm, _ = norm_back(landed_a, own_values, own_factor, gain_a)
+    columns = jnp.arange(1408, dtype=jnp.int32)[None, :]
+    gain_a_part = jnp.sum(
+        jnp.where(columns < 1288, in_sum.astype(F32) * mine[:, :1408].astype(F32), 0.0),
+        axis=1,
+        keepdims=True,
+    )
+    small_part = jnp.where(columns[:, :128] == 17, gain_a_part, in_sum[:, 1280:].astype(F32))
+    small_sent = jnp.broadcast_to(
+        small_part.astype(BF).reshape(4, 1, 64, 128), (4, 4, 64, 128)
+    ).reshape(16, 64, 128)
+    gain_rows = lax.dynamic_slice_in_dim(attn_gain.astype(F32), z * 512 + y * 128 + core * 64, 64)
+
     ends = jnp.concatenate(
         [output_own, core_last((grad_hidden + grad_x_norm).astype(BF))], axis=1
     )
-    both_ends = after(spread(ends, "tensor", 4), gate_up_grad).reshape(count, 2 * MODEL_WIDTH)
+    ends, down_sum = lax.optimization_barrier((ends, down_sum))
+    down_grad = down_sum.astype(F32)[None]
+    both_ends = spread(ends, "tensor", 4)
+    both_ends, small_sent = lax.optimization_barrier((both_ends, small_sent))
+    small_sum = exchange(small_sent, plane).astype(F32).sum(axis=0)
+    both_ends = both_ends.reshape(count, 2 * MODEL_WIDTH)
     output, input_grad = both_ends[:, :MODEL_WIDTH], both_ends[:, MODEL_WIDTH:]
-
-    both_sums = jnp.concatenate([in_sum, out_sum], axis=1).reshape(4, 64, 2432)
-    both_parts = in_order(send_direct(both_sums, "y"), y)
-    in_parts, out_parts = both_parts[:, :, :1408], both_parts[:, :, 1408:]
-    out_grad = heads_last(out_parts)
-    in_grad = heads_last(in_parts[:, :, :1280])
+    both_sums = jnp.concatenate([in_sum[:, :1280], out_sum], axis=1).reshape(4, 64, 2304)
+    both_grads = heads_last(in_order(send_direct(both_sums, "y"), y))
+    in_grad, out_grad = both_grads[:, :10], both_grads[:, 10:]
     query_grad, kv_grad = in_grad[:, :8], in_grad[:, 8:]
-    small_part = jnp.sum(in_parts[:, :, 1280:].astype(F32), axis=0)
-    gain_rows = lax.dynamic_slice_in_dim(attn_gain.astype(F32), z * 512 + y * 128 + core * 64, 64)
-    gain_a_part = (
-        jnp.sum(in_grad * in_own.astype(F32), axis=(1, 2))
-        + jnp.sum(small_part[:, :8] * attn_router.astype(F32), axis=1)
-    ) / gain_rows
-    small_sent = jnp.concatenate([small_part[:, :17], gain_a_part[:, None]], axis=1)
-    small_bf = widen(small_sent.astype(BF))
-    small_sum = sum(
-        p.astype(F32) for p in [small_bf] + [from_ahead(small_bf, "tensor", k) for k in (1, 2, 3)]
-    )
     return (
         output,
         input_grad,
-        small_sum[:, 17],
+        small_sum[:, 17] / gain_rows,
         small_sum[:, 16],
         small_sum[:, :8],
         kv_grad,

time: 621 us -> 623 us (level)
  waiting for transfers between devices: 213 us -> 201 us
  matrix products: 101 us -> 112 us
  local copies, waits for them, and re-layouts: 86.6 us -> 97.2 us
  starting transfers between devices: 100 us -> 90.7 us
    ppermute x2, waiting for transfers between devices: 20.1 us -> 9.22 us  [ring_second(): lax.ppermute(left, axis, DOWN).astype(F32)]
    all_gather x1, waiting for transfers between devices: 24.7 us -> 17.2 us  [body(): lax.all_gather(after(mine, (down_before, down_after)), ('dp', 'core'), ax...]
    all_to_all x12 -> x13, starting transfers between devices: 66.3 us -> 61.1 us  [exchange(): return lax.all_to_all(blocks, axis, split_axis=0, concat_axis=0, tiled=True)]
    ppermute x9 -> x6, starting transfers between devices: 12.7 us -> 8.12 us  [from_ahead(): return lax.ppermute(block, axis, [(i, (i - steps) % 4) for i in range(4)])]
    unnamed x130 -> x128, local copies, waits for them, and re-layouts: 19.2 us -> 17.6 us
    ppermute x9 -> x6, waiting for transfers between devices: 13.7 us -> 12.6 us  [from_ahead(): return lax.ppermute(block, axis, [(i, (i - steps) % 4) for i in range(4)])]
    all_to_all x12 -> x13, waiting for transfers between devices: 113 us -> 113 us  [exchange(): return lax.all_to_all(blocks, axis, split_axis=0, concat_axis=0, tiled=True)]
  transfers between devices with their start and end apart: 41 -> 39, of which waited for: 21 -> 21; matrix products, arithmetic and copies ran while one was open for 34% -> 36% of each run, Pallas kernels for 3% -> 3%
where the time goes in v4:
time: 623 us; the launch traced here: 614 us
  waiting for transfers between devices  201 us (32%)
  matrix products  112 us (18%)
  local copies, waits for them, and re-layouts  97.2 us (16%)
  starting transfers between devices  90.7 us (15%)
  other arithmetic  60.2 us (10%)
  blocking collectives  21.4 us (3%)
  Pallas kernels  16 us (3%)
  between operations  15.5 us (2%)
    all_to_all x13, waiting for transfers between devices, exchange(): return lax.all_to_all(blocks, axis, split_axis=0, concat_axis=0, tiled=True)  113 us
    all_to_all x13, starting transfers between devices, exchange(): return lax.all_to_all(blocks, axis, split_axis=0, concat_axis=0, tiled=True)  61.1 us
    all_to_all x1, blocking collectives, exchange(): return lax.all_to_all(blocks, axis, split_axis=0, concat_axis=0, tiled=True)  21.4 us
    ppermute x1, waiting for transfers between devices, body(): far_high = lax.ppermute(down_after[low_rows:], 'dp', DOWN)  21.3 us
    unnamed x128, local copies, waits for them, and re-layouts  17.6 us
    all_gather x1, waiting for transfers between devices, body(): lax.all_gather(after(mine, (down_before, down_after)), ('dp', 'core'), ax...  17.2 us
    pallas_call x2, Pallas kernels, in_vmem(): pl.pallas_call(kernel, out_shape=outs, in_specs=[spec] * len(args), out_s...  16 us
    ppermute x2, waiting for transfers between devices, ring_first(): low = lax.ppermute(far[:half], axis, UP)  14.7 us
  transfers between devices with their start and end apart: 39, of which 21 were waited for; matrix products, arithmetic and copies ran while one was open for 36% of the time, Pallas kernels for 3%

profile of v4, /device:TPU:0, one launch (start us, length us, event | category | flops | bytes accessed | tf_op | source)
XLA Modules:
  0.0 613.5 jit_solution(17380696555399254307)
XLA Ops:
  15.0 21.4 %all_to_all.70 = bf16[4,64,2432]{2,1,0:T(8,128)(2,1)} all-to-all(bf16[4,64,2432]{2,1,0:T(8,128)(2,1)S(1)} %pad_maximum_fusion.4), channel_id=1, replica_groups=mesh['dp'=4,'y'=4,'core'=2,'tensor'=4] {'y'}, dimensions={0} | all-to-all | bytes 2490368 | tf_op jit(solution)/shard_map/all_to_all | solution.py:24
  36.4 6.9 %collective-permute-done = bf16[1408,512]{1,0:T(8,128)(2,1)} collective-permute-done((bf16[1408,512]{1,0:T(8,128)(2,1)}, bf16[1408,512]{1,0:T(8,128)(2,1)}, u32[]{:S(2)}, u32[]{:S(2)}) %collective-permute-start) | collective-permute-done | bytes 1441824 | tf_op jit(solution)/shard_map/ppermute | solution.py:327
  46.6 4.5 all-to-all-start.1
  51.1 7.5 %reshape.484 = bf16[4,2,64,2816]{3,2,1,0:T(8,128)(2,1)} reshape(bf16[1,512,2,1408]{3,2,1,0:T(2,128)(2,1)} %param.24) | data formatting | bytes 5767168 | tf_op jit(solution)/shard_map/reshape | solution.py:352
  62.2 22.1 %all-to-all-done.1 = bf16[4,160,2176]{2,1,0:T(8,128)(2,1)S(1)} async-done(((bf16[4,160,2176]{2,1,0:T(8,128)(2,1)}), bf16[4,160,2176]{2,1,0:T(8,128)(2,1)S(1)}, u32[]{:S(2)}, u32[]{:S(2)}) %all-to-all-start.1) | async-done | bytes 2785312 | tf_op jit(solution)/shard_map/all_to_all | solution.py:24
  84.2 17.2 %all-gather.3.cloned.1.call-done = bf16[2048,2432]{1,0:T(8,128)(2,1)} async-done(((bf16[256,2432]{1,0:T(8,128)(2,1)}), bf16[2048,2432]{1,0:T(8,128)(2,1)}) %all-gather.3.cloned.1.call-update) | async-done | bytes 9961488 | tf_op jit(solution)/shard_map/all_gather | solution.py:342
  109.4 3.9 convolution_convert_fusion.3
  113.2 4.5 all-to-all-start.2
  123.0 7.6 %fusion.7.proj = f32[640,1408]{1,0:T(8,128)S(1)} fusion(bf16[640,2048]{1,0:T(8,128)(2,1)S(1)} %fusion.4, bf16[2048,2432]{1,0:T(8,128)(2,1)} %all-gather.3.cloned.1.call-done), kind=kOutput, calls=%fused_computation.20 | convolution fusion | flops 3690987520 | bytes 11993088 | tf_op jit(solution)/shard_map/dot_general | solution.py:421
  132.9 6.9 %shard_map.230 = (bf16[4,320,128]{2,1,0:T(8,128)(2,1)S(1)}, f32[4,320,128]{2,1,0:T(8,128)S(1)}, f32[4,320,1]{2,1,0:T(8,128)S(1)}, f32[640,2]{1,0:T(8,128)S(1)}, bf16[640,1024]{1,0:T(8,128)(2,1)S(1)}) custom-call(f32[640,1408]{1,0:T(8,128)S(1)} %fusion.7.proj, bf16[640,256]{1,0:T(8,128)(2,1)S(1)} %pad_maximum_fusion.12.own, ...), custom_call_target="tpu_custom_call" | custom-call | flops 1610612736 | bytes 4935680 | tf_op jit(solution)/shard_map/pallas_call | solution.py:253
  144.0 6.5 %fusion.20 = bf16[640,2048]{1,0:T(8,128)(2,1)} fusion(bf16[640,1024]{1,0:T(8,128)(2,1)S(1)} %get-tuple-element.59, bf16[2048,2432]{1,0:T(8,128)(2,1)} %all-gather.3.cloned.1.call-done), kind=kOutput, calls=%fused_computation.40 | convolution fusion | flops 2685665280 | bytes 8126464 | tf_op jit(solution)/shard_map/dot_general | solution.py:444
  150.5 7.2 %all-to-all-start.3 = ((bf16[16,40,2048]{2,1,0:T(8,128)(2,1)}), bf16[16,40,2048]{2,1,0:T(8,128)(2,1)}, u32[]{:S(2)}, u32[]{:S(2)}) async-start(bf16[16,40,2048]{2,1,0:T(8,128)(2,1)} %bitcast.238), calls=%async_computation.3 | async-start | bytes 5242880 | tf_op jit(solution)/shard_map/all_to_all | solution.py:24
  172.8 21.3 %collective-permute-done.3 = bf16[704,512]{1,0:T(8,128)(2,1)} collective-permute-done((bf16[704,512]{1,0:T(8,128)(2,1)}, bf16[704,512]{1,0:T(8,128)(2,1)}, u32[]{:S(2)}, u32[]{:S(2)}) %collective-permute-start.3) | collective-permute-done | bytes 720928 | tf_op jit(solution)/shard_map/ppermute | solution.py:351
  194.1 4.0 collective-permute-done.2
  198.2 6.8 %fusion.43 = f32[448,1408]{1,0:T(8,128)} fusion(s32[]{:T(128)S(6)} %select_n.92, bf16[448,2048]{1,0:T(8,128)(2,1)S(1)} %slice.282, bf16[1408,512]{1,0:T(8,128)(2,1)} %collective-permute-done, bf16[704,512]{1,0:T(8,128)(2,1)} %collective-permute-done.3, bf16[704,512]{1,0:T(8,128)(2,1)} %collective-permute-done.2, ...), kind=kOutput, calls=%fused_computation.73 | convolution fusion | flops 2616197120 | bytes 10125316 | tf_op jit(solution)/shard_map/dot_general | solution.py:447
  209.8 4.6 all-to-all-start.4
  215.2 8.9 %all-to-all-done.4 = bf16[4,40,2048]{2,1,0:T(8,128)(2,1)} async-done(((bf16[4,40,2048]{2,1,0:T(8,128)(2,1)}), bf16[4,40,2048]{2,1,0:T(8,128)(2,1)}, u32[]{:S(2)}, u32[]{:S(2)}) %all-to-all-start.4) | async-done | bytes 655392 | tf_op jit(solution)/shard_map/all_to_all | solution.py:24
  227.2 4.3 all-to-all-start.5
  235.0 21.0 %all-to-all-done.5 = bf16[8,56,2048]{2,1,0:T(8,128)(2,1)} async-done(((bf16[8,56,2048]{2,1,0:T(8,128)(2,1)}), bf16[8,56,2048]{2,1,0:T(8,128)(2,1)}, u32[]{:S(2)}, u32[]{:S(2)}) %all-to-all-start.5) | async-done | bytes 1835040 | tf_op jit(solution)/shard_map/all_to_all | solution.py:24
  258.5 9.4 %fusion.120 = f32[448,2816]{1,0:T(8,128)S(1)} fusion(bf16[448,2048]{1,0:T(8,128)(2,1)} %bitcast.29, bf16[2048,2816]{1,0:T(8,128)(2,1)} %all-gather.5.cloned.1.call-done), kind=kOutput, calls=%fused_computation.290 | convolution fusion | flops 5167382528 | bytes 18415616 | tf_op jit(solution)/shard_map/dot_general | solution.py:477
  267.9 3.6 multiply_convert_fusion.3
  274.8 8.3 %convolution_convert_fusion.6 = bf16[448,2048]{1,0:T(8,128)(2,1)S(1)} fusion(bf16[2048,2816]{1,0:T(8,128)(2,1)} %all-gather.5.cloned.1.call-done, bf16[448,1408]{1,0:T(8,128)(2,1)S(1)} %copy-done.25, bf16[448,1408]{1,0:T(8,128)(2,1)S(1)} %copy-done.24), kind=kOutput, calls=%fused_computation.42 | convolution fusion | flops 5173346304 | bytes 15892480 | tf_op jit(solution)/shard_map/dot_general | solution.py:491
  284.6 11.1 %convolution_convert_fusion = bf16[2048,2816]{1,0:T(8,128)(2,1)} fusion(bf16[448,2048]{1,0:T(8,128)(2,1)} %bitcast.29, bf16[448,2816]{1,0:T(8,128)(2,1)S(1)} %pad_maximum_fusion.1), kind=kOutput, calls=%fused_computation | convolution fusion | flops 5173149696 | bytes 15892480 | tf_op jit(solution)/shard_map/dot_general | solution.py:495
  304.6 4.5 all-to-all-start.6
  309.1 7.3 %convolution_convert_fusion.7 = bf16[448,2048]{1,0:T(8,128)(2,1)S(1)} fusion(bf16[448,1408]{1,0:T(8,128)(2,1)} %get-tuple-element.70, bf16[1408,512]{1,0:T(8,128)(2,1)} %collective-permute-done, bf16[704,512]{1,0:T(8,128)(2,1)} %collective-permute-done.3, bf16[704,512]{1,0:T(8,128)(2,1)} %collective-permute-done.2, ...), kind=kOutput, calls=%fused_computation.43 | convolution fusion | flops 2613444608 | bytes 8863744 | tf_op jit(solution)/shard_map/dot_general | solution.py:506
  323.6 11.1 %all-to-all-done.6 = bf16[8,56,2176]{2,1,0:T(8,128)(2,1)} async-done(((bf16[8,56,2176]{2,1,0:T(8,128)(2,1)}), bf16[8,56,2176]{2,1,0:T(8,128)(2,1)}, u32[]{:S(2)}, u32[]{:S(2)}) %all-to-all-start.6) | async-done | bytes 1949728 | tf_op jit(solution)/shard_map/all_to_all | solution.py:24
  339.2 4.2 all-to-all-start.7
  347.5 7.3 %all-to-all-done.7 = bf16[4,40,2176]{2,1,0:T(8,128)(2,1)} async-done(((bf16[4,40,2176]{2,1,0:T(8,128)(2,1)}), bf16[4,40,2176]{2,1,0:T(8,128)(2,1)}, u32[]{:S(2)}, u32[]{:S(2)}) %all-to-all-start.7) | async-done | bytes 696352 | tf_op jit(solution)/shard_map/all_to_all | solution.py:24
  357.0 4.1 all-to-all-start.8
  365.8 5.0 all-to-all-done.8
  372.6 4.7 all-to-all-start.9
  379.5 6.5 %convolution_convert_fusion.2 = bf16[1408,2048]{1,0:T(8,128)(2,1)} fusion(bf16[448,1408]{1,0:T(8,128)(2,1)} %get-tuple-element.70, f32[448]{0:T(512)S(1)} %bitcast.258, bf16[448,2176]{1,0:T(8,128)(2,1)S(1)} %bitcast.224), kind=kOutput, calls=%fused_computation.2 | convolution fusion | flops 2589327360 | bytes 8865792 | tf_op jit(solution)/shard_map/dot_general | solution.py:546
  386.0 31.3 %all-to-all-done.9 = bf16[16,40,2048]{2,1,0:T(8,128)(2,1)} async-done(((bf16[16,40,2048]{2,1,0:T(8,128)(2,1)}), bf16[16,40,2048]{2,1,0:T(8,128)(2,1)}, u32[]{:S(2)}, u32[]{:S(2)}) %all-to-all-start.9) | async-done | bytes 2621472 | tf_op jit(solution)/shard_map/all_to_all | solution.py:24
  417.3 5.6 fusion.13.grad_mixed
  423.0 9.1 %shard_map.231 = (bf16[640,1024]{1,0:T(8,128)(2,1)S(1)}, bf16[640,128]{1,0:T(8,128)(2,1)S(1)}, f32[640,256]{1,0:T(8,128)S(1)}, bf16[640,256]{1,0:T(8,128)(2,1)}) custom-call(f32[640,1024]{1,0:T(8,128)S(1)} %fusion.13.grad_mixed, bf16[4,320,128]{2,1,0:T(8,128)(2,1)S(1)} %copy-done.12, bf16[640,256]{1,0:T(8,128)(2,1)S(1)} %pad_maximum_fusion.12.own, ...), custom_call_target="tpu_custom_call" | custom-call | flops 3221225472 | bytes 4945920 | tf_op jit(solution)/shard_map/pallas_call | solution.py:253
  435.5 7.6 %convolution_convert_fusion.4 = bf16[2048,1024]{1,0:T(8,128)(2,1)} fusion(bf16[640,2048]{1,0:T(8,128)(2,1)} %bitcast.51, bf16[640,1024]{1,0:T(8,128)(2,1)} %copy-done.6), kind=kOutput, calls=%fused_computation.29 | convolution fusion | flops 2686451712 | bytes 8126464 | tf_op jit(solution)/shard_map/dot_general | solution.py:573
  448.9 8.3 %fusion.17 = bf16[640,2048]{1,0:T(8,128)(2,1)} fusion(bf16[2048,2432]{1,0:T(8,128)(2,1)} %all-gather.3.cloned.1.call-done, bf16[640,128]{1,0:T(8,128)(2,1)S(1)} %get-tuple-element.82, bf16[640,128]{1,0:T(8,128)(2,1)S(1)} %slice.389, bf16[640,128]{1,0:T(8,128)(2,1)S(1)} %fusion.79, bf16[640,1024]{1,0:T(8,128)(2,1)S(1)} %get-tuple-element.79), kind=kOutput, calls=%fused_computation.39 | convolution fusion | flops 3699507200 | bytes 10190848 | tf_op jit(solution)/shard_map/dot_general | solution.py:586
  461.3 8.2 %convolution_convert_fusion.1 = bf16[2048,1408]{1,0:T(8,128)(2,1)S(1)} fusion(bf16[1,2048]{1,0:T(2,128)(2,1)S(1)} %convert_element_type.490, bf16[40,2048]{1,0:T(8,128)(2,1)S(1)} %copy-done.40, bf16[640,2048]{1,0:T(8,128)(2,1)} %copy-done.30, bf16[40,8]{1,0:T(8,128)(2,1)S(1)} %multiply_reduce_fusion.6, bf16[8,1408]{1,0:T(8,128)(2,1)S(1)} %and_convert_fusion, ...), kind=kOutput, calls=%fused_computation.1 | convolution fusion | flops 3991654400 | bytes 10381952 | tf_op jit(solution)/shard_map/dot_general | solution.py:596
  476.4 6.0 all-to-all-start.11
  493.1 5.7 collective-permute-done.15
  505.2 9.0 %collective-permute-done.11 = bf16[128,1408]{1,0:T(8,128)(2,1)S(1)} collective-permute-done((bf16[128,1408]{1,0:T(8,128)(2,1)S(1)}, bf16[128,1408]{1,0:T(8,128)(2,1)S(1)}, u32[]{:S(2)}, u32[]{:S(2)}) %collective-permute-start.11) | collective-permute-done | bytes 360480 | tf_op jit(solution)/shard_map/ppermute | solution.py:84
  522.9 7.8 %reshape.511 = f32[1,512,2,1408]{3,2,1,0:T(2,128)} reshape(f32[4,2,64,2816]{3,2,1,0:T(8,128)} %copy.305) | data formatting | bytes 11534336 | tf_op jit(solution)/shard_map/convert_element_type | solution.py:503
  533.1 9.2 %collective-permute-done.14 = bf16[256,1408]{1,0:T(8,128)(2,1)} collective-permute-done((bf16[256,1408]{1,0:T(8,128)(2,1)}, bf16[256,1408]{1,0:T(8,128)(2,1)}, u32[]{:S(2)}, u32[]{:S(2)}) %collective-permute-start.14) | collective-permute-done | bytes 720928 | tf_op jit(solution)/shard_map/ppermute | solution.py:96
  552.0 4.3 all-to-all-start.12
  563.7 8.2 %collective-permute-done.19 = bf16[64,2304]{1,0:T(8,128)(2,1)S(1)} collective-permute-done((bf16[64,2304]{1,0:T(8,128)(2,1)S(1)}, bf16[64,2304]{1,0:T(8,128)(2,1)S(1)}, u32[]{:S(2)}, u32[]{:S(2)}) %collective-permute-start.19) | collective-permute-done | bytes 294944 | tf_op jit(solution)/shard_map/ppermute | solution.py:32
  577.6 4.9 copy.308
  590.4 4.8 all-to-all-start.13
  597.7 6.4 %all-to-all-done.13 = bf16[16,64,128]{2,1,0:T(8,128)(2,1)S(1)} async-done(((bf16[16,64,128]{2,1,0:T(8,128)(2,1)}), bf16[16,64,128]{2,1,0:T(8,128)(2,1)S(1)}, u32[]{:S(2)}, u32[]{:S(2)}) %all-to-all-start.13) | async-done | bytes 262176 | tf_op jit(solution)/shard_map/all_to_all | solution.py:24
  (368 shorter events, 187.5 us)
Async XLA Ops:
  7.2 94.2 %all-gather.3.cloned.1.call-start = ((), (), s32[]{:S(2)}) async-start(), calls=%async_computation.16 | async-start | bytes 11206656 | tf_op jit(solution)/shard_map/all_gather | solution.py:342
  7.2 36.1 %collective-permute-start = (bf16[1408,512]{1,0:T(8,128)(2,1)}, bf16[1408,512]{1,0:T(8,128)(2,1)}, u32[]{:S(2)}, u32[]{:S(2)}) collective-permute-start(bf16[1408,512]{1,0:T(8,128)(2,1)} %bitcast.260), channel_id=1, source_target_pairs={{0,32},{32,64},{64,96},{96,0},{1,33},{33,65},{65,97},{97,1},{2,34}... | collective-permute-start | bytes 4325384 | tf_op jit(solution)/shard_map/ppermute | solution.py:327
  9.3 34.0 %collective-permute-start.1 = (bf16[1408,512]{1,0:T(8,128)(2,1)}, bf16[1408,512]{1,0:T(8,128)(2,1)}, u32[]{:S(2)}, u32[]{:S(2)}) collective-permute-start(bf16[1408,512]{1,0:T(8,128)(2,1)} %bitcast.261), channel_id=1, source_target_pairs={{0,96},{32,0},{64,32},{96,64},{1,97},{33,1},{65,33},{97,65},{2,98}... | collective-permute-start | bytes 4325384 | tf_op jit(solution)/shard_map/ppermute | solution.py:328
  14.9 28.5 %copy-start.55 = (s32[160,2]{0,1:T(2,128)S(1)}, s32[160,2]{0,1:T(2,128)}, u32[]{:S(2)}) copy-start(s32[160,2]{0,1:T(2,128)} %param.26) | copy-start | bytes 3844
  14.9 28.5 %copy-start.38 = (bf16[160,2048]{1,0:T(8,128)(2,1)S(1)}, bf16[160,2048]{1,0:T(8,128)(2,1)}, u32[]{:S(2)}) copy-start(bf16[160,2048]{1,0:T(8,128)(2,1)} %param.15) | copy-start | bytes 1966084
  46.6 37.6 %all-to-all-start.1 = ((bf16[4,160,2176]{2,1,0:T(8,128)(2,1)}), bf16[4,160,2176]{2,1,0:T(8,128)(2,1)S(1)}, u32[]{:S(2)}, u32[]{:S(2)}) async-start(bf16[4,160,2176]{2,1,0:T(8,128)(2,1)} %broadcast_in_dim.49), calls=%async_computation.1 | async-start | bytes 5570560 | tf_op jit(solution)/shard_map/all_to_all | solution.py:24
  51.1 207.4 %all-gather.5.cloned.1.call-start = ((), (), s32[]{:S(2)}) async-start(), calls=%async_computation.17 | async-start | bytes 14417920 | tf_op jit(solution)/shard_map/all_gather | solution.py:353
  62.2 39.3 %copy-start.50 = (s32[160,2]{0,1:T(2,128)S(1)}, s32[160,2]{0,1:T(2,128)}, u32[]{:S(2)}) copy-start(s32[160,2]{0,1:T(2,128)} %param.27) | copy-start | bytes 3844
  62.2 39.5 %copy-start.53 = (s32[1,160]{1,0:T(1,128)S(1)}, s32[1,160]{1,0:T(1,128)}, u32[]{:S(2)}) copy-start(s32[1,160]{1,0:T(1,128)} %param.28) | copy-start | bytes 1924
  62.2 40.3 %copy-start.51 = (bf16[2048]{0:T(1024)(128)(2,1)S(1)}, bf16[2048]{0:T(1024)(128)(2,1)}, u32[]{:S(2)}) copy-start(bf16[2048]{0:T(1024)(128)(2,1)} %param.17) | copy-start | bytes 12292
  84.2 20.9 %copy-start.15 = (bf16[4,160,2176]{2,1,0:T(8,128)(2,1)}, bf16[4,160,2176]{2,1,0:T(8,128)(2,1)S(1)}, u32[]{:S(2)}) copy-start(bf16[4,160,2176]{2,1,0:T(8,128)(2,1)S(1)} %all-to-all-done.1) | copy-start | bytes 8355844
  113.2 37.2 %all-to-all-start.2 = ((bf16[8,56,2176]{2,1,0:T(8,128)(2,1)}), bf16[8,56,2176]{2,1,0:T(8,128)(2,1)S(1)}, u32[]{:S(2)}, u32[]{:S(2)}) async-start(bf16[8,56,2176]{2,1,0:T(8,128)(2,1)} %bitcast.243), calls=%async_computation.2 | async-start | bytes 3899392 | tf_op jit(solution)/shard_map/all_to_all | solution.py:24
  131.0 1.9 collective-permute-start.4
  150.5 54.4 %all-to-all-start.3 = ((bf16[16,40,2048]{2,1,0:T(8,128)(2,1)}), bf16[16,40,2048]{2,1,0:T(8,128)(2,1)}, u32[]{:S(2)}, u32[]{:S(2)}) async-start(bf16[16,40,2048]{2,1,0:T(8,128)(2,1)} %bitcast.238), calls=%async_computation.3 | async-start | bytes 5242880 | tf_op jit(solution)/shard_map/all_to_all | solution.py:24
  159.8 34.4 %collective-permute-start.3 = (bf16[704,512]{1,0:T(8,128)(2,1)}, bf16[704,512]{1,0:T(8,128)(2,1)}, u32[]{:S(2)}, u32[]{:S(2)}) collective-permute-start(bf16[704,512]{1,0:T(8,128)(2,1)} %slice.218), channel_id=1, source_target_pairs={{0,96},{32,0},{64,32},{96,64},{1,97},{33,1},{65,33},{97,65},{2,98}... | collective-permute-start | bytes 2162696 | tf_op jit(solution)/shard_map/ppermute | solution.py:351
  162.7 35.5 %collective-permute-start.2 = (bf16[704,512]{1,0:T(8,128)(2,1)}, bf16[704,512]{1,0:T(8,128)(2,1)}, u32[]{:S(2)}, u32[]{:S(2)}) collective-permute-start(bf16[704,512]{1,0:T(8,128)(2,1)} %slice.217), channel_id=1, source_target_pairs={{0,32},{32,64},{64,96},{96,0},{1,33},{33,65},{65,97},{97,1},{2,34}... | collective-permute-start | bytes 2162696 | tf_op jit(solution)/shard_map/ppermute | solution.py:350
  172.6 25.6 %copy-start.56 = (bf16[1,1408,512]{2,1,0:T(8,128)(2,1)S(1)}, bf16[1,1408,512]{2,1,0:T(8,128)(2,1)}, u32[]{:S(2)}) copy-start(bf16[1,1408,512]{2,1,0:T(8,128)(2,1)} %param.25) | copy-start | bytes 4325380
  209.8 14.3 %all-to-all-start.4 = ((bf16[4,40,2048]{2,1,0:T(8,128)(2,1)}), bf16[4,40,2048]{2,1,0:T(8,128)(2,1)}, u32[]{:S(2)}, u32[]{:S(2)}) async-start(bf16[4,40,2048]{2,1,0:T(8,128)(2,1)} %broadcast_in_dim.50), calls=%async_computation.4 | async-start | bytes 1310720 | tf_op jit(solution)/shard_map/all_to_all | solution.py:24
  227.2 28.8 %all-to-all-start.5 = ((bf16[8,56,2048]{2,1,0:T(8,128)(2,1)}), bf16[8,56,2048]{2,1,0:T(8,128)(2,1)}, u32[]{:S(2)}, u32[]{:S(2)}) async-start(bf16[8,56,2048]{2,1,0:T(8,128)(2,1)} %bitcast.226), calls=%async_computation.5 | async-start | bytes 3670016 | tf_op jit(solution)/shard_map/all_to_all | solution.py:24
  231.5 229.8 %reduce-scatter.3.cloned.1.call-start = ((), (), s32[]{:S(2)}) async-start(), calls=%async_computation.18 | async-start | bytes 14417920 | tf_op jit(solution)/shard_map/reduce_scatter | solution.py:498
  304.6 30.1 %all-to-all-start.6 = ((bf16[8,56,2176]{2,1,0:T(8,128)(2,1)}), bf16[8,56,2176]{2,1,0:T(8,128)(2,1)}, u32[]{:S(2)}, u32[]{:S(2)}) async-start(bf16[8,56,2176]{2,1,0:T(8,128)(2,1)} %bitcast.225), calls=%async_computation.6 | async-start | bytes 3899392 | tf_op jit(solution)/shard_map/all_to_all | solution.py:24
  320.2 24.2 %collective-permute-start.7 = (bf16[448,512]{1,0:T(8,128)(2,1)}, bf16[448,512]{1,0:T(8,128)(2,1)}, u32[]{:S(2)}, u32[]{:S(2)}) collective-permute-start(bf16[448,512]{1,0:T(8,128)(2,1)} %get-tuple-element.202), channel_id=1, source_target_pairs={{0,1},{1,2},{2,3},{3,0},{4,5},{5,6},{6,7},{7,4},{8,9},{9,10},{10,1... | collective-permute-start | bytes 1376264 | tf_op jit(solution)/shard_map/ppermute | solution.py:32
  320.8 23.6 %collective-permute-start.6 = (bf16[448,512]{1,0:T(8,128)(2,1)}, bf16[448,512]{1,0:T(8,128)(2,1)}, u32[]{:S(2)}, u32[]{:S(2)}) collective-permute-start(bf16[448,512]{1,0:T(8,128)(2,1)} %get-tuple-element.203), channel_id=1, source_target_pairs={{0,2},{1,3},{2,0},{3,1},{4,6},{5,7},{6,4},{7,5},{8,10},{9,11},{10,... | collective-permute-start | bytes 1376264 | tf_op jit(solution)/shard_map/ppermute | solution.py:32
  322.9 22.1 %collective-permute-start.5 = (bf16[448,512]{1,0:T(8,128)(2,1)}, bf16[448,512]{1,0:T(8,128)(2,1)}, u32[]{:S(2)}, u32[]{:S(2)}) collective-permute-start(bf16[448,512]{1,0:T(8,128)(2,1)} %get-tuple-element.201), channel_id=1, source_target_pairs={{0,3},{1,0},{2,1},{3,2},{4,7},{5,4},{6,5},{7,6},{8,11},{9,8},{10,9... | collective-permute-start | bytes 1376264 | tf_op jit(solution)/shard_map/ppermute | solution.py:32
  339.2 15.7 %all-to-all-start.7 = ((bf16[4,40,2176]{2,1,0:T(8,128)(2,1)}), bf16[4,40,2176]{2,1,0:T(8,128)(2,1)}, u32[]{:S(2)}, u32[]{:S(2)}) async-start(bf16[4,40,2176]{2,1,0:T(8,128)(2,1)} %bitcast.236), calls=%async_computation.7 | async-start | bytes 1392640 | tf_op jit(solution)/shard_map/all_to_all | solution.py:24
  357.0 13.8 %all-to-all-start.8 = ((bf16[8,56,512]{2,1,0:T(8,128)(2,1)}), bf16[8,56,512]{2,1,0:T(8,128)(2,1)}, u32[]{:S(2)}, u32[]{:S(2)}) async-start(bf16[8,56,512]{2,1,0:T(8,128)(2,1)} %bitcast.244), calls=%async_computation.8 | async-start | bytes 917504 | tf_op jit(solution)/shard_map/all_to_all | solution.py:24
  372.6 44.7 %all-to-all-start.9 = ((bf16[16,40,2048]{2,1,0:T(8,128)(2,1)}), bf16[16,40,2048]{2,1,0:T(8,128)(2,1)}, u32[]{:S(2)}, u32[]{:S(2)}) async-start(bf16[16,40,2048]{2,1,0:T(8,128)(2,1)} %broadcast_in_dim.51), calls=%async_computation.9 | async-start | bytes 5242880 | tf_op jit(solution)/shard_map/all_to_all | solution.py:24
  432.1 11.0 %collective-permute-start.8 = (bf16[640,256]{1,0:T(8,128)(2,1)}, bf16[640,256]{1,0:T(8,128)(2,1)S(1)}, u32[]{:S(2)}, u32[]{:S(2)}) collective-permute-start(bf16[640,256]{1,0:T(8,128)(2,1)} %get-tuple-element.76), channel_id=1, source_target_pairs={{0,4},{4,0},{1,5},{5,1},{2,6},{6,2},{3,7},{7,3},{8,12},{12,8},{9,1... | collective-permute-start | bytes 983048 | tf_op jit(solution)/shard_map/ppermute | solution.py:575
  432.1 11.0 %all-to-all-start.10 = ((bf16[4,40,512]{2,1,0:T(8,128)(2,1)}), bf16[4,40,512]{2,1,0:T(8,128)(2,1)S(1)}, u32[]{:S(2)}, u32[]{:S(2)}) async-start(bf16[4,40,512]{2,1,0:T(8,128)(2,1)} %bitcast.249), calls=%async_computation.10 | async-start | bytes 327680 | tf_op jit(solution)/shard_map/all_to_all | solution.py:24
  435.5 115.3 %reduce-scatter.5.cloned.1.call-start = ((), (), s32[]{:S(2)}) async-start(), calls=%async_computation.19 | async-start | bytes 7208960 | tf_op jit(solution)/shard_map/reduce_scatter | solution.py:549
  446.4 12.3 %collective-permute-start.9 = (bf16[4,256,1024]{2,1,0:T(8,128)(2,1)}, bf16[4,256,1024]{2,1,0:T(8,128)(2,1)}, u32[]{:S(2)}, u32[]{:S(2)}) collective-permute-start(bf16[4,256,1024]{2,1,0:T(8,128)(2,1)} %dynamic-slice_bitcast_fusion.1), channel_id=1, source_target_pairs={{0,4},{4,0},{1,5},{5,1},{2,6},{6,2},{3,7},{7,3},{8,12},{12,8},{9,1... | collective-permute-start | bytes 6291464 | tf_op jit(solution)/shard_map/ppermute | solution.py:77
  461.3 21.3 %copy-start.16 = (bf16[4,256,1024]{2,1,0:T(8,128)(2,1)}, bf16[4,256,1024]{2,1,0:T(8,128)(2,1)S(1)}, u32[]{:S(2)}) copy-start(bf16[4,256,1024]{2,1,0:T(8,128)(2,1)S(1)} %fusion.9) | copy-start | bytes 6291460
  472.9 13.2 %collective-permute-start.10 = (bf16[4,256,1408]{2,1,0:T(8,128)(2,1)}, bf16[4,256,1408]{2,1,0:T(8,128)(2,1)}, u32[]{:S(2)}, u32[]{:S(2)}) collective-permute-start(bf16[4,256,1408]{2,1,0:T(8,128)(2,1)} %dynamic-slice_bitcast_fusion), channel_id=1, source_target_pairs={{0,4},{4,0},{1,5},{5,1},{2,6},{6,2},{3,7},{7,3},{8,12},{12,8},{9,1... | collective-permute-start | bytes 8650760 | tf_op jit(solution)/shard_map/ppermute | solution.py:77
  476.4 69.7 %all-to-all-start.11 = ((bf16[16,40,2048]{2,1,0:T(8,128)(2,1)}), bf16[16,40,2048]{2,1,0:T(8,128)(2,1)}, u32[]{:S(2)}, u32[]{:S(2)}) async-start(bf16[16,40,2048]{2,1,0:T(8,128)(2,1)} %bitcast.237), calls=%async_computation.11 | async-start | bytes 5242880 | tf_op jit(solution)/shard_map/all_to_all | solution.py:24
  482.7 16.1 %collective-permute-start.15 = (bf16[128,1024]{1,0:T(8,128)(2,1)S(1)}, bf16[128,1024]{1,0:T(8,128)(2,1)S(1)}, u32[]{:S(2)}, u32[]{:S(2)}) collective-permute-start(bf16[128,1024]{1,0:T(8,128)(2,1)S(1)} %get-tuple-element.197), channel_id=1, source_target_pairs={{0,32},{32,64},{64,96},{96,0},{1,33},{33,65},{65,97},{97,1},{2,34}... | collective-permute-start | bytes 786440 | tf_op jit(solution)/shard_map/ppermute | solution.py:84
  482.8 16.0 %collective-permute-start.17 = (bf16[128,1024]{1,0:T(8,128)(2,1)S(1)}, bf16[128,1024]{1,0:T(8,128)(2,1)S(1)}, u32[]{:S(2)}, u32[]{:S(2)}) collective-permute-start(bf16[128,1024]{1,0:T(8,128)(2,1)S(1)} %get-tuple-element.199), channel_id=1, source_target_pairs={{0,96},{32,0},{64,32},{96,64},{1,97},{33,1},{65,33},{97,65},{2,98}... | collective-permute-start | bytes 786440 | tf_op jit(solution)/shard_map/ppermute | solution.py:85
  489.8 24.4 %collective-permute-start.11 = (bf16[128,1408]{1,0:T(8,128)(2,1)S(1)}, bf16[128,1408]{1,0:T(8,128)(2,1)S(1)}, u32[]{:S(2)}, u32[]{:S(2)}) collective-permute-start(bf16[128,1408]{1,0:T(8,128)(2,1)S(1)} %get-tuple-element.189), channel_id=1, source_target_pairs={{0,32},{32,64},{64,96},{96,0},{1,33},{33,65},{65,97},{97,1},{2,34}... | collective-permute-start | bytes 1081352 | tf_op jit(solution)/shard_map/ppermute | solution.py:84
  489.8 24.4 %collective-permute-start.13 = (bf16[128,1408]{1,0:T(8,128)(2,1)S(1)}, bf16[128,1408]{1,0:T(8,128)(2,1)S(1)}, u32[]{:S(2)}, u32[]{:S(2)}) collective-permute-start(bf16[128,1408]{1,0:T(8,128)(2,1)S(1)} %get-tuple-element.191), channel_id=1, source_target_pairs={{0,96},{32,0},{64,32},{96,64},{1,97},{33,1},{65,33},{97,65},{2,98}... | collective-permute-start | bytes 1081352 | tf_op jit(solution)/shard_map/ppermute | solution.py:85
  500.8 29.8 %collective-permute-start.18 = (bf16[256,1024]{1,0:T(8,128)(2,1)}, bf16[256,1024]{1,0:T(8,128)(2,1)}, u32[]{:S(2)}, u32[]{:S(2)}) collective-permute-start(bf16[256,1024]{1,0:T(8,128)(2,1)} %pad_maximum_fusion.10), channel_id=1, source_target_pairs={{0,96},{32,0},{64,32},{96,64},{1,97},{33,1},{65,33},{97,65},{2,98}... | collective-permute-start | bytes 1572872 | tf_op jit(solution)/shard_map/ppermute | solution.py:96
  505.2 25.5 %collective-permute-start.16 = (bf16[256,1024]{1,0:T(8,128)(2,1)}, bf16[256,1024]{1,0:T(8,128)(2,1)}, u32[]{:S(2)}, u32[]{:S(2)}) collective-permute-start(bf16[256,1024]{1,0:T(8,128)(2,1)} %pad_maximum_fusion.9), channel_id=1, source_target_pairs={{0,32},{32,64},{64,96},{96,0},{1,33},{33,65},{65,97},{97,1},{2,34}... | collective-permute-start | bytes 1572872 | tf_op jit(solution)/shard_map/ppermute | solution.py:95
  515.3 27.0 %collective-permute-start.14 = (bf16[256,1408]{1,0:T(8,128)(2,1)}, bf16[256,1408]{1,0:T(8,128)(2,1)}, u32[]{:S(2)}, u32[]{:S(2)}) collective-permute-start(bf16[256,1408]{1,0:T(8,128)(2,1)} %pad_maximum_fusion.8), channel_id=1, source_target_pairs={{0,96},{32,0},{64,32},{96,64},{1,97},{33,1},{65,33},{97,65},{2,98}... | collective-permute-start | bytes 2162696 | tf_op jit(solution)/shard_map/ppermute | solution.py:96
  519.4 24.3 %collective-permute-start.12 = (bf16[256,1408]{1,0:T(8,128)(2,1)}, bf16[256,1408]{1,0:T(8,128)(2,1)}, u32[]{:S(2)}, u32[]{:S(2)}) collective-permute-start(bf16[256,1408]{1,0:T(8,128)(2,1)} %pad_maximum_fusion.7), channel_id=1, source_target_pairs={{0,32},{32,64},{64,96},{96,0},{1,33},{33,65},{65,97},{97,1},{2,34}... | collective-permute-start | bytes 2162696 | tf_op jit(solution)/shard_map/ppermute | solution.py:95
  552.0 37.6 %all-to-all-start.12 = ((bf16[4,40,4096]{2,1,0:T(8,128)(2,1)}), bf16[4,40,4096]{2,1,0:T(8,128)(2,1)}, u32[]{:S(2)}, u32[]{:S(2)}) async-start(bf16[4,40,4096]{2,1,0:T(8,128)(2,1)} %broadcast_in_dim.52), calls=%async_computation.14 | async-start | bytes 2621440 | tf_op jit(solution)/shard_map/all_to_all | solution.py:24
  556.6 15.3 %collective-permute-start.19 = (bf16[64,2304]{1,0:T(8,128)(2,1)S(1)}, bf16[64,2304]{1,0:T(8,128)(2,1)S(1)}, u32[]{:S(2)}, u32[]{:S(2)}) collective-permute-start(bf16[64,2304]{1,0:T(8,128)(2,1)S(1)} %get-tuple-element.213), channel_id=1, source_target_pairs={{0,24},{8,0},{16,8},{24,16},{1,25},{9,1},{17,9},{25,17},{2,26},{10... | collective-permute-start | bytes 884744 | tf_op jit(solution)/shard_map/ppermute | solution.py:32
  559.4 12.5 %collective-permute-start.20 = (bf16[64,2304]{1,0:T(8,128)(2,1)S(1)}, bf16[64,2304]{1,0:T(8,128)(2,1)S(1)}, u32[]{:S(2)}, u32[]{:S(2)}) collective-permute-start(bf16[64,2304]{1,0:T(8,128)(2,1)S(1)} %get-tuple-element.212), channel_id=1, source_target_pairs={{0,16},{8,24},{16,0},{24,8},{1,17},{9,25},{17,1},{25,9},{2,18},{10... | collective-permute-start | bytes 884744 | tf_op jit(solution)/shard_map/ppermute | solution.py:32
  560.2 15.3 %collective-permute-start.21 = (bf16[64,2304]{1,0:T(8,128)(2,1)S(1)}, bf16[64,2304]{1,0:T(8,128)(2,1)S(1)}, u32[]{:S(2)}, u32[]{:S(2)}) collective-permute-start(bf16[64,2304]{1,0:T(8,128)(2,1)S(1)} %get-tuple-element.210), channel_id=1, source_target_pairs={{0,8},{8,16},{16,24},{24,0},{1,9},{9,17},{17,25},{25,1},{2,10},{10... | collective-permute-start | bytes 884744 | tf_op jit(solution)/shard_map/ppermute | solution.py:32
  588.0 18.7 %copy-start.1 = (bf16[64,8,512]{2,1,0:T(8,128)(2,1)S(1)}, bf16[64,8,512]{2,1,0:T(8,128)(2,1)}, u32[]{:S(2)}) copy-start(bf16[64,8,512]{2,1,0:T(8,128)(2,1)} %param.22) | copy-start | bytes 1572868
  590.4 13.7 %all-to-all-start.13 = ((bf16[16,64,128]{2,1,0:T(8,128)(2,1)}), bf16[16,64,128]{2,1,0:T(8,128)(2,1)S(1)}, u32[]{:S(2)}, u32[]{:S(2)}) async-start(bf16[16,64,128]{2,1,0:T(8,128)(2,1)} %bitcast.83), calls=%async_computation.15 | async-start | bytes 524288 | tf_op jit(solution)/shard_map/all_to_all | solution.py:24
  (49 other events, 258.3 us)
Sparse Core Ops, SparseCore 0:
  43.5 57.9 all-gather.2
  103.7 125.3 all-gather.4
  295.8 101.2 reduce-scatter.2
  447.6 74.3 reduce-scatter.4

commit v5 on v4

--- a/solution.py
+++ b/solution.py
@@ -48,10 +48,6 @@
     ]
 
 
-def sum_direct(blocks, axis):
-    return sum(p.astype(F32) for p in send_direct(blocks, axis))
-
-
 def heads_first(shard):
     columns = shard.shape[1] * HEAD_SIZE
     return shard.reshape(64, -1, 4, HEAD_SIZE).transpose(2, 0, 1, 3).reshape(4, 64, columns)
@@ -69,31 +65,20 @@
     return rows.reshape(-1, 4, 2, 4, 64).transpose(0, 1, 3, 2, 4).reshape(-1, MODEL_WIDTH)
 
 
-def core_sum(grad, core):
-    columns = grad.shape[1]
-    parts = grad.reshape(4, 2, 256, columns)
-    keep = lax.dynamic_index_in_dim(parts, core, 1, keepdims=False)
-    give = lax.dynamic_index_in_dim(parts, 1 - core, 1, keepdims=False)
-    return (keep.astype(F32) + lax.ppermute(give, "core", SWAP).astype(F32)).astype(BF)
-
-
-def ring_first(blocks, axis):
-    me = lax.axis_index(axis)
-    half = blocks.shape[1] // 2
-    far = pick_block(blocks, me + 2)
-    low = lax.ppermute(far[:half], axis, UP)
-    high = lax.ppermute(far[half:], axis, DOWN)
-    right, left = pick_block(blocks, me + 1), pick_block(blocks, me + 3)
-    right = jnp.concatenate([(right[:half].astype(F32) + low.astype(F32)).astype(BF), right[half:]])
-    left = jnp.concatenate([left[:half], (left[half:].astype(F32) + high.astype(F32)).astype(BF)])
-    return right, left
-
-
-def ring_second(blocks, right, left, axis):
+def ring_first(ahead, low, high, back, axis):
+    low = lax.ppermute(low, axis, UP)
+    high = lax.ppermute(high, axis, DOWN)
+    half = low.shape[0]
+    ahead = jnp.concatenate([(ahead[:half].astype(F32) + low.astype(F32)).astype(BF), ahead[half:]])
+    back = jnp.concatenate([back[:half], (back[half:].astype(F32) + high.astype(F32)).astype(BF)])
+    return ahead, back
+
+
+def ring_second(own, ahead, back, axis):
     return (
-        pick_block(blocks, lax.axis_index(axis)).astype(F32)
-        + lax.ppermute(right, axis, UP).astype(F32)
-        + lax.ppermute(left, axis, DOWN).astype(F32)
+        own.astype(F32)
+        + lax.ppermute(ahead, axis, UP).astype(F32)
+        + lax.ppermute(back, axis, DOWN).astype(F32)
     )
 
 
@@ -261,6 +246,288 @@
     )(*args)
 
 
+FREE = pl.CostEstimate(flops=0, bytes_accessed=0, transcendentals=0)
+
+
+def on_grid(kernel, scalars, grid, in_specs, out_specs, outs, scratch, *args, cost=FREE):
+    return pl.pallas_call(
+        kernel,
+        out_shape=outs,
+        grid_spec=pltpu.PrefetchScalarGridSpec(
+            num_scalar_prefetch=1,
+            grid=grid,
+            in_specs=in_specs,
+            out_specs=out_specs,
+            scratch_shapes=scratch,
+        ),
+        compiler_params=pltpu.CompilerParams(vmem_limit_bytes=48 * 1024 * 1024),
+        cost_estimate=cost,
+    )(jnp.stack(scalars).astype(jnp.int32), *args)
+
+
+def give_terms(tall, terms, place, core):
+    depth, columns = terms.shape
+
+    def kernel(at, left, right, out):
+        out[0] = lax.dot_general(left[...], right[...], ROWS, preferred_element_type=F32).astype(BF)
+
+    return on_grid(
+        kernel,
+        (place, core),
+        (4,),
+        [
+            pl.BlockSpec((depth, 256), lambda i, at: (0, 2 * i + 1 - at[1])),
+            pl.BlockSpec((depth, columns), lambda i, at: (0, 0)),
+        ],
+        pl.BlockSpec((1, 256, columns), lambda i, at: (i, 0, 0)),
+        jax.ShapeDtypeStruct((4, 256, columns), BF),
+        [],
+        tall,
+        terms,
+    )
+
+
+def keep_terms(tall, terms, landed, place, core):
+    depth, columns = terms.shape
+
+    def kernel(at, left, right, more, own, ahead, low, high, back):
+        total = lax.dot_general(left[...], right[...], ROWS, preferred_element_type=F32).astype(
+            BF
+        ).astype(F32) + more[0].astype(F32)
+        total = total.astype(BF)
+        step = pl.program_id(0)
+
+        @pl.when(step == 0)
+        def _():
+            own[...] = total
+
+        @pl.when(step == 1)
+        def _():
+            ahead[...] = total
+
+        @pl.when(step == 2)
+        def _():
+            low[...] = total[:128]
+            high[...] = total[128:]
+
+        @pl.when(step == 3)
+        def _():
+            back[...] = total
+
+    def whole(rows):
+        return pl.BlockSpec((rows, columns), lambda i, at: (0, 0))
+
+    return on_grid(
+        kernel,
+        (place, core),
+        (4,),
+        [
+            pl.BlockSpec((depth, 256), lambda i, at: (0, 2 * lax.rem(at[0] + i, 4) + at[1])),
+            whole(depth),
+            pl.BlockSpec((1, 256, columns), lambda i, at: (lax.rem(at[0] + i, 4), 0, 0)),
+        ],
+        [whole(256), whole(256), whole(128), whole(128), whole(256)],
+        [jax.ShapeDtypeStruct((r, columns), BF) for r in (256, 256, 128, 128, 256)],
+        [],
+        tall,
+        terms,
+        landed,
+    )
+
+
+def gate_up_product(rows, pair):
+    def kernel(at, left, right, out):
+        out[...] = lax.dot_general(left[...], right[0], ROWS, preferred_element_type=F32).astype(BF)
+
+    depth, width = pair.shape[1:]
+    return on_grid(
+        kernel,
+        (jnp.int32(0),),
+        (2, 8),
+        [
+            pl.BlockSpec((depth, 256), lambda h, i, at: (0, i)),
+            pl.BlockSpec((1, depth, width), lambda h, i, at: (h, 0, 0)),
+        ],
+        pl.BlockSpec((256, width), lambda h, i, at: (i, h)),
+        jax.ShapeDtypeStruct((MODEL_WIDTH, 2 * width), BF),
+        [],
+        rows,
+        pair,
+    )
+
+
+def down_product(activated, grads, gate):
+    def kernel(at, left, right, scale, out):
+        scaled = (scale[...] * right[...].astype(F32)).astype(BF)
+        out[...] = lax.dot_general(left[...], scaled, ROWS, preferred_element_type=F32).astype(BF)
+
+    depth, width = activated.shape
+    return on_grid(
+        kernel,
+        (jnp.int32(0),),
+        (4,),
+        [
+            pl.BlockSpec((depth, width), lambda i, at: (0, 0)),
+            pl.BlockSpec((depth, 512), lambda i, at: (0, i)),
+            pl.BlockSpec((depth, 1), lambda i, at: (0, 0)),
+        ],
+        pl.BlockSpec((width, 512), lambda i, at: (0, i)),
+        jax.ShapeDtypeStruct((width, MODEL_WIDTH), BF),
+        [],
+        activated,
+        grads,
+        gate,
+    )
+
+
+def down_back(grads, down_w):
+    def kernel(at, left, right, out):
+        out[...] = lax.dot_general(left[...], right[...], LAST, preferred_element_type=F32)
+
+    depth, width = grads.shape[0], down_w.shape[0]
+    return on_grid(
+        kernel,
+        (jnp.int32(0),),
+        (width // 128,),
+        [
+            pl.BlockSpec((depth, MODEL_WIDTH), lambda i, at: (0, 0)),
+            pl.BlockSpec((128, MODEL_WIDTH), lambda i, at: (i, 0)),
+        ],
+        pl.BlockSpec((depth, 128), lambda i, at: (0, i)),
+        jax.ShapeDtypeStruct((depth, width), F32),
+        [],
+        grads,
+        down_w,
+    )
+
+
+def expert_quarters(activated, down_w, place, x):
+    def kernel(at, left, right, out):
+        out[0] = jnp.dot(left[...], right[...], preferred_element_type=F32).astype(BF)
+
+    depth, width = activated.shape
+    return on_grid(
+        kernel,
+        (place, x),
+        (4,),
+        [
+            pl.BlockSpec((depth, width), lambda i, at: (0, 0)),
+            pl.BlockSpec((width, 512), lambda i, at: (0, i)),
+        ],
+        pl.BlockSpec((1, depth, 512), lambda i, at: (lax.rem(at[0] + i + 4 - at[1], 4), 0, 0)),
+        jax.ShapeDtypeStruct((4, depth, 512), BF),
+        [],
+        activated,
+        down_w,
+    )
+
+
+def expert_middle(rows, marks, router, gate_up_w, grad_act, expert):
+    depth, width = grad_act.shape
+    blocks = width // 128
+
+    def kernel(
+        at, rows_ref, marks_ref, router_ref, gate_ref, up_ref, flat_ref, grad_ref,
+        act_out, pair_out, gate_out, back_out, pair_all, row_gate, row_grad,
+    ):
+        step = pl.program_id(0)
+        lane = lax.broadcasted_iota(jnp.int32, (depth, 128), 1)
+
+        @pl.when(step == 0)
+        def _():
+            logits = jnp.dot(rows_ref[...], router_ref[...], preferred_element_type=F32)
+            marks_f = marks_ref[...].astype(F32)
+            own = jnp.sum(jnp.where(lane == at[0], logits, 0.0), axis=1, keepdims=True)
+            other = jnp.sum(jnp.where(lane < 8, logits * marks_f, 0.0), axis=1, keepdims=True)
+            valid = jnp.sum(jnp.where(lane == 8, marks_f, 0.0), axis=1, keepdims=True)
+            top = jnp.maximum(own, other)
+            power = jnp.exp(own - top)
+            row_gate[...] = valid * power / (power + jnp.exp(other - top))
+            gate_out[...] = row_gate[...]
+            row_grad[...] = jnp.zeros_like(row_grad)
+
+        @pl.when(step < blocks)
+        def _():
+            both = jnp.concatenate([gate_ref[...], up_ref[...]], axis=1)
+            gate_up = jnp.dot(rows_ref[...], both, preferred_element_type=F32)
+            gate, up = gate_up[:, :128], gate_up[:, 128:]
+            sigmoid = 1.0 / (1.0 + jnp.exp(-gate))
+            silu = gate * sigmoid
+            act = (silu * up).astype(BF)
+            raw = grad_ref[...]
+            grad = row_gate[...] * raw
+            grad_gate = (grad * up * sigmoid * (1.0 + gate * (1.0 - sigmoid))).astype(BF)
+            grad_up = (grad * silu).astype(BF)
+            act_out[...] = act
+            pair_out[0] = grad_gate
+            pair_out[1] = grad_up
+            at_lane = pl.multiple_of(step * 128, 128)
+            pair_all[:, pl.ds(at_lane, 128)] = grad_gate
+            pair_all[:, pl.ds(at_lane + width, 128)] = grad_up
+            row_grad[...] += jnp.sum(act.astype(F32) * raw, axis=1, keepdims=True)
+
+        @pl.when(step >= blocks)
+        def _():
+            back_out[...] = lax.dot_general(
+                pair_all[...], flat_ref[...], LAST, preferred_element_type=F32
+            ).astype(BF)
+
+        @pl.when(step == blocks + 4)
+        def _():
+            high = row_grad[...].astype(BF).astype(F32)
+            low = row_grad[...] - high
+            wide = lax.broadcasted_iota(jnp.int32, (depth, 512), 1)
+            back_out[...] = jnp.where(wide == 0, high, jnp.where(wide == 1, low, 0.0)).astype(BF)
+
+    def first(i):
+        return jnp.minimum(i, blocks - 1)
+
+    def second(i):
+        return jnp.clip(i - blocks, 0, 3)
+
+    return on_grid(
+        kernel,
+        (expert,),
+        (blocks + 5,),
+        [
+            pl.BlockSpec((depth, MODEL_WIDTH), lambda i, at: (0, 0)),
+            pl.BlockSpec((depth, 128), lambda i, at: (0, 0)),
+            pl.BlockSpec((MODEL_WIDTH, 128), lambda i, at: (0, 0)),
+            pl.BlockSpec((MODEL_WIDTH, 128), lambda i, at: (0, first(i))),
+            pl.BlockSpec((MODEL_WIDTH, 128), lambda i, at: (0, blocks + first(i))),
+            pl.BlockSpec((512, 2 * width), lambda i, at: (second(i), 0)),
+            pl.BlockSpec((depth, 128), lambda i, at: (0, first(i))),
+        ],
+        [
+            pl.BlockSpec((depth, 128), lambda i, at: (0, first(i))),
+            pl.BlockSpec((2, depth, 128), lambda i, at: (0, 0, first(i))),
+            pl.BlockSpec((depth, 1), lambda i, at: (0, 0)),
+            pl.BlockSpec((depth, 512), lambda i, at: (0, jnp.clip(i - blocks, 0, 4))),
+        ],
+        [
+            jax.ShapeDtypeStruct((depth, width), BF),
+            jax.ShapeDtypeStruct((2, depth, width), BF),
+            jax.ShapeDtypeStruct((depth, 1), F32),
+            jax.ShapeDtypeStruct((depth, MODEL_WIDTH + 512), BF),
+        ],
+        [
+            pltpu.VMEM((depth, 2 * width), BF),
+            pltpu.VMEM((depth, 1), F32),
+            pltpu.VMEM((depth, 1), F32),
+        ],
+        rows,
+        marks,
+        router,
+        gate_up_w,
+        gate_up_w,
+        gate_up_w,
+        grad_act,
+        cost=pl.CostEstimate(
+            flops=8 * depth * MODEL_WIDTH * width, bytes_accessed=1 << 24, transcendentals=1 << 20
+        ),
+    )
+
+
 def pick_of(routes):
     return (routes[:, :, None] == jnp.arange(EXPERTS, dtype=jnp.int32)[None, None, :]).astype(F32)
 
@@ -342,21 +609,6 @@
     all_w = lax.all_gather(
         after(mine, (down_before, down_after)), ("dp", "core"), axis=0, tiled=True
     )
-    all_w, down_before, down_after, _ = lax.optimization_barrier(
-        (all_w, down_before, down_after, arrived)
-    )
-    in_w, out_w = all_w[:, :1408], all_w[:, 1408:]
-    low_rows = down_own.shape[0] // 2
-    far_low = lax.ppermute(down_before[:low_rows], "dp", UP)
-    far_high = lax.ppermute(down_after[low_rows:], "dp", DOWN)
-    gate_up_own = gate_up_weight.reshape(4, 2, 64, 2816).transpose(1, 0, 2, 3).reshape(512, 2816)
-    gate_up_w = lax.all_gather(after(gate_up_own, all_w), "dp", axis=0, tiled=True)
-    router_m = in_w[:, 1288:1296]
-
-    down_w = jnp.concatenate(
-        [down_own, down_after, jnp.concatenate([far_low, far_high], axis=0), down_before], axis=1
-    )
-
     def turned(columns, blocks):
         twice = jnp.concatenate([columns, columns], axis=1)
         return lax.dynamic_slice_in_dim(twice, blocks * 512, MODEL_WIDTH, axis=1)
@@ -395,7 +647,22 @@
         ROWS,
         preferred_element_type=F32,
     ).astype(BF)
-    grad_landed = to_experts(after(grad_sent, arrived))
+    all_w, down_before, down_after, xn1, grad_sent = lax.optimization_barrier(
+        (all_w, down_before, down_after, xn1, grad_sent)
+    )
+    in_w, out_w = all_w[:, :1408], all_w[:, 1408:]
+    low_rows = down_own.shape[0] // 2
+    far_low = lax.ppermute(down_before[:low_rows], "dp", UP)
+    far_high = lax.ppermute(down_after[low_rows:], "dp", DOWN)
+    gate_up_own = gate_up_weight.reshape(4, 2, 64, 2816).transpose(1, 0, 2, 3).reshape(512, 2816)
+    gate_up_w = lax.all_gather(after(gate_up_own, all_w), "dp", axis=0, tiled=True)
+    router_m = in_w[:, 1288:1296]
+
+    down_w = jnp.concatenate(
+        [down_own, down_after, jnp.concatenate([far_low, far_high], axis=0), down_before], axis=1
+    )
+
+    grad_landed = to_experts(grad_sent)
 
     def places(half):
         blocks = 2 * jnp.arange(4, dtype=jnp.int32)[:, None] + half
@@ -444,15 +711,13 @@
     branch_part = lax.dot_general(mixed, out_w, LAST, preferred_element_type=F32).astype(BF)
     branch_part = after(branch_part, grad_landed)
     grad_received = grad_landed[:, :MODEL_WIDTH]
-    grad_act_raw = lax.dot_general(
-        turned(grad_received, z), down_w, LAST, preferred_element_type=F32
-    )
+    grad_turned = turned(grad_received, z)
     branch = exchange(branch_part.reshape(16, quarter, MODEL_WIDTH), plane).astype(F32).sum(axis=0)
 
     first = x * quarter
     own_values = core_first(lax.dynamic_slice_in_dim(tokens, first, quarter)).astype(F32)
     own_factor = rms_scale(own_values)
-    hidden = after(own_values, grad_act_raw) + branch
+    hidden = after(own_values, (down_w, grad_turned)) + branch
     factor_m = rms_scale(hidden)
     xn2_own = (hidden * factor_m * gain_m).astype(BF)
     xn2 = spread(xn2_own, "tensor", 4).reshape(count, MODEL_WIDTH)
@@ -462,52 +727,26 @@
     received = to_experts(
         lax.dot_general(any_row, xn2, ROWS, preferred_element_type=F32).astype(BF)
     )
-    other_pick = grad_landed[:, MODEL_WIDTH : MODEL_WIDTH + EXPERTS].astype(F32)
-    valid = grad_landed[:, MODEL_WIDTH + EXPERTS : MODEL_WIDTH + EXPERTS + 1].astype(F32)
-    row_logits = jnp.dot(received, router_m, preferred_element_type=F32)
-    here = (jnp.arange(EXPERTS, dtype=jnp.int32) == 2 * y + core).astype(F32)
-    own_logit = jnp.sum(row_logits * here[None], axis=1, keepdims=True)
-    other_logit = jnp.sum(row_logits * other_pick, axis=1, keepdims=True)
-    top = jnp.maximum(own_logit, other_logit)
-    own_weight = jnp.exp(own_logit - top)
-    row_gate = valid * own_weight / (own_weight + jnp.exp(other_logit - top))
-
-    width = down_weight.shape[1]
-    grad_expert = (row_gate * grad_received.astype(F32)).astype(BF)
-    gate_up = jnp.dot(received, gate_up_w, preferred_element_type=F32)
-    gate_part, up_part = gate_up[:, :width], gate_up[:, width:]
-    sigmoid_gate = jax.nn.sigmoid(gate_part)
-    silu_gate = gate_part * sigmoid_gate
-    activated = (silu_gate * up_part).astype(BF)
-    grad_act = row_gate * grad_act_raw
-    grad_gate_up = jnp.concatenate(
-        [
-            grad_act * up_part * sigmoid_gate * (1.0 + gate_part * (1.0 - sigmoid_gate)),
-            grad_act * silu_gate,
-        ],
-        axis=1,
-    ).astype(BF)
-    row_gate_grad = jnp.sum(activated.astype(F32) * grad_act_raw, axis=1, keepdims=True)
-    grad_rows = lax.dot_general(grad_gate_up, gate_up_w, LAST, preferred_element_type=F32).astype(BF)
-    grad_back = jnp.concatenate([grad_rows, widen(in_two(row_gate_grad))], axis=1)
-    grad_back, late_grad, late_act = lax.optimization_barrier((grad_back, grad_gate_up, activated))
-    grad_returned = to_experts(grad_back)
-    grad_gate_up_w = lax.dot_general(
-        received, late_grad, ROWS, preferred_element_type=F32
-    ).astype(BF)
+    grad_act_raw = down_back(grad_turned, down_w)
+    received, grad_act_raw = lax.optimization_barrier((received, grad_act_raw))
+    activated, grad_pair, row_gate, grad_back = expert_middle(
+        received,
+        grad_landed[:, MODEL_WIDTH:],
+        jnp.pad(router_m, ((0, 0), (0, 120))),
+        gate_up_w,
+        grad_act_raw,
+        2 * y + core,
+    )
+    grad_back, late_pair, late_act = lax.optimization_barrier((grad_back, grad_pair, activated))
+    grad_returned = to_experts(grad_back[:, : MODEL_WIDTH + HEAD_SIZE])
+    grad_gate_up_w = gate_up_product(received, late_pair)
     gate_up_sum = lax.psum_scatter(grad_gate_up_w, "dp", scatter_dimension=0, tiled=True)
-    gate_up_grad = (
-        gate_up_sum.reshape(2, 4, 64, 2816)
-        .transpose(1, 0, 2, 3)
-        .reshape(1, 512, 2, width)
-        .astype(F32)
-    )
-    expert_part = turned(
-        jnp.dot(late_act, down_w, preferred_element_type=F32).astype(BF), lax.rem(4 - z, 4)
-    )
-    late_any = after(any_row, (grad_gate_up_w, expert_part))
-    expert_out = sum_direct(
-        jnp.stack([expert_part[:, 512 * i : 512 * (i + 1)] for i in range(4)]), "tensor"
+    width = down_own.shape[0]
+    quarters = expert_quarters(late_act, down_w, z, x)
+    late_any = after(any_row, (grad_gate_up_w, quarters))
+    expert_out = (
+        quarters[0].astype(F32)
+        + sum(from_ahead(quarters[4 - k], "tensor", k).astype(F32) for k in (1, 2, 3))
     ).astype(BF)
 
     grad_xn2_part = jnp.dot(
@@ -543,9 +782,7 @@
 
     fetched = jnp.einsum("jtr,rd->jtd", to_row, returned, preferred_element_type=F32)
     moe_part = jnp.sum(weight_m.T[:, :, None] * fetched, axis=0).astype(BF)
-    grad_down_w = lax.dot_general(
-        after(late_act, returned), grad_expert, ROWS, preferred_element_type=F32
-    ).astype(BF)
+    grad_down_w = down_product(after(late_act, returned), grad_received, row_gate)
     down_sum = lax.psum_scatter(grad_down_w, "dp", scatter_dimension=1, tiled=True)
     grad_branch, moe_part, _ = lax.optimization_barrier((grad_branch, moe_part, grad_down_w))
     moe_pieces = exchange(moe_part.reshape(4, quarter, MODEL_WIDTH // 4), "tensor")
@@ -570,11 +807,10 @@
         gate_a,
         *shared,
     )
-    out_terms = lax.dot_general(grad_branch, mixed, ROWS, preferred_element_type=F32).astype(BF)
-    kv_back, out_terms, moe_pieces = lax.optimization_barrier(
-        (lax.ppermute(grad_kv_give, "core", SWAP), out_terms, moe_pieces)
-    )
-    out_parts = core_sum(out_terms, core)
+    out_give = lax.ppermute(give_terms(grad_branch, mixed, z, core), "core", SWAP)
+    kv_back, moe_pieces = lax.optimization_barrier(
+        (lax.ppermute(grad_kv_give, "core", SWAP), moe_pieces)
+    )
     moe = moe_pieces.transpose(1, 0, 2).reshape(quarter, MODEL_WIDTH).astype(F32)
     output_own = (core_last(hidden) + moe).astype(BF)
     own_grad_kv = grad_kv_own + kv_back.astype(F32)
@@ -584,21 +820,23 @@
     ).astype(BF)
     grad_in = jnp.concatenate([grad_q_all, grad_kv, grad_logit_a], axis=1)
     grad_xn1_part = lax.dot_general(grad_in, in_w, LAST, preferred_element_type=F32).astype(BF)
-    out_right, out_left = ring_first(out_parts, "dp")
     gain_row = jnp.pad(gain_m_part[None].astype(BF), ((0, 7), (0, 0)))
     tall = jnp.concatenate([xn1, xn2_own, gain_row], axis=0)
     router_cols = jnp.pad(grad_logit_m.astype(BF), ((0, 0), (1288, 112)))
     gain_cols = (
         (jnp.arange(8)[:, None] == 0) & (jnp.arange(1408)[None, :] == 1296)
     ).astype(BF)
-    grad_tall = jnp.concatenate([after(grad_in, (grad_xn1_part, out_parts, gate_up_sum)), router_cols, gain_cols], axis=0)
-    in_parts = core_sum(
-        lax.dot_general(tall, grad_tall, ROWS, preferred_element_type=F32).astype(BF), core
-    )
-    in_right, in_left = ring_first(in_parts, "dp")
-    out_sum = ring_second(after(out_parts, gate_up_grad), out_right, out_left, "dp").astype(BF)
+    grad_tall = jnp.concatenate([grad_in, router_cols, gain_cols], axis=0)
+    in_give = lax.ppermute(give_terms(tall, grad_tall, z, core), "core", SWAP)
+    out_own, *out_rest = keep_terms(grad_branch, mixed, out_give, z, core)
+    out_ahead, out_back = ring_first(*out_rest, "dp")
+    in_own_rows, *in_rest = keep_terms(
+        tall, grad_tall, after(in_give, out_own), z, core
+    )
+    in_ahead, in_back = ring_first(*in_rest, "dp")
+    out_sum = ring_second(out_own, out_ahead, out_back, "dp").astype(BF)
+    in_sum = ring_second(in_own_rows, in_ahead, in_back, "dp").astype(BF)
     landed_raw = exchange(grad_xn1_part.reshape(16, quarter, MODEL_WIDTH), plane)
-    in_sum = ring_second(in_parts, in_right, in_left, "dp").astype(BF)
     landed_raw, in_sum, out_sum = lax.optimization_barrier((landed_raw, in_sum, out_sum))
     landed_a = landed_raw.astype(F32).sum(axis=0)
     grad_x_norm, _ = norm_back(landed_a, own_values, own_factor, gain_a)
@@ -617,11 +855,18 @@
     ends = jnp.concatenate(
         [output_own, core_last((grad_hidden + grad_x_norm).astype(BF))], axis=1
     )
-    ends, down_sum = lax.optimization_barrier((ends, down_sum))
+    ends, gate_up_sum, small_raw = lax.optimization_barrier(
+        (ends, gate_up_sum, exchange(small_sent, plane))
+    )
+    gate_up_grad = (
+        gate_up_sum.reshape(2, 4, 64, 2816)
+        .transpose(1, 0, 2, 3)
+        .reshape(1, 512, 2, width)
+        .astype(F32)
+    )
+    small_sum = small_raw.astype(F32).sum(axis=0)
+    both_ends, down_sum = lax.optimization_barrier((spread(ends, "tensor", 4), down_sum))
     down_grad = down_sum.astype(F32)[None]
-    both_ends = spread(ends, "tensor", 4)
-    both_ends, small_sent = lax.optimization_barrier((both_ends, small_sent))
-    small_sum = exchange(small_sent, plane).astype(F32).sum(axis=0)
     both_ends = both_ends.reshape(count, 2 * MODEL_WIDTH)
     output, input_grad = both_ends[:, :MODEL_WIDTH], both_ends[:, MODEL_WIDTH:]
     both_sums = jnp.concatenate([in_sum[:, :1280], out_sum], axis=1).reshape(4, 64, 2304)

time: 623 us -> 640 us (1.027)
  Pallas kernels: 16 us -> 96.4 us
  matrix products: 112 us -> 40.7 us
  starting transfers between devices: 90.7 us -> 99.2 us
    pallas_call x0 -> x9, Pallas kernels: none -> 80.1 us  [on_grid(): pl.pallas_call(kernel, out_shape=outs, grid_spec=pltpu.PrefetchScalarGrid...]
    dot_general x9 -> x0, matrix products: 67.6 us -> none  [the longest x1 11.1 us: body(): lax.dot_general(received, late_grad, ROWS, preferred_element_type=F32)]
    ppermute x10, waiting for transfers between devices: 25.3 us -> 59.9 us  [the longest x2 25.3 us: ring_first(): high = lax.ppermute(high, axis, DOWN)]
    all_to_all x13, waiting for transfers between devices: 113 us -> 83.3 us  [exchange(): return lax.all_to_all(blocks, axis, split_axis=0, concat_axis=0, tiled=True)]
    ppermute x1, starting transfers between devices: 1.16 us -> 12.4 us  [body(): far_low = lax.ppermute(down_before[:low_rows], 'dp', UP)]
    convert_element_type x9 -> x7, other arithmetic: 14.9 us -> 3.93 us  [the longest x1 2.3 us: body(): expert_out = (quarters[0].astype(F32) + sum((from_ahead(quarters[4 - k],...]
    unnamed x128 -> x202, local copies, waits for them, and re-layouts: 17.6 us -> 27.8 us
    ppermute x1, waiting for transfers between devices: 4 us -> 14.2 us  [body(): far_low = lax.ppermute(down_before[:low_rows], 'dp', UP)]
  transfers between devices with their start and end apart: 39 -> 39, of which waited for: 21 -> 22; matrix products, arithmetic and copies ran while one was open for 36% -> 27% of each run, Pallas kernels for 3% -> 9%
where the time goes in v5:
time: 640 us; the launch traced here: 634 us
  waiting for transfers between devices  206 us (32%)
  local copies, waits for them, and re-layouts  99.8 us (16%)
  starting transfers between devices  99.2 us (16%)
  Pallas kernels  96.4 us (15%)
  other arithmetic  54.7 us (9%)
  matrix products  40.7 us (6%)
  blocking collectives  21.4 us (3%)
  between operations  15.7 us (2%)
    all_to_all x13, waiting for transfers between devices, exchange(): return lax.all_to_all(blocks, axis, split_axis=0, concat_axis=0, tiled=True)  83.3 us
    pallas_call x9, Pallas kernels, on_grid(): pl.pallas_call(kernel, out_shape=outs, grid_spec=pltpu.PrefetchScalarGrid...  80.1 us
    all_to_all x13, starting transfers between devices, exchange(): return lax.all_to_all(blocks, axis, split_axis=0, concat_axis=0, tiled=True)  63.7 us
    unnamed x202, local copies, waits for them, and re-layouts  27.8 us
    ppermute x2, waiting for transfers between devices, ring_first(): high = lax.ppermute(high, axis, DOWN)  25.3 us
    all_to_all x1, blocking collectives, exchange(): return lax.all_to_all(blocks, axis, split_axis=0, concat_axis=0, tiled=True)  21.4 us
    ppermute x2, waiting for transfers between devices, ring_first(): low = lax.ppermute(low, axis, UP)  18.6 us
    ppermute x6, waiting for transfers between devices, from_ahead(): return lax.ppermute(block, axis, [(i, (i - steps) % 4) for i in range(4)])  17 us
  transfers between devices with their start and end apart: 39, of which 22 were waited for; matrix products, arithmetic and copies ran while one was open for 27% of the time, Pallas kernels for 9%

profile of v5, /device:TPU:0, one launch (start us, length us, event | category | flops | bytes accessed | tf_op | source)
XLA Modules:
  0.0 634.2 jit_solution(568654964202009785)
XLA Ops:
  16.8 21.4 %all_to_all.70 = bf16[4,64,2432]{2,1,0:T(8,128)(2,1)} all-to-all(bf16[4,64,2432]{2,1,0:T(8,128)(2,1)S(1)} %pad_maximum_fusion.1), channel_id=1, replica_groups=mesh['dp'=4,'y'=4,'core'=2,'tensor'=4] {'y'}, dimensions={0} | all-to-all | bytes 2490368 | tf_op jit(solution)/shard_map/all_to_all | solution.py:24
  38.3 5.0 collective-permute-done
  47.0 4.6 all-to-all-start.1
  53.3 7.6 %reshape.381 = bf16[4,2,64,2816]{3,2,1,0:T(8,128)(2,1)} reshape(bf16[1,512,2,1408]{3,2,1,0:T(2,128)(2,1)} %param.24) | data formatting | bytes 5767168 | tf_op jit(solution)/shard_map/reshape | solution.py:657
  68.0 16.7 %all-to-all-done.1 = bf16[4,160,2176]{2,1,0:T(8,128)(2,1)S(1)} async-done(((bf16[4,160,2176]{2,1,0:T(8,128)(2,1)}), bf16[4,160,2176]{2,1,0:T(8,128)(2,1)S(1)}, u32[]{:S(2)}, u32[]{:S(2)}) %all-to-all-start.1) | async-done | bytes 2785312 | tf_op jit(solution)/shard_map/all_to_all | solution.py:24
  87.5 13.9 %all-gather.3.cloned.1.call-done = bf16[2048,2432]{1,0:T(8,128)(2,1)} async-done(((bf16[256,2432]{1,0:T(8,128)(2,1)}), bf16[2048,2432]{1,0:T(8,128)(2,1)}) %all-gather.3.cloned.1.call-update) | async-done | bytes 9961488 | tf_op jit(solution)/shard_map/all_gather | solution.py:609
  105.8 4.6 all-to-all-start.2
  110.4 7.0 %fusion.6.proj = f32[640,1408]{1,0:T(8,128)S(1)} fusion(bf16[640,2048]{1,0:T(8,128)(2,1)S(1)} %copy-done.45, bf16[2048,2432]{1,0:T(8,128)(2,1)} %all-gather.3.cloned.1.call-done), kind=kOutput, calls=%fused_computation.15 | convolution fusion | flops 3690987520 | bytes 11993088 | tf_op jit(solution)/shard_map/dot_general | solution.py:688
  120.0 7.0 %shard_map.230 = (bf16[4,320,128]{2,1,0:T(8,128)(2,1)S(1)}, f32[4,320,128]{2,1,0:T(8,128)S(1)}, f32[4,320,1]{2,1,0:T(8,128)S(1)}, f32[640,2]{1,0:T(8,128)S(1)}, bf16[640,1024]{1,0:T(8,128)(2,1)S(1)}) custom-call(f32[640,1408]{1,0:T(8,128)S(1)} %fusion.6.proj, bf16[640,256]{1,0:T(8,128)(2,1)S(1)} %pad_maximum_fusion.9.own, ...), custom_call_target="tpu_custom_call" | custom-call | flops 1610612736 | bytes 4935680 | tf_op jit(solution)/shard_map/pallas_call | solution.py:238
  130.2 6.5 %fusion.17 = bf16[640,2048]{1,0:T(8,128)(2,1)} fusion(bf16[640,1024]{1,0:T(8,128)(2,1)S(1)} %get-tuple-element.76.right, bf16[2048,2432]{1,0:T(8,128)(2,1)} %all-gather.3.cloned.1.call-done), kind=kOutput, calls=%fused_computation.27 | convolution fusion | flops 2685665280 | bytes 8126464 | tf_op jit(solution)/shard_map/dot_general | solution.py:711
  137.8 7.2 %all-to-all-start.3 = ((bf16[16,40,2048]{2,1,0:T(8,128)(2,1)}), bf16[16,40,2048]{2,1,0:T(8,128)(2,1)S(1)}, u32[]{:S(2)}, u32[]{:S(2)}) async-start(bf16[16,40,2048]{2,1,0:T(8,128)(2,1)} %bitcast.168), calls=%async_computation.3 | async-start | bytes 5242880 | tf_op jit(solution)/shard_map/all_to_all | solution.py:24
  149.3 12.4 %collective-permute-start.2 = (bf16[704,512]{1,0:T(8,128)(2,1)}, bf16[704,512]{1,0:T(8,128)(2,1)}, u32[]{:S(2)}, u32[]{:S(2)}) collective-permute-start(bf16[704,512]{1,0:T(8,128)(2,1)} %slice.171), channel_id=1, source_target_pairs={{0,32},{32,64},{64,96},{96,0},{1,33},{33,65},{65,97},{97,1},{2,34}... | collective-permute-start | bytes 2162696 | tf_op jit(solution)/shard_map/ppermute | solution.py:655
  168.7 12.6 %collective-permute-done.3 = bf16[704,512]{1,0:T(8,128)(2,1)} collective-permute-done((bf16[704,512]{1,0:T(8,128)(2,1)}, bf16[704,512]{1,0:T(8,128)(2,1)}, u32[]{:S(2)}, u32[]{:S(2)}) %collective-permute-start.3) | collective-permute-done | bytes 720928 | tf_op jit(solution)/shard_map/ppermute | solution.py:656
  181.4 14.2 %collective-permute-done.2 = bf16[704,512]{1,0:T(8,128)(2,1)} collective-permute-done((bf16[704,512]{1,0:T(8,128)(2,1)}, bf16[704,512]{1,0:T(8,128)(2,1)}, u32[]{:S(2)}, u32[]{:S(2)}) %collective-permute-start.2) | collective-permute-done | bytes 720928 | tf_op jit(solution)/shard_map/ppermute | solution.py:655
  195.6 7.5 %pad_maximum_fusion.right = bf16[1408,2048]{1,0:T(8,128)(2,1)} fusion(bf16[1408,512]{1,0:T(8,128)(2,1)} %copy-done.53, bf16[704,512]{1,0:T(8,128)(2,1)} %collective-permute-done.3, bf16[704,512]{1,0:T(8,128)(2,1)} %collective-permute-done.2, bf16[1408,512]{1,0:T(8,128)(2,1)} %collective-permute-done.1, bf16[1408,512]{1,0:T(8,128)(2,1)} %bitcast.177), kind=kLoop, calls=%fused_computation.4 | loop fusion | flops 28835840 | bytes 11534336 | tf_op jit(solution)/shard_map/concatenate | solution.py:661
  211.4 4.6 all-to-all-start.4
  216.1 9.3 %all-to-all-done.4 = bf16[4,40,2048]{2,1,0:T(8,128)(2,1)S(1)} async-done(((bf16[4,40,2048]{2,1,0:T(8,128)(2,1)}), bf16[4,40,2048]{2,1,0:T(8,128)(2,1)S(1)}, u32[]{:S(2)}, u32[]{:S(2)}) %all-to-all-start.4) | async-done | bytes 655392 | tf_op jit(solution)/shard_map/all_to_all | solution.py:24
  227.4 4.3 all-to-all-start.5
  234.9 10.4 %shard_map.231.grad_ref = f32[448,1408]{1,0:T(8,128)S(1)} custom-call(s32[1]{0:T(128)} %constant.116.clone.1.at, bf16[448,2048]{1,0:T(8,128)(2,1)S(1)} %copy-done.10, bf16[1408,2048]{1,0:T(8,128)(2,1)} %pad_maximum_fusion.right), custom_call_target="tpu_custom_call" | custom-call | tf_op jit(solution)/shard_map/pallas_call | solution.py:253
  246.7 9.3 %all-to-all-done.5 = bf16[8,56,2048]{2,1,0:T(8,128)(2,1)S(1)} async-done(((bf16[8,56,2048]{2,1,0:T(8,128)(2,1)}), bf16[8,56,2048]{2,1,0:T(8,128)(2,1)S(1)}, u32[]{:S(2)}, u32[]{:S(2)}) %all-to-all-start.5) | async-done | bytes 1835040 | tf_op jit(solution)/shard_map/all_to_all | solution.py:24
  257.1 24.6 %shard_map.232 = (bf16[448,1408]{1,0:T(8,128)(2,1)S(1)}, bf16[2,448,1408]{2,1,0:T(8,128)(2,1)}, f32[448,1]{1,0:T(8,128)S(1)}, bf16[448,2560]{1,0:T(8,128)(2,1)}) custom-call(s32[1]{0:T(128)} %bitcast.30.at, bf16[448,2048]{1,0:T(8,128)(2,1)S(1)} %bitcast.147, bf16[448,128]{1,0:T(8,128)(2,1)S(1)} %slice.231.marks_ref, bf16[2048,128]{1,0:T(8,128)(2,1)S(1)} %copy-done.17, ...), custom_call_target="tpu_custom_call" | custom-call | flops 10334765056 | bytes 16777216 | tf_op jit(solution)/shard_map/pallas_call | solution.py:253
  284.5 13.1 %shard_map.233 = bf16[2048,2816]{1,0:T(8,128)(2,1)} custom-call(s32[1]{0:T(128)} %constant.116.clone.1.at, bf16[448,2048]{1,0:T(8,128)(2,1)S(1)} %bitcast.148, bf16[2,448,1408]{2,1,0:T(8,128)(2,1)S(1)} %copy-done.16), custom_call_target="tpu_custom_call" | custom-call | tf_op jit(solution)/shard_map/pallas_call | solution.py:253
  300.6 4.5 all-to-all-start.6
  310.9 6.0 shard_map.234
  321.5 9.3 %all-to-all-done.6 = bf16[8,56,2176]{2,1,0:T(8,128)(2,1)} async-done(((bf16[8,56,2176]{2,1,0:T(8,128)(2,1)}), bf16[8,56,2176]{2,1,0:T(8,128)(2,1)}, u32[]{:S(2)}, u32[]{:S(2)}) %all-to-all-start.6) | async-done | bytes 1949728 | tf_op jit(solution)/shard_map/all_to_all | solution.py:24
  346.1 4.0 all-to-all-done.7
  350.5 4.1 all-to-all-start.8
  358.9 5.3 all-to-all-done.8
  366.0 5.8 all-to-all-start.9
  374.9 5.5 shard_map.235
  382.5 28.4 %all-to-all-done.9 = bf16[16,40,2048]{2,1,0:T(8,128)(2,1)S(1)} async-done(((bf16[16,40,2048]{2,1,0:T(8,128)(2,1)}), bf16[16,40,2048]{2,1,0:T(8,128)(2,1)S(1)}, u32[]{:S(2)}, u32[]{:S(2)}) %all-to-all-start.9) | async-done | bytes 2621472 | tf_op jit(solution)/shard_map/all_to_all | solution.py:24
  411.0 5.6 fusion.10.grad_mixed
  416.7 9.2 %shard_map.236 = (bf16[640,1024]{1,0:T(8,128)(2,1)S(1)}, bf16[640,128]{1,0:T(8,128)(2,1)S(1)}, f32[640,256]{1,0:T(8,128)S(1)}, bf16[640,256]{1,0:T(8,128)(2,1)}) custom-call(f32[640,1024]{1,0:T(8,128)S(1)} %fusion.10.grad_mixed, bf16[4,320,128]{2,1,0:T(8,128)(2,1)S(1)} %copy-done.41, bf16[640,256]{1,0:T(8,128)(2,1)S(1)} %copy-done.25, ...), custom_call_target="tpu_custom_call" | custom-call | flops 3221225472 | bytes 4945920 | tf_op jit(solution)/shard_map/pallas_call | solution.py:238
  435.0 4.2 shard_map.238
  446.7 4.9 shard_map.237
  455.2 5.6 shard_map.239
  461.3 8.5 %fusion.14 = bf16[640,2048]{1,0:T(8,128)(2,1)} fusion(bf16[2048,2432]{1,0:T(8,128)(2,1)} %all-gather.3.cloned.1.call-done, bf16[640,128]{1,0:T(8,128)(2,1)S(1)} %copy-done.33, bf16[640,128]{1,0:T(8,128)(2,1)S(1)} %copy-done.69, bf16[640,128]{1,0:T(8,128)(2,1)S(1)} %copy-done.67, bf16[640,1024]{1,0:T(8,128)(2,1)S(1)} %copy-done.22), kind=kOutput, calls=%fused_computation.26 | convolution fusion | flops 3699507200 | bytes 10190848 | tf_op jit(solution)/shard_map/dot_general | solution.py:822
  469.8 6.5 %all-to-all-start.11 = ((bf16[16,40,2048]{2,1,0:T(8,128)(2,1)}), bf16[16,40,2048]{2,1,0:T(8,128)(2,1)}, u32[]{:S(2)}, u32[]{:S(2)}) async-start(bf16[16,40,2048]{2,1,0:T(8,128)(2,1)} %bitcast.167), calls=%async_computation.11 | async-start | bytes 5242880 | tf_op jit(solution)/shard_map/all_to_all | solution.py:24
  479.9 5.8 shard_map.240
  485.8 6.3 collective-permute-done.15
  493.9 25.3 %collective-permute-done.13 = bf16[128,1408]{1,0:T(8,128)(2,1)S(1)} collective-permute-done((bf16[128,1408]{1,0:T(8,128)(2,1)S(1)}, bf16[128,1408]{1,0:T(8,128)(2,1)S(1)}, u32[]{:S(2)}, u32[]{:S(2)}) %collective-permute-start.13) | collective-permute-done | bytes 360480 | tf_op jit(solution)/shard_map/ppermute | solution.py:70
  522.3 12.3 %collective-permute-done.11 = bf16[128,1408]{1,0:T(8,128)(2,1)S(1)} collective-permute-done((bf16[128,1408]{1,0:T(8,128)(2,1)S(1)}, bf16[128,1408]{1,0:T(8,128)(2,1)S(1)}, u32[]{:S(2)}, u32[]{:S(2)}) %collective-permute-start.11) | collective-permute-done | bytes 360480 | tf_op jit(solution)/shard_map/ppermute | solution.py:69
  536.8 12.2 %collective-permute-done.14 = bf16[256,1408]{1,0:T(8,128)(2,1)S(1)} collective-permute-done((bf16[256,1408]{1,0:T(8,128)(2,1)S(1)}, bf16[256,1408]{1,0:T(8,128)(2,1)S(1)}, u32[]{:S(2)}, u32[]{:S(2)}) %collective-permute-start.14) | collective-permute-done | bytes 720928 | tf_op jit(solution)/shard_map/ppermute | solution.py:81
  549.0 3.7 collective-permute-done.12
  562.5 6.6 %all-to-all-start.12 = ((bf16[16,64,128]{2,1,0:T(8,128)(2,1)}), bf16[16,64,128]{2,1,0:T(8,128)(2,1)}, u32[]{:S(2)}, u32[]{:S(2)}) async-start(bf16[16,64,128]{2,1,0:T(8,128)(2,1)} %bitcast.57), calls=%async_computation.13 | async-start | bytes 524288 | tf_op jit(solution)/shard_map/all_to_all | solution.py:24
  574.3 9.9 %collective-permute-done.19 = bf16[64,2304]{1,0:T(8,128)(2,1)S(1)} collective-permute-done((bf16[64,2304]{1,0:T(8,128)(2,1)S(1)}, bf16[64,2304]{1,0:T(8,128)(2,1)S(1)}, u32[]{:S(2)}, u32[]{:S(2)}) %collective-permute-start.19) | collective-permute-done | bytes 294944 | tf_op jit(solution)/shard_map/ppermute | solution.py:32
  602.5 4.1 all-to-all-start.13
  614.3 7.8 %reshape.402 = f32[1,512,2,1408]{3,2,1,0:T(2,128)} reshape(f32[4,2,64,2816]{3,2,1,0:T(8,128)} %copy.280) | data formatting | bytes 11534336 | tf_op jit(solution)/shard_map/convert_element_type | solution.py:865
  (436 shorter events, 183.1 us)
Async XLA Ops:
  7.2 94.2 %all-gather.3.cloned.1.call-start = ((), (), s32[]{:S(2)}) async-start(), calls=%async_computation.16 | async-start | bytes 11206656 | tf_op jit(solution)/shard_map/all_gather | solution.py:609
  7.2 36.0 %collective-permute-start = (bf16[1408,512]{1,0:T(8,128)(2,1)}, bf16[1408,512]{1,0:T(8,128)(2,1)S(1)}, u32[]{:S(2)}, u32[]{:S(2)}) collective-permute-start(bf16[1408,512]{1,0:T(8,128)(2,1)} %bitcast.175), channel_id=1, source_target_pairs={{0,32},{32,64},{64,96},{96,0},{1,33},{33,65},{65,97},{97,1},{2,34}... | collective-permute-start | bytes 4325384 | tf_op jit(solution)/shard_map/ppermute | solution.py:594
  9.3 33.9 %collective-permute-start.1 = (bf16[1408,512]{1,0:T(8,128)(2,1)}, bf16[1408,512]{1,0:T(8,128)(2,1)}, u32[]{:S(2)}, u32[]{:S(2)}) collective-permute-start(bf16[1408,512]{1,0:T(8,128)(2,1)} %bitcast.176), channel_id=1, source_target_pairs={{0,96},{32,0},{64,32},{96,64},{1,97},{33,1},{65,33},{97,65},{2,98}... | collective-permute-start | bytes 4325384 | tf_op jit(solution)/shard_map/ppermute | solution.py:595
  16.8 26.4 %copy-start.94 = (s32[160,2]{0,1:T(2,128)S(1)}, s32[160,2]{0,1:T(2,128)}, u32[]{:S(2)}) copy-start(s32[160,2]{0,1:T(2,128)} %param.26) | copy-start | bytes 3844
  16.8 26.5 %copy-start.63 = (bf16[160,2048]{1,0:T(8,128)(2,1)S(1)}, bf16[160,2048]{1,0:T(8,128)(2,1)}, u32[]{:S(2)}) copy-start(bf16[160,2048]{1,0:T(8,128)(2,1)} %param.15) | copy-start | bytes 1966084
  47.0 37.7 %all-to-all-start.1 = ((bf16[4,160,2176]{2,1,0:T(8,128)(2,1)}), bf16[4,160,2176]{2,1,0:T(8,128)(2,1)S(1)}, u32[]{:S(2)}, u32[]{:S(2)}) async-start(bf16[4,160,2176]{2,1,0:T(8,128)(2,1)} %broadcast_in_dim.48), calls=%async_computation.1 | async-start | bytes 5570560 | tf_op jit(solution)/shard_map/all_to_all | solution.py:24
  51.6 204.4 %all-gather.5.cloned.1.call-start = ((), (), s32[]{:S(2)}) async-start(), calls=%async_computation.17 | async-start | bytes 14417920 | tf_op jit(solution)/shard_map/all_gather | solution.py:658
  51.8 33.6 %copy-start.82 = (f32[2048]{0:T(1024)}, f32[2048]{0:T(1024)S(1)}, u32[]{:S(2)}) copy-start(f32[2048]{0:T(1024)S(1)} %mul.289) | copy-start | bytes 24580
  53.2 162.7 %copy-start.86 = (s32[2,160]{1,0:T(2,128)}, s32[2,160]{1,0:T(2,128)S(1)}, u32[]{:S(2)}) copy-start(s32[2,160]{1,0:T(2,128)S(1)} %copy.256) | copy-start | bytes 3844
  105.8 32.0 %all-to-all-start.2 = ((bf16[8,56,2176]{2,1,0:T(8,128)(2,1)}), bf16[8,56,2176]{2,1,0:T(8,128)(2,1)}, u32[]{:S(2)}, u32[]{:S(2)}) async-start(bf16[8,56,2176]{2,1,0:T(8,128)(2,1)} %bitcast.173), calls=%async_computation.2 | async-start | bytes 3899392 | tf_op jit(solution)/shard_map/all_to_all | solution.py:24
  118.0 2.0 collective-permute-start.4
  137.8 70.5 %all-to-all-start.3 = ((bf16[16,40,2048]{2,1,0:T(8,128)(2,1)}), bf16[16,40,2048]{2,1,0:T(8,128)(2,1)S(1)}, u32[]{:S(2)}, u32[]{:S(2)}) async-start(bf16[16,40,2048]{2,1,0:T(8,128)(2,1)} %bitcast.168), calls=%async_computation.3 | async-start | bytes 5242880 | tf_op jit(solution)/shard_map/all_to_all | solution.py:24
  147.0 34.4 %collective-permute-start.3 = (bf16[704,512]{1,0:T(8,128)(2,1)}, bf16[704,512]{1,0:T(8,128)(2,1)}, u32[]{:S(2)}, u32[]{:S(2)}) collective-permute-start(bf16[704,512]{1,0:T(8,128)(2,1)} %slice.172), channel_id=1, source_target_pairs={{0,96},{32,0},{64,32},{96,64},{1,97},{33,1},{65,33},{97,65},{2,98}... | collective-permute-start | bytes 2162696 | tf_op jit(solution)/shard_map/ppermute | solution.py:656
  149.3 19.2 %copy-start.93 = (bf16[2048]{0:T(1024)(128)(2,1)S(1)}, bf16[2048]{0:T(1024)(128)(2,1)}, u32[]{:S(2)}) copy-start(bf16[2048]{0:T(1024)(128)(2,1)} %param.18) | copy-start | bytes 12292
  149.3 46.2 %collective-permute-start.2 = (bf16[704,512]{1,0:T(8,128)(2,1)}, bf16[704,512]{1,0:T(8,128)(2,1)}, u32[]{:S(2)}, u32[]{:S(2)}) collective-permute-start(bf16[704,512]{1,0:T(8,128)(2,1)} %slice.171), channel_id=1, source_target_pairs={{0,32},{32,64},{64,96},{96,0},{1,33},{33,65},{65,97},{97,1},{2,34}... | collective-permute-start | bytes 2162696 | tf_op jit(solution)/shard_map/ppermute | solution.py:655
  168.5 40.3 %copy-start.54 = (f32[40,2048]{1,0:T(8,128)}, f32[40,2048]{1,0:T(8,128)S(1)}, u32[]{:S(2)}) copy-start(f32[40,2048]{1,0:T(8,128)S(1)} %reshape.396) | copy-start | bytes 983044
  168.7 40.3 %copy-start.80 = (f32[2048]{0:T(1024)}, f32[2048]{0:T(1024)S(1)}, u32[]{:S(2)}) copy-start(f32[2048]{0:T(1024)S(1)} %reshape.398) | copy-start | bytes 24580
  211.4 14.1 %all-to-all-start.4 = ((bf16[4,40,2048]{2,1,0:T(8,128)(2,1)}), bf16[4,40,2048]{2,1,0:T(8,128)(2,1)S(1)}, u32[]{:S(2)}, u32[]{:S(2)}) async-start(bf16[4,40,2048]{2,1,0:T(8,128)(2,1)} %broadcast_in_dim.56), calls=%async_computation.4 | async-start | bytes 1310720 | tf_op jit(solution)/shard_map/all_to_all | solution.py:24
  227.4 28.6 %all-to-all-start.5 = ((bf16[8,56,2048]{2,1,0:T(8,128)(2,1)}), bf16[8,56,2048]{2,1,0:T(8,128)(2,1)S(1)}, u32[]{:S(2)}, u32[]{:S(2)}) async-start(bf16[8,56,2048]{2,1,0:T(8,128)(2,1)} %bitcast.157), calls=%async_computation.5 | async-start | bytes 3670016 | tf_op jit(solution)/shard_map/all_to_all | solution.py:24
  231.6 369.7 %reduce-scatter.3.cloned.1.call-start = ((), (), s32[]{:S(2)}) async-start(), calls=%async_computation.18 | async-start | bytes 14417920 | tf_op jit(solution)/shard_map/reduce_scatter | solution.py:743
  282.4 28.6 %copy-start.14 = (bf16[448,1408]{1,0:T(8,128)(2,1)}, bf16[448,1408]{1,0:T(8,128)(2,1)S(1)}, u32[]{:S(2)}) copy-start(bf16[448,1408]{1,0:T(8,128)(2,1)S(1)} %get-tuple-element.92.left) | copy-start | bytes 3784708
  300.6 30.1 %all-to-all-start.6 = ((bf16[8,56,2176]{2,1,0:T(8,128)(2,1)}), bf16[8,56,2176]{2,1,0:T(8,128)(2,1)}, u32[]{:S(2)}, u32[]{:S(2)}) async-start(bf16[8,56,2176]{2,1,0:T(8,128)(2,1)} %bitcast.156), calls=%async_computation.6 | async-start | bytes 3899392 | tf_op jit(solution)/shard_map/all_to_all | solution.py:24
  318.1 24.2 %collective-permute-start.7 = (bf16[448,512]{1,0:T(8,128)(2,1)}, bf16[448,512]{1,0:T(8,128)(2,1)}, u32[]{:S(2)}, u32[]{:S(2)}) collective-permute-start(bf16[448,512]{1,0:T(8,128)(2,1)} %get-tuple-element.214), channel_id=1, source_target_pairs={{0,1},{1,2},{2,3},{3,0},{4,5},{5,6},{6,7},{7,4},{8,9},{9,10},{10,1... | collective-permute-start | bytes 1376264 | tf_op jit(solution)/shard_map/ppermute | solution.py:32
  318.8 23.5 %collective-permute-start.6 = (bf16[448,512]{1,0:T(8,128)(2,1)}, bf16[448,512]{1,0:T(8,128)(2,1)}, u32[]{:S(2)}, u32[]{:S(2)}) collective-permute-start(bf16[448,512]{1,0:T(8,128)(2,1)} %get-tuple-element.215), channel_id=1, source_target_pairs={{0,2},{1,3},{2,0},{3,1},{4,6},{5,7},{6,4},{7,5},{8,10},{9,11},{10,... | collective-permute-start | bytes 1376264 | tf_op jit(solution)/shard_map/ppermute | solution.py:32
  320.9 22.9 %collective-permute-start.5 = (bf16[448,512]{1,0:T(8,128)(2,1)}, bf16[448,512]{1,0:T(8,128)(2,1)}, u32[]{:S(2)}, u32[]{:S(2)}) collective-permute-start(bf16[448,512]{1,0:T(8,128)(2,1)} %get-tuple-element.213), channel_id=1, source_target_pairs={{0,3},{1,0},{2,1},{3,2},{4,7},{5,4},{6,5},{7,6},{8,11},{9,8},{10,9... | collective-permute-start | bytes 1376264 | tf_op jit(solution)/shard_map/ppermute | solution.py:32
  335.2 14.9 %all-to-all-start.7 = ((bf16[4,40,2176]{2,1,0:T(8,128)(2,1)}), bf16[4,40,2176]{2,1,0:T(8,128)(2,1)S(1)}, u32[]{:S(2)}, u32[]{:S(2)}) async-start(bf16[4,40,2176]{2,1,0:T(8,128)(2,1)} %bitcast.166), calls=%async_computation.7 | async-start | bytes 1392640 | tf_op jit(solution)/shard_map/all_to_all | solution.py:24
  350.5 13.7 %all-to-all-start.8 = ((bf16[8,56,512]{2,1,0:T(8,128)(2,1)}), bf16[8,56,512]{2,1,0:T(8,128)(2,1)S(1)}, u32[]{:S(2)}, u32[]{:S(2)}) async-start(bf16[8,56,512]{2,1,0:T(8,128)(2,1)} %bitcast.174), calls=%async_computation.8 | async-start | bytes 917504 | tf_op jit(solution)/shard_map/all_to_all | solution.py:24
  366.0 44.9 %all-to-all-start.9 = ((bf16[16,40,2048]{2,1,0:T(8,128)(2,1)}), bf16[16,40,2048]{2,1,0:T(8,128)(2,1)S(1)}, u32[]{:S(2)}, u32[]{:S(2)}) async-start(bf16[16,40,2048]{2,1,0:T(8,128)(2,1)} %broadcast_in_dim.57), calls=%async_computation.9 | async-start | bytes 5242880 | tf_op jit(solution)/shard_map/all_to_all | solution.py:24
  428.5 11.3 %collective-permute-start.8 = (bf16[640,256]{1,0:T(8,128)(2,1)}, bf16[640,256]{1,0:T(8,128)(2,1)}, u32[]{:S(2)}, u32[]{:S(2)}) collective-permute-start(bf16[640,256]{1,0:T(8,128)(2,1)} %get-tuple-element.99), channel_id=1, source_target_pairs={{0,4},{4,0},{1,5},{5,1},{2,6},{6,2},{3,7},{7,3},{8,12},{12,8},{9,1... | collective-permute-start | bytes 983048 | tf_op jit(solution)/shard_map/ppermute | solution.py:812
  428.6 11.2 %all-to-all-start.10 = ((bf16[4,40,512]{2,1,0:T(8,128)(2,1)}), bf16[4,40,512]{2,1,0:T(8,128)(2,1)S(1)}, u32[]{:S(2)}, u32[]{:S(2)}) async-start(bf16[4,40,512]{2,1,0:T(8,128)(2,1)} %bitcast.49), calls=%async_computation.10 | async-start | bytes 327680 | tf_op jit(solution)/shard_map/all_to_all | solution.py:24
  432.0 191.4 %reduce-scatter.5.cloned.1.call-start = ((), (), s32[]{:S(2)}) async-start(), calls=%async_computation.19 | async-start | bytes 7208960 | tf_op jit(solution)/shard_map/reduce_scatter | solution.py:786
  439.1 14.8 %collective-permute-start.10 = (bf16[4,256,1024]{2,1,0:T(8,128)(2,1)}, bf16[4,256,1024]{2,1,0:T(8,128)(2,1)}, u32[]{:S(2)}, u32[]{:S(2)}) collective-permute-start(bf16[4,256,1024]{2,1,0:T(8,128)(2,1)} %shard_map.238), channel_id=1, source_target_pairs={{0,4},{4,0},{1,5},{5,1},{2,6},{6,2},{3,7},{7,3},{8,12},{12,8},{9,1... | collective-permute-start | bytes 6291464 | tf_op jit(solution)/shard_map/ppermute | solution.py:810
  451.6 28.3 %collective-permute-start.9 = (bf16[4,256,1408]{2,1,0:T(8,128)(2,1)}, bf16[4,256,1408]{2,1,0:T(8,128)(2,1)}, u32[]{:S(2)}, u32[]{:S(2)}) collective-permute-start(bf16[4,256,1408]{2,1,0:T(8,128)(2,1)} %shard_map.237), channel_id=1, source_target_pairs={{0,4},{4,0},{1,5},{5,1},{2,6},{6,2},{3,7},{7,3},{8,12},{12,8},{9,1... | collective-permute-start | bytes 8650760 | tf_op jit(solution)/shard_map/ppermute | solution.py:830
  460.8 17.2 %collective-permute-start.17 = (bf16[128,1024]{1,0:T(8,128)(2,1)}, bf16[128,1024]{1,0:T(8,128)(2,1)S(1)}, u32[]{:S(2)}, u32[]{:S(2)}) collective-permute-start(bf16[128,1024]{1,0:T(8,128)(2,1)} %get-tuple-element.116), channel_id=1, source_target_pairs={{0,96},{32,0},{64,32},{96,64},{1,97},{33,1},{65,33},{97,65},{2,98}... | collective-permute-start | bytes 786440 | tf_op jit(solution)/shard_map/ppermute | solution.py:70
  469.8 83.3 %all-to-all-start.11 = ((bf16[16,40,2048]{2,1,0:T(8,128)(2,1)}), bf16[16,40,2048]{2,1,0:T(8,128)(2,1)}, u32[]{:S(2)}, u32[]{:S(2)}) async-start(bf16[16,40,2048]{2,1,0:T(8,128)(2,1)} %bitcast.167), calls=%async_computation.11 | async-start | bytes 5242880 | tf_op jit(solution)/shard_map/all_to_all | solution.py:24
  476.4 15.7 %collective-permute-start.15 = (bf16[128,1024]{1,0:T(8,128)(2,1)S(1)}, bf16[128,1024]{1,0:T(8,128)(2,1)S(1)}, u32[]{:S(2)}, u32[]{:S(2)}) collective-permute-start(bf16[128,1024]{1,0:T(8,128)(2,1)S(1)} %get-tuple-element.114), channel_id=1, source_target_pairs={{0,32},{32,64},{64,96},{96,0},{1,33},{33,65},{65,97},{97,1},{2,34}... | collective-permute-start | bytes 786440 | tf_op jit(solution)/shard_map/ppermute | solution.py:69
  478.1 57.6 %collective-permute-start.18 = (bf16[256,1024]{1,0:T(8,128)(2,1)S(1)}, bf16[256,1024]{1,0:T(8,128)(2,1)S(1)}, u32[]{:S(2)}, u32[]{:S(2)}) collective-permute-start(bf16[256,1024]{1,0:T(8,128)(2,1)S(1)} %pad_maximum_fusion.7), channel_id=1, source_target_pairs={{0,96},{32,0},{64,32},{96,64},{1,97},{33,1},{65,33},{97,65},{2,98}... | collective-permute-start | bytes 1572872 | tf_op jit(solution)/shard_map/ppermute | solution.py:81
  485.8 33.4 %collective-permute-start.13 = (bf16[128,1408]{1,0:T(8,128)(2,1)S(1)}, bf16[128,1408]{1,0:T(8,128)(2,1)S(1)}, u32[]{:S(2)}, u32[]{:S(2)}) collective-permute-start(bf16[128,1408]{1,0:T(8,128)(2,1)S(1)} %get-tuple-element.112), channel_id=1, source_target_pairs={{0,96},{32,0},{64,32},{96,64},{1,97},{33,1},{65,33},{97,65},{2,98}... | collective-permute-start | bytes 1081352 | tf_op jit(solution)/shard_map/ppermute | solution.py:70
  492.3 43.5 %collective-permute-start.16 = (bf16[256,1024]{1,0:T(8,128)(2,1)S(1)}, bf16[256,1024]{1,0:T(8,128)(2,1)S(1)}, u32[]{:S(2)}, u32[]{:S(2)}) collective-permute-start(bf16[256,1024]{1,0:T(8,128)(2,1)S(1)} %pad_maximum_fusion.6), channel_id=1, source_target_pairs={{0,32},{32,64},{64,96},{96,0},{1,33},{33,65},{65,97},{97,1},{2,34}... | collective-permute-start | bytes 1572872 | tf_op jit(solution)/shard_map/ppermute | solution.py:80
  492.7 42.3 %copy-start.62 = (f32[40,2048]{1,0:T(8,128)S(1)}, f32[40,2048]{1,0:T(8,128)}, u32[]{:S(2)}) copy-start(f32[40,2048]{1,0:T(8,128)} %reshape.376) | copy-start | bytes 983044
  492.8 41.9 %collective-permute-start.11 = (bf16[128,1408]{1,0:T(8,128)(2,1)S(1)}, bf16[128,1408]{1,0:T(8,128)(2,1)S(1)}, u32[]{:S(2)}, u32[]{:S(2)}) collective-permute-start(bf16[128,1408]{1,0:T(8,128)(2,1)S(1)} %get-tuple-element.110), channel_id=1, source_target_pairs={{0,32},{32,64},{64,96},{96,0},{1,33},{33,65},{65,97},{97,1},{2,34}... | collective-permute-start | bytes 1081352 | tf_op jit(solution)/shard_map/ppermute | solution.py:69
  519.3 29.7 %collective-permute-start.14 = (bf16[256,1408]{1,0:T(8,128)(2,1)S(1)}, bf16[256,1408]{1,0:T(8,128)(2,1)S(1)}, u32[]{:S(2)}, u32[]{:S(2)}) collective-permute-start(bf16[256,1408]{1,0:T(8,128)(2,1)S(1)} %pad_maximum_fusion.5), channel_id=1, source_target_pairs={{0,96},{32,0},{64,32},{96,64},{1,97},{33,1},{65,33},{97,65},{2,98}... | collective-permute-start | bytes 2162696 | tf_op jit(solution)/shard_map/ppermute | solution.py:81
  534.8 18.0 %collective-permute-start.12 = (bf16[256,1408]{1,0:T(8,128)(2,1)S(1)}, bf16[256,1408]{1,0:T(8,128)(2,1)S(1)}, u32[]{:S(2)}, u32[]{:S(2)}) collective-permute-start(bf16[256,1408]{1,0:T(8,128)(2,1)S(1)} %pad_maximum_fusion.4), channel_id=1, source_target_pairs={{0,32},{32,64},{64,96},{96,0},{1,33},{33,65},{65,97},{97,1},{2,34}... | collective-permute-start | bytes 2162696 | tf_op jit(solution)/shard_map/ppermute | solution.py:80
  562.5 38.8 %all-to-all-start.12 = ((bf16[16,64,128]{2,1,0:T(8,128)(2,1)}), bf16[16,64,128]{2,1,0:T(8,128)(2,1)}, u32[]{:S(2)}, u32[]{:S(2)}) async-start(bf16[16,64,128]{2,1,0:T(8,128)(2,1)} %bitcast.57), calls=%async_computation.13 | async-start | bytes 524288 | tf_op jit(solution)/shard_map/all_to_all | solution.py:24
  569.4 14.8 %collective-permute-start.19 = (bf16[64,2304]{1,0:T(8,128)(2,1)S(1)}, bf16[64,2304]{1,0:T(8,128)(2,1)S(1)}, u32[]{:S(2)}, u32[]{:S(2)}) collective-permute-start(bf16[64,2304]{1,0:T(8,128)(2,1)S(1)} %get-tuple-element.221), channel_id=1, source_target_pairs={{0,24},{8,0},{16,8},{24,16},{1,25},{9,1},{17,9},{25,17},{2,26},{10... | collective-permute-start | bytes 884744 | tf_op jit(solution)/shard_map/ppermute | solution.py:32
  572.5 11.6 %collective-permute-start.20 = (bf16[64,2304]{1,0:T(8,128)(2,1)S(1)}, bf16[64,2304]{1,0:T(8,128)(2,1)S(1)}, u32[]{:S(2)}, u32[]{:S(2)}) collective-permute-start(bf16[64,2304]{1,0:T(8,128)(2,1)S(1)} %get-tuple-element.220), channel_id=1, source_target_pairs={{0,16},{8,24},{16,0},{24,8},{1,17},{9,25},{17,1},{25,9},{2,18},{10... | collective-permute-start | bytes 884744 | tf_op jit(solution)/shard_map/ppermute | solution.py:32
  573.4 13.8 %collective-permute-start.21 = (bf16[64,2304]{1,0:T(8,128)(2,1)S(1)}, bf16[64,2304]{1,0:T(8,128)(2,1)S(1)}, u32[]{:S(2)}, u32[]{:S(2)}) collective-permute-start(bf16[64,2304]{1,0:T(8,128)(2,1)S(1)} %get-tuple-element.218), channel_id=1, source_target_pairs={{0,8},{8,16},{16,24},{24,0},{1,9},{9,17},{17,25},{25,1},{2,10},{10... | collective-permute-start | bytes 884744 | tf_op jit(solution)/shard_map/ppermute | solution.py:32
  602.5 21.8 %all-to-all-start.13 = ((bf16[4,40,4096]{2,1,0:T(8,128)(2,1)}), bf16[4,40,4096]{2,1,0:T(8,128)(2,1)S(1)}, u32[]{:S(2)}, u32[]{:S(2)}) async-start(bf16[4,40,4096]{2,1,0:T(8,128)(2,1)} %broadcast_in_dim.103), calls=%async_computation.14 | async-start | bytes 2621440 | tf_op jit(solution)/shard_map/all_to_all | solution.py:24
  (86 other events, 453.5 us)
Sparse Core Ops, SparseCore 0:
  43.4 58.0 all-gather.2
  103.1 125.3 all-gather.4
  297.8 101.5 reduce-scatter.2
  454.0 93.1 reduce-scatter.4

commit v6 on v5

--- a/solution.py
+++ b/solution.py
@@ -79,16 +79,6 @@
         own.astype(F32)
         + lax.ppermute(ahead, axis, UP).astype(F32)
         + lax.ppermute(back, axis, DOWN).astype(F32)
-    )
-
-
-def heads_last(blocks):
-    heads = blocks.shape[2] // HEAD_SIZE
-    return (
-        blocks.reshape(4, 64, heads, HEAD_SIZE)
-        .transpose(1, 2, 0, 3)
-        .reshape(64, heads, 4 * HEAD_SIZE)
-        .astype(F32)
     )
 
 
@@ -246,10 +236,10 @@
     )(*args)
 
 
-FREE = pl.CostEstimate(flops=0, bytes_accessed=0, transcendentals=0)
-
-
-def on_grid(kernel, scalars, grid, in_specs, out_specs, outs, scratch, *args, cost=FREE):
+SOME = pl.CostEstimate(flops=1 << 35, bytes_accessed=1 << 27, transcendentals=0)
+
+
+def on_grid(kernel, scalars, grid, in_specs, out_specs, outs, scratch, *args, cost=SOME):
     return pl.pallas_call(
         kernel,
         out_shape=outs,
@@ -335,7 +325,7 @@
     )
 
 
-def gate_up_product(rows, pair):
+def half_product(rows, pair, half):
     def kernel(at, left, right, out):
         out[...] = lax.dot_general(left[...], right[0], ROWS, preferred_element_type=F32).astype(BF)
 
@@ -343,13 +333,13 @@
     return on_grid(
         kernel,
         (jnp.int32(0),),
-        (2, 8),
+        (8,),
         [
-            pl.BlockSpec((depth, 256), lambda h, i, at: (0, i)),
-            pl.BlockSpec((1, depth, width), lambda h, i, at: (h, 0, 0)),
+            pl.BlockSpec((depth, 256), lambda i, at: (0, i)),
+            pl.BlockSpec((1, depth, width), lambda i, at: (half, 0, 0)),
         ],
-        pl.BlockSpec((256, width), lambda h, i, at: (i, h)),
-        jax.ShapeDtypeStruct((MODEL_WIDTH, 2 * width), BF),
+        pl.BlockSpec((256, width), lambda i, at: (i, 0)),
+        jax.ShapeDtypeStruct((MODEL_WIDTH, width), BF),
         [],
         rows,
         pair,
@@ -380,45 +370,54 @@
     )
 
 
-def down_back(grads, down_w):
-    def kernel(at, left, right, out):
-        out[...] = lax.dot_general(left[...], right[...], LAST, preferred_element_type=F32)
-
-    depth, width = grads.shape[0], down_w.shape[0]
+def down_back(grads, pieces, place):
+    def kernel(at, left, own, ahead, far_a, far_b, back, out):
+        total = None
+        for shift, start, piece in (
+            (0, 0, own), (1, 0, ahead), (2, 0, far_a), (2, 256, far_b), (3, 0, back)
+        ):
+            size = piece.shape[1]
+            lanes = pl.ds(pl.multiple_of(lax.rem(at[0] + shift, 4) * 512 + start, 256), size)
+            term = lax.dot_general(left[:, lanes], piece[...], LAST, preferred_element_type=F32)
+            total = term if total is None else total + term
+        out[...] = total
+
+    depth, width = grads.shape[0], pieces[0].shape[0]
     return on_grid(
         kernel,
-        (jnp.int32(0),),
+        (place,),
         (width // 128,),
-        [
-            pl.BlockSpec((depth, MODEL_WIDTH), lambda i, at: (0, 0)),
-            pl.BlockSpec((128, MODEL_WIDTH), lambda i, at: (i, 0)),
-        ],
+        [pl.BlockSpec(grads.shape, lambda i, at: (0, 0))]
+        + [pl.BlockSpec((128, p.shape[1]), lambda i, at: (i, 0)) for p in pieces],
         pl.BlockSpec((depth, 128), lambda i, at: (0, i)),
         jax.ShapeDtypeStruct((depth, width), F32),
         [],
         grads,
-        down_w,
-    )
-
-
-def expert_quarters(activated, down_w, place, x):
-    def kernel(at, left, right, out):
-        out[0] = jnp.dot(left[...], right[...], preferred_element_type=F32).astype(BF)
-
-    depth, width = activated.shape
+        *pieces,
+    )
+
+
+def expert_quarters(activated, pieces, place, x):
+    def kernel(at, left, own, ahead, far_a, far_b, back, out):
+        step = pl.program_id(0)
+        for shift, refs in enumerate(((own,), (ahead,), (far_a, far_b), (back,))):
+
+            @pl.when(step == shift)
+            def _():
+                terms = [jnp.dot(left[...], r[...], preferred_element_type=F32) for r in refs]
+                out[0] = jnp.concatenate(terms, axis=1).astype(BF)
+
+    depth = activated.shape[0]
     return on_grid(
         kernel,
         (place, x),
         (4,),
-        [
-            pl.BlockSpec((depth, width), lambda i, at: (0, 0)),
-            pl.BlockSpec((width, 512), lambda i, at: (0, i)),
-        ],
+        [pl.BlockSpec(a.shape, lambda i, at: (0, 0)) for a in (activated, *pieces)],
         pl.BlockSpec((1, depth, 512), lambda i, at: (lax.rem(at[0] + i + 4 - at[1], 4), 0, 0)),
         jax.ShapeDtypeStruct((4, depth, 512), BF),
         [],
         activated,
-        down_w,
+        *pieces,
     )
 
 
@@ -468,16 +467,18 @@
 
         @pl.when(step >= blocks)
         def _():
-            back_out[...] = lax.dot_general(
+            back_lane = pl.multiple_of((step - blocks) * 512, 512)
+            back_out[:, pl.ds(back_lane, 512)] = lax.dot_general(
                 pair_all[...], flat_ref[...], LAST, preferred_element_type=F32
             ).astype(BF)
 
-        @pl.when(step == blocks + 4)
+        @pl.when(step == blocks + 3)
         def _():
             high = row_grad[...].astype(BF).astype(F32)
             low = row_grad[...] - high
-            wide = lax.broadcasted_iota(jnp.int32, (depth, 512), 1)
-            back_out[...] = jnp.where(wide == 0, high, jnp.where(wide == 1, low, 0.0)).astype(BF)
+            back_out[:, MODEL_WIDTH:] = jnp.where(
+                lane == 0, high, jnp.where(lane == 1, low, 0.0)
+            ).astype(BF)
 
     def first(i):
         return jnp.minimum(i, blocks - 1)
@@ -488,7 +489,7 @@
     return on_grid(
         kernel,
         (expert,),
-        (blocks + 5,),
+        (blocks + 4,),
         [
             pl.BlockSpec((depth, MODEL_WIDTH), lambda i, at: (0, 0)),
             pl.BlockSpec((depth, 128), lambda i, at: (0, 0)),
@@ -502,13 +503,13 @@
             pl.BlockSpec((depth, 128), lambda i, at: (0, first(i))),
             pl.BlockSpec((2, depth, 128), lambda i, at: (0, 0, first(i))),
             pl.BlockSpec((depth, 1), lambda i, at: (0, 0)),
-            pl.BlockSpec((depth, 512), lambda i, at: (0, jnp.clip(i - blocks, 0, 4))),
+            pl.BlockSpec((depth, MODEL_WIDTH + 128), lambda i, at: (0, 0)),
         ],
         [
             jax.ShapeDtypeStruct((depth, width), BF),
             jax.ShapeDtypeStruct((2, depth, width), BF),
             jax.ShapeDtypeStruct((depth, 1), F32),
-            jax.ShapeDtypeStruct((depth, MODEL_WIDTH + 512), BF),
+            jax.ShapeDtypeStruct((depth, MODEL_WIDTH + 128), BF),
         ],
         [
             pltpu.VMEM((depth, 2 * width), BF),
@@ -525,6 +526,33 @@
         cost=pl.CostEstimate(
             flops=8 * depth * MODEL_WIDTH * width, bytes_accessed=1 << 24, transcendentals=1 << 20
         ),
+    )
+
+
+def heads_placed(pieces, y):
+    def kernel(at, p0, p1, p2, p3, query, kv, out):
+        for k, piece in enumerate((p0, p1, p2, p3)):
+            lanes = pl.ds(pl.multiple_of(lax.rem(at[0] + k, 4) * 128, 128), 128)
+            for e in range(18):
+                block = piece[:, 128 * e : 128 * (e + 1)].astype(F32)
+                if e < 8:
+                    query[:, e, lanes] = block
+                elif e < 10:
+                    kv[:, e - 8, lanes] = block
+                else:
+                    out[:, e - 10, lanes] = block
+
+    shapes = [(64, 8, 512), (64, 2, 512), (64, 8, 512)]
+    return on_grid(
+        kernel,
+        (y,),
+        (1,),
+        [pl.BlockSpec((64, 2432), lambda i, at: (0, 0))] * 4,
+        [pl.BlockSpec(s, lambda i, at: (0, 0, 0)) for s in shapes],
+        [jax.ShapeDtypeStruct(s, F32) for s in shapes],
+        [],
+        *pieces,
+        cost=pl.CostEstimate(flops=0, bytes_accessed=0, transcendentals=0),
     )
 
 
@@ -609,10 +637,6 @@
     all_w = lax.all_gather(
         after(mine, (down_before, down_after)), ("dp", "core"), axis=0, tiled=True
     )
-    def turned(columns, blocks):
-        twice = jnp.concatenate([columns, columns], axis=1)
-        return lax.dynamic_slice_in_dim(twice, blocks * 512, MODEL_WIDTH, axis=1)
-
     values = arrived[:, :MODEL_WIDTH].astype(F32)
     routes = arrived[:, MODEL_WIDTH : MODEL_WIDTH + 2].astype(jnp.int32)
     gain_a = core_first(attn_gain.astype(F32))[0]
@@ -651,16 +675,12 @@
         (all_w, down_before, down_after, xn1, grad_sent)
     )
     in_w, out_w = all_w[:, :1408], all_w[:, 1408:]
-    low_rows = down_own.shape[0] // 2
-    far_low = lax.ppermute(down_before[:low_rows], "dp", UP)
-    far_high = lax.ppermute(down_after[low_rows:], "dp", DOWN)
+    far_a = lax.ppermute(down_before[:, :256], "dp", UP)
+    far_b = lax.ppermute(down_after[:, 256:], "dp", DOWN)
+    down_pieces = (down_own, down_after, far_a, far_b, down_before)
     gate_up_own = gate_up_weight.reshape(4, 2, 64, 2816).transpose(1, 0, 2, 3).reshape(512, 2816)
     gate_up_w = lax.all_gather(after(gate_up_own, all_w), "dp", axis=0, tiled=True)
     router_m = in_w[:, 1288:1296]
-
-    down_w = jnp.concatenate(
-        [down_own, down_after, jnp.concatenate([far_low, far_high], axis=0), down_before], axis=1
-    )
 
     grad_landed = to_experts(grad_sent)
 
@@ -711,13 +731,12 @@
     branch_part = lax.dot_general(mixed, out_w, LAST, preferred_element_type=F32).astype(BF)
     branch_part = after(branch_part, grad_landed)
     grad_received = grad_landed[:, :MODEL_WIDTH]
-    grad_turned = turned(grad_received, z)
     branch = exchange(branch_part.reshape(16, quarter, MODEL_WIDTH), plane).astype(F32).sum(axis=0)
 
     first = x * quarter
     own_values = core_first(lax.dynamic_slice_in_dim(tokens, first, quarter)).astype(F32)
     own_factor = rms_scale(own_values)
-    hidden = after(own_values, (down_w, grad_turned)) + branch
+    hidden = after(own_values, (far_a, far_b)) + branch
     factor_m = rms_scale(hidden)
     xn2_own = (hidden * factor_m * gain_m).astype(BF)
     xn2 = spread(xn2_own, "tensor", 4).reshape(count, MODEL_WIDTH)
@@ -727,7 +746,7 @@
     received = to_experts(
         lax.dot_general(any_row, xn2, ROWS, preferred_element_type=F32).astype(BF)
     )
-    grad_act_raw = down_back(grad_turned, down_w)
+    grad_act_raw = down_back(grad_received, down_pieces, z)
     received, grad_act_raw = lax.optimization_barrier((received, grad_act_raw))
     activated, grad_pair, row_gate, grad_back = expert_middle(
         received,
@@ -738,12 +757,11 @@
         2 * y + core,
     )
     grad_back, late_pair, late_act = lax.optimization_barrier((grad_back, grad_pair, activated))
-    grad_returned = to_experts(grad_back[:, : MODEL_WIDTH + HEAD_SIZE])
-    grad_gate_up_w = gate_up_product(received, late_pair)
-    gate_up_sum = lax.psum_scatter(grad_gate_up_w, "dp", scatter_dimension=0, tiled=True)
-    width = down_own.shape[0]
-    quarters = expert_quarters(late_act, down_w, z, x)
-    late_any = after(any_row, (grad_gate_up_w, quarters))
+    grad_returned = to_experts(grad_back)
+    grad_down_w = down_product(late_act, grad_received, row_gate)
+    down_sum = lax.psum_scatter(grad_down_w, "dp", scatter_dimension=1, tiled=True)
+    quarters = expert_quarters(late_act, down_pieces, z, x)
+    late_any = after(any_row, (grad_down_w, quarters))
     expert_out = (
         quarters[0].astype(F32)
         + sum(from_ahead(quarters[4 - k], "tensor", k).astype(F32) for k in (1, 2, 3))
@@ -782,9 +800,14 @@
 
     fetched = jnp.einsum("jtr,rd->jtd", to_row, returned, preferred_element_type=F32)
     moe_part = jnp.sum(weight_m.T[:, :, None] * fetched, axis=0).astype(BF)
-    grad_down_w = down_product(after(late_act, returned), grad_received, row_gate)
-    down_sum = lax.psum_scatter(grad_down_w, "dp", scatter_dimension=1, tiled=True)
-    grad_branch, moe_part, _ = lax.optimization_barrier((grad_branch, moe_part, grad_down_w))
+    grad_gate_w = half_product(after(received, returned), late_pair, 0)
+    gate_sum = lax.psum_scatter(grad_gate_w, "dp", scatter_dimension=0, tiled=True)
+    grad_up_w = half_product(after(received, returned), late_pair, 1)
+    up_sum = lax.psum_scatter(grad_up_w, "dp", scatter_dimension=0, tiled=True)
+    width = down_own.shape[0]
+    grad_branch, moe_part, *_ = lax.optimization_barrier(
+        (grad_branch, moe_part, grad_gate_w, grad_up_w)
+    )
     moe_pieces = exchange(moe_part.reshape(4, quarter, MODEL_WIDTH // 4), "tensor")
 
     grad_mixed = jnp.dot(grad_branch, out_w, preferred_element_type=F32)
@@ -797,7 +820,7 @@
             jax.ShapeDtypeStruct((half, 2 * HEAD_SIZE), BF),
         ],
         [pltpu.VMEM((2, half, 2 * HEAD_SIZE), F32)],
-        12 << 28,
+        40 << 28,
         grad_mixed,
         query,
         kv_own,
@@ -826,9 +849,11 @@
     gain_cols = (
         (jnp.arange(8)[:, None] == 0) & (jnp.arange(1408)[None, :] == 1296)
     ).astype(BF)
-    grad_tall = jnp.concatenate([grad_in, router_cols, gain_cols], axis=0)
+    grad_tall = jnp.concatenate([after(grad_in, grad_xn1_part), router_cols, gain_cols], axis=0)
     in_give = lax.ppermute(give_terms(tall, grad_tall, z, core), "core", SWAP)
-    out_own, *out_rest = keep_terms(grad_branch, mixed, out_give, z, core)
+    out_own, *out_rest = keep_terms(
+        grad_branch, mixed, after(out_give, grad_xn1_part), z, core
+    )
     out_ahead, out_back = ring_first(*out_rest, "dp")
     in_own_rows, *in_rest = keep_terms(
         tall, grad_tall, after(in_give, out_own), z, core
@@ -837,7 +862,9 @@
     out_sum = ring_second(out_own, out_ahead, out_back, "dp").astype(BF)
     in_sum = ring_second(in_own_rows, in_ahead, in_back, "dp").astype(BF)
     landed_raw = exchange(grad_xn1_part.reshape(16, quarter, MODEL_WIDTH), plane)
-    landed_raw, in_sum, out_sum = lax.optimization_barrier((landed_raw, in_sum, out_sum))
+    landed_raw, in_sum, out_sum, down_sum = lax.optimization_barrier(
+        (landed_raw, in_sum, out_sum, down_sum)
+    )
     landed_a = landed_raw.astype(F32).sum(axis=0)
     grad_x_norm, _ = norm_back(landed_a, own_values, own_factor, gain_a)
     columns = jnp.arange(1408, dtype=jnp.int32)[None, :]
@@ -847,32 +874,34 @@
         keepdims=True,
     )
     small_part = jnp.where(columns[:, :128] == 17, gain_a_part, in_sum[:, 1280:].astype(F32))
-    small_sent = jnp.broadcast_to(
-        small_part.astype(BF).reshape(4, 1, 64, 128), (4, 4, 64, 128)
-    ).reshape(16, 64, 128)
     gain_rows = lax.dynamic_slice_in_dim(attn_gain.astype(F32), z * 512 + y * 128 + core * 64, 64)
 
     ends = jnp.concatenate(
         [output_own, core_last((grad_hidden + grad_x_norm).astype(BF))], axis=1
     )
-    ends, gate_up_sum, small_raw = lax.optimization_barrier(
-        (ends, gate_up_sum, exchange(small_sent, plane))
-    )
+    both_sums = jnp.concatenate(
+        [in_sum[:, :1280], out_sum, small_part.astype(BF)], axis=1
+    ).reshape(4, 64, 2432)
+    y_parts = send_direct(both_sums, "y")
+    ends, gate_sum = lax.optimization_barrier((ends, gate_sum))
     gate_up_grad = (
-        gate_up_sum.reshape(2, 4, 64, 2816)
-        .transpose(1, 0, 2, 3)
+        jnp.stack([gate_sum, up_sum], axis=1)
+        .reshape(2, 4, 64, 2, width)
+        .transpose(1, 0, 2, 3, 4)
         .reshape(1, 512, 2, width)
         .astype(F32)
     )
-    small_sum = small_raw.astype(F32).sum(axis=0)
-    both_ends, down_sum = lax.optimization_barrier((spread(ends, "tensor", 4), down_sum))
+    _, _, *y_parts = lax.optimization_barrier((gate_up_grad, ends, *y_parts))
+    both_ends = spread(ends, "tensor", 4)
+    small_y = sum(p[:, 2304:].astype(F32) for p in y_parts).astype(BF)
+    small_y = after(small_y, both_ends)
+    small_sum = small_y.astype(F32) + sum(
+        from_ahead(small_y, "tensor", k).astype(F32) for k in (1, 2, 3)
+    )
     down_grad = down_sum.astype(F32)[None]
     both_ends = both_ends.reshape(count, 2 * MODEL_WIDTH)
     output, input_grad = both_ends[:, :MODEL_WIDTH], both_ends[:, MODEL_WIDTH:]
-    both_sums = jnp.concatenate([in_sum[:, :1280], out_sum], axis=1).reshape(4, 64, 2304)
-    both_grads = heads_last(in_order(send_direct(both_sums, "y"), y))
-    in_grad, out_grad = both_grads[:, :10], both_grads[:, 10:]
-    query_grad, kv_grad = in_grad[:, :8], in_grad[:, 8:]
+    query_grad, kv_grad, out_grad = heads_placed(y_parts, y)
     return (
         output,
         input_grad,

time: 640 us -> 579 us (0.905)
  waiting for transfers between devices: 206 us -> 152 us
  starting transfers between devices: 99.2 us -> 85.7 us
  local copies, waits for them, and re-layouts: 99.8 us -> 108 us
    ppermute x2, waiting for transfers between devices: 18.6 us -> 3.24 us  [ring_first(): low = lax.ppermute(low, axis, UP)]
    concatenate x4 -> x3, other arithmetic: 13.3 us -> 0.39 us  [the longest x1 0.16 us: body(): grad_in = jnp.concatenate([grad_q_all, grad_kv, grad_logit_a], axis=1)]
    all_gather x1, waiting for transfers between devices: 13.9 us -> 1.32 us  [body(): lax.all_gather(after(mine, (down_before, down_after)), ('dp', 'core'), ax...]
    convert_element_type x5 -> x1, local copies, waits for them, and re-layouts: 18.9 us -> 6.98 us  [body(): gate_up_grad = jnp.stack([gate_sum, up_sum], axis=1).reshape(2, 4, 64, 2,...]
    ppermute x2, waiting for transfers between devices: 25.3 us -> 14.9 us  [ring_first(): high = lax.ppermute(high, axis, DOWN)]
    all_to_all x13 -> x12, starting transfers between devices: 63.7 us -> 53.4 us  [exchange(): return lax.all_to_all(blocks, axis, split_axis=0, concat_axis=0, tiled=True)]
    ppermute x6 -> x9, waiting for transfers between devices: 17 us -> 7.05 us  [from_ahead(): return lax.ppermute(block, axis, [(i, (i - steps) % 4) for i in range(4)])]
    ppermute x2, starting transfers between devices: 12.8 us -> 3.24 us  [the longest x1 2.58 us: body(): far_b = lax.ppermute(down_after[:, 256:], 'dp', DOWN)]
  transfers between devices with their start and end apart: 39 -> 42, of which waited for: 22 -> 20; matrix products, arithmetic and copies ran while one was open for 27% -> 30% of each run, Pallas kernels for 9% -> 12%
where the time goes in v6:
time: 579 us; the launch traced here: 572 us
  waiting for transfers between devices  152 us (26%)
  local copies, waits for them, and re-layouts  108 us (19%)
  Pallas kernels  97.7 us (17%)
  starting transfers between devices  85.7 us (15%)
  other arithmetic  52.1 us (9%)
  matrix products  40.2 us (7%)
  blocking collectives  21.3 us (4%)
  between operations  15.3 us (3%)
    all_to_all x12, waiting for transfers between devices, exchange(): return lax.all_to_all(blocks, axis, split_axis=0, concat_axis=0, tiled=True)  82.9 us
    pallas_call x11, Pallas kernels, on_grid(): pl.pallas_call(kernel, out_shape=outs, grid_spec=pltpu.PrefetchScalarGrid...  82.4 us
    all_to_all x12, starting transfers between devices, exchange(): return lax.all_to_all(blocks, axis, split_axis=0, concat_axis=0, tiled=True)  53.4 us
    unnamed x164, local copies, waits for them, and re-layouts  32.1 us
    ppermute x1, waiting for transfers between devices, body(): far_a = lax.ppermute(down_before[:, :256], 'dp', UP)  26.2 us
    all_to_all x1, blocking collectives, exchange(): return lax.all_to_all(blocks, axis, split_axis=0, concat_axis=0, tiled=True)  21.3 us
    pallas_call x2, Pallas kernels, in_vmem(): pl.pallas_call(kernel, out_shape=outs, in_specs=[spec] * len(args), out_s...  15.3 us
    ppermute x2, waiting for transfers between devices, ring_first(): high = lax.ppermute(high, axis, DOWN)  14.9 us
  transfers between devices with their start and end apart: 42, of which 20 were waited for; matrix products, arithmetic and copies ran while one was open for 30% of the time, Pallas kernels for 12%

profile of v6, /device:TPU:0, one launch (start us, length us, event | category | flops | bytes accessed | tf_op | source)
XLA Modules:
  0.0 572.0 jit_solution(7547030563055683098)
XLA Ops:
  24.8 21.3 %all_to_all.65 = bf16[4,64,2432]{2,1,0:T(8,128)(2,1)} all-to-all(bf16[4,64,2432]{2,1,0:T(8,128)(2,1)S(1)} %pad_maximum_fusion.1), channel_id=1, replica_groups=mesh['dp'=4,'y'=4,'core'=2,'tensor'=4] {'y'}, dimensions={0} | all-to-all | bytes 2490368 | tf_op jit(solution)/shard_map/all_to_all | solution.py:24
  56.4 4.7 all-to-all-start.1
  62.8 7.4 %reshape.372 = bf16[4,2,64,2816]{3,2,1,0:T(8,128)(2,1)} reshape(bf16[1,512,2,1408]{3,2,1,0:T(2,128)(2,1)} %param.24) | data formatting | bytes 5767168 | tf_op jit(solution)/shard_map/reshape | solution.py:681
  70.3 3.7 copy.175
  77.4 16.3 %all-to-all-done.1 = bf16[4,160,2176]{2,1,0:T(8,128)(2,1)} async-done(((bf16[4,160,2176]{2,1,0:T(8,128)(2,1)}), bf16[4,160,2176]{2,1,0:T(8,128)(2,1)}, u32[]{:S(2)}, u32[]{:S(2)}) %all-to-all-start.1) | async-done | bytes 2785312 | tf_op jit(solution)/shard_map/all_to_all | solution.py:24
  96.0 4.0 fusion.3
  108.0 7.4 %fusion.6.proj = f32[640,1408]{1,0:T(8,128)S(1)} fusion(bf16[640,2048]{1,0:T(8,128)(2,1)} %fusion.3, bf16[2048,2432]{1,0:T(8,128)(2,1)} %all-gather.3.cloned.1.call-done), kind=kOutput, calls=%fused_computation.14 | convolution fusion | flops 3690987520 | bytes 11993088 | tf_op jit(solution)/shard_map/dot_general | solution.py:708
  117.9 4.4 all-to-all-start.2
  128.2 6.9 %shard_map.230 = (bf16[4,320,128]{2,1,0:T(8,128)(2,1)S(1)}, f32[4,320,128]{2,1,0:T(8,128)S(1)}, f32[4,320,1]{2,1,0:T(8,128)S(1)}, f32[640,2]{1,0:T(8,128)S(1)}, bf16[640,1024]{1,0:T(8,128)(2,1)S(1)}) custom-call(f32[640,1408]{1,0:T(8,128)S(1)} %copy-done.12, bf16[640,256]{1,0:T(8,128)(2,1)S(1)} %pad_maximum_fusion.9.own, ...), custom_call_target="tpu_custom_call" | custom-call | flops 1610612736 | bytes 4935680 | tf_op jit(solution)/shard_map/pallas_call | solution.py:228
  138.3 6.4 %fusion.17 = bf16[640,2048]{1,0:T(8,128)(2,1)} fusion(bf16[640,1024]{1,0:T(8,128)(2,1)S(1)} %get-tuple-element.83.right, bf16[2048,2432]{1,0:T(8,128)(2,1)} %all-gather.3.cloned.1.call-done), kind=kOutput, calls=%fused_computation.24 | convolution fusion | flops 2685665280 | bytes 8126464 | tf_op jit(solution)/shard_map/dot_general | solution.py:731
  148.0 5.1 all-to-all-start.3
  163.2 26.2 %collective-permute-done.2.far_a = bf16[1408,256]{1,0:T(8,128)(2,1)S(1)} collective-permute-done((bf16[1408,256]{1,0:T(8,128)(2,1)}, bf16[1408,256]{1,0:T(8,128)(2,1)S(1)}, u32[]{:S(2)}, u32[]{:S(2)}) %collective-permute-start.2) | collective-permute-done | bytes 720928 | tf_op jit(solution)/shard_map/ppermute | solution.py:678
  189.9 3.8 all-to-all-done.3
  197.2 3.9 all-to-all-start.4
  205.6 5.7 all-to-all-done.4
  213.3 3.6 all-to-all-start.5
  222.1 9.5 %shard_map.231.grad_ref = f32[448,1408]{1,0:T(8,128)} custom-call(s32[1]{0:T(128)} %bitcast.31.at, bf16[448,2048]{1,0:T(8,128)(2,1)} %slice.227.left.right, bf16[1408,512]{1,0:T(8,128)(2,1)S(1)} %bitcast.139, bf16[1408,512]{1,0:T(8,128)(2,1)S(1)} %copy-done.16, bf16[1408,256]{1,0:T(8,128)(2,1)S(1)} %collective-permute-done.2.far_a, ...), custom_call_target="tpu_custom_call" | custom-call | flops 34359738368 | bytes 134217728 | tf_op jit(solution)/shard_map/pallas_call | solution.py:243
  232.5 8.7 %all-to-all-done.5 = bf16[8,56,2048]{2,1,0:T(8,128)(2,1)S(1)} async-done(((bf16[8,56,2048]{2,1,0:T(8,128)(2,1)}), bf16[8,56,2048]{2,1,0:T(8,128)(2,1)S(1)}, u32[]{:S(2)}, u32[]{:S(2)}) %all-to-all-start.5) | async-done | bytes 1835040 | tf_op jit(solution)/shard_map/all_to_all | solution.py:24
  241.2 22.7 %shard_map.232 = (bf16[448,1408]{1,0:T(8,128)(2,1)S(1)}, bf16[2,448,1408]{2,1,0:T(8,128)(2,1)}, f32[448,1]{1,0:T(8,128)S(1)}, bf16[448,2176]{1,0:T(8,128)(2,1)S(1)}) custom-call(s32[1]{0:T(128)} %bitcast.26.at, bf16[448,2048]{1,0:T(8,128)(2,1)S(1)} %bitcast.133, bf16[448,128]{1,0:T(8,128)(2,1)S(1)} %slice.228.marks_ref, ...), custom_call_target="tpu_custom_call" | custom-call | flops 10334765056 | bytes 16777216 | tf_op jit(solution)/shard_map/pallas_call | solution.py:243
  265.2 5.5 shard_map.233
  280.6 4.3 all-to-all-start.6
  290.2 6.3 %shard_map.234 = bf16[4,448,512]{2,1,0:T(8,128)(2,1)} custom-call(s32[2]{0:T(128)S(1)} %pad_add_fusion.2.at, bf16[448,1408]{1,0:T(8,128)(2,1)S(1)} %copy-done.31, bf16[1408,512]{1,0:T(8,128)(2,1)S(1)} %bitcast.140, bf16[1408,512]{1,0:T(8,128)(2,1)S(1)} %copy-done.17, bf16[1408,256]{1,0:T(8,128)(2,1)S(1)} %collective-permute-done.2.far_a, ...), custom_call_target="tpu_custom_call" | custom-call | flops 34359738368 | bytes 134217728 | tf_op jit(solution)/shard_map/pallas_call | solution.py:243
  302.4 8.2 %all-to-all-done.6 = bf16[8,56,2176]{2,1,0:T(8,128)(2,1)} async-done(((bf16[8,56,2176]{2,1,0:T(8,128)(2,1)}), bf16[8,56,2176]{2,1,0:T(8,128)(2,1)}, u32[]{:S(2)}, u32[]{:S(2)}) %all-to-all-start.6) | async-done | bytes 1949728 | tf_op jit(solution)/shard_map/all_to_all | solution.py:24
  315.0 3.5 all-to-all-start.7
  318.7 4.7 collective-permute-done.7
  327.0 3.5 all-to-all-done.7
  331.0 4.4 all-to-all-start.8
  339.9 5.1 all-to-all-done.8
  346.8 6.8 %shard_map.235 = bf16[2048,1408]{1,0:T(8,128)(2,1)} custom-call(s32[1]{0:T(128)} %constant.110.clone.1.at, bf16[448,2048]{1,0:T(8,128)(2,1)S(1)} %bitcast.134, bf16[2,448,1408]{2,1,0:T(8,128)(2,1)S(1)} %copy-done.26), custom_call_target="tpu_custom_call" | custom-call | flops 34359738368 | bytes 134217728 | tf_op jit(solution)/shard_map/pallas_call | solution.py:243
  359.3 5.3 all-to-all-start.9
  366.4 6.6 %shard_map.236 = bf16[2048,1408]{1,0:T(8,128)(2,1)} custom-call(s32[1]{0:T(128)} %constant.110.clone.1.at, bf16[448,2048]{1,0:T(8,128)(2,1)S(1)} %bitcast.135, bf16[2,448,1408]{2,1,0:T(8,128)(2,1)S(1)} %copy-done.27), custom_call_target="tpu_custom_call" | custom-call | flops 34359738368 | bytes 134217728 | tf_op jit(solution)/shard_map/pallas_call | solution.py:243
  374.1 29.5 %all-to-all-done.9 = bf16[16,40,2048]{2,1,0:T(8,128)(2,1)} async-done(((bf16[16,40,2048]{2,1,0:T(8,128)(2,1)}), bf16[16,40,2048]{2,1,0:T(8,128)(2,1)}, u32[]{:S(2)}, u32[]{:S(2)}) %all-to-all-start.9) | async-done | bytes 2621472 | tf_op jit(solution)/shard_map/all_to_all | solution.py:24
  403.7 5.7 %fusion.10.grad_mixed = f32[640,1024]{1,0:T(8,128)S(1)} fusion(bf16[640,2048]{1,0:T(8,128)(2,1)} %bitcast.46.left, bf16[2048,2432]{1,0:T(8,128)(2,1)} %all-gather.3.cloned.1.call-done), kind=kOutput, calls=%fused_computation.19 | convolution fusion | flops 2684354560 | bytes 9437184 | tf_op jit(solution)/shard_map/dot_general | solution.py:813
  409.6 8.4 %shard_map.237 = (bf16[640,1024]{1,0:T(8,128)(2,1)S(1)}, bf16[640,128]{1,0:T(8,128)(2,1)S(1)}, f32[640,256]{1,0:T(8,128)S(1)}, bf16[640,256]{1,0:T(8,128)(2,1)S(1)}) custom-call(f32[640,1024]{1,0:T(8,128)S(1)} %fusion.10.grad_mixed, bf16[4,320,128]{2,1,0:T(8,128)(2,1)S(1)} %copy-done.46, bf16[640,256]{1,0:T(8,128)(2,1)S(1)} %copy-done.19, ...), custom_call_target="tpu_custom_call" | custom-call | flops 10737418240 | bytes 4945920 | tf_op jit(solution)/shard_map/pallas_call | solution.py:228
  418.1 3.8 all-to-all-start.10
  423.2 5.5 shard_map.239
  431.2 8.3 %fusion.14 = bf16[640,2048]{1,0:T(8,128)(2,1)} fusion(bf16[2048,2432]{1,0:T(8,128)(2,1)} %all-gather.3.cloned.1.call-done, bf16[640,128]{1,0:T(8,128)(2,1)S(1)} %get-tuple-element.113, bf16[640,128]{1,0:T(8,128)(2,1)S(1)} %slice.316, bf16[640,128]{1,0:T(8,128)(2,1)S(1)} %fusion.40, bf16[640,1024]{1,0:T(8,128)(2,1)S(1)} %get-tuple-element.110), kind=kOutput, calls=%fused_computation.23 | convolution fusion | flops 3699507200 | bytes 10190848 | tf_op jit(solution)/shard_map/dot_general | solution.py:845
  441.6 4.9 shard_map.238
  446.5 5.7 shard_map.240
  461.7 6.3 %all-to-all-start.11 = ((bf16[16,40,2048]{2,1,0:T(8,128)(2,1)}), bf16[16,40,2048]{2,1,0:T(8,128)(2,1)}, u32[]{:S(2)}, u32[]{:S(2)}) async-start(bf16[16,40,2048]{2,1,0:T(8,128)(2,1)} %bitcast.153), calls=%async_computation.11 | async-start | bytes 5242880 | tf_op jit(solution)/shard_map/all_to_all | solution.py:24
  473.4 5.8 %shard_map.241 = (bf16[256,1408]{1,0:T(8,128)(2,1)S(1)}, bf16[256,1408]{1,0:T(8,128)(2,1)S(1)}, bf16[128,1408]{1,0:T(8,128)(2,1)S(1)}, bf16[128,1408]{1,0:T(8,128)(2,1)S(1)}, bf16[256,1408]{1,0:T(8,128)(2,1)S(1)}) custom-call(s32[2]{0:T(128)S(1)} %pad_add_fusion.3.at, bf16[688,2048]{1,0:T(8,128)(2,1)} %fusion.20.left, bf16[688,1408]{1,0:T(8,128)(2,1)S(1)} %fusion.23.right, ...), custom_call_target="tpu_custom_call" | custom-call | flops 34359738368 | bytes 134217728 | tf_op jit(solution)/shard_map/pallas_call | solution.py:243
  481.7 14.9 %collective-permute-done.13 = bf16[128,1408]{1,0:T(8,128)(2,1)S(1)} collective-permute-done((bf16[128,1408]{1,0:T(8,128)(2,1)S(1)}, bf16[128,1408]{1,0:T(8,128)(2,1)S(1)}, u32[]{:S(2)}, u32[]{:S(2)}) %collective-permute-start.13) | collective-permute-done | bytes 360480 | tf_op jit(solution)/shard_map/ppermute | solution.py:70
  498.3 3.2 collective-permute-done.11
  504.1 10.3 %collective-permute-done.14 = bf16[256,1408]{1,0:T(8,128)(2,1)S(1)} collective-permute-done((bf16[256,1408]{1,0:T(8,128)(2,1)S(1)}, bf16[256,1408]{1,0:T(8,128)(2,1)S(1)}, u32[]{:S(2)}, u32[]{:S(2)}) %collective-permute-start.14) | collective-permute-done | bytes 720928 | tf_op jit(solution)/shard_map/ppermute | solution.py:81
  514.5 4.9 collective-permute-done.12
  534.2 4.1 all-to-all-start.12
  538.4 3.3 bitcast_convert_fusion
  543.9 7.0 %copy.188 = f32[4,2,64,2,1408]{4,3,2,1,0:T(2,128)} copy(f32[4,2,64,2,1408]{4,2,0,1,3:T(8,128)S(1)} %convert_bitcast_fusion) | data formatting | bytes 11534336 | tf_op jit(solution)/shard_map/convert_element_type | solution.py:892
  (397 shorter events, 189.0 us)
Async XLA Ops:
  7.2 94.1 %all-gather.3.cloned.1.call-start = ((), (), s32[]{:S(2)}) async-start(), calls=%async_computation.16 | async-start | bytes 11206656 | tf_op jit(solution)/shard_map/all_gather | solution.py:637
  7.2 38.9 %collective-permute-start = (bf16[1408,512]{1,0:T(8,128)(2,1)}, bf16[1408,512]{1,0:T(8,128)(2,1)S(1)}, u32[]{:S(2)}, u32[]{:S(2)}) collective-permute-start(bf16[1408,512]{1,0:T(8,128)(2,1)} %bitcast.137), channel_id=1, source_target_pairs={{0,32},{32,64},{64,96},{96,0},{1,33},{33,65},{65,97},{97,1},{2,34}... | collective-permute-start | bytes 4325384 | tf_op jit(solution)/shard_map/ppermute | solution.py:622
  9.3 36.8 %collective-permute-start.1 = (bf16[1408,512]{1,0:T(8,128)(2,1)}, bf16[1408,512]{1,0:T(8,128)(2,1)S(1)}, u32[]{:S(2)}, u32[]{:S(2)}) collective-permute-start(bf16[1408,512]{1,0:T(8,128)(2,1)} %bitcast.138), channel_id=1, source_target_pairs={{0,96},{32,0},{64,32},{96,64},{1,97},{33,1},{65,33},{97,65},{2,98}... | collective-permute-start | bytes 4325384 | tf_op jit(solution)/shard_map/ppermute | solution.py:623
  46.1 106.9 %copy-start.13 = (bf16[1408,512]{1,0:T(8,128)(2,1)}, bf16[1408,512]{1,0:T(8,128)(2,1)S(1)}, u32[]{:S(2)}) copy-start(bf16[1408,512]{1,0:T(8,128)(2,1)S(1)} %collective-permute-done.back) | copy-start | bytes 4325380
  46.1 108.5 %copy-start.15 = (bf16[1408,512]{1,0:T(8,128)(2,1)}, bf16[1408,512]{1,0:T(8,128)(2,1)S(1)}, u32[]{:S(2)}) copy-start(bf16[1408,512]{1,0:T(8,128)(2,1)S(1)} %collective-permute-done.1.ahead) | copy-start | bytes 4325380
  56.4 37.3 %all-to-all-start.1 = ((bf16[4,160,2176]{2,1,0:T(8,128)(2,1)}), bf16[4,160,2176]{2,1,0:T(8,128)(2,1)}, u32[]{:S(2)}, u32[]{:S(2)}) async-start(bf16[4,160,2176]{2,1,0:T(8,128)(2,1)} %broadcast_in_dim.44), calls=%async_computation.1 | async-start | bytes 5570560 | tf_op jit(solution)/shard_map/all_to_all | solution.py:24
  61.1 180.0 %all-gather.5.cloned.1.call-start = ((), (), s32[]{:S(2)}) async-start(), calls=%async_computation.17 | async-start | bytes 14417920 | tf_op jit(solution)/shard_map/all_gather | solution.py:682
  61.6 34.5 %copy-start.69 = (f32[2048]{0:T(1024)}, f32[2048]{0:T(1024)S(1)}, u32[]{:S(2)}) copy-start(f32[2048]{0:T(1024)S(1)} %mul.288) | copy-start | bytes 24580
  117.9 30.0 %all-to-all-start.2 = ((bf16[8,56,2176]{2,1,0:T(8,128)(2,1)}), bf16[8,56,2176]{2,1,0:T(8,128)(2,1)}, u32[]{:S(2)}, u32[]{:S(2)}) async-start(bf16[8,56,2176]{2,1,0:T(8,128)(2,1)} %bitcast.159), calls=%async_computation.2 | async-start | bytes 3899392 | tf_op jit(solution)/shard_map/all_to_all | solution.py:24
  126.2 2.0 collective-permute-start.4
  148.0 45.7 %all-to-all-start.3 = ((bf16[16,40,2048]{2,1,0:T(8,128)(2,1)}), bf16[16,40,2048]{2,1,0:T(8,128)(2,1)}, u32[]{:S(2)}, u32[]{:S(2)}) async-start(bf16[16,40,2048]{2,1,0:T(8,128)(2,1)} %bitcast.154), calls=%async_computation.3 | async-start | bytes 5242880 | tf_op jit(solution)/shard_map/all_to_all | solution.py:24
  154.0 35.5 %collective-permute-start.2 = (bf16[1408,256]{1,0:T(8,128)(2,1)}, bf16[1408,256]{1,0:T(8,128)(2,1)S(1)}, u32[]{:S(2)}, u32[]{:S(2)}) collective-permute-start(bf16[1408,256]{1,0:T(8,128)(2,1)} %slice.168), channel_id=1, source_target_pairs={{0,32},{32,64},{64,96},{96,0},{1,33},{33,65},{65,97},{97,1},{2,34}... | collective-permute-start | bytes 2162696 | tf_op jit(solution)/shard_map/ppermute | solution.py:678
  155.6 34.4 %collective-permute-start.3 = (bf16[1408,256]{1,0:T(8,128)(2,1)}, bf16[1408,256]{1,0:T(8,128)(2,1)S(1)}, u32[]{:S(2)}, u32[]{:S(2)}) collective-permute-start(bf16[1408,256]{1,0:T(8,128)(2,1)} %slice.169), channel_id=1, source_target_pairs={{0,96},{32,0},{64,32},{96,64},{1,97},{33,1},{65,33},{97,65},{2,98}... | collective-permute-start | bytes 2162696 | tf_op jit(solution)/shard_map/ppermute | solution.py:679
  160.4 35.6 %copy-start.51 = (f32[40,4,4,2,64]{4,3,2,1,0:T(2,128)}, f32[40,4,4,2,64]{4,3,2,1,0:T(2,128)S(1)}, u32[]{:S(2)}) copy-start(f32[40,4,4,2,64]{4,3,2,1,0:T(2,128)S(1)} %reshape.394) | copy-start | bytes 983044
  163.1 34.1 %copy-start.54 = (f32[40,2048]{1,0:T(8,128)}, f32[40,2048]{1,0:T(8,128)S(1)}, u32[]{:S(2)}) copy-start(f32[40,2048]{1,0:T(8,128)S(1)} %reshape.386) | copy-start | bytes 983044
  196.1 141.9 %copy-start.50 = (f32[40,2048]{1,0:T(8,128)}, f32[40,2048]{1,0:T(8,128)S(1)}, u32[]{:S(2)}) copy-start(f32[40,2048]{1,0:T(8,128)S(1)} %get-tuple-element.211) | copy-start | bytes 983044
  197.2 14.2 %all-to-all-start.4 = ((bf16[4,40,2048]{2,1,0:T(8,128)(2,1)}), bf16[4,40,2048]{2,1,0:T(8,128)(2,1)S(1)}, u32[]{:S(2)}, u32[]{:S(2)}) async-start(bf16[4,40,2048]{2,1,0:T(8,128)(2,1)} %broadcast_in_dim.46), calls=%async_computation.4 | async-start | bytes 1310720 | tf_op jit(solution)/shard_map/all_to_all | solution.py:24
  213.3 27.9 %all-to-all-start.5 = ((bf16[8,56,2048]{2,1,0:T(8,128)(2,1)}), bf16[8,56,2048]{2,1,0:T(8,128)(2,1)S(1)}, u32[]{:S(2)}, u32[]{:S(2)}) async-start(bf16[8,56,2048]{2,1,0:T(8,128)(2,1)} %bitcast.144), calls=%async_computation.5 | async-start | bytes 3670016 | tf_op jit(solution)/shard_map/all_to_all | solution.py:24
  216.9 302.8 %reduce-scatter.4.cloned.1.call-start = ((), (), s32[]{:S(2)}) async-start(), calls=%async_computation.18 | async-start | bytes 7208960 | tf_op jit(solution)/shard_map/reduce_scatter | solution.py:762
  280.6 30.0 %all-to-all-start.6 = ((bf16[8,56,2176]{2,1,0:T(8,128)(2,1)}), bf16[8,56,2176]{2,1,0:T(8,128)(2,1)}, u32[]{:S(2)}, u32[]{:S(2)}) async-start(bf16[8,56,2176]{2,1,0:T(8,128)(2,1)} %bitcast.136), calls=%async_computation.6 | async-start | bytes 3899392 | tf_op jit(solution)/shard_map/all_to_all | solution.py:24
  299.0 24.4 %collective-permute-start.7 = (bf16[448,512]{1,0:T(8,128)(2,1)}, bf16[448,512]{1,0:T(8,128)(2,1)}, u32[]{:S(2)}, u32[]{:S(2)}) collective-permute-start(bf16[448,512]{1,0:T(8,128)(2,1)} %get-tuple-element.217), channel_id=1, source_target_pairs={{0,1},{1,2},{2,3},{3,0},{4,5},{5,6},{6,7},{7,4},{8,9},{9,10},{10,1... | collective-permute-start | bytes 1376264 | tf_op jit(solution)/shard_map/ppermute | solution.py:32
  299.7 23.7 %collective-permute-start.6 = (bf16[448,512]{1,0:T(8,128)(2,1)}, bf16[448,512]{1,0:T(8,128)(2,1)}, u32[]{:S(2)}, u32[]{:S(2)}) collective-permute-start(bf16[448,512]{1,0:T(8,128)(2,1)} %get-tuple-element.218), channel_id=1, source_target_pairs={{0,2},{1,3},{2,0},{3,1},{4,6},{5,7},{6,4},{7,5},{8,10},{9,11},{10,... | collective-permute-start | bytes 1376264 | tf_op jit(solution)/shard_map/ppermute | solution.py:32
  302.0 22.6 %collective-permute-start.5 = (bf16[448,512]{1,0:T(8,128)(2,1)}, bf16[448,512]{1,0:T(8,128)(2,1)}, u32[]{:S(2)}, u32[]{:S(2)}) collective-permute-start(bf16[448,512]{1,0:T(8,128)(2,1)} %get-tuple-element.216), channel_id=1, source_target_pairs={{0,3},{1,0},{2,1},{3,2},{4,7},{5,4},{6,5},{7,6},{8,11},{9,8},{10,9... | collective-permute-start | bytes 1376264 | tf_op jit(solution)/shard_map/ppermute | solution.py:32
  315.0 15.6 %all-to-all-start.7 = ((bf16[4,40,2176]{2,1,0:T(8,128)(2,1)}), bf16[4,40,2176]{2,1,0:T(8,128)(2,1)S(1)}, u32[]{:S(2)}, u32[]{:S(2)}) async-start(bf16[4,40,2176]{2,1,0:T(8,128)(2,1)} %bitcast.152), calls=%async_computation.7 | async-start | bytes 1392640 | tf_op jit(solution)/shard_map/all_to_all | solution.py:24
  331.0 14.1 %all-to-all-start.8 = ((bf16[8,56,512]{2,1,0:T(8,128)(2,1)}), bf16[8,56,512]{2,1,0:T(8,128)(2,1)S(1)}, u32[]{:S(2)}, u32[]{:S(2)}) async-start(bf16[8,56,512]{2,1,0:T(8,128)(2,1)} %bitcast.44), calls=%async_computation.8 | async-start | bytes 917504 | tf_op jit(solution)/shard_map/all_to_all | solution.py:24
  335.4 197.6 %reduce-scatter.6.cloned.1.call-start = ((), (), s32[]{:S(2)}) async-start(), calls=%async_computation.19 | async-start | bytes 7208960 | tf_op jit(solution)/shard_map/reduce_scatter | solution.py:804
  359.3 44.3 %all-to-all-start.9 = ((bf16[16,40,2048]{2,1,0:T(8,128)(2,1)}), bf16[16,40,2048]{2,1,0:T(8,128)(2,1)}, u32[]{:S(2)}, u32[]{:S(2)}) async-start(bf16[16,40,2048]{2,1,0:T(8,128)(2,1)} %broadcast_in_dim.47), calls=%async_computation.9 | async-start | bytes 5242880 | tf_op jit(solution)/shard_map/all_to_all | solution.py:24
  364.7 177.1 %reduce-scatter.8.cloned.1.call-start = ((), (), s32[]{:S(2)}) async-start(), calls=%async_computation.20 | async-start | bytes 7208960 | tf_op jit(solution)/shard_map/reduce_scatter | solution.py:806
  418.0 11.1 %collective-permute-start.8 = (bf16[640,256]{1,0:T(8,128)(2,1)S(1)}, bf16[640,256]{1,0:T(8,128)(2,1)}, u32[]{:S(2)}, u32[]{:S(2)}) collective-permute-start(bf16[640,256]{1,0:T(8,128)(2,1)S(1)} %get-tuple-element.107), channel_id=1, source_target_pairs={{0,4},{4,0},{1,5},{5,1},{2,6},{6,2},{3,7},{7,3},{8,12},{12,8},{9,1... | collective-permute-start | bytes 983048 | tf_op jit(solution)/shard_map/ppermute | solution.py:835
  418.1 11.0 %all-to-all-start.10 = ((bf16[4,40,512]{2,1,0:T(8,128)(2,1)}), bf16[4,40,512]{2,1,0:T(8,128)(2,1)S(1)}, u32[]{:S(2)}, u32[]{:S(2)}) async-start(bf16[4,40,512]{2,1,0:T(8,128)(2,1)} %bitcast.166), calls=%async_computation.10 | async-start | bytes 327680 | tf_op jit(solution)/shard_map/all_to_all | solution.py:24
  428.6 17.9 %collective-permute-start.10 = (bf16[4,256,1024]{2,1,0:T(8,128)(2,1)}, bf16[4,256,1024]{2,1,0:T(8,128)(2,1)}, u32[]{:S(2)}, u32[]{:S(2)}) collective-permute-start(bf16[4,256,1024]{2,1,0:T(8,128)(2,1)} %shard_map.239), channel_id=1, source_target_pairs={{0,4},{4,0},{1,5},{5,1},{2,6},{6,2},{3,7},{7,3},{8,12},{12,8},{9,1... | collective-permute-start | bytes 6291464 | tf_op jit(solution)/shard_map/ppermute | solution.py:833
  446.5 27.0 %collective-permute-start.9 = (bf16[4,256,1408]{2,1,0:T(8,128)(2,1)}, bf16[4,256,1408]{2,1,0:T(8,128)(2,1)}, u32[]{:S(2)}, u32[]{:S(2)}) collective-permute-start(bf16[4,256,1408]{2,1,0:T(8,128)(2,1)} %shard_map.238), channel_id=1, source_target_pairs={{0,4},{4,0},{1,5},{5,1},{2,6},{6,2},{3,7},{7,3},{8,12},{12,8},{9,1... | collective-permute-start | bytes 8650760 | tf_op jit(solution)/shard_map/ppermute | solution.py:853
  452.9 16.7 %collective-permute-start.17 = (bf16[128,1024]{1,0:T(8,128)(2,1)}, bf16[128,1024]{1,0:T(8,128)(2,1)}, u32[]{:S(2)}, u32[]{:S(2)}) collective-permute-start(bf16[128,1024]{1,0:T(8,128)(2,1)} %get-tuple-element.126), channel_id=1, source_target_pairs={{0,96},{32,0},{64,32},{96,64},{1,97},{33,1},{65,33},{97,65},{2,98}... | collective-permute-start | bytes 786440 | tf_op jit(solution)/shard_map/ppermute | solution.py:70
  461.7 58.0 %all-to-all-start.11 = ((bf16[16,40,2048]{2,1,0:T(8,128)(2,1)}), bf16[16,40,2048]{2,1,0:T(8,128)(2,1)}, u32[]{:S(2)}, u32[]{:S(2)}) async-start(bf16[16,40,2048]{2,1,0:T(8,128)(2,1)} %bitcast.153), calls=%async_computation.11 | async-start | bytes 5242880 | tf_op jit(solution)/shard_map/all_to_all | solution.py:24
  469.0 10.5 %collective-permute-start.15 = (bf16[128,1024]{1,0:T(8,128)(2,1)}, bf16[128,1024]{1,0:T(8,128)(2,1)S(1)}, u32[]{:S(2)}, u32[]{:S(2)}) collective-permute-start(bf16[128,1024]{1,0:T(8,128)(2,1)} %copy-done.37), channel_id=1, source_target_pairs={{0,32},{32,64},{64,96},{96,0},{1,33},{33,65},{65,97},{97,1},{2,34}... | collective-permute-start | bytes 786440 | tf_op jit(solution)/shard_map/ppermute | solution.py:69
  470.6 32.5 %collective-permute-start.18 = (bf16[256,1024]{1,0:T(8,128)(2,1)S(1)}, bf16[256,1024]{1,0:T(8,128)(2,1)S(1)}, u32[]{:S(2)}, u32[]{:S(2)}) collective-permute-start(bf16[256,1024]{1,0:T(8,128)(2,1)S(1)} %pad_maximum_fusion.7), channel_id=1, source_target_pairs={{0,96},{32,0},{64,32},{96,64},{1,97},{33,1},{65,33},{97,65},{2,98}... | collective-permute-start | bytes 1572872 | tf_op jit(solution)/shard_map/ppermute | solution.py:81
  479.2 17.3 %collective-permute-start.13 = (bf16[128,1408]{1,0:T(8,128)(2,1)S(1)}, bf16[128,1408]{1,0:T(8,128)(2,1)S(1)}, u32[]{:S(2)}, u32[]{:S(2)}) collective-permute-start(bf16[128,1408]{1,0:T(8,128)(2,1)S(1)} %get-tuple-element.122), channel_id=1, source_target_pairs={{0,96},{32,0},{64,32},{96,64},{1,97},{33,1},{65,33},{97,65},{2,98}... | collective-permute-start | bytes 1081352 | tf_op jit(solution)/shard_map/ppermute | solution.py:70
  479.6 23.5 %collective-permute-start.16 = (bf16[256,1024]{1,0:T(8,128)(2,1)S(1)}, bf16[256,1024]{1,0:T(8,128)(2,1)S(1)}, u32[]{:S(2)}, u32[]{:S(2)}) collective-permute-start(bf16[256,1024]{1,0:T(8,128)(2,1)S(1)} %pad_maximum_fusion.6), channel_id=1, source_target_pairs={{0,32},{32,64},{64,96},{96,0},{1,33},{33,65},{65,97},{97,1},{2,34}... | collective-permute-start | bytes 1572872 | tf_op jit(solution)/shard_map/ppermute | solution.py:80
  481.6 19.9 %collective-permute-start.11 = (bf16[128,1408]{1,0:T(8,128)(2,1)S(1)}, bf16[128,1408]{1,0:T(8,128)(2,1)S(1)}, u32[]{:S(2)}, u32[]{:S(2)}) collective-permute-start(bf16[128,1408]{1,0:T(8,128)(2,1)S(1)} %get-tuple-element.120), channel_id=1, source_target_pairs={{0,32},{32,64},{64,96},{96,0},{1,33},{33,65},{65,97},{97,1},{2,34}... | collective-permute-start | bytes 1081352 | tf_op jit(solution)/shard_map/ppermute | solution.py:69
  496.7 17.7 %collective-permute-start.14 = (bf16[256,1408]{1,0:T(8,128)(2,1)S(1)}, bf16[256,1408]{1,0:T(8,128)(2,1)S(1)}, u32[]{:S(2)}, u32[]{:S(2)}) collective-permute-start(bf16[256,1408]{1,0:T(8,128)(2,1)S(1)} %pad_maximum_fusion.5), channel_id=1, source_target_pairs={{0,96},{32,0},{64,32},{96,64},{1,97},{33,1},{65,33},{97,65},{2,98}... | collective-permute-start | bytes 2162696 | tf_op jit(solution)/shard_map/ppermute | solution.py:81
  501.6 17.7 %collective-permute-start.12 = (bf16[256,1408]{1,0:T(8,128)(2,1)S(1)}, bf16[256,1408]{1,0:T(8,128)(2,1)S(1)}, u32[]{:S(2)}, u32[]{:S(2)}) collective-permute-start(bf16[256,1408]{1,0:T(8,128)(2,1)S(1)} %pad_maximum_fusion.4), channel_id=1, source_target_pairs={{0,32},{32,64},{64,96},{96,0},{1,33},{33,65},{65,97},{97,1},{2,34}... | collective-permute-start | bytes 2162696 | tf_op jit(solution)/shard_map/ppermute | solution.py:80
  528.8 22.1 %collective-permute-start.19 = (bf16[64,2432]{1,0:T(8,128)(2,1)}, bf16[64,2432]{1,0:T(8,128)(2,1)S(1)}, u32[]{:S(2)}, u32[]{:S(2)}) collective-permute-start(bf16[64,2432]{1,0:T(8,128)(2,1)} %get-tuple-element.223), channel_id=1, source_target_pairs={{0,24},{8,0},{16,8},{24,16},{1,25},{9,1},{17,9},{25,17},{2,26},{10... | collective-permute-start | bytes 933896 | tf_op jit(solution)/shard_map/ppermute | solution.py:32
  531.2 19.6 %collective-permute-start.20 = (bf16[64,2432]{1,0:T(8,128)(2,1)}, bf16[64,2432]{1,0:T(8,128)(2,1)S(1)}, u32[]{:S(2)}, u32[]{:S(2)}) collective-permute-start(bf16[64,2432]{1,0:T(8,128)(2,1)} %get-tuple-element.222), channel_id=1, source_target_pairs={{0,16},{8,24},{16,0},{24,8},{1,17},{9,25},{17,1},{25,9},{2,18},{10... | collective-permute-start | bytes 933896 | tf_op jit(solution)/shard_map/ppermute | solution.py:32
  532.0 18.9 %collective-permute-start.21 = (bf16[64,2432]{1,0:T(8,128)(2,1)S(1)}, bf16[64,2432]{1,0:T(8,128)(2,1)S(1)}, u32[]{:S(2)}, u32[]{:S(2)}) collective-permute-start(bf16[64,2432]{1,0:T(8,128)(2,1)S(1)} %get-tuple-element.221), channel_id=1, source_target_pairs={{0,8},{8,16},{16,24},{24,0},{1,9},{9,17},{17,25},{25,1},{2,10},{10... | collective-permute-start | bytes 933896 | tf_op jit(solution)/shard_map/ppermute | solution.py:32
  534.2 19.8 %all-to-all-start.12 = ((bf16[4,40,4096]{2,1,0:T(8,128)(2,1)}), bf16[4,40,4096]{2,1,0:T(8,128)(2,1)S(1)}, u32[]{:S(2)}, u32[]{:S(2)}) async-start(bf16[4,40,4096]{2,1,0:T(8,128)(2,1)} %broadcast_in_dim.48), calls=%async_computation.14 | async-start | bytes 2621440 | tf_op jit(solution)/shard_map/all_to_all | solution.py:24
  554.1 7.4 %collective-permute-start.24 = (bf16[64,128]{1,0:T(8,128)(2,1)S(1)}, bf16[64,128]{1,0:T(8,128)(2,1)S(1)}, u32[]{:S(2)}, u32[]{:S(2)}) collective-permute-start(bf16[64,128]{1,0:T(8,128)(2,1)S(1)} %add_convert_fusion.8), channel_id=1, source_target_pairs={{0,1},{1,2},{2,3},{3,0},{4,5},{5,6},{6,7},{7,4},{8,9},{9,10},{10,1... | collective-permute-start | bytes 49160 | tf_op jit(solution)/shard_map/ppermute | solution.py:32
  556.2 5.3 collective-permute-start.23
  558.8 3.7 collective-permute-start.22
  (74 other events, 413.9 us)
Sparse Core Ops, SparseCore 0:
  46.3 54.9 all-gather.2
  103.0 125.3 all-gather.4
  271.8 56.5 reduce-scatter.3
  353.7 58.9 reduce-scatter.5
  415.5 68.2 reduce-scatter.7

commit v7 on v6

--- a/solution.py
+++ b/solution.py
@@ -255,36 +255,44 @@
     )(jnp.stack(scalars).astype(jnp.int32), *args)
 
 
-def give_terms(tall, terms, place, core):
-    depth, columns = terms.shape
-
-    def kernel(at, left, right, out):
-        out[0] = lax.dot_general(left[...], right[...], ROWS, preferred_element_type=F32).astype(BF)
-
+def give_terms(pairs, place, core):
+    columns = pairs[0][1].shape[1]
+
+    def kernel(at, *refs):
+        out = refs[-1]
+        total = sum(
+            lax.dot_general(refs[j][...], refs[j + 1][...], ROWS, preferred_element_type=F32)
+            for j in range(0, len(refs) - 1, 2)
+        )
+        out[0] = total.astype(BF)
+
+    specs = []
+    for tall, terms in pairs:
+        specs.append(pl.BlockSpec((tall.shape[0], 256), lambda i, at: (0, 2 * i + 1 - at[1])))
+        specs.append(pl.BlockSpec(terms.shape, lambda i, at: (0, 0)))
     return on_grid(
         kernel,
         (place, core),
         (4,),
-        [
-            pl.BlockSpec((depth, 256), lambda i, at: (0, 2 * i + 1 - at[1])),
-            pl.BlockSpec((depth, columns), lambda i, at: (0, 0)),
-        ],
+        specs,
         pl.BlockSpec((1, 256, columns), lambda i, at: (i, 0, 0)),
         jax.ShapeDtypeStruct((4, 256, columns), BF),
         [],
-        tall,
-        terms,
-    )
-
-
-def keep_terms(tall, terms, landed, place, core):
-    depth, columns = terms.shape
-
-    def kernel(at, left, right, more, own, ahead, low, high, back):
-        total = lax.dot_general(left[...], right[...], ROWS, preferred_element_type=F32).astype(
-            BF
-        ).astype(F32) + more[0].astype(F32)
-        total = total.astype(BF)
+        *[a for pair in pairs for a in pair],
+    )
+
+
+def keep_terms(pairs, landed, place, core):
+    columns = pairs[0][1].shape[1]
+    count = 2 * len(pairs)
+
+    def kernel(at, *refs):
+        more, own, ahead, low, high, back = refs[count:]
+        total = sum(
+            lax.dot_general(refs[j][...], refs[j + 1][...], ROWS, preferred_element_type=F32)
+            for j in range(0, count, 2)
+        )
+        total = (total.astype(BF).astype(F32) + more[0].astype(F32)).astype(BF)
         step = pl.program_id(0)
 
         @pl.when(step == 0)
@@ -307,25 +315,29 @@
     def whole(rows):
         return pl.BlockSpec((rows, columns), lambda i, at: (0, 0))
 
+    specs = []
+    for tall, terms in pairs:
+        specs.append(
+            pl.BlockSpec(
+                (tall.shape[0], 256), lambda i, at: (0, 2 * lax.rem(at[0] + i, 4) + at[1])
+            )
+        )
+        specs.append(pl.BlockSpec(terms.shape, lambda i, at: (0, 0)))
+    specs.append(pl.BlockSpec((1, 256, columns), lambda i, at: (lax.rem(at[0] + i, 4), 0, 0)))
     return on_grid(
         kernel,
         (place, core),
         (4,),
-        [
-            pl.BlockSpec((depth, 256), lambda i, at: (0, 2 * lax.rem(at[0] + i, 4) + at[1])),
-            whole(depth),
-            pl.BlockSpec((1, 256, columns), lambda i, at: (lax.rem(at[0] + i, 4), 0, 0)),
-        ],
+        specs,
         [whole(256), whole(256), whole(128), whole(128), whole(256)],
         [jax.ShapeDtypeStruct((r, columns), BF) for r in (256, 256, 128, 128, 256)],
         [],
-        tall,
-        terms,
+        *[a for pair in pairs for a in pair],
         landed,
     )
 
 
-def half_product(rows, pair, half):
+def gate_up_product(rows, pair):
     def kernel(at, left, right, out):
         out[...] = lax.dot_general(left[...], right[0], ROWS, preferred_element_type=F32).astype(BF)
 
@@ -333,13 +345,13 @@
     return on_grid(
         kernel,
         (jnp.int32(0),),
-        (8,),
+        (2, 8),
         [
-            pl.BlockSpec((depth, 256), lambda i, at: (0, i)),
-            pl.BlockSpec((1, depth, width), lambda i, at: (half, 0, 0)),
+            pl.BlockSpec((depth, 256), lambda h, i, at: (0, i)),
+            pl.BlockSpec((1, depth, width), lambda h, i, at: (h, 0, 0)),
         ],
-        pl.BlockSpec((256, width), lambda i, at: (i, 0)),
-        jax.ShapeDtypeStruct((MODEL_WIDTH, width), BF),
+        pl.BlockSpec((256, width), lambda h, i, at: (i, h)),
+        jax.ShapeDtypeStruct((MODEL_WIDTH, 2 * width), BF),
         [],
         rows,
         pair,
@@ -617,14 +629,14 @@
     plane = ("y", "tensor")
 
     routers_own = jnp.concatenate([attn_router, mlp_router], axis=1)
-    in_own = jnp.concatenate([query_matrix, key_value_weight], axis=1)
     down_own = down_weight[0]
     down_before = lax.ppermute(down_own, "dp", UP)
     down_after = lax.ppermute(down_own, "dp", DOWN)
     mine = exchange(
         jnp.concatenate(
             [
-                heads_first(in_own),
+                heads_first(query_matrix),
+                heads_first(key_value_weight),
                 jnp.broadcast_to(widen(routers_own), (4, 64, HEAD_SIZE)),
                 heads_first(output_matrix),
             ],
@@ -671,8 +683,21 @@
         ROWS,
         preferred_element_type=F32,
     ).astype(BF)
-    all_w, down_before, down_after, xn1, grad_sent = lax.optimization_barrier(
-        (all_w, down_before, down_after, xn1, grad_sent)
+    def places(half):
+        blocks = 2 * jnp.arange(4, dtype=jnp.int32)[:, None] + half
+        return (blocks * count + jnp.arange(count, dtype=jnp.int32)[None, :]).reshape(-1)
+
+    inverse = 10000.0 ** (-(jnp.arange(HEAD_SIZE // 2).astype(F32) * 2.0 / HEAD_SIZE))
+    angle = places(core).astype(F32)[:, None] * inverse[None, :]
+    cosine = jnp.tile(jnp.cos(angle), (1, 2))
+    sine = jnp.concatenate([-jnp.sin(angle), jnp.sin(angle)], axis=1)
+
+    first = x * quarter
+    cot_own = core_first(lax.dynamic_slice_in_dim(cotangent, first, quarter)).astype(F32)
+    all_w, down_before, down_after, xn1, grad_sent, cosine, sine, cot_own = (
+        lax.optimization_barrier(
+            (all_w, down_before, down_after, xn1, grad_sent, cosine, sine, cot_own)
+        )
     )
     in_w, out_w = all_w[:, :1408], all_w[:, 1408:]
     far_a = lax.ppermute(down_before[:, :256], "dp", UP)
@@ -684,10 +709,6 @@
 
     grad_landed = to_experts(grad_sent)
 
-    def places(half):
-        blocks = 2 * jnp.arange(4, dtype=jnp.int32)[:, None] + half
-        return (blocks * count + jnp.arange(count, dtype=jnp.int32)[None, :]).reshape(-1)
-
     of_sequence = lax.dynamic_slice_in_dim(segments, z * sequence, sequence).reshape(4, 2, count)
 
     def meta(half):
@@ -696,11 +717,6 @@
 
     key_meta = jnp.stack([meta(core), meta(1 - core)])
     row_meta = key_meta[0].T
-    inverse = 10000.0 ** (-(jnp.arange(HEAD_SIZE // 2).astype(F32) * 2.0 / HEAD_SIZE))
-    angle = places(core).astype(F32)[:, None] * inverse[None, :]
-    cosine = jnp.tile(jnp.cos(angle), (1, 2))
-    sine = jnp.concatenate([-jnp.sin(angle), jnp.sin(angle)], axis=1)
-
     def swapped(rows):
         return jnp.concatenate([rows[:, 64:], rows[:, :64]], axis=1)
 
@@ -733,21 +749,22 @@
     grad_received = grad_landed[:, :MODEL_WIDTH]
     branch = exchange(branch_part.reshape(16, quarter, MODEL_WIDTH), plane).astype(F32).sum(axis=0)
 
-    first = x * quarter
-    own_values = core_first(lax.dynamic_slice_in_dim(tokens, first, quarter)).astype(F32)
+    own_values = lax.dynamic_slice_in_dim(values, y * count + first, quarter)
     own_factor = rms_scale(own_values)
     hidden = after(own_values, (far_a, far_b)) + branch
     factor_m = rms_scale(hidden)
     xn2_own = (hidden * factor_m * gain_m).astype(BF)
     xn2 = spread(xn2_own, "tensor", 4).reshape(count, MODEL_WIDTH)
     gate_m = pair_gates(jnp.dot(xn2, router_m, preferred_element_type=F32), pick_m)
-    weight_m = gate_m * kept.astype(F32)
 
     received = to_experts(
         lax.dot_general(any_row, xn2, ROWS, preferred_element_type=F32).astype(BF)
     )
     grad_act_raw = down_back(grad_received, down_pieces, z)
-    received, grad_act_raw = lax.optimization_barrier((received, grad_act_raw))
+    received, grad_act_raw, hidden_last, gate_m = lax.optimization_barrier(
+        (received, grad_act_raw, core_last(hidden), gate_m)
+    )
+    weight_m = gate_m * kept.astype(F32)
     activated, grad_pair, row_gate, grad_back = expert_middle(
         received,
         grad_landed[:, MODEL_WIDTH:],
@@ -761,7 +778,9 @@
     grad_down_w = down_product(late_act, grad_received, row_gate)
     down_sum = lax.psum_scatter(grad_down_w, "dp", scatter_dimension=1, tiled=True)
     quarters = expert_quarters(late_act, down_pieces, z, x)
-    late_any = after(any_row, (grad_down_w, quarters))
+    grad_gate_up_w = gate_up_product(received, late_pair)
+    gate_up_sum = lax.psum_scatter(grad_gate_up_w, "dp", scatter_dimension=0, tiled=True)
+    late_any = after(any_row, (grad_down_w, quarters, grad_gate_up_w))
     expert_out = (
         quarters[0].astype(F32)
         + sum(from_ahead(quarters[4 - k], "tensor", k).astype(F32) for k in (1, 2, 3))
@@ -794,20 +813,14 @@
         grad_logit_m, router_m.astype(F32), LAST, preferred_element_type=F32
     )
     grad_norm, gain_m_part = norm_back(grad_xn2, hidden, factor_m, gain_m)
-    grad_hidden = core_first(quarter_of(cotangent)).astype(F32) + grad_norm
+    grad_hidden = cot_own + grad_norm
     grad_sent_back, returned = lax.optimization_barrier((grad_hidden.astype(BF), returned))
     grad_branch = spread(grad_sent_back, plane, 16).reshape(4 * count, MODEL_WIDTH)
 
     fetched = jnp.einsum("jtr,rd->jtd", to_row, returned, preferred_element_type=F32)
     moe_part = jnp.sum(weight_m.T[:, :, None] * fetched, axis=0).astype(BF)
-    grad_gate_w = half_product(after(received, returned), late_pair, 0)
-    gate_sum = lax.psum_scatter(grad_gate_w, "dp", scatter_dimension=0, tiled=True)
-    grad_up_w = half_product(after(received, returned), late_pair, 1)
-    up_sum = lax.psum_scatter(grad_up_w, "dp", scatter_dimension=0, tiled=True)
     width = down_own.shape[0]
-    grad_branch, moe_part, *_ = lax.optimization_barrier(
-        (grad_branch, moe_part, grad_gate_w, grad_up_w)
-    )
+    grad_branch, moe_part = lax.optimization_barrier((grad_branch, moe_part))
     moe_pieces = exchange(moe_part.reshape(4, quarter, MODEL_WIDTH // 4), "tensor")
 
     grad_mixed = jnp.dot(grad_branch, out_w, preferred_element_type=F32)
@@ -830,12 +843,11 @@
         gate_a,
         *shared,
     )
-    out_give = lax.ppermute(give_terms(grad_branch, mixed, z, core), "core", SWAP)
     kv_back, moe_pieces = lax.optimization_barrier(
         (lax.ppermute(grad_kv_give, "core", SWAP), moe_pieces)
     )
     moe = moe_pieces.transpose(1, 0, 2).reshape(quarter, MODEL_WIDTH).astype(F32)
-    output_own = (core_last(hidden) + moe).astype(BF)
+    output_own = (hidden_last + moe).astype(BF)
     own_grad_kv = grad_kv_own + kv_back.astype(F32)
     grad_key = own_grad_kv[:, :HEAD_SIZE]
     grad_kv = jnp.concatenate(
@@ -844,21 +856,23 @@
     grad_in = jnp.concatenate([grad_q_all, grad_kv, grad_logit_a], axis=1)
     grad_xn1_part = lax.dot_general(grad_in, in_w, LAST, preferred_element_type=F32).astype(BF)
     gain_row = jnp.pad(gain_m_part[None].astype(BF), ((0, 7), (0, 0)))
-    tall = jnp.concatenate([xn1, xn2_own, gain_row], axis=0)
+    lane = jnp.arange(1408, dtype=jnp.int32)[None, :]
     router_cols = jnp.pad(grad_logit_m.astype(BF), ((0, 0), (1288, 112)))
-    gain_cols = (
-        (jnp.arange(8)[:, None] == 0) & (jnp.arange(1408)[None, :] == 1296)
-    ).astype(BF)
-    grad_tall = jnp.concatenate([after(grad_in, grad_xn1_part), router_cols, gain_cols], axis=0)
-    in_give = lax.ppermute(give_terms(tall, grad_tall, z, core), "core", SWAP)
-    out_own, *out_rest = keep_terms(
-        grad_branch, mixed, after(out_give, grad_xn1_part), z, core
-    )
+    gain_cols = ((jnp.arange(8)[:, None] == 0) & (lane == 1296)).astype(BF)
+    in_pairs = [
+        (xn1, after(grad_in, grad_xn1_part)),
+        (
+            jnp.concatenate([xn2_own, gain_row], axis=0),
+            jnp.concatenate([router_cols, gain_cols], axis=0),
+        ),
+    ]
+    in_give = lax.ppermute(give_terms(in_pairs, z, core), "core", SWAP)
+    out_pairs = [(grad_branch, after(mixed, in_give))]
+    out_give = lax.ppermute(give_terms(out_pairs, z, core), "core", SWAP)
+    in_own_rows, *in_rest = keep_terms(in_pairs, in_give, z, core)
+    in_ahead, in_back = ring_first(*in_rest, "dp")
+    out_own, *out_rest = keep_terms(out_pairs, out_give, z, core)
     out_ahead, out_back = ring_first(*out_rest, "dp")
-    in_own_rows, *in_rest = keep_terms(
-        tall, grad_tall, after(in_give, out_own), z, core
-    )
-    in_ahead, in_back = ring_first(*in_rest, "dp")
     out_sum = ring_second(out_own, out_ahead, out_back, "dp").astype(BF)
     in_sum = ring_second(in_own_rows, in_ahead, in_back, "dp").astype(BF)
     landed_raw = exchange(grad_xn1_part.reshape(16, quarter, MODEL_WIDTH), plane)
@@ -883,11 +897,9 @@
         [in_sum[:, :1280], out_sum, small_part.astype(BF)], axis=1
     ).reshape(4, 64, 2432)
     y_parts = send_direct(both_sums, "y")
-    ends, gate_sum = lax.optimization_barrier((ends, gate_sum))
     gate_up_grad = (
-        jnp.stack([gate_sum, up_sum], axis=1)
-        .reshape(2, 4, 64, 2, width)
-        .transpose(1, 0, 2, 3, 4)
+        gate_up_sum.reshape(2, 4, 64, 2816)
+        .transpose(1, 0, 2, 3)
         .reshape(1, 512, 2, width)
         .astype(F32)
     )

time: 579 us -> 570 us (0.984)
  other arithmetic: 52.1 us -> 37 us
  waiting for transfers between devices: 152 us -> 164 us
  local copies, waits for them, and re-layouts: 108 us -> 98.9 us
    ppermute x1, waiting for transfers between devices: 0.46 us -> 30.9 us  [body(): far_b = lax.ppermute(down_after[:, 256:], 'dp', DOWN)]
    ppermute x1, waiting for transfers between devices: 26.2 us -> 2.17 us  [body(): far_a = lax.ppermute(down_before[:, :256], 'dp', UP)]
    all_to_all x12, waiting for transfers between devices: 82.9 us -> 75.1 us  [exchange(): return lax.all_to_all(blocks, axis, split_axis=0, concat_axis=0, tiled=True)]
    ppermute x2, waiting for transfers between devices: 14.9 us -> 22.5 us  [ring_first(): high = lax.ppermute(high, axis, DOWN)]
    all_gather x1, waiting for transfers between devices: 1.32 us -> 8.62 us  [body(): lax.all_gather(after(mine, (down_before, down_after)), ('dp', 'core'), ax...]
    ppermute x2, waiting for transfers between devices: 10.3 us -> 3.2 us  [ring_second(): lax.ppermute(back, axis, DOWN).astype(F32)]
    ppermute x9, waiting for transfers between devices: 7.05 us -> 0.17 us  [from_ahead(): return lax.ppermute(block, axis, [(i, (i - steps) % 4) for i in range(4)])]
    unnamed x164 -> x188, local copies, waits for them, and re-layouts: 32.1 us -> 29.2 us
  transfers between devices with their start and end apart: 42 -> 41, of which waited for: 20 -> 21; matrix products, arithmetic and copies ran while one was open for 30% -> 26% of each run, Pallas kernels for 12% -> 13%
where the time goes in v7:
time: 570 us; the launch traced here: 559 us
  waiting for transfers between devices  164 us (29%)
  local copies, waits for them, and re-layouts  98.9 us (17%)
  Pallas kernels  96.3 us (17%)
  starting transfers between devices  85.7 us (15%)
  matrix products  39.8 us (7%)
  other arithmetic  37 us (6%)
  blocking collectives  21.4 us (4%)
  between operations  15.7 us (3%)
    pallas_call x10, Pallas kernels, on_grid(): pl.pallas_call(kernel, out_shape=outs, grid_spec=pltpu.PrefetchScalarGrid...  80.3 us
    all_to_all x12, waiting for transfers between devices, exchange(): return lax.all_to_all(blocks, axis, split_axis=0, concat_axis=0, tiled=True)  75.1 us
    all_to_all x12, starting transfers between devices, exchange(): return lax.all_to_all(blocks, axis, split_axis=0, concat_axis=0, tiled=True)  54.1 us
    ppermute x1, waiting for transfers between devices, body(): far_b = lax.ppermute(down_after[:, 256:], 'dp', DOWN)  30.9 us
    unnamed x188, local copies, waits for them, and re-layouts  29.2 us
    ppermute x2, waiting for transfers between devices, ring_first(): high = lax.ppermute(high, axis, DOWN)  22.5 us
    all_to_all x1, blocking collectives, exchange(): return lax.all_to_all(blocks, axis, split_axis=0, concat_axis=0, tiled=True)  21.4 us
    pallas_call x2, Pallas kernels, in_vmem(): pl.pallas_call(kernel, out_shape=outs, in_specs=[spec] * len(args), out_s...  16 us
  transfers between devices with their start and end apart: 41, of which 21 were waited for; matrix products, arithmetic and copies ran while one was open for 26% of the time, Pallas kernels for 13%

profile of v7, /device:TPU:0, one launch (start us, length us, event | category | flops | bytes accessed | tf_op | source)
XLA Modules:
  0.0 559.1 jit_solution(7296073181168097930)
XLA Ops:
  7.2 4.2 collective-permute-start.1
  19.9 21.4 %all_to_all.65 = bf16[4,64,2432]{2,1,0:T(8,128)(2,1)} all-to-all(bf16[4,64,2432]{2,1,0:T(8,128)(2,1)S(1)} %pad_maximum_fusion.1), channel_id=1, replica_groups=mesh['dp'=4,'y'=4,'core'=2,'tensor'=4] {'y'}, dimensions={0} | all-to-all | bytes 2490368 | tf_op jit(solution)/shard_map/all_to_all | solution.py:24
  42.6 3.3 collective-permute-done.back
  51.8 4.6 all-to-all-start.1
  67.1 7.4 %reshape.363 = bf16[4,2,64,2816]{3,2,1,0:T(8,128)(2,1)} reshape(bf16[1,512,2,1408]{3,2,1,0:T(2,128)(2,1)} %param.24) | data formatting | bytes 5767168 | tf_op jit(solution)/shard_map/reshape | solution.py:706
  74.6 3.7 copy.170
  81.9 7.0 %all-to-all-done.1 = bf16[4,160,2176]{2,1,0:T(8,128)(2,1)S(1)} async-done(((bf16[4,160,2176]{2,1,0:T(8,128)(2,1)}), bf16[4,160,2176]{2,1,0:T(8,128)(2,1)S(1)}, u32[]{:S(2)}, u32[]{:S(2)}) %all-to-all-start.1) | async-done | bytes 2785312 | tf_op jit(solution)/shard_map/all_to_all | solution.py:24
  92.9 8.6 %all-gather.3.cloned.1.call-done = bf16[2048,2432]{1,0:T(8,128)(2,1)} async-done(((bf16[256,2432]{1,0:T(8,128)(2,1)}), bf16[2048,2432]{1,0:T(8,128)(2,1)}) %all-gather.3.cloned.1.call-update) | async-done | bytes 9961488 | tf_op jit(solution)/shard_map/all_gather | solution.py:649
  105.7 4.6 all-to-all-start.2
  110.3 6.6 %fusion.2.proj = f32[640,1408]{1,0:T(8,128)S(1)} fusion(bf16[640,2048]{1,0:T(8,128)(2,1)S(1)} %multiply_convert_fusion.refs_0_, bf16[2048,2432]{1,0:T(8,128)(2,1)} %all-gather.3.cloned.1.call-done), kind=kOutput, calls=%fused_computation.7 | convolution fusion | flops 3690987520 | bytes 11993088 | tf_op jit(solution)/shard_map/dot_general | solution.py:724
  119.4 6.9 %shard_map.230 = (bf16[4,320,128]{2,1,0:T(8,128)(2,1)S(1)}, f32[4,320,128]{2,1,0:T(8,128)S(1)}, f32[4,320,1]{2,1,0:T(8,128)S(1)}, f32[640,2]{1,0:T(8,128)S(1)}, bf16[640,1024]{1,0:T(8,128)(2,1)S(1)}) custom-call(f32[640,1408]{1,0:T(8,128)S(1)} %fusion.2.proj, bf16[640,256]{1,0:T(8,128)(2,1)S(1)} %pad_maximum_fusion.8.own, ...), custom_call_target="tpu_custom_call" | custom-call | flops 1610612736 | bytes 4935680 | tf_op jit(solution)/shard_map/pallas_call | solution.py:228
  129.5 7.0 %fusion.11 = bf16[640,2048]{1,0:T(8,128)(2,1)} fusion(bf16[640,1024]{1,0:T(8,128)(2,1)S(1)} %get-tuple-element.125.refs_1_, bf16[2048,2432]{1,0:T(8,128)(2,1)} %all-gather.3.cloned.1.call-done), kind=kOutput, calls=%fused_computation.15 | convolution fusion | flops 2685665280 | bytes 8126464 | tf_op jit(solution)/shard_map/dot_general | solution.py:747
  136.5 7.5 %all-to-all-start.3 = ((bf16[16,40,2048]{2,1,0:T(8,128)(2,1)}), bf16[16,40,2048]{2,1,0:T(8,128)(2,1)}, u32[]{:S(2)}, u32[]{:S(2)}) async-start(bf16[16,40,2048]{2,1,0:T(8,128)(2,1)} %bitcast.157), calls=%async_computation.3 | async-start | bytes 5242880 | tf_op jit(solution)/shard_map/all_to_all | solution.py:24
  147.5 30.9 %collective-permute-done.3.far_b = bf16[1408,256]{1,0:T(8,128)(2,1)S(1)} collective-permute-done((bf16[1408,256]{1,0:T(8,128)(2,1)S(1)}, bf16[1408,256]{1,0:T(8,128)(2,1)S(1)}, u32[]{:S(2)}, u32[]{:S(2)}) %collective-permute-start.3) | collective-permute-done | bytes 720928 | tf_op jit(solution)/shard_map/ppermute | solution.py:704
  181.4 3.2 all-to-all-done.3
  188.2 3.5 all-to-all-start.4
  196.3 5.6 %all-to-all-done.4 = bf16[4,40,2048]{2,1,0:T(8,128)(2,1)S(1)} async-done(((bf16[4,40,2048]{2,1,0:T(8,128)(2,1)}), bf16[4,40,2048]{2,1,0:T(8,128)(2,1)S(1)}, u32[]{:S(2)}, u32[]{:S(2)}) %all-to-all-start.4) | async-done | bytes 655392 | tf_op jit(solution)/shard_map/all_to_all | solution.py:24
  203.9 3.6 all-to-all-start.5
  212.7 9.5 %shard_map.231.grad_ref = f32[448,1408]{1,0:T(8,128)} custom-call(s32[1]{0:T(128)} %bitcast.29.at, bf16[448,2048]{1,0:T(8,128)(2,1)} %slice.227.left.right, bf16[1408,512]{1,0:T(8,128)(2,1)S(1)} %bitcast.139, bf16[1408,512]{1,0:T(8,128)(2,1)S(1)} %copy-done.16, bf16[1408,256]{1,0:T(8,128)(2,1)S(1)} %copy-done.41, ...), custom_call_target="tpu_custom_call" | custom-call | flops 34359738368 | bytes 134217728 | tf_op jit(solution)/shard_map/pallas_call | solution.py:243
  231.8 22.7 %shard_map.232 = (bf16[448,1408]{1,0:T(8,128)(2,1)S(1)}, bf16[2,448,1408]{2,1,0:T(8,128)(2,1)}, f32[448,1]{1,0:T(8,128)S(1)}, bf16[448,2176]{1,0:T(8,128)(2,1)S(1)}) custom-call(s32[1]{0:T(128)} %bitcast.31.at, bf16[448,2048]{1,0:T(8,128)(2,1)S(1)} %bitcast.131, bf16[448,128]{1,0:T(8,128)(2,1)S(1)} %slice.228.marks_ref, ...), custom_call_target="tpu_custom_call" | custom-call | flops 10334765056 | bytes 16777216 | tf_op jit(solution)/shard_map/pallas_call | solution.py:243
  256.8 4.5 all-to-all-start.6
  262.9 5.3 shard_map.233
  274.5 6.8 %shard_map.234 = bf16[4,448,512]{2,1,0:T(8,128)(2,1)} custom-call(s32[2]{0:T(128)S(1)} %pad_add_fusion.2.at, bf16[448,1408]{1,0:T(8,128)(2,1)S(1)} %copy-done.37, bf16[1408,512]{1,0:T(8,128)(2,1)S(1)} %bitcast.140, bf16[1408,512]{1,0:T(8,128)(2,1)S(1)} %copy-done.17, bf16[1408,256]{1,0:T(8,128)(2,1)S(1)} %copy-done.42, bf16[1408,256]{1,0:T(8,128)(2,1)S(1)} %copy-done.39, ...), custom_call_target="tpu_custom_call" | custom-call | flops 34359738368 | bytes 134217728 | tf_op jit(solution)/shard_map/pallas_call | solution.py:243
  286.1 13.1 %shard_map.235 = bf16[2048,2816]{1,0:T(8,128)(2,1)} custom-call(s32[1]{0:T(128)} %constant.113.clone.1.at, bf16[448,2048]{1,0:T(8,128)(2,1)S(1)} %bitcast.132, bf16[2,448,1408]{2,1,0:T(8,128)(2,1)S(1)} %copy-done.32), custom_call_target="tpu_custom_call" | custom-call | flops 34359738368 | bytes 134217728 | tf_op jit(solution)/shard_map/pallas_call | solution.py:243
  303.5 4.6 all-to-all-start.7
  310.5 8.7 %all-to-all-done.7 = bf16[4,40,2176]{2,1,0:T(8,128)(2,1)S(1)} async-done(((bf16[4,40,2176]{2,1,0:T(8,128)(2,1)}), bf16[4,40,2176]{2,1,0:T(8,128)(2,1)S(1)}, u32[]{:S(2)}, u32[]{:S(2)}) %all-to-all-start.7) | async-done | bytes 696352 | tf_op jit(solution)/shard_map/all_to_all | solution.py:24
  319.7 4.5 all-to-all-start.8
  327.5 6.3 %all-to-all-done.8 = bf16[8,56,512]{2,1,0:T(8,128)(2,1)S(1)} async-done(((bf16[8,56,512]{2,1,0:T(8,128)(2,1)}), bf16[8,56,512]{2,1,0:T(8,128)(2,1)S(1)}, u32[]{:S(2)}, u32[]{:S(2)}) %all-to-all-start.8) | async-done | bytes 458784 | tf_op jit(solution)/shard_map/all_to_all | solution.py:24
  335.6 3.9 all-to-all-start.9
  341.5 37.9 %all-to-all-done.9 = bf16[16,40,2048]{2,1,0:T(8,128)(2,1)S(1)} async-done(((bf16[16,40,2048]{2,1,0:T(8,128)(2,1)}), bf16[16,40,2048]{2,1,0:T(8,128)(2,1)S(1)}, u32[]{:S(2)}, u32[]{:S(2)}) %all-to-all-start.9) | async-done | bytes 2621472 | tf_op jit(solution)/shard_map/all_to_all | solution.py:24
  379.5 5.7 %fusion.4.grad_mixed = f32[640,1024]{1,0:T(8,128)S(1)} fusion(bf16[640,2048]{1,0:T(8,128)(2,1)S(1)} %bitcast.133, bf16[2048,2432]{1,0:T(8,128)(2,1)} %all-gather.3.cloned.1.call-done), kind=kOutput, calls=%fused_computation.10 | convolution fusion | flops 2684354560 | bytes 9437184 | tf_op jit(solution)/shard_map/dot_general | solution.py:826
  385.4 9.1 %shard_map.236 = (bf16[640,1024]{1,0:T(8,128)(2,1)S(1)}, bf16[640,128]{1,0:T(8,128)(2,1)S(1)}, f32[640,256]{1,0:T(8,128)S(1)}, bf16[640,256]{1,0:T(8,128)(2,1)}) custom-call(f32[640,1024]{1,0:T(8,128)S(1)} %fusion.4.grad_mixed, bf16[4,320,128]{2,1,0:T(8,128)(2,1)S(1)} %copy-done.53, bf16[640,256]{1,0:T(8,128)(2,1)S(1)} %copy-done.22, ...), custom_call_target="tpu_custom_call" | custom-call | flops 10737418240 | bytes 4945920 | tf_op jit(solution)/shard_map/pallas_call | solution.py:228
  397.1 4.2 all-to-all-start.10
  402.0 5.9 %all-to-all-done.10 = bf16[4,40,512]{2,1,0:T(8,128)(2,1)} async-done(((bf16[4,40,512]{2,1,0:T(8,128)(2,1)}), bf16[4,40,512]{2,1,0:T(8,128)(2,1)}, u32[]{:S(2)}, u32[]{:S(2)}) %all-to-all-start.10) | async-done | bytes 163872 | tf_op jit(solution)/shard_map/all_to_all | solution.py:24
  409.7 8.3 %fusion.8 = bf16[640,2048]{1,0:T(8,128)(2,1)} fusion(bf16[2048,2432]{1,0:T(8,128)(2,1)} %all-gather.3.cloned.1.call-done, bf16[640,128]{1,0:T(8,128)(2,1)S(1)} %copy-done.28, bf16[640,128]{1,0:T(8,128)(2,1)S(1)} %slice.319, bf16[640,128]{1,0:T(8,128)(2,1)S(1)} %fusion.32, bf16[640,1024]{1,0:T(8,128)(2,1)S(1)} %copy-done.12), kind=kOutput, calls=%fused_computation.14 | convolution fusion | flops 3699507200 | bytes 10190848 | tf_op jit(solution)/shard_map/dot_general | solution.py:857
  419.7 5.6 shard_map.237
  426.4 4.5 all-to-all-start.11
  432.4 3.2 shard_map.239
  436.1 6.4 %shard_map.238 = (bf16[256,1408]{1,0:T(8,128)(2,1)S(1)}, bf16[256,1408]{1,0:T(8,128)(2,1)S(1)}, bf16[128,1408]{1,0:T(8,128)(2,1)S(1)}, bf16[128,1408]{1,0:T(8,128)(2,1)S(1)}, bf16[256,1408]{1,0:T(8,128)(2,1)S(1)}) custom-call(s32[2]{0:T(128)S(1)} %pad_add_fusion.3.at, bf16[640,2048]{1,0:T(8,128)(2,1)} %copy-done.5, bf16[640,1408]{1,0:T(8,128)(2,1)S(1)} %copy-done.10, ...), custom_call_target="tpu_custom_call" | custom-call | flops 34359738368 | bytes 134217728 | tf_op jit(solution)/shard_map/pallas_call | solution.py:243
  445.5 8.1 %collective-permute-done.12 = bf16[128,1408]{1,0:T(8,128)(2,1)S(1)} collective-permute-done((bf16[128,1408]{1,0:T(8,128)(2,1)S(1)}, bf16[128,1408]{1,0:T(8,128)(2,1)S(1)}, u32[]{:S(2)}, u32[]{:S(2)}) %collective-permute-start.12) | collective-permute-done | bytes 360480 | tf_op jit(solution)/shard_map/ppermute | solution.py:70
  455.2 4.6 shard_map.240
  462.8 14.5 %collective-permute-done.17 = bf16[128,1024]{1,0:T(8,128)(2,1)S(1)} collective-permute-done((bf16[128,1024]{1,0:T(8,128)(2,1)S(1)}, bf16[128,1024]{1,0:T(8,128)(2,1)S(1)}, u32[]{:S(2)}, u32[]{:S(2)}) %collective-permute-start.17) | collective-permute-done | bytes 262176 | tf_op jit(solution)/shard_map/ppermute | solution.py:70
  479.9 6.5 %collective-permute-done.15 = bf16[128,1024]{1,0:T(8,128)(2,1)S(1)} collective-permute-done((bf16[128,1024]{1,0:T(8,128)(2,1)S(1)}, bf16[128,1024]{1,0:T(8,128)(2,1)S(1)}, u32[]{:S(2)}, u32[]{:S(2)}) %collective-permute-start.15) | collective-permute-done | bytes 262176 | tf_op jit(solution)/shard_map/ppermute | solution.py:69
  487.1 3.2 collective-permute-done.18
  490.3 10.0 %collective-permute-done.16 = bf16[256,1024]{1,0:T(8,128)(2,1)S(1)} collective-permute-done((bf16[256,1024]{1,0:T(8,128)(2,1)S(1)}, bf16[256,1024]{1,0:T(8,128)(2,1)S(1)}, u32[]{:S(2)}, u32[]{:S(2)}) %collective-permute-start.16) | collective-permute-done | bytes 524320 | tf_op jit(solution)/shard_map/ppermute | solution.py:80
  518.2 4.2 all-to-all-start.12
  522.4 3.3 bitcast_convert_fusion
  531.1 7.8 %reshape.381 = f32[1,512,2,1408]{3,2,1,0:T(2,128)} reshape(f32[4,2,64,2816]{3,2,1,0:T(8,128)} %copy.180) | data formatting | bytes 11534336 | tf_op jit(solution)/shard_map/convert_element_type | solution.py:904
  (418 shorter events, 161.0 us)
Async XLA Ops:
  7.2 94.3 %all-gather.3.cloned.1.call-start = ((), (), s32[]{:S(2)}) async-start(), calls=%async_computation.15 | async-start | bytes 11206656 | tf_op jit(solution)/shard_map/all_gather | solution.py:649
  7.2 35.3 %collective-permute-start.1 = (bf16[1408,512]{1,0:T(8,128)(2,1)}, bf16[1408,512]{1,0:T(8,128)(2,1)S(1)}, u32[]{:S(2)}, u32[]{:S(2)}) collective-permute-start(bf16[1408,512]{1,0:T(8,128)(2,1)} %bitcast.137), channel_id=1, source_target_pairs={{0,96},{32,0},{64,32},{96,64},{1,97},{33,1},{65,33},{97,65},{2,98}... | collective-permute-start | bytes 4325384 | tf_op jit(solution)/shard_map/ppermute | solution.py:634
  11.4 34.5 %collective-permute-start = (bf16[1408,512]{1,0:T(8,128)(2,1)}, bf16[1408,512]{1,0:T(8,128)(2,1)S(1)}, u32[]{:S(2)}, u32[]{:S(2)}) collective-permute-start(bf16[1408,512]{1,0:T(8,128)(2,1)} %bitcast.138), channel_id=1, source_target_pairs={{0,32},{32,64},{64,96},{96,0},{1,33},{33,65},{65,97},{97,1},{2,34}... | collective-permute-start | bytes 4325384 | tf_op jit(solution)/shard_map/ppermute | solution.py:633
  51.8 37.1 %all-to-all-start.1 = ((bf16[4,160,2176]{2,1,0:T(8,128)(2,1)}), bf16[4,160,2176]{2,1,0:T(8,128)(2,1)S(1)}, u32[]{:S(2)}, u32[]{:S(2)}) async-start(bf16[4,160,2176]{2,1,0:T(8,128)(2,1)} %broadcast_in_dim.45), calls=%async_computation.1 | async-start | bytes 5570560 | tf_op jit(solution)/shard_map/all_to_all | solution.py:24
  56.4 175.5 %all-gather.5.cloned.1.call-start = ((), (), s32[]{:S(2)}) async-start(), calls=%async_computation.16 | async-start | bytes 14417920 | tf_op jit(solution)/shard_map/all_gather | solution.py:707
  56.9 33.6 %copy-start.76 = (f32[2048]{0:T(1024)}, f32[2048]{0:T(1024)S(1)}, u32[]{:S(2)}) copy-start(f32[2048]{0:T(1024)S(1)} %mul.285) | copy-start | bytes 24580
  57.2 134.5 %copy-start.83 = (s32[2,160]{1,0:T(2,128)}, s32[2,160]{1,0:T(2,128)S(1)}, u32[]{:S(2)}) copy-start(s32[2,160]{1,0:T(2,128)S(1)} %copy.150) | copy-start | bytes 3844
  79.2 40.1 %copy-start.2 = (f32[640,128]{1,0:T(8,128)}, f32[640,128]{1,0:T(8,128)S(1)}, u32[]{:S(2)}) copy-start(f32[640,128]{1,0:T(8,128)S(1)} %pad_maximum_fusion.7.sine) | copy-start | bytes 983044
  105.7 30.7 %all-to-all-start.2 = ((bf16[8,56,2176]{2,1,0:T(8,128)(2,1)}), bf16[8,56,2176]{2,1,0:T(8,128)(2,1)}, u32[]{:S(2)}, u32[]{:S(2)}) async-start(bf16[8,56,2176]{2,1,0:T(8,128)(2,1)} %bitcast.160), calls=%async_computation.2 | async-start | bytes 3899392 | tf_op jit(solution)/shard_map/all_to_all | solution.py:24
  117.4 2.0 collective-permute-start.4
  136.5 48.2 %all-to-all-start.3 = ((bf16[16,40,2048]{2,1,0:T(8,128)(2,1)}), bf16[16,40,2048]{2,1,0:T(8,128)(2,1)}, u32[]{:S(2)}, u32[]{:S(2)}) async-start(bf16[16,40,2048]{2,1,0:T(8,128)(2,1)} %bitcast.157), calls=%async_computation.3 | async-start | bytes 5242880 | tf_op jit(solution)/shard_map/all_to_all | solution.py:24
  144.2 43.0 %copy-start.78 = (f32[2048]{0:T(1024)}, f32[2048]{0:T(1024)S(1)}, u32[]{:S(2)}) copy-start(f32[2048]{0:T(1024)S(1)} %reshape.378) | copy-start | bytes 24580
  144.3 34.1 %collective-permute-start.3 = (bf16[1408,256]{1,0:T(8,128)(2,1)S(1)}, bf16[1408,256]{1,0:T(8,128)(2,1)S(1)}, u32[]{:S(2)}, u32[]{:S(2)}) collective-permute-start(bf16[1408,256]{1,0:T(8,128)(2,1)S(1)} %slice.171), channel_id=1, source_target_pairs={{0,96},{32,0},{64,32},{96,64},{1,97},{33,1},{65,33},{97,65},{2,98}... | collective-permute-start | bytes 2162696 | tf_op jit(solution)/shard_map/ppermute | solution.py:704
  145.0 35.6 %collective-permute-start.2 = (bf16[1408,256]{1,0:T(8,128)(2,1)S(1)}, bf16[1408,256]{1,0:T(8,128)(2,1)S(1)}, u32[]{:S(2)}, u32[]{:S(2)}) collective-permute-start(bf16[1408,256]{1,0:T(8,128)(2,1)S(1)} %slice.170), channel_id=1, source_target_pairs={{0,32},{32,64},{64,96},{96,0},{1,33},{33,65},{65,97},{97,1},{2,34}... | collective-permute-start | bytes 2162696 | tf_op jit(solution)/shard_map/ppermute | solution.py:703
  147.5 30.9 %copy-start.61 = (f32[640,2048]{1,0:T(8,128)}, f32[640,2048]{1,0:T(8,128)S(1)}, u32[]{:S(2)}) copy-start(f32[640,2048]{1,0:T(8,128)S(1)} %slice_convert_fusion) | copy-start | bytes 15728644
  187.1 36.0 %copy-start.59 = (f32[40,2048]{1,0:T(8,128)}, f32[40,2048]{1,0:T(8,128)S(1)}, u32[]{:S(2)}) copy-start(f32[40,2048]{1,0:T(8,128)S(1)} %get-tuple-element.211) | copy-start | bytes 983044
  188.2 13.8 %all-to-all-start.4 = ((bf16[4,40,2048]{2,1,0:T(8,128)(2,1)}), bf16[4,40,2048]{2,1,0:T(8,128)(2,1)S(1)}, u32[]{:S(2)}, u32[]{:S(2)}) async-start(bf16[4,40,2048]{2,1,0:T(8,128)(2,1)} %broadcast_in_dim.46), calls=%async_computation.4 | async-start | bytes 1310720 | tf_op jit(solution)/shard_map/all_to_all | solution.py:24
  203.9 27.9 %all-to-all-start.5 = ((bf16[8,56,2048]{2,1,0:T(8,128)(2,1)}), bf16[8,56,2048]{2,1,0:T(8,128)(2,1)S(1)}, u32[]{:S(2)}, u32[]{:S(2)}) async-start(bf16[8,56,2048]{2,1,0:T(8,128)(2,1)} %bitcast.148), calls=%async_computation.5 | async-start | bytes 3670016 | tf_op jit(solution)/shard_map/all_to_all | solution.py:24
  256.8 42.3 %all-to-all-start.6 = ((bf16[8,56,2176]{2,1,0:T(8,128)(2,1)}), bf16[8,56,2176]{2,1,0:T(8,128)(2,1)}, u32[]{:S(2)}, u32[]{:S(2)}) async-start(bf16[8,56,2176]{2,1,0:T(8,128)(2,1)} %bitcast.136), calls=%async_computation.6 | async-start | bytes 3899392 | tf_op jit(solution)/shard_map/all_to_all | solution.py:24
  261.3 239.3 %reduce-scatter.3.cloned.1.call-start = ((), (), s32[]{:S(2)}) async-start(), calls=%async_computation.17 | async-start | bytes 7208960 | tf_op jit(solution)/shard_map/reduce_scatter | solution.py:779
  283.7 24.4 %collective-permute-start.5 = (bf16[448,512]{1,0:T(8,128)(2,1)}, bf16[448,512]{1,0:T(8,128)(2,1)S(1)}, u32[]{:S(2)}, u32[]{:S(2)}) collective-permute-start(bf16[448,512]{1,0:T(8,128)(2,1)} %get-tuple-element.214), channel_id=1, source_target_pairs={{0,3},{1,0},{2,1},{3,2},{4,7},{5,4},{6,5},{7,6},{8,11},{9,8},{10,9... | collective-permute-start | bytes 1376264 | tf_op jit(solution)/shard_map/ppermute | solution.py:32
  284.4 23.9 %collective-permute-start.7 = (bf16[448,512]{1,0:T(8,128)(2,1)}, bf16[448,512]{1,0:T(8,128)(2,1)S(1)}, u32[]{:S(2)}, u32[]{:S(2)}) collective-permute-start(bf16[448,512]{1,0:T(8,128)(2,1)} %get-tuple-element.215), channel_id=1, source_target_pairs={{0,1},{1,2},{2,3},{3,0},{4,5},{5,6},{6,7},{7,4},{8,9},{9,10},{10,1... | collective-permute-start | bytes 1376264 | tf_op jit(solution)/shard_map/ppermute | solution.py:32
  285.7 22.6 %collective-permute-start.6 = (bf16[448,512]{1,0:T(8,128)(2,1)S(1)}, bf16[448,512]{1,0:T(8,128)(2,1)}, u32[]{:S(2)}, u32[]{:S(2)}) collective-permute-start(bf16[448,512]{1,0:T(8,128)(2,1)S(1)} %get-tuple-element.216), channel_id=1, source_target_pairs={{0,2},{1,3},{2,0},{3,1},{4,6},{5,7},{6,4},{7,5},{8,10},{9,11},{10,... | collective-permute-start | bytes 1376264 | tf_op jit(solution)/shard_map/ppermute | solution.py:32
  303.5 15.7 %all-to-all-start.7 = ((bf16[4,40,2176]{2,1,0:T(8,128)(2,1)}), bf16[4,40,2176]{2,1,0:T(8,128)(2,1)S(1)}, u32[]{:S(2)}, u32[]{:S(2)}) async-start(bf16[4,40,2176]{2,1,0:T(8,128)(2,1)} %bitcast.39), calls=%async_computation.7 | async-start | bytes 1392640 | tf_op jit(solution)/shard_map/all_to_all | solution.py:24
  319.7 14.1 %all-to-all-start.8 = ((bf16[8,56,512]{2,1,0:T(8,128)(2,1)}), bf16[8,56,512]{2,1,0:T(8,128)(2,1)S(1)}, u32[]{:S(2)}, u32[]{:S(2)}) async-start(bf16[8,56,512]{2,1,0:T(8,128)(2,1)} %bitcast.44), calls=%async_computation.8 | async-start | bytes 917504 | tf_op jit(solution)/shard_map/all_to_all | solution.py:24
  335.6 43.8 %all-to-all-start.9 = ((bf16[16,40,2048]{2,1,0:T(8,128)(2,1)}), bf16[16,40,2048]{2,1,0:T(8,128)(2,1)S(1)}, u32[]{:S(2)}, u32[]{:S(2)}) async-start(bf16[16,40,2048]{2,1,0:T(8,128)(2,1)} %broadcast_in_dim.47), calls=%async_computation.9 | async-start | bytes 5242880 | tf_op jit(solution)/shard_map/all_to_all | solution.py:24
  339.5 186.3 %reduce-scatter.5.cloned.1.call-start = ((), (), s32[]{:S(2)}) async-start(), calls=%async_computation.18 | async-start | bytes 14417920 | tf_op jit(solution)/shard_map/reduce_scatter | solution.py:782
  379.4 51.6 %copy-start.4 = (bf16[16,40,2048]{2,1,0:T(8,128)(2,1)}, bf16[16,40,2048]{2,1,0:T(8,128)(2,1)S(1)}, u32[]{:S(2)}) copy-start(bf16[16,40,2048]{2,1,0:T(8,128)(2,1)S(1)} %all-to-all-done.9) | copy-start | bytes 7864324
  397.1 10.8 %collective-permute-start.8 = (bf16[640,256]{1,0:T(8,128)(2,1)}, bf16[640,256]{1,0:T(8,128)(2,1)}, u32[]{:S(2)}, u32[]{:S(2)}) collective-permute-start(bf16[640,256]{1,0:T(8,128)(2,1)} %get-tuple-element.112), channel_id=1, source_target_pairs={{0,4},{4,0},{1,5},{5,1},{2,6},{6,2},{3,7},{7,3},{8,12},{12,8},{9,1... | collective-permute-start | bytes 983048 | tf_op jit(solution)/shard_map/ppermute | solution.py:847
  397.1 10.8 %all-to-all-start.10 = ((bf16[4,40,512]{2,1,0:T(8,128)(2,1)}), bf16[4,40,512]{2,1,0:T(8,128)(2,1)}, u32[]{:S(2)}, u32[]{:S(2)}) async-start(bf16[4,40,512]{2,1,0:T(8,128)(2,1)} %bitcast.168), calls=%async_computation.10 | async-start | bytes 327680 | tf_op jit(solution)/shard_map/all_to_all | solution.py:24
  425.3 5.6 %collective-permute-start.9 = (bf16[4,256,1408]{2,1,0:T(8,128)(2,1)}, bf16[4,256,1408]{2,1,0:T(8,128)(2,1)}, u32[]{:S(2)}, u32[]{:S(2)}) collective-permute-start(bf16[4,256,1408]{2,1,0:T(8,128)(2,1)} %shard_map.237), channel_id=1, source_target_pairs={{0,4},{4,0},{1,5},{5,1},{2,6},{6,2},{3,7},{7,3},{8,12},{12,8},{9,1... | collective-permute-start | bytes 8650760 | tf_op jit(solution)/shard_map/ppermute | solution.py:869
  426.4 74.2 %all-to-all-start.11 = ((bf16[16,40,2048]{2,1,0:T(8,128)(2,1)}), bf16[16,40,2048]{2,1,0:T(8,128)(2,1)}, u32[]{:S(2)}, u32[]{:S(2)}) async-start(bf16[16,40,2048]{2,1,0:T(8,128)(2,1)} %bitcast.156), calls=%async_computation.11 | async-start | bytes 5242880 | tf_op jit(solution)/shard_map/all_to_all | solution.py:24
  435.6 19.6 %collective-permute-start.14 = (bf16[4,256,1024]{2,1,0:T(8,128)(2,1)S(1)}, bf16[4,256,1024]{2,1,0:T(8,128)(2,1)S(1)}, u32[]{:S(2)}, u32[]{:S(2)}) collective-permute-start(bf16[4,256,1024]{2,1,0:T(8,128)(2,1)S(1)} %shard_map.239), channel_id=1, source_target_pairs={{0,4},{4,0},{1,5},{5,1},{2,6},{6,2},{3,7},{7,3},{8,12},{12,8},{9,1... | collective-permute-start | bytes 6291464 | tf_op jit(solution)/shard_map/ppermute | solution.py:871
  442.5 11.0 %collective-permute-start.12 = (bf16[128,1408]{1,0:T(8,128)(2,1)S(1)}, bf16[128,1408]{1,0:T(8,128)(2,1)S(1)}, u32[]{:S(2)}, u32[]{:S(2)}) collective-permute-start(bf16[128,1408]{1,0:T(8,128)(2,1)S(1)} %get-tuple-element.124), channel_id=1, source_target_pairs={{0,96},{32,0},{64,32},{96,64},{1,97},{33,1},{65,33},{97,65},{2,98}... | collective-permute-start | bytes 1081352 | tf_op jit(solution)/shard_map/ppermute | solution.py:70
  443.9 17.9 %collective-permute-start.10 = (bf16[128,1408]{1,0:T(8,128)(2,1)S(1)}, bf16[128,1408]{1,0:T(8,128)(2,1)S(1)}, u32[]{:S(2)}, u32[]{:S(2)}) collective-permute-start(bf16[128,1408]{1,0:T(8,128)(2,1)S(1)} %get-tuple-element.122), channel_id=1, source_target_pairs={{0,32},{32,64},{64,96},{96,0},{1,33},{33,65},{65,97},{97,1},{2,34}... | collective-permute-start | bytes 1081352 | tf_op jit(solution)/shard_map/ppermute | solution.py:69
  453.7 33.1 %collective-permute-start.13 = (bf16[256,1408]{1,0:T(8,128)(2,1)S(1)}, bf16[256,1408]{1,0:T(8,128)(2,1)S(1)}, u32[]{:S(2)}, u32[]{:S(2)}) collective-permute-start(bf16[256,1408]{1,0:T(8,128)(2,1)S(1)} %pad_maximum_fusion.4), channel_id=1, source_target_pairs={{0,96},{32,0},{64,32},{96,64},{1,97},{33,1},{65,33},{97,65},{2,98}... | collective-permute-start | bytes 2162696 | tf_op jit(solution)/shard_map/ppermute | solution.py:81
  459.8 17.5 %collective-permute-start.17 = (bf16[128,1024]{1,0:T(8,128)(2,1)S(1)}, bf16[128,1024]{1,0:T(8,128)(2,1)S(1)}, u32[]{:S(2)}, u32[]{:S(2)}) collective-permute-start(bf16[128,1024]{1,0:T(8,128)(2,1)S(1)} %get-tuple-element.130), channel_id=1, source_target_pairs={{0,96},{32,0},{64,32},{96,64},{1,97},{33,1},{65,33},{97,65},{2,98}... | collective-permute-start | bytes 786440 | tf_op jit(solution)/shard_map/ppermute | solution.py:70
  462.0 24.8 %collective-permute-start.11 = (bf16[256,1408]{1,0:T(8,128)(2,1)S(1)}, bf16[256,1408]{1,0:T(8,128)(2,1)S(1)}, u32[]{:S(2)}, u32[]{:S(2)}) collective-permute-start(bf16[256,1408]{1,0:T(8,128)(2,1)S(1)} %pad_maximum_fusion.3), channel_id=1, source_target_pairs={{0,32},{32,64},{64,96},{96,0},{1,33},{33,65},{65,97},{97,1},{2,34}... | collective-permute-start | bytes 2162696 | tf_op jit(solution)/shard_map/ppermute | solution.py:80
  462.2 24.2 %collective-permute-start.15 = (bf16[128,1024]{1,0:T(8,128)(2,1)S(1)}, bf16[128,1024]{1,0:T(8,128)(2,1)S(1)}, u32[]{:S(2)}, u32[]{:S(2)}) collective-permute-start(bf16[128,1024]{1,0:T(8,128)(2,1)S(1)} %get-tuple-element.128), channel_id=1, source_target_pairs={{0,32},{32,64},{64,96},{96,0},{1,33},{33,65},{65,97},{97,1},{2,34}... | collective-permute-start | bytes 786440 | tf_op jit(solution)/shard_map/ppermute | solution.py:69
  477.4 12.9 %collective-permute-start.18 = (bf16[256,1024]{1,0:T(8,128)(2,1)S(1)}, bf16[256,1024]{1,0:T(8,128)(2,1)S(1)}, u32[]{:S(2)}, u32[]{:S(2)}) collective-permute-start(bf16[256,1024]{1,0:T(8,128)(2,1)S(1)} %pad_maximum_fusion.6), channel_id=1, source_target_pairs={{0,96},{32,0},{64,32},{96,64},{1,97},{33,1},{65,33},{97,65},{2,98}... | collective-permute-start | bytes 1572872 | tf_op jit(solution)/shard_map/ppermute | solution.py:81
  486.5 13.9 %collective-permute-start.16 = (bf16[256,1024]{1,0:T(8,128)(2,1)S(1)}, bf16[256,1024]{1,0:T(8,128)(2,1)S(1)}, u32[]{:S(2)}, u32[]{:S(2)}) collective-permute-start(bf16[256,1024]{1,0:T(8,128)(2,1)S(1)} %pad_maximum_fusion.5), channel_id=1, source_target_pairs={{0,32},{32,64},{64,96},{96,0},{1,33},{33,65},{65,97},{97,1},{2,34}... | collective-permute-start | bytes 1572872 | tf_op jit(solution)/shard_map/ppermute | solution.py:80
  511.2 27.7 %collective-permute-start.21 = (bf16[64,2432]{1,0:T(8,128)(2,1)}, bf16[64,2432]{1,0:T(8,128)(2,1)S(1)}, u32[]{:S(2)}, u32[]{:S(2)}) collective-permute-start(bf16[64,2432]{1,0:T(8,128)(2,1)} %get-tuple-element.219), channel_id=1, source_target_pairs={{0,8},{8,16},{16,24},{24,0},{1,9},{9,17},{17,25},{25,1},{2,10},{10... | collective-permute-start | bytes 933896 | tf_op jit(solution)/shard_map/ppermute | solution.py:32
  512.8 26.1 %collective-permute-start.20 = (bf16[64,2432]{1,0:T(8,128)(2,1)}, bf16[64,2432]{1,0:T(8,128)(2,1)S(1)}, u32[]{:S(2)}, u32[]{:S(2)}) collective-permute-start(bf16[64,2432]{1,0:T(8,128)(2,1)} %get-tuple-element.220), channel_id=1, source_target_pairs={{0,16},{8,24},{16,0},{24,8},{1,17},{9,25},{17,1},{25,9},{2,18},{10... | collective-permute-start | bytes 933896 | tf_op jit(solution)/shard_map/ppermute | solution.py:32
  515.5 23.4 %collective-permute-start.19 = (bf16[64,2432]{1,0:T(8,128)(2,1)S(1)}, bf16[64,2432]{1,0:T(8,128)(2,1)S(1)}, u32[]{:S(2)}, u32[]{:S(2)}) collective-permute-start(bf16[64,2432]{1,0:T(8,128)(2,1)S(1)} %get-tuple-element.221), channel_id=1, source_target_pairs={{0,24},{8,0},{16,8},{24,16},{1,25},{9,1},{17,9},{25,17},{2,26},{10... | collective-permute-start | bytes 933896 | tf_op jit(solution)/shard_map/ppermute | solution.py:32
  518.2 20.7 %all-to-all-start.12 = ((bf16[4,40,4096]{2,1,0:T(8,128)(2,1)}), bf16[4,40,4096]{2,1,0:T(8,128)(2,1)S(1)}, u32[]{:S(2)}, u32[]{:S(2)}) async-start(bf16[4,40,4096]{2,1,0:T(8,128)(2,1)} %broadcast_in_dim.48), calls=%async_computation.13 | async-start | bytes 2621440 | tf_op jit(solution)/shard_map/all_to_all | solution.py:24
  538.9 10.5 %collective-permute-start.24 = (bf16[64,128]{1,0:T(8,128)(2,1)S(1)}, bf16[64,128]{1,0:T(8,128)(2,1)S(1)}, u32[]{:S(2)}, u32[]{:S(2)}) collective-permute-start(bf16[64,128]{1,0:T(8,128)(2,1)S(1)} %add_convert_fusion.8), channel_id=1, source_target_pairs={{0,1},{1,2},{2,3},{3,0},{4,5},{5,6},{6,7},{7,4},{8,9},{9,10},{10,1... | collective-permute-start | bytes 49160 | tf_op jit(solution)/shard_map/ppermute | solution.py:32
  541.0 8.4 %collective-permute-start.23 = (bf16[64,128]{1,0:T(8,128)(2,1)S(1)}, bf16[64,128]{1,0:T(8,128)(2,1)S(1)}, u32[]{:S(2)}, u32[]{:S(2)}) collective-permute-start(bf16[64,128]{1,0:T(8,128)(2,1)S(1)} %add_convert_fusion.8), channel_id=1, source_target_pairs={{0,2},{1,3},{2,0},{3,1},{4,6},{5,7},{6,4},{7,5},{8,10},{9,11},{10,... | collective-permute-start | bytes 49160 | tf_op jit(solution)/shard_map/ppermute | solution.py:32
  543.7 5.8 %collective-permute-start.22 = (bf16[64,128]{1,0:T(8,128)(2,1)S(1)}, bf16[64,128]{1,0:T(8,128)(2,1)S(1)}, u32[]{:S(2)}, u32[]{:S(2)}) collective-permute-start(bf16[64,128]{1,0:T(8,128)(2,1)S(1)} %add_convert_fusion.8), channel_id=1, source_target_pairs={{0,3},{1,0},{2,1},{3,2},{4,7},{5,4},{6,5},{7,6},{8,11},{9,8},{10,9... | collective-permute-start | bytes 49160 | tf_op jit(solution)/shard_map/ppermute | solution.py:32
  (85 other events, 535.5 us)
Sparse Core Ops, SparseCore 0:
  46.0 55.4 all-gather.2
  103.8 125.3 all-gather.4
  268.4 58.5 reduce-scatter.2
  342.5 106.2 reduce-scatter.4
